TPU v7x, 32 devices: a whole 2x2x4 slice. The times are simulated.
32 devices in a mesh: gx: 8 (over z, x), gy: 4 (over y, core).
Axes of the slice: x: 2, y: 2, z: 4, core: 2. Of those that a mesh axis runs over, the one named last changes fastest.
Arguments:
- cotangent: float32 [8, 4, 42, 1024], P('gx', 'gy'), may hold values from -6 to 6
- section_states: bfloat16 [3, 8, 4, 42, 1024], P(None, 'gx', 'gy'), may hold values from -6 to 6
- inverse_area: float32 [8, 4, 1024], P('gx', 'gy'), may hold values from 0.5 to 2
- edge_length: float32 [8, 4, 3, 1024], P('gx', 'gy'), may hold values from 0.5 to 1.5
- roughness: float32 [8, 4, 1024], P('gx', 'gy'), may hold values from 0.5 to 2
- soil_conductance: float32 [8, 4, 1024], P('gx', 'gy'), may hold values from 0.5 to 2
- zone_friction: float32 [128], replicated, may hold values from 0.25 to 1
- zone_conductivity: float32 [128], replicated, may hold values from 0.25 to 1
- wet_mask: int32 [8, 4, 1024], P('gx', 'gy'), may hold values 0 or 1
- element_zone: int32 [8, 4, 1024], P('gx', 'gy'), may hold values from 0 to 127, as said below
- send_face: int32 [8, 4, 8, 256], P('gx', 'gy'), may hold values from 0 to 3071, as said below
- send_count: int32 [8, 4, 8], P('gx', 'gy'), may hold values from 0 to 256, as said below
- face_partner: int32 [8, 4, 3, 1024], P('gx', 'gy'), may hold values from 0 to 4867, as said below
- volume_matrix: float32 [12, 12], replicated, may hold values from -1.75 to 1.75
- flux_in: float32 [8, 8], replicated, may hold values from -2 to 2
- flux_out: float32 [8, 8], replicated, may hold values from -2 to 2
Outputs:
- adjoint: float32 [8, 4, 42, 1024], P('gx', 'gy')
- zone_grads: float32 [2, 128], replicated
Inputs may be any that keep to these rules, and one draw needn't show every extreme that they name: `element_zone`: zones lie near their partition: an element of partition (a, b) has a zone among the 8 zones from (a*4+b)*4 on, modulo 128. send_count[a, b, n] equals send_count of the partition at offset n for offset 7 - n; it is 0 where that partition lies outside the grid, 1 to 4 for the four diagonal offsets (4 for some pair in every draw), at least 192 for the others, and 256 for some pair in every draw. `send_face`: the live slots of a partition name distinct faces; slots at or beyond the count hold 0. `face_partner`: the faces are paired: a face sent in slot j to offset n faces entry 3072 + n*256 + j, the other faces face a local face whose partner they are, or themselves.
All inputs are finite; a program needn't handle non-finite values. No bound on the sum of `wet_mask` on one device may be relied on, other than what follows from the above.
Results may differ from a plain program's by a relative error of at most 0.0003.
Values may be sent and summed in bfloat16 or wider, within the bound.
No kernel may reach another device: no remote copies, remote signals or barrier semaphores. Data moves between devices by JAX's collectives and lax.ppermute only.
A program may use at most 64 MiB of HBM per device.

v0:
```python
import jax
import jax.numpy as jnp
import numpy as np
from jax import lax
from jax.sharding import PartitionSpec as P

LAYERS = 10
ZONE_DEV = 4


TIME_STEP = 0.2
SALT_RETURN = 0.5
LATERAL = 0.5
GRAD_WEIGHT = 1.0 / 64.0
FACE_NODES = ((1, 2), (2, 0), (0, 1))
MOMENTUM_ROWS = np.array([0, 0, 0, 1, 1, 1, 1, 1, 1, 0, 0, 0], np.float32)


def shifted(x, axis, by):
    peers = lax.axis_size(axis)
    pairs = [(i, i + by) for i in range(peers) if 0 <= i + by < peers]
    return lax.ppermute(x, axis, pairs)


def trace_rows():
    channels = 8 + 2 * LAYERS
    rows = np.zeros((channels, 3), np.int32)
    for face_no in range(3):
        for end_no in range(2):
            node_no = FACE_NODES[face_no][end_no]
            for comp_no in range(4):
                rows[comp_no * 2 + end_no, face_no] = comp_no * 3 + node_no
            for layer_no in range(LAYERS):
                rows[8 + layer_no * 2 + end_no, face_no] = 12 + layer_no * 3 + node_no
    return rows.reshape(-1)


def take_traces(state, rows):
    channels = rows.shape[0] // 3
    return state[rows].reshape(channels, 3 * state.shape[1])


def lift_back(flux, rows, row_count):
    return jnp.zeros((row_count, flux.shape[-1]), jnp.float32).at[rows].add(flux)


def section_speed(flat_traces, outer_flat):
    return jnp.sqrt(1.0 + 0.25 * jnp.mean(flat_traces[:8] ** 2 + outer_flat[:8] ** 2, axis=0))


def local_operator(
    state,
    received,
    conductivity,
    friction,
    wave_speed,
    inverse_area,
    edge_length,
    wet_mask,
    partner,
    volume_matrix,
    flux_in,
    flux_out,
    rows,
):
    element_count = state.shape[1]
    channels = rows.shape[0] // 3
    flat_traces = take_traces(state, rows)
    trace_table = jnp.concatenate([flat_traces, received.reshape(channels, -1)], axis=1)
    outer_traces = trace_table[:, partner.reshape(-1)].reshape(channels, 3, element_count)
    inner_traces = flat_traces.reshape(channels, 3, element_count)
    surf_inner = inner_traces[:8]
    surf_outer = outer_traces[:8]
    flux_surface = (
        jnp.einsum("ab,bfe->afe", flux_in, surf_inner, precision=lax.Precision.HIGHEST)
        - jnp.einsum("ab,bfe->afe", flux_out, surf_outer, precision=lax.Precision.HIGHEST)
        + 0.5 * wave_speed[None] * (surf_inner - surf_outer)
    )
    flux_pore = LATERAL * conductivity[None, None] * (outer_traces[8:] - inner_traces[8:])
    flux_all = jnp.concatenate([flux_surface, flux_pore], axis=0) * edge_length[None]
    lifted = lift_back(flux_all.reshape(channels * 3, element_count), rows, state.shape[0])
    volume = jnp.dot(volume_matrix, state[:12], precision=lax.Precision.HIGHEST)
    top_exchange = conductivity[None] * (state[9:12] - state[12:15])
    momentum = jnp.asarray(MOMENTUM_ROWS, dtype=jnp.float32)[:, None]
    surface = inverse_area[None] * (volume + lifted[:12]) - momentum * friction[None] * state[:12]
    surface = (
        jnp.concatenate([surface[:9], surface[9:12] - SALT_RETURN * top_exchange], axis=0)
        * wet_mask[None]
    )
    layers = state[12:].reshape(LAYERS, 3, element_count)
    between = conductivity[None, None] * (layers[:-1] - layers[1:])
    from_above = jnp.concatenate([top_exchange[None], between], axis=0)
    to_below = jnp.concatenate([between, jnp.zeros((1, 3, element_count), jnp.float32)], axis=0)
    pore = (from_above - to_below).reshape(3 * LAYERS, element_count) + inverse_area[None] * lifted[
        12:
    ]
    return jnp.concatenate([surface, pore], axis=0)


def forward_estuary(block, by_count):
    return shifted(block, "gx", by_count)


def forward_across(block, by_count):
    return shifted(block, "gy", by_count)


def backward_estuary(block, by_count):
    return shifted(block, "gx", by_count)


def backward_across(block, by_count):
    return shifted(block, "gy", by_count)


def route_blocks(blocks, estuary_hop, across_hop):
    pieces = [
        across_hop(estuary_hop(blocks[..., 7, :], 1), 1),
        estuary_hop(blocks[..., 6, :], 1),
        across_hop(estuary_hop(blocks[..., 5, :], 1), -1),
        across_hop(blocks[..., 4, :], 1),
        across_hop(blocks[..., 3, :], -1),
        across_hop(estuary_hop(blocks[..., 2, :], -1), 1),
        estuary_hop(blocks[..., 1, :], -1),
        across_hop(estuary_hop(blocks[..., 0, :], -1), -1),
    ]
    return jnp.stack(pieces, axis=-2)


def local(
    cotangent,
    section_states,
    inverse_area,
    edge_length,
    roughness,
    soil_conductance,
    zone_friction,
    zone_conductivity,
    wet_mask,
    element_zone,
    send_face,
    send_count,
    face_partner,
    volume_matrix,
    flux_in,
    flux_out,
):
    rows = jnp.asarray(trace_rows(), dtype=jnp.int32)
    channels = rows.shape[0] // 3
    cotangent_local = cotangent[0, 0]
    row_count = cotangent_local.shape[0]
    element_count = cotangent_local.shape[1]
    area_local = inverse_area[0, 0]
    edges_local = edge_length[0, 0]
    rough_local = roughness[0, 0]
    conduct_local = soil_conductance[0, 0]
    wetness = wet_mask[0, 0].astype(jnp.float32)
    zones_local = element_zone[0, 0]
    faces_sent = send_face[0, 0]
    counts_sent = send_count[0, 0]
    partner = face_partner[0, 0]
    zone_total = zone_friction.shape[0]
    conductivity = zone_conductivity[zones_local] * conduct_local
    zone_factor = zone_friction[zones_local]
    slot_index = jnp.arange(faces_sent.shape[1])
    live_slots = (slot_index[None, :] < counts_sent[:, None]).astype(jnp.float32)
    device_number = lax.axis_index("gx") * lax.axis_size("gy") + lax.axis_index("gy")
    zone_base = device_number * ZONE_DEV
    near_count = 2 * ZONE_DEV
    offset_zone = (zones_local - zone_base) % zone_total
    near_onehot = (offset_zone[None, :] == jnp.arange(near_count, dtype=jnp.int32)[:, None]).astype(
        jnp.float32
    )
    near_ids = (zone_base + jnp.arange(near_count, dtype=jnp.int32)) % zone_total
    forward_all = section_states[:, 0, 0].astype(jnp.float32)

    def section_received(states):
        flat_states = jax.vmap(lambda one: take_traces(one, rows))(states)
        outgoing = (flat_states[:, :, faces_sent] * live_slots[None, None]).astype(jnp.bfloat16)
        return route_blocks(outgoing, forward_estuary, forward_across).astype(jnp.float32)

    def received_of(section_no):
        return section_received(forward_all[section_no : section_no + 1])[0]

    def section_adjoint(section_no, weight_field):
        forward_state = forward_all[section_no]
        flat_forward = take_traces(forward_state, rows)
        received = received_of(section_no)
        trace_table = jnp.concatenate([flat_forward, received.reshape(channels, -1)], axis=1)
        outer_forward = trace_table[:, partner.reshape(-1)]
        wave_speed = section_speed(flat_forward, outer_forward).reshape(3, element_count)
        moment = jnp.sqrt(1.0 + jnp.mean(forward_state[3:9] ** 2, axis=0))
        friction_base = rough_local * moment
        friction = zone_factor * friction_base

        def section_operator(state, incoming, conduct_in, friction_in):
            return local_operator(
                state,
                incoming,
                conduct_in,
                friction_in,
                wave_speed,
                area_local,
                edges_local,
                wetness,
                partner,
                volume_matrix,
                flux_in,
                flux_out,
                rows,
            )

        unused, pullback = jax.vjp(
            section_operator, forward_state, received, conductivity, friction
        )
        state_bar, received_bar, conduct_bar, friction_bar = pullback(TIME_STEP * weight_field)
        returned = route_blocks(received_bar, backward_estuary, backward_across)
        flat_bar = (
            jnp.zeros((channels, 3 * element_count), jnp.float32)
            .at[:, faces_sent]
            .add(returned * live_slots[None])
        )
        state_bar = state_bar + lift_back(
            flat_bar.reshape(channels * 3, element_count), rows, row_count
        )
        element_terms = jnp.stack(
            [friction_base * friction_bar, conduct_local * conduct_bar], axis=0
        )
        near_terms = jnp.einsum(
            "ke,ze->kz", element_terms, near_onehot, precision=lax.Precision.HIGHEST
        )
        zone_terms = jnp.zeros((2, zone_total), jnp.float32).at[:, near_ids].add(near_terms)
        return (state_bar, zone_terms)

    bar_two, terms_two = section_adjoint(2, cotangent_local)
    lam_two = 2.0 / 3.0 * (cotangent_local + bar_two)
    bar_one, terms_one = section_adjoint(1, lam_two)
    lam_one = 0.25 * (lam_two + bar_one)
    bar_zero, terms_zero = section_adjoint(0, lam_one)
    adjoint = cotangent_local / 3.0 + 0.75 * lam_two + lam_one + bar_zero
    summed = [lax.psum(terms, ("gx", "gy")) for terms in (terms_two, terms_one, terms_zero)]
    zone_grads = GRAD_WEIGHT * (2.0 / 3.0 * summed[0] + 0.25 * summed[1] + summed[2])
    return (adjoint[None, None], zone_grads)


def solution(mesh):
    placed = (
        P("gx", "gy", None, None),
        P(None, "gx", "gy", None, None),
        P("gx", "gy", None),
        P("gx", "gy", None, None),
        P("gx", "gy", None),
        P("gx", "gy", None),
        P(),
        P(),
        P("gx", "gy", None),
        P("gx", "gy", None),
        P("gx", "gy", None, None),
        P("gx", "gy", None),
        P("gx", "gy", None, None),
        P(),
        P(),
        P(),
    )
    return jax.shard_map(
        local,
        mesh=mesh,
        in_specs=placed,
        out_specs=(P("gx", "gy", None, None), P()),
        check_vma=False,
    )
```

profile of v0, /device:TPU:11, one launch (start us, length us, event | category | flops | bytes accessed | tf_op | source)
XLA Modules:
  0.0 611.7 jit_solution(8066436451531297909)
XLA Ops:
  5.4 7.6 %gather_fusion.12 = f32[2048,28]{1,0:T(8,128)} fusion(f32[28,3072]{0,1:T(8,128)S(1)} %copy.369, s32[2048]{0:T(1024)S(1)} %broadcast_clamp_fusion.1), kind=kCustom, calls=%fused_computation.15 | custom fusion | bytes 466944 | tf_op jit(solution)/shard_map/gather | solution.py:179
  17.5 7.6 %gather_fusion.8 = f32[2048,28]{1,0:T(8,128)} fusion(f32[28,3072]{0,1:T(8,128)S(1)} %copy.340, s32[2048]{0:T(1024)S(1)} %broadcast_clamp_fusion.1), kind=kCustom, calls=%fused_computation.10 | custom fusion | bytes 466944 | tf_op jit(solution)/shard_map/gather | solution.py:179
  28.9 7.6 %gather_fusion.4 = f32[2048,28]{1,0:T(8,128)} fusion(f32[28,3072]{0,1:T(8,128)S(1)} %copy.311, s32[2048]{0:T(1024)S(1)} %broadcast_clamp_fusion.1), kind=kCustom, calls=%fused_computation.5 | custom fusion | bytes 466944 | tf_op jit(solution)/shard_map/gather | solution.py:179
  50.2 4.5 collective-permute-start.5
  59.5 6.6 %gather_fusion = f32[1024]{0:T(1024)S(1)} fusion(f32[128]{0:T(128)S(1)} %copy-done.1, s32[1024]{0:T(1024)S(1)} %broadcast_clamp_fusion.2), kind=kCustom, calls=%fused_computation | custom fusion | bytes 12288 | tf_op jit(solution)/shard_map/gather | solution.py:163
  66.2 6.6 %gather_fusion.1 = f32[1024]{0:T(1024)S(1)} fusion(f32[128]{0:T(128)S(1)} %copy-done.2, s32[1024]{0:T(1024)S(1)} %broadcast_clamp_fusion.2), kind=kCustom, calls=%fused_computation.1 | custom fusion | bytes 12288 | tf_op jit(solution)/shard_map/gather | solution.py:164
  93.7 4.8 collective-permute-start.29
  102.4 4.3 collective-permute-start.50
  106.7 4.2 collective-permute-start.53
  119.1 4.5 collective-permute-start.24
  155.0 4.3 collective-permute-start.48
  159.3 4.5 collective-permute-start.25
  169.4 10.9 %gather_fusion.5 = f32[3072,28]{1,0:T(8,128)} fusion(f32[28,5120]{0,1:T(8,128)S(1)} %copy.321, s32[3072]{0:T(1024)S(1)} %copy-done.58), kind=kCustom, calls=%fused_computation.6 | custom fusion | bytes 700416 | tf_op jit(solution)/shard_map/gather | solution.py:190
  186.9 17.9 %scatter_custom_fusion = f32[28,5120]{0,1:T(8,128)S(1)} fusion(s32[3072]{0:T(1024)} %bitcast.397, f32[3072,28]{1,0:T(8,128)} %copy.327, f32[]{:T(128)} %constant.38.clone.1), kind=kCustom, calls=%fused_computation.36 | custom fusion | flops 86016 | bytes 573952 | tf_op jit(solution)/shard_map/transpose(jvp())/scatter-add | solution.py:70
  214.0 4.2 collective-permute-start.32
  236.4 4.5 collective-permute-start.12
  245.0 12.0 %gather_fusion.9 = f32[3072,28]{1,0:T(8,128)} fusion(f32[28,5120]{0,1:T(8,128)S(1)} %copy.350, s32[3072]{0:T(1024)} %broadcast_clamp_fusion), kind=kCustom, calls=%fused_computation.11 | custom fusion | bytes 700416 | tf_op jit(solution)/shard_map/gather | solution.py:190
  265.2 4.4 collective-permute-start.15
  270.3 4.5 collective-permute-start.17
  281.5 12.0 %gather_fusion.13 = f32[3072,28]{1,0:T(8,128)} fusion(f32[28,5120]{0,1:T(8,128)S(1)} %copy.379, s32[3072]{0:T(1024)} %broadcast_clamp_fusion), kind=kCustom, calls=%fused_computation.16 | custom fusion | bytes 700416 | tf_op jit(solution)/shard_map/gather | solution.py:190
  329.3 14.1 %scatter_custom_fusion.2 = f32[28,3072]{0,1:T(8,128)S(1)} fusion(s32[2048]{0:T(1024)} %bitcast.407, f32[2048,28]{1,0:T(8,128)} %bitcast.370, f32[]{:T(128)} %constant.38.clone.1), kind=kCustom, calls=%fused_computation.57 | custom fusion | flops 57344 | bytes 344576 | tf_op jit(solution)/shard_map/scatter-add | solution.py:221
  356.1 17.9 %scatter_custom_fusion.4 = f32[28,5120]{0,1:T(8,128)S(1)} fusion(s32[3072]{0:T(1024)} %bitcast.398, f32[3072,28]{1,0:T(8,128)} %copy.356, f32[]{:T(128)} %constant.38.clone.1), kind=kCustom, calls=%fused_computation.34 | custom fusion | flops 86016 | bytes 573952 | tf_op jit(solution)/shard_map/transpose(jvp())/scatter-add | solution.py:70
  376.7 4.5 collective-permute-start.36
  392.2 4.5 collective-permute-start.41
  416.8 4.2 collective-permute-start.37
  441.1 13.8 %scatter_custom_fusion.6 = f32[28,3072]{0,1:T(8,128)S(1)} fusion(s32[2048]{0:T(1024)} %bitcast.408, f32[2048,28]{1,0:T(8,128)S(1)} %bitcast.371, f32[]{:T(128)} %constant.38.clone.1), kind=kCustom, calls=%fused_computation.55 | custom fusion | flops 57344 | bytes 344576 | tf_op jit(solution)/shard_map/scatter-add | solution.py:221
  468.6 17.9 %scatter_custom_fusion.8 = f32[28,5120]{0,1:T(8,128)S(1)} fusion(s32[3072]{0:T(1024)} %bitcast.399, f32[3072,28]{1,0:T(8,128)} %copy.385, f32[]{:T(128)} %constant.38.clone.1), kind=kCustom, calls=%fused_computation.32 | custom fusion | flops 86016 | bytes 573952 | tf_op jit(solution)/shard_map/transpose(jvp())/scatter-add | solution.py:70
  489.4 4.5 collective-permute-start.60
  504.8 4.5 collective-permute-start.65
  516.0 39.9 %all-reduce.42 = (f32[2,128]{0,1:T(8,128)S(1)}, f32[2,128]{0,1:T(8,128)S(1)}, f32[2,128]{0,1:T(8,128)S(1)}) all-reduce(f32[2,128]{0,1:T(8,128)S(1)} %scatter_custom_fusion.14, f32[2,128]{0,1:T(8,128)S(1)} %scatter_custom_fusion.13, f32[2,128]{0,1:T(8,128)S(1)} %scatter_custom_fusion.12), channel_id=1, replica_groups=mesh['gx'=8,'gy'=4] {'gx','gy'}, use_global_device_ids=true, to_apply=%region_35.36 | all-reduce | flops 768 | bytes 6144 | tf_op jit(solution)/shard_map/psum | solution.py:241
  572.3 5.3 collective-permute-start.61
  594.5 13.8 %scatter_custom_fusion.10 = f32[28,3072]{0,1:T(8,128)S(1)} fusion(s32[2048]{0:T(1024)} %bitcast.409, f32[2048,28]{1,0:T(8,128)S(1)} %bitcast.369, f32[]{:T(128)} %constant.38.clone.1), kind=kCustom, calls=%fused_computation.53 | custom fusion | flops 57344 | bytes 344576 | tf_op jit(solution)/shard_map/scatter-add | solution.py:221
  (732 shorter events, 324.6 us)
Async XLA Ops:
  40.7 41.0 %collective-permute-start = (bf16[1,28,256]{2,1,0:T(8,128)(2,1)}, bf16[1,28,256]{2,1,0:T(8,128)(2,1)}, u32[]{:S(2)}, u32[]{:S(2)}) collective-permute-start(bf16[1,28,256]{2,1,0:T(8,128)(2,1)} %get-tuple-element.115), channel_id=1, source_target_pairs={{0,4},{4,8},{8,12},{12,16},{16,20},{20,24},{24,28},{1,5},{5,9},{9,... | collective-permute-start | bytes 43016 | tf_op jit(solution)/shard_map/ppermute | solution.py:22
  43.9 40.0 %collective-permute-start.2 = (bf16[1,28,256]{2,1,0:T(8,128)(2,1)}, bf16[1,28,256]{2,1,0:T(8,128)(2,1)}, u32[]{:S(2)}, u32[]{:S(2)}) collective-permute-start(bf16[1,28,256]{2,1,0:T(8,128)(2,1)} %get-tuple-element.114), channel_id=1, source_target_pairs={{0,4},{4,8},{8,12},{12,16},{16,20},{20,24},{24,28},{1,5},{5,9},{9,... | collective-permute-start | bytes 43016 | tf_op jit(solution)/shard_map/ppermute | solution.py:22
  47.0 40.5 %collective-permute-start.3 = (bf16[1,28,256]{2,1,0:T(8,128)(2,1)}, bf16[1,28,256]{2,1,0:T(8,128)(2,1)}, u32[]{:S(2)}, u32[]{:S(2)}) collective-permute-start(bf16[1,28,256]{2,1,0:T(8,128)(2,1)} %get-tuple-element.113), channel_id=1, source_target_pairs={{0,4},{4,8},{8,12},{12,16},{16,20},{20,24},{24,28},{1,5},{5,9},{9,... | collective-permute-start | bytes 43016 | tf_op jit(solution)/shard_map/ppermute | solution.py:22
  50.2 40.0 %collective-permute-start.5 = (bf16[1,28,256]{2,1,0:T(8,128)(2,1)}, bf16[1,28,256]{2,1,0:T(8,128)(2,1)}, u32[]{:S(2)}, u32[]{:S(2)}) collective-permute-start(bf16[1,28,256]{2,1,0:T(8,128)(2,1)} %get-tuple-element.112), channel_id=1, source_target_pairs={{0,1},{1,2},{2,3},{4,5},{5,6},{6,7},{8,9},{9,10},{10,11},{12,13},{... | collective-permute-start | bytes 43016 | tf_op jit(solution)/shard_map/ppermute | solution.py:22
  54.7 39.0 %collective-permute-start.6 = (bf16[1,28,256]{2,1,0:T(8,128)(2,1)}, bf16[1,28,256]{2,1,0:T(8,128)(2,1)}, u32[]{:S(2)}, u32[]{:S(2)}) collective-permute-start(bf16[1,28,256]{2,1,0:T(8,128)(2,1)} %get-tuple-element.111), channel_id=1, source_target_pairs={{1,0},{2,1},{3,2},{5,4},{6,5},{7,6},{9,8},{10,9},{11,10},{13,12},{... | collective-permute-start | bytes 43016 | tf_op jit(solution)/shard_map/ppermute | solution.py:22
  119.1 35.9 %collective-permute-start.24 = (bf16[1,28,256]{2,1,0:T(8,128)(2,1)S(1)}, bf16[1,28,256]{2,1,0:T(8,128)(2,1)}, u32[]{:S(2)}, u32[]{:S(2)}) collective-permute-start(bf16[1,28,256]{2,1,0:T(8,128)(2,1)S(1)} %get-tuple-element.107), channel_id=1, source_target_pairs={{0,4},{4,8},{8,12},{12,16},{16,20},{20,24},{24,28},{1,5},{5,9},{9,... | collective-permute-start | bytes 43016 | tf_op jit(solution)/shard_map/ppermute | solution.py:22
  123.7 35.6 %collective-permute-start.27 = (bf16[1,28,256]{2,1,0:T(8,128)(2,1)S(1)}, bf16[1,28,256]{2,1,0:T(8,128)(2,1)}, u32[]{:S(2)}, u32[]{:S(2)}) collective-permute-start(bf16[1,28,256]{2,1,0:T(8,128)(2,1)S(1)} %get-tuple-element.105), channel_id=1, source_target_pairs={{0,4},{4,8},{8,12},{12,16},{16,20},{20,24},{24,28},{1,5},{5,9},{9,... | collective-permute-start | bytes 43016 | tf_op jit(solution)/shard_map/ppermute | solution.py:22
  127.6 24.7 %collective-permute-start.8 = (bf16[1,28,256]{2,1,0:T(8,128)(2,1)}, bf16[1,28,256]{2,1,0:T(8,128)(2,1)}, u32[]{:S(2)}, u32[]{:S(2)}) collective-permute-start(bf16[1,28,256]{2,1,0:T(8,128)(2,1)} %collective-permute-done.7), channel_id=1, source_target_pairs={{0,1},{1,2},{2,3},{4,5},{5,6},{6,7},{8,9},{9,10},{10,11},{12,13},{... | collective-permute-start | bytes 43016 | tf_op jit(solution)/shard_map/ppermute | solution.py:22
  131.2 32.5 %collective-permute-start.11 = (bf16[1,28,256]{2,1,0:T(8,128)(2,1)}, bf16[1,28,256]{2,1,0:T(8,128)(2,1)S(1)}, u32[]{:S(2)}, u32[]{:S(2)}) collective-permute-start(bf16[1,28,256]{2,1,0:T(8,128)(2,1)} %collective-permute-done.10), channel_id=1, source_target_pairs={{1,0},{2,1},{3,2},{5,4},{6,5},{7,6},{9,8},{10,9},{11,10},{13,12},{... | collective-permute-start | bytes 43016 | tf_op jit(solution)/shard_map/ppermute | solution.py:22
  148.2 58.4 %collective-permute-start.31 = (bf16[1,28,256]{2,1,0:T(8,128)(2,1)}, bf16[1,28,256]{2,1,0:T(8,128)(2,1)}, u32[]{:S(2)}, u32[]{:S(2)}) collective-permute-start(bf16[1,28,256]{2,1,0:T(8,128)(2,1)} %get-tuple-element.102), channel_id=1, source_target_pairs={{4,0},{8,4},{12,8},{16,12},{20,16},{24,20},{28,24},{5,1},{9,5},{13... | collective-permute-start | bytes 43016 | tf_op jit(solution)/shard_map/ppermute | solution.py:22
  152.3 56.3 %collective-permute-start.34 = (bf16[1,28,256]{2,1,0:T(8,128)(2,1)}, bf16[1,28,256]{2,1,0:T(8,128)(2,1)}, u32[]{:S(2)}, u32[]{:S(2)}) collective-permute-start(bf16[1,28,256]{2,1,0:T(8,128)(2,1)} %get-tuple-element.100), channel_id=1, source_target_pairs={{4,0},{8,4},{12,8},{16,12},{20,16},{24,20},{28,24},{5,1},{9,5},{13... | collective-permute-start | bytes 43016 | tf_op jit(solution)/shard_map/ppermute | solution.py:22
  155.0 57.0 %collective-permute-start.48 = (bf16[1,28,256]{2,1,0:T(8,128)(2,1)}, bf16[1,28,256]{2,1,0:T(8,128)(2,1)}, u32[]{:S(2)}, u32[]{:S(2)}) collective-permute-start(bf16[1,28,256]{2,1,0:T(8,128)(2,1)} %get-tuple-element.99), channel_id=1, source_target_pairs={{0,4},{4,8},{8,12},{12,16},{16,20},{20,24},{24,28},{1,5},{5,9},{9,... | collective-permute-start | bytes 43016 | tf_op jit(solution)/shard_map/ppermute | solution.py:22
  159.3 54.7 %collective-permute-start.25 = (bf16[1,28,256]{2,1,0:T(8,128)(2,1)}, bf16[1,28,256]{2,1,0:T(8,128)(2,1)}, u32[]{:S(2)}, u32[]{:S(2)}) collective-permute-start(bf16[1,28,256]{2,1,0:T(8,128)(2,1)} %collective-permute-done.24), channel_id=1, source_target_pairs={{0,1},{1,2},{2,3},{4,5},{5,6},{6,7},{8,9},{9,10},{10,11},{12,13},{... | collective-permute-start | bytes 43016 | tf_op jit(solution)/shard_map/ppermute | solution.py:22
  163.8 54.4 %collective-permute-start.28 = (bf16[1,28,256]{2,1,0:T(8,128)(2,1)}, bf16[1,28,256]{2,1,0:T(8,128)(2,1)}, u32[]{:S(2)}, u32[]{:S(2)}) collective-permute-start(bf16[1,28,256]{2,1,0:T(8,128)(2,1)} %collective-permute-done.27), channel_id=1, source_target_pairs={{1,0},{2,1},{3,2},{5,4},{6,5},{7,6},{9,8},{10,9},{11,10},{13,12},{... | collective-permute-start | bytes 43016 | tf_op jit(solution)/shard_map/ppermute | solution.py:22
  225.1 37.4 %collective-permute-start.49 = (bf16[1,28,256]{2,1,0:T(8,128)(2,1)}, bf16[1,28,256]{2,1,0:T(8,128)(2,1)}, u32[]{:S(2)}, u32[]{:S(2)}) collective-permute-start(bf16[1,28,256]{2,1,0:T(8,128)(2,1)} %collective-permute-done.48), channel_id=1, source_target_pairs={{0,1},{1,2},{2,3},{4,5},{5,6},{6,7},{8,9},{9,10},{10,11},{12,13},{... | collective-permute-start | bytes 43016 | tf_op jit(solution)/shard_map/ppermute | solution.py:22
  228.8 36.4 %collective-permute-start.52 = (bf16[1,28,256]{2,1,0:T(8,128)(2,1)}, bf16[1,28,256]{2,1,0:T(8,128)(2,1)}, u32[]{:S(2)}, u32[]{:S(2)}) collective-permute-start(bf16[1,28,256]{2,1,0:T(8,128)(2,1)} %collective-permute-done.51), channel_id=1, source_target_pairs={{1,0},{2,1},{3,2},{5,4},{6,5},{7,6},{9,8},{10,9},{11,10},{13,12},{... | collective-permute-start | bytes 43016 | tf_op jit(solution)/shard_map/ppermute | solution.py:22
  230.7 39.6 %collective-permute-start.56 = (bf16[1,28,256]{2,1,0:T(8,128)(2,1)}, bf16[1,28,256]{2,1,0:T(8,128)(2,1)}, u32[]{:S(2)}, u32[]{:S(2)}) collective-permute-start(bf16[1,28,256]{2,1,0:T(8,128)(2,1)} %collective-permute-done.55), channel_id=1, source_target_pairs={{0,1},{1,2},{2,3},{4,5},{5,6},{6,7},{8,9},{9,10},{10,11},{12,13},{... | collective-permute-start | bytes 43016 | tf_op jit(solution)/shard_map/ppermute | solution.py:22
  234.4 41.1 %collective-permute-start.59 = (bf16[1,28,256]{2,1,0:T(8,128)(2,1)}, bf16[1,28,256]{2,1,0:T(8,128)(2,1)}, u32[]{:S(2)}, u32[]{:S(2)}) collective-permute-start(bf16[1,28,256]{2,1,0:T(8,128)(2,1)} %collective-permute-done.58), channel_id=1, source_target_pairs={{1,0},{2,1},{3,2},{5,4},{6,5},{7,6},{9,8},{10,9},{11,10},{13,12},{... | collective-permute-start | bytes 43016 | tf_op jit(solution)/shard_map/ppermute | solution.py:22
  236.4 59.4 %collective-permute-start.12 = (f32[28,256]{1,0:T(8,128)}, f32[28,256]{1,0:T(8,128)}, u32[]{:S(2)}, u32[]{:S(2)}) collective-permute-start(f32[28,256]{1,0:T(8,128)} %bitcast.43), channel_id=1, source_target_pairs={{0,4},{4,8},{8,12},{12,16},{16,20},{20,24},{24,28},{1,5},{5,9},{9,... | collective-permute-start | bytes 86024 | tf_op jit(solution)/shard_map/ppermute | solution.py:22
  262.5 35.2 %collective-permute-start.14 = (f32[28,256]{1,0:T(8,128)}, f32[28,256]{1,0:T(8,128)}, u32[]{:S(2)}, u32[]{:S(2)}) collective-permute-start(f32[28,256]{1,0:T(8,128)} %bitcast.44), channel_id=1, source_target_pairs={{0,4},{4,8},{8,12},{12,16},{16,20},{20,24},{24,28},{1,5},{5,9},{9,... | collective-permute-start | bytes 86024 | tf_op jit(solution)/shard_map/ppermute | solution.py:22
  265.2 36.5 %collective-permute-start.15 = (f32[28,256]{1,0:T(8,128)}, f32[28,256]{1,0:T(8,128)}, u32[]{:S(2)}, u32[]{:S(2)}) collective-permute-start(f32[28,256]{1,0:T(8,128)} %bitcast.45), channel_id=1, source_target_pairs={{0,4},{4,8},{8,12},{12,16},{16,20},{20,24},{24,28},{1,5},{5,9},{9,... | collective-permute-start | bytes 86024 | tf_op jit(solution)/shard_map/ppermute | solution.py:22
  270.3 33.3 %collective-permute-start.17 = (f32[28,256]{1,0:T(8,128)}, f32[28,256]{1,0:T(8,128)}, u32[]{:S(2)}, u32[]{:S(2)}) collective-permute-start(f32[28,256]{1,0:T(8,128)} %bitcast.46), channel_id=1, source_target_pairs={{0,1},{1,2},{2,3},{4,5},{5,6},{6,7},{8,9},{9,10},{10,11},{12,13},{... | collective-permute-start | bytes 86024 | tf_op jit(solution)/shard_map/ppermute | solution.py:22
  275.5 32.2 %collective-permute-start.18 = (f32[28,256]{1,0:T(8,128)}, f32[28,256]{1,0:T(8,128)}, u32[]{:S(2)}, u32[]{:S(2)}) collective-permute-start(f32[28,256]{1,0:T(8,128)} %bitcast.47), channel_id=1, source_target_pairs={{1,0},{2,1},{3,2},{5,4},{6,5},{7,6},{9,8},{10,9},{11,10},{13,12},{... | collective-permute-start | bytes 86024 | tf_op jit(solution)/shard_map/ppermute | solution.py:22
  301.7 25.0 %collective-permute-start.21 = (f32[28,256]{1,0:T(8,128)}, f32[28,256]{1,0:T(8,128)S(1)}, u32[]{:S(2)}, u32[]{:S(2)}) collective-permute-start(f32[28,256]{1,0:T(8,128)} %bitcast.49), channel_id=1, source_target_pairs={{4,0},{8,4},{12,8},{16,12},{20,16},{24,20},{28,24},{5,1},{9,5},{13... | collective-permute-start | bytes 86024 | tf_op jit(solution)/shard_map/ppermute | solution.py:22
  376.7 30.2 %collective-permute-start.36 = (f32[28,256]{1,0:T(8,128)}, f32[28,256]{1,0:T(8,128)}, u32[]{:S(2)}, u32[]{:S(2)}) collective-permute-start(f32[28,256]{1,0:T(8,128)} %bitcast.81), channel_id=1, source_target_pairs={{0,4},{4,8},{8,12},{12,16},{16,20},{20,24},{24,28},{1,5},{5,9},{9,... | collective-permute-start | bytes 86024 | tf_op jit(solution)/shard_map/ppermute | solution.py:22
  382.8 26.0 %collective-permute-start.38 = (f32[28,256]{1,0:T(8,128)}, f32[28,256]{1,0:T(8,128)}, u32[]{:S(2)}, u32[]{:S(2)}) collective-permute-start(f32[28,256]{1,0:T(8,128)} %bitcast.82), channel_id=1, source_target_pairs={{0,4},{4,8},{8,12},{12,16},{16,20},{20,24},{24,28},{1,5},{5,9},{9,... | collective-permute-start | bytes 86024 | tf_op jit(solution)/shard_map/ppermute | solution.py:22
  386.4 28.5 %collective-permute-start.39 = (f32[28,256]{1,0:T(8,128)}, f32[28,256]{1,0:T(8,128)}, u32[]{:S(2)}, u32[]{:S(2)}) collective-permute-start(f32[28,256]{1,0:T(8,128)} %bitcast.83), channel_id=1, source_target_pairs={{0,4},{4,8},{8,12},{12,16},{16,20},{20,24},{24,28},{1,5},{5,9},{9,... | collective-permute-start | bytes 86024 | tf_op jit(solution)/shard_map/ppermute | solution.py:22
  489.4 70.8 %collective-permute-start.60 = (f32[28,256]{1,0:T(8,128)}, f32[28,256]{1,0:T(8,128)}, u32[]{:S(2)}, u32[]{:S(2)}) collective-permute-start(f32[28,256]{1,0:T(8,128)} %bitcast.119), channel_id=1, source_target_pairs={{0,4},{4,8},{8,12},{12,16},{16,20},{20,24},{24,28},{1,5},{5,9},{9,... | collective-permute-start | bytes 86024 | tf_op jit(solution)/shard_map/ppermute | solution.py:22
  495.5 68.2 %collective-permute-start.62 = (f32[28,256]{1,0:T(8,128)}, f32[28,256]{1,0:T(8,128)}, u32[]{:S(2)}, u32[]{:S(2)}) collective-permute-start(f32[28,256]{1,0:T(8,128)} %bitcast.120), channel_id=1, source_target_pairs={{0,4},{4,8},{8,12},{12,16},{16,20},{20,24},{24,28},{1,5},{5,9},{9,... | collective-permute-start | bytes 86024 | tf_op jit(solution)/shard_map/ppermute | solution.py:22
  499.1 69.9 %collective-permute-start.63 = (f32[28,256]{1,0:T(8,128)}, f32[28,256]{1,0:T(8,128)}, u32[]{:S(2)}, u32[]{:S(2)}) collective-permute-start(f32[28,256]{1,0:T(8,128)} %bitcast.121), channel_id=1, source_target_pairs={{0,4},{4,8},{8,12},{12,16},{16,20},{20,24},{24,28},{1,5},{5,9},{9,... | collective-permute-start | bytes 86024 | tf_op jit(solution)/shard_map/ppermute | solution.py:22
  504.8 67.5 %collective-permute-start.65 = (f32[28,256]{1,0:T(8,128)}, f32[28,256]{1,0:T(8,128)}, u32[]{:S(2)}, u32[]{:S(2)}) collective-permute-start(f32[28,256]{1,0:T(8,128)} %bitcast.122), channel_id=1, source_target_pairs={{0,1},{1,2},{2,3},{4,5},{5,6},{6,7},{8,9},{9,10},{10,11},{12,13},{... | collective-permute-start | bytes 86024 | tf_op jit(solution)/shard_map/ppermute | solution.py:22
  510.0 67.6 %collective-permute-start.66 = (f32[28,256]{1,0:T(8,128)}, f32[28,256]{1,0:T(8,128)}, u32[]{:S(2)}, u32[]{:S(2)}) collective-permute-start(f32[28,256]{1,0:T(8,128)} %bitcast.123), channel_id=1, source_target_pairs={{1,0},{2,1},{3,2},{5,4},{6,5},{7,6},{9,8},{10,9},{11,10},{13,12},{... | collective-permute-start | bytes 86024 | tf_op jit(solution)/shard_map/ppermute | solution.py:22
  (197 other events, 2873.4 us)
where the time goes:
time: 624 us; the launch traced here: 612 us
  starting transfers between devices  219 us (35%)
  local copies, waits for them, and re-layouts  198 us (32%)
  other arithmetic  143 us (23%)
  blocking collectives  39.9 us (6%)
  matrix products  7.04 us (1%)
    ppermute x72, starting transfers between devices, shifted(): return lax.ppermute(x, axis, pairs)  219 us
    scatter-add x3, other arithmetic, local_operator(): trace_table[:, partner.reshape(-1)].reshape(channels, 3, element_count)  53.6 us
    scatter-add x3, other arithmetic, section_adjoint(): flat_bar = jnp.zeros((channels, 3 * element_count), jnp.float32).at[:, fa...  41.7 us
    gather x6, local copies, waits for them, and re-layouts, section_adjoint(): outer_forward = trace_table[:, partner.reshape(-1)]  40.7 us
    psum x1, blocking collectives, local(): lax.psum(terms, ('gx', 'gy'))  39.9 us
    unnamed x351, local copies, waits for them, and re-layouts  38.3 us
    gather x6, local copies, waits for them, and re-layouts, section_received(): flat_states[:, :, faces_sent] * live_slots[None, None]  28.8 us
    another operation x54, local copies, waits for them, and re-layouts, route_blocks(): return jnp.stack(pieces, axis=-2)  28.8 us
  transfers between devices with their start and end apart: 72, of which 0 were waited for; matrix products, arithmetic and copies ran while one was open for 30% of the time, Pallas kernels for 0%

commit v1 on v0

v1 whole, which is shorter than its diff:
```python
import functools
import jax
import jax.numpy as jnp
from jax import lax
from jax.experimental import pallas as pl
from jax.experimental.pallas import tpu as pltpu
from jax.sharding import PartitionSpec as P

TIME_STEP = 0.2
SALT_RETURN = 0.5
LATERAL = 0.5
GRAD_WEIGHT = 1.0 / 64.0
FACE_NODES = ((1, 2), (2, 0), (0, 1))
NODE_FACES = (((1, 1), (2, 0)), ((0, 0), (2, 1)), ((0, 1), (1, 0)))
SUB = 8
LANES = 128


WET_AREA, KAPPA, HALF_KAPPA_AREA, WET, EDGE, FRICTION_BASE, ZONE_FRICTION, ZONE_ID = (
    0,
    1,
    2,
    3,
    4,
    7,
    10,
    11,
)
STAT_ROWS = 12
OUTER_EDGE, OUTER_ZONE, HALF_SPEED = 0, 3, 6
FACT_ROWS = 15
REMOTE_BLOCKS = (
    (0, 0),
    (0, 1),
    (1, 0),
    (1, 1),
    (2, 0),
    (2, 1),
    (3, 0),
    (3, 1),
    (2, 2),
    (3, 2),
)


def shifted(x, axis, by):
    peers = lax.axis_size(axis)
    pairs = [(i, i + by) for i in range(peers) if 0 <= i + by < peers]
    return lax.ppermute(x, axis, pairs)


def tile(ref, row):
    return ref[row * SUB : (row + 1) * SUB, :]


def put(ref, row, value):
    ref[row * SUB : (row + 1) * SUB, :] = value


def take(row, lane_index):
    return jnp.take_along_axis(row, lane_index, axis=1, mode="promise_in_bounds")


def spread(ref, row):
    return jnp.broadcast_to(ref[pl.ds(row, 1), :], (SUB, LANES))


def rows_to_tiles(read, tiles_ref, count):
    for block in range(SUB):
        tiles_ref[pl.ds(block, count, stride=SUB), :] = read(block)


def lanes_of(block):
    return slice(block * LANES, (block + 1) * LANES)


def gather_tile(src, row, lane_index, sublane_index):
    found = [None] * len(lane_index)
    for sub in range(SUB):
        line = spread(src, row * SUB + sub)
        for d, lane in enumerate(lane_index):
            got = take(line, lane)
            found[d] = got if sub == 0 else jnp.where(sublane_index[d] == sub, got, found[d])
    return found


def pick(face, for_zero, for_one, for_two):
    return jnp.where(face == 0, for_zero, jnp.where(face == 1, for_one, for_two))


def gather_ends(src, row, lane_index, sublane_index, face):
    nodes = [gather_tile(src, row + i, lane_index, sublane_index) for i in range(3)]
    ends = []
    for d, which in enumerate(face):
        n0, n1, n2 = nodes[0][d], nodes[1][d], nodes[2][d]
        ends.append((pick(which, n1, n2, n0), pick(which, n2, n0, n1)))
    return ends


def gather_by_face(src, row, lane_index, sublane_index, face):
    faces = [gather_tile(src, row + i, lane_index, sublane_index) for i in range(3)]
    return [pick(which, faces[0][d], faces[1][d], faces[2][d]) for d, which in enumerate(face)]


def fill_remote(received, row, lane_index, remote_index, values):
    values = list(values)
    for number, (message, block) in enumerate(REMOTE_BLOCKS):
        line = spread(received[message].at[block], row)
        for d, lane in enumerate(lane_index):
            values[d] = jnp.where(remote_index[d] == number, take(line, lane), values[d])
    return values


def partner_index(index_ref):
    return [[tile(index_ref, part * 3 + f) for f in range(3)] for part in range(4)]


def sent_index(index_ref):
    return [[tile(index_ref, 12 + part * 2 + d) for d in range(2)] for part in range(3)]


INDEX_ROWS = 18


def send_states(src, first_comp, comps, first_row, sent, sent_ref):
    lane, sublane, face = sent

    def body(step, carry):
        ends = gather_ends(src, (first_comp + step) * 3, lane, sublane, face)
        for d in range(2):
            for j in range(2):
                at = pl.multiple_of((first_row + step * 2 + j) * SUB, SUB)
                sent_ref[d, pl.ds(at, SUB), :] = ends[d][j]
        return carry

    lax.fori_loop(0, comps, body, 0)


def write_messages(sent_ref, messages):
    to_right, to_left, to_up, to_down = messages
    count = to_right.shape[1]
    for ref, direction in ((to_right, 6), (to_left, 1), (to_up, 4), (to_down, 3)):
        for block in range(2):
            ref[block] = sent_ref[block, pl.ds(direction, count, stride=SUB), :]
    for ref, direction in ((to_right, 5), (to_left, 2)):
        ref[2] = sent_ref[0, pl.ds(direction, count, stride=SUB), :]


def prepare_kernel(
    cot_ref,
    x_ref,
    area_ref,
    edge_ref,
    rough_ref,
    soil_ref,
    friction_ref,
    conduct_ref,
    wet_ref,
    zone_ref,
    send_ref,
    partner_ref,
    lam_ref,
    table_ref,
    stat_ref,
    index_ref,
    to_right,
    to_left,
    to_up,
    to_down,
    x_tiles,
    int_tiles,
    sent_ref,
):
    rows = cot_ref.shape[2]
    sections = x_ref.shape[0]
    rows_to_tiles(lambda b: cot_ref[0, 0, :, lanes_of(b)], lam_ref, rows)
    rows_to_tiles(lambda b: partner_ref[0, 0, :, lanes_of(b)], int_tiles, 3)
    face_total = 3 * SUB * LANES
    for f in range(3):
        partner = tile(int_tiles, f)
        beyond = partner - face_total
        direction = jnp.right_shift(beyond, 8)
        half = jnp.bitwise_and(jnp.right_shift(beyond, 7), 1)
        lane = jnp.bitwise_and(partner, LANES - 1)
        remote = jnp.where(beyond >= 0, 8, -1)
        remote = jnp.where((direction == 2) | (direction == 7), 9, remote)
        for number, first in ((1, 0), (6, 2), (3, 4), (4, 6)):
            remote = jnp.where(direction == number, first + half, remote)
        lane = jnp.where((direction == 0) | (direction == 7), jnp.bitwise_and(lane + 4, LANES - 1), lane)
        put(index_ref, f, lane)
        put(index_ref, 3 + f, jnp.bitwise_and(jnp.right_shift(partner, 7), SUB - 1))
        put(index_ref, 6 + f, jnp.right_shift(partner, 10))
        put(index_ref, 9 + f, remote)
    sub_iota = lax.broadcasted_iota(jnp.int32, (SUB, LANES), 0)
    lane_iota = lax.broadcasted_iota(jnp.int32, (SUB, LANES), 1)
    for d in range(2):
        slots = send_ref[0, 0, :, lanes_of(d)]
        if d == 0:
            moved = pltpu.roll(slots, 4, 1)
            second = (lane_iota >= 4) & (lane_iota < 8)
            slots = jnp.where(second & (sub_iota == 5), pltpu.roll(moved, 6, 0), slots)
            slots = jnp.where(second & (sub_iota == 2), pltpu.roll(moved, 2, 0), slots)
        put(index_ref, 12 + d, jnp.bitwise_and(slots, LANES - 1))
        put(index_ref, 14 + d, jnp.bitwise_and(jnp.right_shift(slots, 7), SUB - 1))
        put(index_ref, 16 + d, jnp.right_shift(slots, 10))
    zone = zone_ref[...]
    zone_lane = jnp.bitwise_and(zone, LANES - 1)
    zone_block = jnp.right_shift(zone, 7)
    factors = []
    for ref in (friction_ref, conduct_ref):
        found = None
        for block in range(ref.shape[0]):
            got = take(spread(ref, block), zone_lane)
            found = got if block == 0 else jnp.where(zone_block == block, got, found)
        factors.append(found)
    area = area_ref[...]
    wet = wet_ref[...].astype(jnp.float32)
    kappa = factors[1] * soil_ref[...]
    wet_area = wet * area
    half_kappa_area = LATERAL * kappa * area
    put(stat_ref, WET_AREA, wet_area)
    put(stat_ref, KAPPA, kappa)
    put(stat_ref, HALF_KAPPA_AREA, half_kappa_area)
    put(stat_ref, WET, wet)
    put(stat_ref, ZONE_FRICTION, factors[0])
    put(stat_ref, ZONE_ID, zone.astype(jnp.float32))
    rows_to_tiles(lambda b: edge_ref[0, 0, :, lanes_of(b)], stat_ref.at[EDGE * SUB : (EDGE + 3) * SUB], 3)
    for k in range(sections):
        rows_to_tiles(
            lambda b: x_ref[k, 0, 0, 0:16, lanes_of(b)].astype(jnp.float32), x_tiles, 16
        )
        squares = [tile(x_tiles, r) * tile(x_tiles, r) for r in range(12)]
        node_sum = [squares[i] + squares[3 + i] + squares[6 + i] + squares[9 + i] for i in range(3)]
        for f in range(3):
            first, second = FACE_NODES[f]
            put(table_ref, rows + 3 + 3 * k + f, node_sum[first] + node_sum[second])
        momentum = squares[3]
        for r in range(4, 9):
            momentum = momentum + squares[r]
        put(
            stat_ref,
            FRICTION_BASE + k,
            rough_ref[...] * jnp.sqrt(1.0 + momentum * (1.0 / 6.0)),
        )
    for f in range(3):
        put(table_ref, rows + f, tile(stat_ref, EDGE + f))
    put(table_ref, rows + 12, zone.astype(jnp.float32))
    for r in range(rows):
        put(table_ref, r, tile(lam_ref, r) * (wet_area if r < 12 else half_kappa_area))
    sent = sent_index(index_ref)
    comps = rows // 3
    send_states(table_ref, 0, comps, 0, sent, sent_ref)
    for group in range(4):
        values = gather_by_face(table_ref, rows + 3 * group, *sent)
        for d in range(2):
            at = (comps * 2 + group) * SUB
            sent_ref[d, at : at + SUB, :] = values[d]
    values = gather_tile(table_ref, rows + 12, sent[0], sent[1])
    for d in range(2):
        at = (comps * 2 + 4) * SUB
        sent_ref[d, at : at + SUB, :] = values[d]
    write_messages(sent_ref, (to_right, to_left, to_up, to_down))


def corner_kernel(left_ref, right_ref, up_in, down_in, up_ref, down_ref):
    first = lax.broadcasted_iota(jnp.int32, left_ref.shape, 2) < 4
    left, right = left_ref[...], right_ref[...]
    up_ref[...] = jnp.where(first, right, left)
    down_ref[...] = jnp.where(first, left, right)


def outer_states(src, first_comp, comps, first_row, received, index, out_ref):
    lane, sublane, face, remote = index

    def body(step, carry):
        ends = gather_ends(src, (first_comp + step) * 3, lane, sublane, face)
        for j in range(2):
            values = fill_remote(
                received, first_row + step * 2 + j, lane, remote, [ends[f][j] for f in range(3)]
            )
            for f in range(3):
                at = pl.multiple_of((f * comps * 2 + step * 2 + j) * SUB, SUB)
                out_ref[pl.ds(at, SUB), :] = values[f]
        return carry

    lax.fori_loop(0, comps, body, 0)


def transposed_section(
    section, lam_ref, y_ref, outer_ref, stat_ref, fact_ref, in_ref, out_ref, volume_ref, emit
):
    rows = lam_ref.shape[0] // SUB
    channels = rows // 3 * 2
    layers = (rows - 12) // 3
    edge = [tile(stat_ref, EDGE + f) for f in range(3)]
    outer_edge = [tile(fact_ref, OUTER_EDGE + f) for f in range(3)]
    half_speed = [tile(fact_ref, HALF_SPEED + 3 * section + f) for f in range(3)]
    kappa = tile(stat_ref, KAPPA)
    wet = tile(stat_ref, WET)
    own = [tile(y_ref, r) for r in range(12)]
    result = []
    for r in range(12):
        total = volume_ref[0, r] * own[0]
        for q in range(1, 12):
            total = total + volume_ref[q, r] * own[q]
        result.append(total)
    for f in range(3):
        ends = FACE_NODES[f]
        inner = [edge[f] * own[(ch // 2) * 3 + ends[ch % 2]] for ch in range(8)]
        outer = [outer_edge[f] * tile(outer_ref, f * channels + ch) for ch in range(8)]
        for b in range(8):
            total = half_speed[f] * (inner[b] - outer[b])
            for a in range(8):
                total = total + in_ref[a, b] * inner[a] - out_ref[a, b] * outer[a]
            at = (b // 2) * 3 + ends[b % 2]
            result[at] = result[at] + total
    friction = tile(stat_ref, ZONE_FRICTION) * tile(stat_ref, FRICTION_BASE + section) * wet
    for r in range(3, 9):
        result[r] = result[r] - friction * tile(lam_ref, r)
    exchange = []
    for i in range(3):
        top = tile(lam_ref, 12 + i) - SALT_RETURN * wet * tile(lam_ref, 9 + i)
        exchange.append(kappa * top)
        result[9 + i] = result[9 + i] + exchange[i]
    for r in range(12):
        emit(r, result[r])
    for i in range(3):
        (f0, j0), (f1, j1) = NODE_FACES[i]
        both = edge[f0] + edge[f1]
        from_above = exchange[i]
        for layer in range(layers):
            r = 12 + layer * 3 + i
            value = (
                outer_edge[f0] * tile(outer_ref, f0 * channels + 8 + layer * 2 + j0)
                + outer_edge[f1] * tile(outer_ref, f1 * channels + 8 + layer * 2 + j1)
                - both * tile(y_ref, r)
                - from_above
            )
            if layer + 1 < layers:
                from_above = kappa * (tile(lam_ref, r + 3) - tile(lam_ref, r))
                value = value + from_above
            emit(r, value)


def own_gradients(section, weight, lam_ref, y_ref, x_tiles, stat_ref):
    rows = lam_ref.shape[0] // SUB
    layers = (rows - 12) // 3
    wet = tile(stat_ref, WET)
    kappa = tile(stat_ref, KAPPA)
    momentum = tile(lam_ref, 3) * tile(x_tiles, 3)
    for r in range(4, 9):
        momentum = momentum + tile(lam_ref, r) * tile(x_tiles, r)
    friction = -(weight * wet * tile(stat_ref, FRICTION_BASE + section)) * momentum
    vertical = None
    lateral = None
    for i in range(3):
        (f0, _), (f1, _) = NODE_FACES[i]
        top = tile(lam_ref, 12 + i) - SALT_RETURN * wet * tile(lam_ref, 9 + i)
        total = top * (tile(x_tiles, 9 + i) - tile(x_tiles, 12 + i))
        dots = None
        for layer in range(layers):
            r = 12 + layer * 3 + i
            term = tile(y_ref, r) * tile(x_tiles, r)
            dots = term if dots is None else dots + term
            if layer + 1 < layers:
                total = total + (tile(lam_ref, r + 3) - tile(lam_ref, r)) * (
                    tile(x_tiles, r) - tile(x_tiles, r + 3)
                )
        side = (tile(stat_ref, EDGE + f0) + tile(stat_ref, EDGE + f1)) * dots
        vertical = total if vertical is None else vertical + total
        lateral = side if lateral is None else lateral + side
    return friction, weight * (kappa * vertical - lateral)


def outer_gradients(weight, outer_ref, x_tiles, fact_ref):
    channels = outer_ref.shape[0] // SUB // 3
    values = []
    for f in range(3):
        total = None
        for ch in range(8, channels):
            row = 12 + (ch - 8) // 2 * 3 + FACE_NODES[f][ch % 2]
            term = tile(outer_ref, f * channels + ch) * tile(x_tiles, row)
            total = term if total is None else total + term
        values.append(weight * tile(fact_ref, OUTER_EDGE + f) * total)
    return values


def x_to_tiles(x_ref, section, x_tiles):
    rows = x_ref.shape[3]
    rows_to_tiles(
        lambda b: x_ref[section, 0, 0, :, lanes_of(b)].astype(jnp.float32), x_tiles, rows
    )


def second_kernel(
    cot_ref,
    table_ref,
    stat_ref,
    index_ref,
    x_ref,
    in_ref,
    out_ref,
    volume_ref,
    from_left,
    from_right,
    from_down,
    from_up,
    lam_ref,
    y_ref,
    fact_ref,
    term_ref,
    to_right,
    to_left,
    to_up,
    to_down,
    outer_ref,
    x_tiles,
    sent_ref,
):
    received = (from_left, from_right, from_down, from_up)
    rows = cot_ref.shape[0] // SUB
    comps = rows // 3
    index = partner_index(index_ref)
    lane, sublane, face, remote = index
    outer_states(table_ref, 0, comps, 0, received, index, outer_ref)
    for group in range(4):
        values = gather_by_face(table_ref, rows + 3 * group, lane, sublane, face)
        values = fill_remote(received, comps * 2 + group, lane, remote, values)
        for f in range(3):
            if group == 0:
                put(fact_ref, OUTER_EDGE + f, values[f])
            else:
                k = group - 1
                both = tile(table_ref, rows + 3 * group + f) + values[f]
                put(
                    fact_ref,
                    HALF_SPEED + 3 * k + f,
                    0.5 * jnp.sqrt(1.0 + (0.25 / 8.0) * both),
                )
    values = gather_tile(table_ref, rows + 12, lane, sublane)
    values = fill_remote(received, comps * 2 + 4, lane, remote, values)
    for f in range(3):
        put(fact_ref, OUTER_ZONE + f, values[f])
    wet_area = tile(stat_ref, WET_AREA)
    half_kappa_area = tile(stat_ref, HALF_KAPPA_AREA)

    def emit(r, value):
        lam = (2.0 / 3.0) * (tile(cot_ref, r) + TIME_STEP * value)
        put(lam_ref, r, lam)
        put(y_ref, r, lam * (wet_area if r < 12 else half_kappa_area))

    transposed_section(
        2, cot_ref, table_ref, outer_ref, stat_ref, fact_ref, in_ref, out_ref, volume_ref, emit
    )
    x_to_tiles(x_ref, 0, x_tiles)
    sent = sent_index(index_ref)
    send_states(y_ref, 0, comps, 0, sent, sent_ref)
    send_states(x_tiles, 4, comps - 4, comps * 2, sent, sent_ref)
    write_messages(sent_ref, (to_right, to_left, to_up, to_down))
    x_to_tiles(x_ref, 2, x_tiles)
    weight = TIME_STEP * 2.0 / 3.0
    friction, conduct = own_gradients(2, weight, cot_ref, table_ref, x_tiles, stat_ref)
    put(term_ref, 0, friction)
    put(term_ref, 1, conduct)
    for f, value in enumerate(outer_gradients(weight, outer_ref, x_tiles, fact_ref)):
        put(term_ref, 2 + f, value)


def first_kernel(
    cot_ref,
    lam_ref,
    y_ref,
    stat_ref,
    index_ref,
    fact_ref,
    term_ref,
    x_ref,
    in_ref,
    out_ref,
    volume_ref,
    from_left,
    from_right,
    from_down,
    from_up,
    base_ref,
    next_ref,
    next_y_ref,
    new_term_ref,
    to_right,
    to_left,
    to_up,
    to_down,
    outer_ref,
    x_outer_ref,
    x_tiles,
    sent_ref,
):
    received = (from_left, from_right, from_down, from_up)
    rows = lam_ref.shape[0] // SUB
    comps = rows // 3
    index = partner_index(index_ref)
    outer_states(y_ref, 0, comps, 0, received, index, outer_ref)
    wet_area = tile(stat_ref, WET_AREA)
    half_kappa_area = tile(stat_ref, HALF_KAPPA_AREA)

    def emit(r, value):
        old = tile(lam_ref, r)
        lam = 0.25 * (old + TIME_STEP * value)
        put(next_ref, r, lam)
        put(next_y_ref, r, lam * (wet_area if r < 12 else half_kappa_area))
        put(base_ref, r, (1.0 / 3.0) * tile(cot_ref, r) + 0.75 * old + lam)

    transposed_section(
        1, lam_ref, y_ref, outer_ref, stat_ref, fact_ref, in_ref, out_ref, volume_ref, emit
    )
    send_states(next_y_ref, 0, comps, 0, sent_index(index_ref), sent_ref)
    write_messages(sent_ref, (to_right, to_left, to_up, to_down))
    x_to_tiles(x_ref, 1, x_tiles)
    weight = TIME_STEP * 0.25
    friction, conduct = own_gradients(1, weight, lam_ref, y_ref, x_tiles, stat_ref)
    for f, value in enumerate(outer_gradients(weight, outer_ref, x_tiles, fact_ref)):
        put(new_term_ref, 2 + f, tile(term_ref, 2 + f) + value)
    x_to_tiles(x_ref, 0, x_tiles)
    outer_states(x_tiles, 4, comps - 4, comps * 2, received, index, x_outer_ref)
    friction_0, conduct_0 = own_gradients(0, TIME_STEP, next_ref, next_y_ref, x_tiles, stat_ref)
    friction = friction + friction_0
    conduct = conduct + conduct_0
    channels = (comps - 4) * 2
    for f in range(3):
        total = None
        for ch in range(channels):
            row = 12 + ch // 2 * 3 + FACE_NODES[f][ch % 2]
            term = tile(x_outer_ref, f * channels + ch) * tile(next_y_ref, row)
            total = term if total is None else total + term
        conduct = conduct + TIME_STEP * tile(stat_ref, EDGE + f) * total
    put(new_term_ref, 0, tile(term_ref, 0) + friction)
    put(new_term_ref, 1, tile(term_ref, 1) + conduct)


def zone_kernel(term_ref, stat_ref, fact_ref, conduct_ref, out_ref):
    zones = out_ref.shape[1]
    zone_iota = lax.broadcasted_iota(jnp.int32, (zones, LANES), 0).astype(jnp.float32)
    sub_iota = lax.broadcasted_iota(jnp.int32, (SUB, zones), 0)

    def thirds(value):
        high = value.astype(jnp.bfloat16).astype(jnp.float32)
        rest = value - high
        middle = rest.astype(jnp.bfloat16).astype(jnp.float32)
        return [high, middle, rest - middle]

    def by_zone(values, zone_of, zone_row):
        pieces = sum([thirds(value) for value in values], [])
        left = jnp.concatenate(pieces, axis=0).astype(jnp.bfloat16)
        totals = [jnp.zeros((SUB, zones), jnp.float32) for _ in values]
        for sub in range(SUB):
            line = zone_of[pl.ds(zone_row * SUB + sub, 1), :]
            hot = (jnp.broadcast_to(line, (zones, LANES)) == zone_iota).astype(jnp.float32)
            dots = lax.dot_general(
                left,
                hot.astype(jnp.bfloat16),
                (((1,), (1,)), ((), ())),
                preferred_element_type=jnp.float32,
            )
            for n in range(len(values)):
                at = n * 3 * SUB
                three = dots[at : at + SUB] + dots[at + SUB : at + 2 * SUB]
                three = three + dots[at + 2 * SUB : at + 3 * SUB]
                totals[n] = totals[n] + jnp.where(sub_iota == sub, three, 0.0)
        return totals

    friction, conduct = by_zone([tile(term_ref, 0), tile(term_ref, 1)], stat_ref, ZONE_ID)
    for f in range(3):
        conduct = conduct + by_zone([tile(term_ref, 2 + f)], fact_ref, OUTER_ZONE + f)[0]
    out_ref[0:1, :] = GRAD_WEIGHT * jnp.sum(friction, axis=0, keepdims=True)
    out_ref[1:2, :] = (
        GRAD_WEIGHT * jnp.sum(conduct, axis=0, keepdims=True) / conduct_ref[...]
    )


def last_kernel(
    base_ref,
    lam_ref,
    y_ref,
    stat_ref,
    index_ref,
    fact_ref,
    in_ref,
    out_ref,
    volume_ref,
    from_left,
    from_right,
    from_down,
    from_up,
    adjoint_ref,
    outer_ref,
    sum_ref,
):
    received = (from_left, from_right, from_down, from_up)
    rows = lam_ref.shape[0] // SUB
    outer_states(y_ref, 0, rows // 3, 0, received, partner_index(index_ref), outer_ref)

    def emit(r, value):
        put(sum_ref, r, tile(base_ref, r) + TIME_STEP * value)

    transposed_section(
        0, lam_ref, y_ref, outer_ref, stat_ref, fact_ref, in_ref, out_ref, volume_ref, emit
    )
    for block in range(SUB):
        adjoint_ref[0, 0, :, lanes_of(block)] = sum_ref[pl.ds(block, rows, stride=SUB), :]


def exchange(messages):
    to_right, to_left, to_up, to_down = messages
    from_left = shifted(to_right, "gx", 1)
    from_right = shifted(to_left, "gx", -1)
    corner = pl.BlockSpec((1, to_right.shape[1], LANES), lambda i: (2, 0, 0))
    whole = pl.BlockSpec(memory_space=pl.ANY)
    to_up, to_down = pl.pallas_call(
        corner_kernel,
        grid=(1,),
        in_specs=[corner, corner, whole, whole],
        out_specs=[corner, corner],
        out_shape=[jax.ShapeDtypeStruct(to_up.shape, to_up.dtype)] * 2,
        input_output_aliases={2: 0, 3: 1},
        name="corners",
    )(from_left, from_right, to_up, to_down)
    from_down = shifted(to_up, "gy", 1)
    from_up = shifted(to_down, "gy", -1)
    return from_left, from_right, from_down, from_up


def call(kernel, name, outs, scratch, operands, scalars=()):
    in_memory = pl.BlockSpec(memory_space=pltpu.VMEM)
    in_scalar = pl.BlockSpec(memory_space=pltpu.SMEM)
    return pl.pallas_call(
        kernel,
        in_specs=[in_scalar if n in scalars else in_memory for n in range(len(operands))],
        out_specs=[in_memory] * len(outs),
        out_shape=outs,
        scratch_shapes=scratch,
        compiler_params=pltpu.CompilerParams(vmem_limit_bytes=32 * 1024 * 1024),
        name=name,
    )(*operands)


def local(
    cotangent,
    section_states,
    inverse_area,
    edge_length,
    roughness,
    soil_conductance,
    zone_friction,
    zone_conductivity,
    wet_mask,
    element_zone,
    send_face,
    send_count,
    face_partner,
    volume_matrix,
    flux_in,
    flux_out,
):
    rows = cotangent.shape[2]
    channels = rows // 3 * 2
    zones = zone_friction.shape[0]
    slots = send_face.shape[3]
    f32 = jnp.float32

    def tiles(count, dtype=f32):
        return jax.ShapeDtypeStruct((count * SUB, LANES), dtype)

    def tile_scratch(count, dtype=f32):
        return pltpu.VMEM((count * SUB, LANES), dtype)

    def messages(count):
        return [jax.ShapeDtypeStruct((slots // LANES + 1, count, LANES), f32)] * 4

    def sent_scratch(count):
        return pltpu.VMEM((slots // LANES, count * SUB, LANES), f32)

    square = lambda one: one.reshape(SUB, LANES)
    cot, table, stat, index, *to_send = call(
        prepare_kernel,
        "prepare",
        [tiles(rows), tiles(rows + 13), tiles(STAT_ROWS), tiles(INDEX_ROWS, jnp.int32)]
        + messages(channels + 5),
        [tile_scratch(16), tile_scratch(3, jnp.int32), sent_scratch(channels + 5)],
        [
            cotangent,
            section_states,
            square(inverse_area),
            edge_length,
            square(roughness),
            square(soil_conductance),
            zone_friction.reshape(-1, LANES),
            zone_conductivity.reshape(-1, LANES),
            square(wet_mask),
            square(element_zone),
            send_face,
            face_partner,
        ],
    )
    received = exchange(to_send)
    lam, y, fact, term, *to_send = call(
        second_kernel,
        "section_two",
        [tiles(rows), tiles(rows), tiles(FACT_ROWS), tiles(5)]
        + messages(channels + channels - 8),
        [tile_scratch(3 * channels), tile_scratch(rows), sent_scratch(2 * channels - 8)],
        [cot, table, stat, index, section_states, flux_in, flux_out, volume_matrix, *received],
        (5, 6, 7),
    )
    received = exchange(to_send)
    base, lam, y, term, *to_send = call(
        first_kernel,
        "section_one",
        [tiles(rows), tiles(rows), tiles(rows), tiles(5)] + messages(channels),
        [
            tile_scratch(3 * channels),
            tile_scratch(3 * (channels - 8)),
            tile_scratch(rows),
            sent_scratch(channels),
        ],
        [
            cot,
            lam,
            y,
            stat,
            index,
            fact,
            term,
            section_states,
            flux_in,
            flux_out,
            volume_matrix,
            *received,
        ],
        (8, 9, 10),
    )
    (zone_terms,) = call(
        zone_kernel,
        "zone_sums",
        [jax.ShapeDtypeStruct((2, zones), f32)],
        [],
        [term, stat, fact, zone_conductivity.reshape(1, zones)],
    )
    zone_grads = lax.psum(zone_terms, ("gx", "gy"))
    received = exchange(to_send)
    (adjoint,) = call(
        last_kernel,
        "section_zero",
        [jax.ShapeDtypeStruct(cotangent.shape, f32)],
        [tile_scratch(3 * channels), tile_scratch(rows)],
        [base, lam, y, stat, index, fact, flux_in, flux_out, volume_matrix, *received],
        (6, 7, 8),
    )
    return adjoint, zone_grads


def solution(mesh):
    placed = (
        P("gx", "gy", None, None),
        P(None, "gx", "gy", None, None),
        P("gx", "gy", None),
        P("gx", "gy", None, None),
        P("gx", "gy", None),
        P("gx", "gy", None),
        P(),
        P(),
        P("gx", "gy", None),
        P("gx", "gy", None),
        P("gx", "gy", None, None),
        P("gx", "gy", None),
        P("gx", "gy", None, None),
        P(),
        P(),
        P(),
    )
    return jax.shard_map(
        local,
        mesh=mesh,
        in_specs=placed,
        out_specs=(P("gx", "gy", None, None), P()),
        check_vma=False,
    )
```

time: 624 us -> 145 us (0.23)
  the two profiles are of different devices: /device:TPU:11 before, /device:TPU:1 now
where the time goes in v1:
time: 145 us; the launch traced here: 143 us
  blocking collectives  40.6 us (28%)
  Pallas kernels  37.3 us (26%)
  starting transfers between devices  32.8 us (23%)
  waiting for transfers between devices  18.7 us (13%)
  local copies, waits for them, and re-layouts  12.3 us (8%)
    psum x1, blocking collectives, local(): zone_grads = lax.psum(zone_terms, ('gx', 'gy'))  40.6 us
    pallas_call x5, Pallas kernels, call(): pl.pallas_call(kernel, in_specs=[in_scalar if n in scalars else in_memory...  33.2 us
    ppermute x12, starting transfers between devices, shifted(): return lax.ppermute(x, axis, pairs)  32.8 us
    ppermute x12, waiting for transfers between devices, shifted(): return lax.ppermute(x, axis, pairs)  18.7 us
    unnamed x66, local copies, waits for them, and re-layouts  12.3 us
    pallas_call x3, Pallas kernels, exchange(): pl.pallas_call(corner_kernel, grid=(1,), in_specs=[corner, corner, whole,...  4.13 us
  transfers between devices with their start and end apart: 12, of which 6 were waited for; matrix products, arithmetic and copies ran while one was open for 0% of the time, Pallas kernels for 0%

profile of v1, /device:TPU:1, one launch (start us, length us, event | category | flops | bytes accessed | tf_op | source)
XLA Modules:
  0.0 142.7 jit_solution(16321372021313381139)
XLA Ops:
  0.7 0.8 copy.24.edge_ref
  1.5 1.0 copy.23.cot_ref
  3.2 2.2 %prepare.1 = (f32[336,128]{1,0:T(8,128)S(1)}, f32[440,128]{1,0:T(8,128)S(1)}, f32[96,128]{1,0:T(8,128)S(1)}, s32[144,128]{1,0:T(8,128)S(1)}, f32[3,33,128]{2,1,0...) custom-call(f32[1,1,42,1024]{3,2,1,0:T(8,128)S(1)} %copy.23.cot_ref, ...), custom_call_target="tpu_custom_call" | custom-call | tf_op jit(solution)/shard_map/prepare/pallas_call | solution.py:635
  6.6 3.9 %collective-permute-start = (f32[3,33,128]{2,1,0:T(8,128)S(1)}, f32[3,33,128]{2,1,0:T(8,128)S(1)}, u32[]{:S(2)}, u32[]{:S(2)}) collective-permute-start(f32[3,33,128]{2,1,0:T(8,128)S(1)} %get-tuple-element.36), channel_id=1, source_target_pairs={{0,4},{4,8},{8,12},{12,16},{16,20},{20,24},{24,28},{1,5},{5,9},{9,... | collective-permute-start | bytes 152072 | tf_op jit(solution)/shard_map/ppermute | solution.py:49
  10.5 1.3 collective-permute-start.1
  11.8 3.6 %collective-permute-done.1.right_ref.from_right = f32[3,33,128]{2,1,0:T(8,128)S(1)} collective-permute-done((f32[3,33,128]{2,1,0:T(8,128)S(1)}, f32[3,33,128]{2,1,0:T(8,128)S(1)}, u32[]{:S(2)}, u32[]{:S(2)}) %collective-permute-start.1) | collective-permute-done | bytes 50720 | tf_op jit(solution)/shard_map/ppermute | solution.py:49
  16.1 1.4 corners.3
  17.5 5.3 %collective-permute-start.2 = (f32[3,33,128]{2,1,0:T(8,128)}, f32[3,33,128]{2,1,0:T(8,128)S(1)}, u32[]{:S(2)}, u32[]{:S(2)}) collective-permute-start(f32[3,33,128]{2,1,0:T(8,128)} %get-tuple-element.40), channel_id=1, source_target_pairs={{0,1},{1,2},{2,3},{4,5},{5,6},{6,7},{8,9},{9,10},{10,11},{12,13},{... | collective-permute-start | bytes 152072 | tf_op jit(solution)/shard_map/ppermute | solution.py:49
  22.8 1.9 %collective-permute-start.3 = (f32[3,33,128]{2,1,0:T(8,128)}, f32[3,33,128]{2,1,0:T(8,128)S(1)}, u32[]{:S(2)}, u32[]{:S(2)}) collective-permute-start(f32[3,33,128]{2,1,0:T(8,128)} %get-tuple-element.41), channel_id=1, source_target_pairs={{1,0},{2,1},{3,2},{5,4},{6,5},{7,6},{9,8},{10,9},{11,10},{13,12},{... | collective-permute-start | bytes 152072 | tf_op jit(solution)/shard_map/ppermute | solution.py:49
  24.7 3.8 %collective-permute-done.3.from_up = f32[3,33,128]{2,1,0:T(8,128)S(1)} collective-permute-done((f32[3,33,128]{2,1,0:T(8,128)}, f32[3,33,128]{2,1,0:T(8,128)S(1)}, u32[]{:S(2)}, u32[]{:S(2)}) %collective-permute-start.3) | collective-permute-done | bytes 50720 | tf_op jit(solution)/shard_map/ppermute | solution.py:49
  28.5 0.8 copy-done.6
  29.4 0.8 copy-done.8
  30.2 10.9 %section_two.1 = (f32[336,128]{1,0:T(8,128)S(1)}, f32[336,128]{1,0:T(8,128)S(1)}, f32[120,128]{1,0:T(8,128)S(1)}, f32[40,128]{1,0:T(8,128)S(1)}, f32[3,48,128]{2...) custom-call(f32[336,128]{1,0:T(8,128)S(1)} %get-tuple-element.32.cot_ref, ...), custom_call_target="tpu_custom_call" | custom-call | tf_op jit(solution)/shard_map/section_two/pallas_call | solution.py:635
  42.3 4.1 %collective-permute-start.4 = (f32[3,48,128]{2,1,0:T(8,128)S(1)}, f32[3,48,128]{2,1,0:T(8,128)S(1)}, u32[]{:S(2)}, u32[]{:S(2)}) collective-permute-start(f32[3,48,128]{2,1,0:T(8,128)S(1)} %get-tuple-element.46), channel_id=1, source_target_pairs={{0,4},{4,8},{8,12},{12,16},{16,20},{20,24},{24,28},{1,5},{5,9},{9,... | collective-permute-start | bytes 221192 | tf_op jit(solution)/shard_map/ppermute | solution.py:49
  46.4 1.3 collective-permute-start.5
  47.8 3.7 %collective-permute-done.5.right_ref.from_right = f32[3,48,128]{2,1,0:T(8,128)S(1)} collective-permute-done((f32[3,48,128]{2,1,0:T(8,128)S(1)}, f32[3,48,128]{2,1,0:T(8,128)S(1)}, u32[]{:S(2)}, u32[]{:S(2)}) %collective-permute-start.5) | collective-permute-done | bytes 73760 | tf_op jit(solution)/shard_map/ppermute | solution.py:49
  52.1 1.4 corners.4
  53.5 3.4 %collective-permute-start.6 = (f32[3,48,128]{2,1,0:T(8,128)}, f32[3,48,128]{2,1,0:T(8,128)S(1)}, u32[]{:S(2)}, u32[]{:S(2)}) collective-permute-start(f32[3,48,128]{2,1,0:T(8,128)} %get-tuple-element.50), channel_id=1, source_target_pairs={{0,1},{1,2},{2,3},{4,5},{5,6},{6,7},{8,9},{9,10},{10,11},{12,13},{... | collective-permute-start | bytes 221192 | tf_op jit(solution)/shard_map/ppermute | solution.py:49
  56.9 1.9 %collective-permute-start.7 = (f32[3,48,128]{2,1,0:T(8,128)}, f32[3,48,128]{2,1,0:T(8,128)S(1)}, u32[]{:S(2)}, u32[]{:S(2)}) collective-permute-start(f32[3,48,128]{2,1,0:T(8,128)} %get-tuple-element.51), channel_id=1, source_target_pairs={{1,0},{2,1},{3,2},{5,4},{6,5},{7,6},{9,8},{10,9},{11,10},{13,12},{... | collective-permute-start | bytes 221192 | tf_op jit(solution)/shard_map/ppermute | solution.py:49
  58.8 3.9 %collective-permute-done.7.from_up = f32[3,48,128]{2,1,0:T(8,128)S(1)} collective-permute-done((f32[3,48,128]{2,1,0:T(8,128)}, f32[3,48,128]{2,1,0:T(8,128)S(1)}, u32[]{:S(2)}, u32[]{:S(2)}) %collective-permute-start.7) | collective-permute-done | bytes 73760 | tf_op jit(solution)/shard_map/ppermute | solution.py:49
  62.8 0.9 copy-done.2
  63.7 0.9 copy-done.4
  64.6 12.7 %section_one.1 = (f32[336,128]{1,0:T(8,128)S(1)}, f32[336,128]{1,0:T(8,128)S(1)}, f32[336,128]{1,0:T(8,128)S(1)}, f32[40,128]{1,0:T(8,128)S(1)}, f32[3,28,128]{2...) custom-call(f32[336,128]{1,0:T(8,128)S(1)} %get-tuple-element.32.cot_ref, ...), custom_call_target="tpu_custom_call" | custom-call | tf_op jit(solution)/shard_map/section_one/pallas_call | solution.py:635
  78.5 3.1 %collective-permute-start.8 = (f32[3,28,128]{2,1,0:T(8,128)S(1)}, f32[3,28,128]{2,1,0:T(8,128)S(1)}, u32[]{:S(2)}, u32[]{:S(2)}) collective-permute-start(f32[3,28,128]{2,1,0:T(8,128)S(1)} %get-tuple-element.55), channel_id=1, source_target_pairs={{0,4},{4,8},{8,12},{12,16},{16,20},{20,24},{24,28},{1,5},{5,9},{9,... | collective-permute-start | bytes 129032 | tf_op jit(solution)/shard_map/ppermute | solution.py:49
  81.6 1.3 collective-permute-start.9
  82.9 3.5 %collective-permute-done.9.right_ref.from_right = f32[3,28,128]{2,1,0:T(8,128)S(1)} collective-permute-done((f32[3,28,128]{2,1,0:T(8,128)S(1)}, f32[3,28,128]{2,1,0:T(8,128)S(1)}, u32[]{:S(2)}, u32[]{:S(2)}) %collective-permute-start.9) | collective-permute-done | bytes 43040 | tf_op jit(solution)/shard_map/ppermute | solution.py:49
  87.0 1.4 corners.5
  88.4 3.4 %collective-permute-start.10 = (f32[3,28,128]{2,1,0:T(8,128)}, f32[3,28,128]{2,1,0:T(8,128)S(1)}, u32[]{:S(2)}, u32[]{:S(2)}) collective-permute-start(f32[3,28,128]{2,1,0:T(8,128)} %get-tuple-element.59), channel_id=1, source_target_pairs={{0,1},{1,2},{2,3},{4,5},{5,6},{6,7},{8,9},{9,10},{10,11},{12,13},{... | collective-permute-start | bytes 129032 | tf_op jit(solution)/shard_map/ppermute | solution.py:49
  91.8 1.9 %collective-permute-start.11 = (f32[3,28,128]{2,1,0:T(8,128)}, f32[3,28,128]{2,1,0:T(8,128)S(1)}, u32[]{:S(2)}, u32[]{:S(2)}) collective-permute-start(f32[3,28,128]{2,1,0:T(8,128)} %get-tuple-element.60), channel_id=1, source_target_pairs={{1,0},{2,1},{3,2},{5,4},{6,5},{7,6},{9,8},{10,9},{11,10},{13,12},{... | collective-permute-start | bytes 129032 | tf_op jit(solution)/shard_map/ppermute | solution.py:49
  94.4 40.6 %psum.7 = f32[2,128]{1,0:T(2,128)} all-reduce(f32[2,128]{1,0:T(2,128)S(1)} %zone_sums.1), channel_id=1, replica_groups=mesh['gx'=8,'gy'=4] {'gx','gy'}, use_global_device_ids=true, to_apply=%region_0.0 | all-reduce | flops 256 | bytes 2048 | tf_op jit(solution)/shard_map/psum | solution.py:748
  135.1 6.7 %section_zero.1 = f32[1,1,42,1024]{3,2,1,0:T(8,128)S(1)} custom-call(f32[336,128]{1,0:T(8,128)S(1)} %get-tuple-element.52.base_ref, f32[336,128]{1,0:T(8,128)S(1)} %get-tuple-element.53.lam_ref, f32[336,128]{1,0:T(8,128)S(1)} %get-tuple-element.54.y_ref, f32[96,128]{1,0:T(8,128)S(1)} %get-tuple-element.34.stat_ref, ...), custom_call_target="tpu_custom_call" | custom-call | tf_op jit(solution)/shard_map/section_zero/pallas_call | solution.py:635
  141.8 0.8 copy.26
  (67 shorter events, 7.1 us)
Async XLA Ops:
  0.6 0.8 copy-start.30
  0.6 1.9 %copy-start = (bf16[3,1,1,42,1024]{4,3,2,1,0:T(8,128)(2,1)S(1)}, bf16[3,1,1,42,1024]{4,3,2,1,0:T(8,128)(2,1)}, u32[]{:S(2)}) copy-start(bf16[3,1,1,42,1024]{4,3,2,1,0:T(8,128)(2,1)} %x_ref.5) | copy-start | bytes 774148
  1.4 1.1 copy-start.24
  1.4 1.1 copy-start.25
  1.4 1.1 copy-start.26
  1.5 1.1 copy-start.27
  2.4 0.7 copy-start.22
  2.5 0.7 copy-start.23
  6.6 5.2 %collective-permute-start = (f32[3,33,128]{2,1,0:T(8,128)S(1)}, f32[3,33,128]{2,1,0:T(8,128)S(1)}, u32[]{:S(2)}, u32[]{:S(2)}) collective-permute-start(f32[3,33,128]{2,1,0:T(8,128)S(1)} %get-tuple-element.36), channel_id=1, source_target_pairs={{0,4},{4,8},{8,12},{12,16},{16,20},{20,24},{24,28},{1,5},{5,9},{9,... | collective-permute-start | bytes 152072 | tf_op jit(solution)/shard_map/ppermute | solution.py:49
  10.5 5.0 %collective-permute-start.1 = (f32[3,33,128]{2,1,0:T(8,128)S(1)}, f32[3,33,128]{2,1,0:T(8,128)S(1)}, u32[]{:S(2)}, u32[]{:S(2)}) collective-permute-start(f32[3,33,128]{2,1,0:T(8,128)S(1)} %get-tuple-element.37), channel_id=1, source_target_pairs={{4,0},{8,4},{12,8},{16,12},{20,16},{24,20},{28,24},{5,1},{9,5},{13... | collective-permute-start | bytes 152072 | tf_op jit(solution)/shard_map/ppermute | solution.py:49
  11.8 3.7 %copy-start.5 = (f32[3,33,128]{2,1,0:T(8,128)}, f32[3,33,128]{2,1,0:T(8,128)S(1)}, u32[]{:S(2)}) copy-start(f32[3,33,128]{2,1,0:T(8,128)S(1)} %collective-permute-done.left_ref.from_left) | copy-start | bytes 152068
  16.1 12.4 %copy-start.20 = (f32[8,8]{1,0:T(8,128)S(1)}, f32[8,8]{1,0:T(8,128)}, u32[]{:S(2)}) copy-start(f32[8,8]{1,0:T(8,128)} %in_ref.5) | copy-start | bytes 772
  16.1 12.4 %copy-start.21 = (f32[8,8]{1,0:T(8,128)S(1)}, f32[8,8]{1,0:T(8,128)}, u32[]{:S(2)}) copy-start(f32[8,8]{1,0:T(8,128)} %out_ref.5) | copy-start | bytes 772
  17.5 11.0 %copy-start.15 = (f32[12,12]{1,0:T(8,128)S(1)}, f32[12,12]{1,0:T(8,128)}, u32[]{:S(2)}) copy-start(f32[12,12]{1,0:T(8,128)} %volume_ref.5) | copy-start | bytes 1732
  17.5 7.2 %collective-permute-start.2 = (f32[3,33,128]{2,1,0:T(8,128)}, f32[3,33,128]{2,1,0:T(8,128)S(1)}, u32[]{:S(2)}, u32[]{:S(2)}) collective-permute-start(f32[3,33,128]{2,1,0:T(8,128)} %get-tuple-element.40), channel_id=1, source_target_pairs={{0,1},{1,2},{2,3},{4,5},{5,6},{6,7},{8,9},{9,10},{10,11},{12,13},{... | collective-permute-start | bytes 152072 | tf_op jit(solution)/shard_map/ppermute | solution.py:49
  22.8 5.8 %collective-permute-start.3 = (f32[3,33,128]{2,1,0:T(8,128)}, f32[3,33,128]{2,1,0:T(8,128)S(1)}, u32[]{:S(2)}, u32[]{:S(2)}) collective-permute-start(f32[3,33,128]{2,1,0:T(8,128)} %get-tuple-element.41), channel_id=1, source_target_pairs={{1,0},{2,1},{3,2},{5,4},{6,5},{7,6},{9,8},{10,9},{11,10},{13,12},{... | collective-permute-start | bytes 152072 | tf_op jit(solution)/shard_map/ppermute | solution.py:49
  28.5 0.8 copy-start.6
  29.4 0.8 copy-start.8
  42.3 5.5 %collective-permute-start.4 = (f32[3,48,128]{2,1,0:T(8,128)S(1)}, f32[3,48,128]{2,1,0:T(8,128)S(1)}, u32[]{:S(2)}, u32[]{:S(2)}) collective-permute-start(f32[3,48,128]{2,1,0:T(8,128)S(1)} %get-tuple-element.46), channel_id=1, source_target_pairs={{0,4},{4,8},{8,12},{12,16},{16,20},{20,24},{24,28},{1,5},{5,9},{9,... | collective-permute-start | bytes 221192 | tf_op jit(solution)/shard_map/ppermute | solution.py:49
  46.4 5.1 %collective-permute-start.5 = (f32[3,48,128]{2,1,0:T(8,128)S(1)}, f32[3,48,128]{2,1,0:T(8,128)S(1)}, u32[]{:S(2)}, u32[]{:S(2)}) collective-permute-start(f32[3,48,128]{2,1,0:T(8,128)S(1)} %get-tuple-element.47), channel_id=1, source_target_pairs={{4,0},{8,4},{12,8},{16,12},{20,16},{24,20},{28,24},{5,1},{9,5},{13... | collective-permute-start | bytes 221192 | tf_op jit(solution)/shard_map/ppermute | solution.py:49
  47.8 3.7 %copy-start.1 = (f32[3,48,128]{2,1,0:T(8,128)}, f32[3,48,128]{2,1,0:T(8,128)S(1)}, u32[]{:S(2)}) copy-start(f32[3,48,128]{2,1,0:T(8,128)S(1)} %collective-permute-done.4.left_ref.from_left) | copy-start | bytes 221188
  53.5 5.3 %collective-permute-start.6 = (f32[3,48,128]{2,1,0:T(8,128)}, f32[3,48,128]{2,1,0:T(8,128)S(1)}, u32[]{:S(2)}, u32[]{:S(2)}) collective-permute-start(f32[3,48,128]{2,1,0:T(8,128)} %get-tuple-element.50), channel_id=1, source_target_pairs={{0,1},{1,2},{2,3},{4,5},{5,6},{6,7},{8,9},{9,10},{10,11},{12,13},{... | collective-permute-start | bytes 221192 | tf_op jit(solution)/shard_map/ppermute | solution.py:49
  56.9 5.9 %collective-permute-start.7 = (f32[3,48,128]{2,1,0:T(8,128)}, f32[3,48,128]{2,1,0:T(8,128)S(1)}, u32[]{:S(2)}, u32[]{:S(2)}) collective-permute-start(f32[3,48,128]{2,1,0:T(8,128)} %get-tuple-element.51), channel_id=1, source_target_pairs={{1,0},{2,1},{3,2},{5,4},{6,5},{7,6},{9,8},{10,9},{11,10},{13,12},{... | collective-permute-start | bytes 221192 | tf_op jit(solution)/shard_map/ppermute | solution.py:49
  62.8 0.9 copy-start.2
  63.7 0.9 copy-start.4
  78.5 4.4 %collective-permute-start.8 = (f32[3,28,128]{2,1,0:T(8,128)S(1)}, f32[3,28,128]{2,1,0:T(8,128)S(1)}, u32[]{:S(2)}, u32[]{:S(2)}) collective-permute-start(f32[3,28,128]{2,1,0:T(8,128)S(1)} %get-tuple-element.55), channel_id=1, source_target_pairs={{0,4},{4,8},{8,12},{12,16},{16,20},{20,24},{24,28},{1,5},{5,9},{9,... | collective-permute-start | bytes 129032 | tf_op jit(solution)/shard_map/ppermute | solution.py:49
  81.6 4.8 %collective-permute-start.9 = (f32[3,28,128]{2,1,0:T(8,128)S(1)}, f32[3,28,128]{2,1,0:T(8,128)S(1)}, u32[]{:S(2)}, u32[]{:S(2)}) collective-permute-start(f32[3,28,128]{2,1,0:T(8,128)S(1)} %get-tuple-element.56), channel_id=1, source_target_pairs={{4,0},{8,4},{12,8},{16,12},{20,16},{24,20},{28,24},{5,1},{9,5},{13... | collective-permute-start | bytes 129032 | tf_op jit(solution)/shard_map/ppermute | solution.py:49
  82.9 3.5 %copy-start.9 = (f32[3,28,128]{2,1,0:T(8,128)}, f32[3,28,128]{2,1,0:T(8,128)S(1)}, u32[]{:S(2)}) copy-start(f32[3,28,128]{2,1,0:T(8,128)S(1)} %collective-permute-done.8.left_ref.from_left) | copy-start | bytes 129028
  88.4 46.7 %collective-permute-start.10 = (f32[3,28,128]{2,1,0:T(8,128)}, f32[3,28,128]{2,1,0:T(8,128)S(1)}, u32[]{:S(2)}, u32[]{:S(2)}) collective-permute-start(f32[3,28,128]{2,1,0:T(8,128)} %get-tuple-element.59), channel_id=1, source_target_pairs={{0,1},{1,2},{2,3},{4,5},{5,6},{6,7},{8,9},{9,10},{10,11},{12,13},{... | collective-permute-start | bytes 129032 | tf_op jit(solution)/shard_map/ppermute | solution.py:49
  91.8 43.3 %collective-permute-start.11 = (f32[3,28,128]{2,1,0:T(8,128)}, f32[3,28,128]{2,1,0:T(8,128)S(1)}, u32[]{:S(2)}, u32[]{:S(2)}) collective-permute-start(f32[3,28,128]{2,1,0:T(8,128)} %get-tuple-element.60), channel_id=1, source_target_pairs={{1,0},{2,1},{3,2},{5,4},{6,5},{7,6},{9,8},{10,9},{11,10},{13,12},{... | collective-permute-start | bytes 129032 | tf_op jit(solution)/shard_map/ppermute | solution.py:49
  93.7 41.4 %copy-start.10 = (f32[3,28,128]{2,1,0:T(8,128)S(1)}, f32[3,28,128]{2,1,0:T(8,128)}, u32[]{:S(2)}) copy-start(f32[3,28,128]{2,1,0:T(8,128)} %copy-done.9) | copy-start | bytes 129028
  93.7 41.4 %copy-start.12 = (f32[3,28,128]{2,1,0:T(8,128)S(1)}, f32[3,28,128]{2,1,0:T(8,128)}, u32[]{:S(2)}) copy-start(f32[3,28,128]{2,1,0:T(8,128)} %copy-done.11) | copy-start | bytes 129028
  (11 other events, 6.9 us)

commit v2 on v1

--- a/solution.py
+++ b/solution.py
@@ -141,9 +141,9 @@
     count = to_right.shape[1]
     for ref, direction in ((to_right, 6), (to_left, 1), (to_up, 4), (to_down, 3)):
         for block in range(2):
-            ref[block] = sent_ref[block, pl.ds(direction, count, stride=SUB), :]
+            ref[block] = sent_ref.at[block][pl.ds(direction, count, stride=SUB), :]
     for ref, direction in ((to_right, 5), (to_left, 2)):
-        ref[2] = sent_ref[0, pl.ds(direction, count, stride=SUB), :]
+        ref[2] = sent_ref.at[0][pl.ds(direction, count, stride=SUB), :]
 
 
 def prepare_kernel(
@@ -159,7 +159,6 @@
     zone_ref,
     send_ref,
     partner_ref,
-    lam_ref,
     table_ref,
     stat_ref,
     index_ref,
@@ -168,16 +167,13 @@
     to_up,
     to_down,
     x_tiles,
-    int_tiles,
     sent_ref,
 ):
-    rows = cot_ref.shape[2]
+    rows = cot_ref.shape[0] // SUB
     sections = x_ref.shape[0]
-    rows_to_tiles(lambda b: cot_ref[0, 0, :, lanes_of(b)], lam_ref, rows)
-    rows_to_tiles(lambda b: partner_ref[0, 0, :, lanes_of(b)], int_tiles, 3)
     face_total = 3 * SUB * LANES
     for f in range(3):
-        partner = tile(int_tiles, f)
+        partner = tile(partner_ref, f)
         beyond = partner - face_total
         direction = jnp.right_shift(beyond, 8)
         half = jnp.bitwise_and(jnp.right_shift(beyond, 7), 1)
@@ -224,7 +220,7 @@
     put(stat_ref, WET, wet)
     put(stat_ref, ZONE_FRICTION, factors[0])
     put(stat_ref, ZONE_ID, zone.astype(jnp.float32))
-    rows_to_tiles(lambda b: edge_ref[0, 0, :, lanes_of(b)], stat_ref.at[EDGE * SUB : (EDGE + 3) * SUB], 3)
+    stat_ref[EDGE * SUB : (EDGE + 3) * SUB, :] = edge_ref[...]
     for k in range(sections):
         rows_to_tiles(
             lambda b: x_ref[k, 0, 0, 0:16, lanes_of(b)].astype(jnp.float32), x_tiles, 16
@@ -246,7 +242,7 @@
         put(table_ref, rows + f, tile(stat_ref, EDGE + f))
     put(table_ref, rows + 12, zone.astype(jnp.float32))
     for r in range(rows):
-        put(table_ref, r, tile(lam_ref, r) * (wet_area if r < 12 else half_kappa_area))
+        put(table_ref, r, tile(cot_ref, r) * (wet_area if r < 12 else half_kappa_area))
     sent = sent_index(index_ref)
     comps = rows // 3
     send_states(table_ref, 0, comps, 0, sent, sent_ref)
@@ -262,7 +258,8 @@
     write_messages(sent_ref, (to_right, to_left, to_up, to_down))
 
 
-def corner_kernel(left_ref, right_ref, up_in, down_in, up_ref, down_ref):
+def corner_kernel(left_ref, right_ref, up_in, down_in, *rest):
+    up_ref, down_ref = rest[-2:]
     first = lax.broadcasted_iota(jnp.int32, left_ref.shape, 2) < 4
     left, right = left_ref[...], right_ref[...]
     up_ref[...] = jnp.where(first, right, left)
@@ -593,23 +590,24 @@
     from_up,
     adjoint_ref,
     outer_ref,
-    sum_ref,
 ):
     received = (from_left, from_right, from_down, from_up)
     rows = lam_ref.shape[0] // SUB
     outer_states(y_ref, 0, rows // 3, 0, received, partner_index(index_ref), outer_ref)
 
     def emit(r, value):
-        put(sum_ref, r, tile(base_ref, r) + TIME_STEP * value)
+        put(adjoint_ref, r, tile(base_ref, r) + TIME_STEP * value)
 
     transposed_section(
         0, lam_ref, y_ref, outer_ref, stat_ref, fact_ref, in_ref, out_ref, volume_ref, emit
     )
-    for block in range(SUB):
-        adjoint_ref[0, 0, :, lanes_of(block)] = sum_ref[pl.ds(block, rows, stride=SUB), :]
-
-
-def exchange(messages):
+
+
+def total_kernel(zone_ref, adjoint_ref, grads_ref):
+    grads_ref[...] = jnp.sum(zone_ref[...], axis=0)
+
+
+def exchange(messages, *ahead):
     to_right, to_left, to_up, to_down = messages
     from_left = shifted(to_right, "gx", 1)
     from_right = shifted(to_left, "gx", -1)
@@ -618,23 +616,28 @@
     to_up, to_down = pl.pallas_call(
         corner_kernel,
         grid=(1,),
-        in_specs=[corner, corner, whole, whole],
+        in_specs=[corner, corner, whole, whole] + [pl.BlockSpec(memory_space=pltpu.HBM)] * len(ahead),
         out_specs=[corner, corner],
         out_shape=[jax.ShapeDtypeStruct(to_up.shape, to_up.dtype)] * 2,
         input_output_aliases={2: 0, 3: 1},
         name="corners",
-    )(from_left, from_right, to_up, to_down)
+    )(from_left, from_right, to_up, to_down, *ahead)
     from_down = shifted(to_up, "gy", 1)
     from_up = shifted(to_down, "gy", -1)
     return from_left, from_right, from_down, from_up
 
 
-def call(kernel, name, outs, scratch, operands, scalars=()):
+def call(kernel, name, outs, scratch, operands, scalars=(), anywhere=()):
     in_memory = pl.BlockSpec(memory_space=pltpu.VMEM)
     in_scalar = pl.BlockSpec(memory_space=pltpu.SMEM)
+    unread = pl.BlockSpec(memory_space=pltpu.HBM)
+    specs = [
+        in_scalar if n in scalars else unread if n in anywhere else in_memory
+        for n in range(len(operands))
+    ]
     return pl.pallas_call(
         kernel,
-        in_specs=[in_scalar if n in scalars else in_memory for n in range(len(operands))],
+        in_specs=specs,
         out_specs=[in_memory] * len(outs),
         out_shape=outs,
         scratch_shapes=scratch,
@@ -680,17 +683,18 @@
         return pltpu.VMEM((slots // LANES, count * SUB, LANES), f32)
 
     square = lambda one: one.reshape(SUB, LANES)
-    cot, table, stat, index, *to_send = call(
+    cot = cotangent.reshape(rows * SUB, LANES)
+    table, stat, index, *to_send = call(
         prepare_kernel,
         "prepare",
-        [tiles(rows), tiles(rows + 13), tiles(STAT_ROWS), tiles(INDEX_ROWS, jnp.int32)]
+        [tiles(rows + 13), tiles(STAT_ROWS), tiles(INDEX_ROWS, jnp.int32)]
         + messages(channels + 5),
-        [tile_scratch(16), tile_scratch(3, jnp.int32), sent_scratch(channels + 5)],
+        [tile_scratch(16), sent_scratch(channels + 5)],
         [
-            cotangent,
+            cot,
             section_states,
             square(inverse_area),
-            edge_length,
+            edge_length.reshape(3 * SUB, LANES),
             square(roughness),
             square(soil_conductance),
             zone_friction.reshape(-1, LANES),
@@ -698,7 +702,7 @@
             square(wet_mask),
             square(element_zone),
             send_face,
-            face_partner,
+            face_partner.reshape(3 * SUB, LANES),
         ],
     )
     received = exchange(to_send)
@@ -745,17 +749,36 @@
         [],
         [term, stat, fact, zone_conductivity.reshape(1, zones)],
     )
-    zone_grads = lax.psum(zone_terms, ("gx", "gy"))
-    received = exchange(to_send)
+    all_terms = lax.all_gather(zone_terms, ("gx", "gy"))
+    received = exchange(to_send, zone_terms)
     (adjoint,) = call(
         last_kernel,
         "section_zero",
-        [jax.ShapeDtypeStruct(cotangent.shape, f32)],
-        [tile_scratch(3 * channels), tile_scratch(rows)],
-        [base, lam, y, stat, index, fact, flux_in, flux_out, volume_matrix, *received],
+        [tiles(rows)],
+        [tile_scratch(3 * channels)],
+        [
+            base,
+            lam,
+            y,
+            stat,
+            index,
+            fact,
+            flux_in,
+            flux_out,
+            volume_matrix,
+            *received,
+        ],
         (6, 7, 8),
     )
-    return adjoint, zone_grads
+    (zone_grads,) = call(
+        total_kernel,
+        "zone_total",
+        [jax.ShapeDtypeStruct((2, zones), f32)],
+        [],
+        [all_terms, adjoint],
+        anywhere=(1,),
+    )
+    return adjoint.reshape(cotangent.shape), zone_grads
 
 
 def solution(mesh):

time: 145 us -> 147 us (1.014)
  local copies, waits for them, and re-layouts: 12.3 us -> 17.1 us
  blocking collectives: 40.6 us -> 38.3 us
    psum x1 -> x0, blocking collectives: 40.6 us -> none  [local(): zone_grads = lax.psum(zone_terms, ('gx', 'gy'))]
    all_gather x0 -> x1, blocking collectives: none -> 38.3 us  [local(): all_terms = lax.all_gather(zone_terms, ('gx', 'gy'))]
    unnamed x66 -> x76, local copies, waits for them, and re-layouts: 12.3 us -> 17.1 us
    pallas_call x5 -> x6, Pallas kernels: 33.2 us -> 34.4 us  [call(): pl.pallas_call(kernel, in_specs=specs, out_specs=[in_memory] * len(outs),...]
where the time goes in v2:
time: 147 us; the launch traced here: 146 us
  Pallas kernels  38.5 us (26%)
  blocking collectives  38.3 us (26%)
  starting transfers between devices  32.9 us (22%)
  waiting for transfers between devices  18 us (12%)
  local copies, waits for them, and re-layouts  17.1 us (12%)
    all_gather x1, blocking collectives, local(): all_terms = lax.all_gather(zone_terms, ('gx', 'gy'))  38.3 us
    pallas_call x6, Pallas kernels, call(): pl.pallas_call(kernel, in_specs=specs, out_specs=[in_memory] * len(outs),...  34.4 us
    ppermute x12, starting transfers between devices, shifted(): return lax.ppermute(x, axis, pairs)  32.9 us
    ppermute x12, waiting for transfers between devices, shifted(): return lax.ppermute(x, axis, pairs)  18 us
    unnamed x76, local copies, waits for them, and re-layouts  17.1 us
    pallas_call x3, Pallas kernels, exchange(): pl.pallas_call(corner_kernel, grid=(1,), in_specs=[corner, corner, whole,...  4.12 us
  transfers between devices with their start and end apart: 12, of which 6 were waited for; matrix products, arithmetic and copies ran while one was open for 0% of the time, Pallas kernels for 0%

profile of v2, /device:TPU:1, one launch (start us, length us, event | category | flops | bytes accessed | tf_op | source)
XLA Modules:
  0.0 145.7 jit_solution(5850874571785688342)
XLA Ops:
  1.4 1.0 copy-done
  2.3 0.9 copy-done.2
  7.4 2.1 %prepare.1 = (f32[440,128]{1,0:T(8,128)S(1)}, f32[96,128]{1,0:T(8,128)S(1)}, s32[144,128]{1,0:T(8,128)S(1)}, f32[3,33,128]{2,1,0:T(8,128)S(1)}, f32[3,33,128]{2,...) custom-call(f32[336,128]{1,0:T(8,128)S(1)} %bitcast.12, bf16[3,1,1,42,1024]{4,3,2,1,0:T(8,128)(2,1)S(1)} %copy-done, ...), custom_call_target="tpu_custom_call" | custom-call | tf_op jit(solution)/shard_map/prepare/pallas_call | solution.py:638
  10.8 4.1 %collective-permute-start = (f32[3,33,128]{2,1,0:T(8,128)S(1)}, f32[3,33,128]{2,1,0:T(8,128)S(1)}, u32[]{:S(2)}, u32[]{:S(2)}) collective-permute-start(f32[3,33,128]{2,1,0:T(8,128)S(1)} %get-tuple-element.34), channel_id=1, source_target_pairs={{0,4},{4,8},{8,12},{12,16},{16,20},{20,24},{24,28},{1,5},{5,9},{9,... | collective-permute-start | bytes 152072 | tf_op jit(solution)/shard_map/ppermute | solution.py:49
  14.9 1.3 collective-permute-start.1
  16.2 3.6 %collective-permute-done.1.right_ref.from_right = f32[3,33,128]{2,1,0:T(8,128)S(1)} collective-permute-done((f32[3,33,128]{2,1,0:T(8,128)S(1)}, f32[3,33,128]{2,1,0:T(8,128)S(1)}, u32[]{:S(2)}, u32[]{:S(2)}) %collective-permute-start.1) | collective-permute-done | bytes 50720 | tf_op jit(solution)/shard_map/ppermute | solution.py:49
  20.4 1.4 corners.3
  21.8 5.3 %collective-permute-start.2 = (f32[3,33,128]{2,1,0:T(8,128)}, f32[3,33,128]{2,1,0:T(8,128)S(1)}, u32[]{:S(2)}, u32[]{:S(2)}) collective-permute-start(f32[3,33,128]{2,1,0:T(8,128)} %get-tuple-element.38), channel_id=1, source_target_pairs={{0,1},{1,2},{2,3},{4,5},{5,6},{6,7},{8,9},{9,10},{10,11},{12,13},{... | collective-permute-start | bytes 152072 | tf_op jit(solution)/shard_map/ppermute | solution.py:49
  27.1 1.9 %collective-permute-start.3 = (f32[3,33,128]{2,1,0:T(8,128)}, f32[3,33,128]{2,1,0:T(8,128)S(1)}, u32[]{:S(2)}, u32[]{:S(2)}) collective-permute-start(f32[3,33,128]{2,1,0:T(8,128)} %get-tuple-element.39), channel_id=1, source_target_pairs={{1,0},{2,1},{3,2},{5,4},{6,5},{7,6},{9,8},{10,9},{11,10},{13,12},{... | collective-permute-start | bytes 152072 | tf_op jit(solution)/shard_map/ppermute | solution.py:49
  29.0 3.8 %collective-permute-done.3.from_up = f32[3,33,128]{2,1,0:T(8,128)S(1)} collective-permute-done((f32[3,33,128]{2,1,0:T(8,128)}, f32[3,33,128]{2,1,0:T(8,128)S(1)}, u32[]{:S(2)}, u32[]{:S(2)}) %collective-permute-start.3) | collective-permute-done | bytes 50720 | tf_op jit(solution)/shard_map/ppermute | solution.py:49
  32.9 0.8 copy-done.10
  33.7 0.8 copy-done.12
  34.5 10.9 %section_two.1 = (f32[336,128]{1,0:T(8,128)S(1)}, f32[336,128]{1,0:T(8,128)S(1)}, f32[120,128]{1,0:T(8,128)S(1)}, f32[40,128]{1,0:T(8,128)S(1)}, f32[3,48,128]{2...) custom-call(f32[336,128]{1,0:T(8,128)S(1)} %bitcast.13, ...), custom_call_target="tpu_custom_call" | custom-call | tf_op jit(solution)/shard_map/section_two/pallas_call | solution.py:638
  46.7 4.1 %collective-permute-start.4 = (f32[3,48,128]{2,1,0:T(8,128)S(1)}, f32[3,48,128]{2,1,0:T(8,128)S(1)}, u32[]{:S(2)}, u32[]{:S(2)}) collective-permute-start(f32[3,48,128]{2,1,0:T(8,128)S(1)} %get-tuple-element.44), channel_id=1, source_target_pairs={{0,4},{4,8},{8,12},{12,16},{16,20},{20,24},{24,28},{1,5},{5,9},{9,... | collective-permute-start | bytes 221192 | tf_op jit(solution)/shard_map/ppermute | solution.py:49
  50.8 1.3 collective-permute-start.5
  52.2 3.7 %collective-permute-done.5.right_ref.from_right = f32[3,48,128]{2,1,0:T(8,128)S(1)} collective-permute-done((f32[3,48,128]{2,1,0:T(8,128)S(1)}, f32[3,48,128]{2,1,0:T(8,128)S(1)}, u32[]{:S(2)}, u32[]{:S(2)}) %collective-permute-start.5) | collective-permute-done | bytes 73760 | tf_op jit(solution)/shard_map/ppermute | solution.py:49
  56.5 1.4 corners.4
  57.9 3.4 %collective-permute-start.6 = (f32[3,48,128]{2,1,0:T(8,128)}, f32[3,48,128]{2,1,0:T(8,128)S(1)}, u32[]{:S(2)}, u32[]{:S(2)}) collective-permute-start(f32[3,48,128]{2,1,0:T(8,128)} %get-tuple-element.48), channel_id=1, source_target_pairs={{0,1},{1,2},{2,3},{4,5},{5,6},{6,7},{8,9},{9,10},{10,11},{12,13},{... | collective-permute-start | bytes 221192 | tf_op jit(solution)/shard_map/ppermute | solution.py:49
  61.3 1.9 %collective-permute-start.7 = (f32[3,48,128]{2,1,0:T(8,128)}, f32[3,48,128]{2,1,0:T(8,128)S(1)}, u32[]{:S(2)}, u32[]{:S(2)}) collective-permute-start(f32[3,48,128]{2,1,0:T(8,128)} %get-tuple-element.49), channel_id=1, source_target_pairs={{1,0},{2,1},{3,2},{5,4},{6,5},{7,6},{9,8},{10,9},{11,10},{13,12},{... | collective-permute-start | bytes 221192 | tf_op jit(solution)/shard_map/ppermute | solution.py:49
  63.2 3.9 %collective-permute-done.7.from_up = f32[3,48,128]{2,1,0:T(8,128)S(1)} collective-permute-done((f32[3,48,128]{2,1,0:T(8,128)}, f32[3,48,128]{2,1,0:T(8,128)S(1)}, u32[]{:S(2)}, u32[]{:S(2)}) %collective-permute-start.7) | collective-permute-done | bytes 73760 | tf_op jit(solution)/shard_map/ppermute | solution.py:49
  67.2 0.9 copy-done.6
  68.0 0.9 copy-done.8
  68.9 12.7 %section_one.1 = (f32[336,128]{1,0:T(8,128)S(1)}, f32[336,128]{1,0:T(8,128)S(1)}, f32[336,128]{1,0:T(8,128)S(1)}, f32[40,128]{1,0:T(8,128)S(1)}, f32[3,28,128]{2...) custom-call(f32[336,128]{1,0:T(8,128)S(1)} %bitcast.14, ...), custom_call_target="tpu_custom_call" | custom-call | tf_op jit(solution)/shard_map/section_one/pallas_call | solution.py:638
  81.6 3.1 %collective-permute-start.8 = (f32[3,28,128]{2,1,0:T(8,128)S(1)}, f32[3,28,128]{2,1,0:T(8,128)S(1)}, u32[]{:S(2)}, u32[]{:S(2)}) collective-permute-start(f32[3,28,128]{2,1,0:T(8,128)S(1)} %get-tuple-element.53), channel_id=1, source_target_pairs={{0,4},{4,8},{8,12},{12,16},{16,20},{20,24},{24,28},{1,5},{5,9},{9,... | collective-permute-start | bytes 129032 | tf_op jit(solution)/shard_map/ppermute | solution.py:49
  84.8 1.3 collective-permute-start.9
  86.8 2.8 %collective-permute-done.9.right_ref.from_right = f32[3,28,128]{2,1,0:T(8,128)S(1)} collective-permute-done((f32[3,28,128]{2,1,0:T(8,128)S(1)}, f32[3,28,128]{2,1,0:T(8,128)S(1)}, u32[]{:S(2)}, u32[]{:S(2)}) %collective-permute-start.9) | collective-permute-done | bytes 43040 | tf_op jit(solution)/shard_map/ppermute | solution.py:49
  90.2 1.4 corners.5
  91.6 3.4 %collective-permute-start.10 = (f32[3,28,128]{2,1,0:T(8,128)}, f32[3,28,128]{2,1,0:T(8,128)S(1)}, u32[]{:S(2)}, u32[]{:S(2)}) collective-permute-start(f32[3,28,128]{2,1,0:T(8,128)} %get-tuple-element.58), channel_id=1, source_target_pairs={{0,1},{1,2},{2,3},{4,5},{5,6},{6,7},{8,9},{9,10},{10,11},{12,13},{... | collective-permute-start | bytes 129032 | tf_op jit(solution)/shard_map/ppermute | solution.py:49
  95.0 1.9 %collective-permute-start.11 = (f32[3,28,128]{2,1,0:T(8,128)}, f32[3,28,128]{2,1,0:T(8,128)S(1)}, u32[]{:S(2)}, u32[]{:S(2)}) collective-permute-start(f32[3,28,128]{2,1,0:T(8,128)} %get-tuple-element.59), channel_id=1, source_target_pairs={{1,0},{2,1},{3,2},{5,4},{6,5},{7,6},{9,8},{10,9},{11,10},{13,12},{... | collective-permute-start | bytes 129032 | tf_op jit(solution)/shard_map/ppermute | solution.py:49
  96.9 38.3 %all-gather.1.zone_ref = f32[32,2,128]{2,1,0:T(2,128)S(1)} all-gather(f32[1,2,128]{2,1,0:T(2,128)S(1)} %bitcast.18), channel_id=2, replica_groups=mesh['gx'=8,'gy'=4] {'gx','gy'}, dimensions={0}, use_global_device_ids=true | all-gather | bytes 33792 | tf_op jit(solution)/shard_map/all_gather | solution.py:752
  136.8 7.4 %section_zero.1.adjoint_ref = f32[336,128]{1,0:T(8,128)} custom-call(f32[336,128]{1,0:T(8,128)S(1)} %get-tuple-element.50.base_ref, f32[336,128]{1,0:T(8,128)S(1)} %get-tuple-element.51.lam_ref, f32[336,128]{1,0:T(8,128)S(1)} %get-tuple-element.52.y_ref, f32[96,128]{1,0:T(8,128)S(1)} %get-tuple-element.32.stat_ref, ...), custom_call_target="tpu_custom_call" | custom-call | tf_op jit(solution)/shard_map/section_zero/pallas_call | solution.py:638
  144.2 0.9 copy-done.4
  (78 shorter events, 12.3 us)
Async XLA Ops:
  1.4 1.0 copy-start
  2.3 0.9 copy-start.2
  7.4 25.5 %copy-start.1 = (bf16[3,1,1,42,1024]{4,3,2,1,0:T(8,128)(2,1)S(1)}, bf16[3,1,1,42,1024]{4,3,2,1,0:T(8,128)(2,1)}, u32[]{:S(2)}) copy-start(bf16[3,1,1,42,1024]{4,3,2,1,0:T(8,128)(2,1)} %x_ref.5) | copy-start | bytes 774148
  10.8 22.1 %copy-start.3 = (f32[1,1,42,1024]{3,1,2,0:T(1,128)S(1)}, f32[1,1,42,1024]{3,1,2,0:T(1,128)}, u32[]{:S(2)}) copy-start(f32[1,1,42,1024]{3,1,2,0:T(1,128)} %param.16) | copy-start | bytes 516100
  10.8 5.4 %collective-permute-start = (f32[3,33,128]{2,1,0:T(8,128)S(1)}, f32[3,33,128]{2,1,0:T(8,128)S(1)}, u32[]{:S(2)}, u32[]{:S(2)}) collective-permute-start(f32[3,33,128]{2,1,0:T(8,128)S(1)} %get-tuple-element.34), channel_id=1, source_target_pairs={{0,4},{4,8},{8,12},{12,16},{16,20},{20,24},{24,28},{1,5},{5,9},{9,... | collective-permute-start | bytes 152072 | tf_op jit(solution)/shard_map/ppermute | solution.py:49
  14.9 5.0 %collective-permute-start.1 = (f32[3,33,128]{2,1,0:T(8,128)S(1)}, f32[3,33,128]{2,1,0:T(8,128)S(1)}, u32[]{:S(2)}, u32[]{:S(2)}) collective-permute-start(f32[3,33,128]{2,1,0:T(8,128)S(1)} %get-tuple-element.35), channel_id=1, source_target_pairs={{4,0},{8,4},{12,8},{16,12},{20,16},{24,20},{28,24},{5,1},{9,5},{13... | collective-permute-start | bytes 152072 | tf_op jit(solution)/shard_map/ppermute | solution.py:49
  16.2 3.7 %copy-start.9 = (f32[3,33,128]{2,1,0:T(8,128)}, f32[3,33,128]{2,1,0:T(8,128)S(1)}, u32[]{:S(2)}) copy-start(f32[3,33,128]{2,1,0:T(8,128)S(1)} %collective-permute-done.left_ref.from_left) | copy-start | bytes 152068
  20.4 12.4 %copy-start.24 = (f32[8,8]{1,0:T(8,128)S(1)}, f32[8,8]{1,0:T(8,128)}, u32[]{:S(2)}) copy-start(f32[8,8]{1,0:T(8,128)} %in_ref.5) | copy-start | bytes 772
  20.4 12.4 %copy-start.25 = (f32[8,8]{1,0:T(8,128)S(1)}, f32[8,8]{1,0:T(8,128)}, u32[]{:S(2)}) copy-start(f32[8,8]{1,0:T(8,128)} %out_ref.5) | copy-start | bytes 772
  21.8 11.0 %copy-start.19 = (f32[12,12]{1,0:T(8,128)S(1)}, f32[12,12]{1,0:T(8,128)}, u32[]{:S(2)}) copy-start(f32[12,12]{1,0:T(8,128)} %volume_ref.5) | copy-start | bytes 1732
  21.8 7.2 %collective-permute-start.2 = (f32[3,33,128]{2,1,0:T(8,128)}, f32[3,33,128]{2,1,0:T(8,128)S(1)}, u32[]{:S(2)}, u32[]{:S(2)}) collective-permute-start(f32[3,33,128]{2,1,0:T(8,128)} %get-tuple-element.38), channel_id=1, source_target_pairs={{0,1},{1,2},{2,3},{4,5},{5,6},{6,7},{8,9},{9,10},{10,11},{12,13},{... | collective-permute-start | bytes 152072 | tf_op jit(solution)/shard_map/ppermute | solution.py:49
  27.1 5.8 %collective-permute-start.3 = (f32[3,33,128]{2,1,0:T(8,128)}, f32[3,33,128]{2,1,0:T(8,128)S(1)}, u32[]{:S(2)}, u32[]{:S(2)}) collective-permute-start(f32[3,33,128]{2,1,0:T(8,128)} %get-tuple-element.39), channel_id=1, source_target_pairs={{1,0},{2,1},{3,2},{5,4},{6,5},{7,6},{9,8},{10,9},{11,10},{13,12},{... | collective-permute-start | bytes 152072 | tf_op jit(solution)/shard_map/ppermute | solution.py:49
  32.9 0.8 copy-start.10
  33.7 0.8 copy-start.12
  46.7 5.5 %collective-permute-start.4 = (f32[3,48,128]{2,1,0:T(8,128)S(1)}, f32[3,48,128]{2,1,0:T(8,128)S(1)}, u32[]{:S(2)}, u32[]{:S(2)}) collective-permute-start(f32[3,48,128]{2,1,0:T(8,128)S(1)} %get-tuple-element.44), channel_id=1, source_target_pairs={{0,4},{4,8},{8,12},{12,16},{16,20},{20,24},{24,28},{1,5},{5,9},{9,... | collective-permute-start | bytes 221192 | tf_op jit(solution)/shard_map/ppermute | solution.py:49
  50.8 5.1 %collective-permute-start.5 = (f32[3,48,128]{2,1,0:T(8,128)S(1)}, f32[3,48,128]{2,1,0:T(8,128)S(1)}, u32[]{:S(2)}, u32[]{:S(2)}) collective-permute-start(f32[3,48,128]{2,1,0:T(8,128)S(1)} %get-tuple-element.45), channel_id=1, source_target_pairs={{4,0},{8,4},{12,8},{16,12},{20,16},{24,20},{28,24},{5,1},{9,5},{13... | collective-permute-start | bytes 221192 | tf_op jit(solution)/shard_map/ppermute | solution.py:49
  52.1 3.7 %copy-start.5 = (f32[3,48,128]{2,1,0:T(8,128)}, f32[3,48,128]{2,1,0:T(8,128)S(1)}, u32[]{:S(2)}) copy-start(f32[3,48,128]{2,1,0:T(8,128)S(1)} %collective-permute-done.4.left_ref.from_left) | copy-start | bytes 221188
  57.9 5.3 %collective-permute-start.6 = (f32[3,48,128]{2,1,0:T(8,128)}, f32[3,48,128]{2,1,0:T(8,128)S(1)}, u32[]{:S(2)}, u32[]{:S(2)}) collective-permute-start(f32[3,48,128]{2,1,0:T(8,128)} %get-tuple-element.48), channel_id=1, source_target_pairs={{0,1},{1,2},{2,3},{4,5},{5,6},{6,7},{8,9},{9,10},{10,11},{12,13},{... | collective-permute-start | bytes 221192 | tf_op jit(solution)/shard_map/ppermute | solution.py:49
  61.3 5.9 %collective-permute-start.7 = (f32[3,48,128]{2,1,0:T(8,128)}, f32[3,48,128]{2,1,0:T(8,128)S(1)}, u32[]{:S(2)}, u32[]{:S(2)}) collective-permute-start(f32[3,48,128]{2,1,0:T(8,128)} %get-tuple-element.49), channel_id=1, source_target_pairs={{1,0},{2,1},{3,2},{5,4},{6,5},{7,6},{9,8},{10,9},{11,10},{13,12},{... | collective-permute-start | bytes 221192 | tf_op jit(solution)/shard_map/ppermute | solution.py:49
  67.2 0.9 copy-start.6
  68.0 0.9 copy-start.8
  81.6 5.2 %copy-start.22 = (f32[3,28,128]{2,1,0:T(8,128)}, f32[3,28,128]{2,1,0:T(8,128)S(1)}, u32[]{:S(2)}) copy-start(f32[3,28,128]{2,1,0:T(8,128)S(1)} %get-tuple-element.55.up_in) | copy-start | bytes 129028
  81.6 5.2 %copy-start.23 = (f32[3,28,128]{2,1,0:T(8,128)}, f32[3,28,128]{2,1,0:T(8,128)S(1)}, u32[]{:S(2)}) copy-start(f32[3,28,128]{2,1,0:T(8,128)S(1)} %get-tuple-element.56.down_in) | copy-start | bytes 129028
  81.6 5.2 %collective-permute-start.8 = (f32[3,28,128]{2,1,0:T(8,128)S(1)}, f32[3,28,128]{2,1,0:T(8,128)S(1)}, u32[]{:S(2)}, u32[]{:S(2)}) collective-permute-start(f32[3,28,128]{2,1,0:T(8,128)S(1)} %get-tuple-element.53), channel_id=1, source_target_pairs={{0,4},{4,8},{8,12},{12,16},{16,20},{20,24},{24,28},{1,5},{5,9},{9,... | collective-permute-start | bytes 129032 | tf_op jit(solution)/shard_map/ppermute | solution.py:49
  84.8 4.8 %collective-permute-start.9 = (f32[3,28,128]{2,1,0:T(8,128)S(1)}, f32[3,28,128]{2,1,0:T(8,128)S(1)}, u32[]{:S(2)}, u32[]{:S(2)}) collective-permute-start(f32[3,28,128]{2,1,0:T(8,128)S(1)} %get-tuple-element.54), channel_id=1, source_target_pairs={{4,0},{8,4},{12,8},{16,12},{20,16},{24,20},{28,24},{5,1},{9,5},{13... | collective-permute-start | bytes 129032 | tf_op jit(solution)/shard_map/ppermute | solution.py:49
  86.8 2.8 %copy-start.28 = (f32[2,128]{1,0:T(2,128)}, f32[2,128]{1,0:T(2,128)S(1)}, u32[]{:S(2)}) copy-start(f32[2,128]{1,0:T(2,128)S(1)} %zone_sums.1.rest_0_) | copy-start | bytes 3076
  86.8 2.8 %copy-start.13 = (f32[3,28,128]{2,1,0:T(8,128)}, f32[3,28,128]{2,1,0:T(8,128)S(1)}, u32[]{:S(2)}) copy-start(f32[3,28,128]{2,1,0:T(8,128)S(1)} %collective-permute-done.8.left_ref.from_left) | copy-start | bytes 129028
  91.6 43.6 %collective-permute-start.10 = (f32[3,28,128]{2,1,0:T(8,128)}, f32[3,28,128]{2,1,0:T(8,128)S(1)}, u32[]{:S(2)}, u32[]{:S(2)}) collective-permute-start(f32[3,28,128]{2,1,0:T(8,128)} %get-tuple-element.58), channel_id=1, source_target_pairs={{0,1},{1,2},{2,3},{4,5},{5,6},{6,7},{8,9},{9,10},{10,11},{12,13},{... | collective-permute-start | bytes 129032 | tf_op jit(solution)/shard_map/ppermute | solution.py:49
  95.0 1.9 %copy-start.29 = (f32[2,128]{1,0:T(2,128)S(1)}, f32[2,128]{1,0:T(2,128)}, u32[]{:S(2)}) copy-start(f32[2,128]{1,0:T(2,128)} %copy-done.28) | copy-start | bytes 3076
  95.0 40.2 %collective-permute-start.11 = (f32[3,28,128]{2,1,0:T(8,128)}, f32[3,28,128]{2,1,0:T(8,128)S(1)}, u32[]{:S(2)}, u32[]{:S(2)}) collective-permute-start(f32[3,28,128]{2,1,0:T(8,128)} %get-tuple-element.59), channel_id=1, source_target_pairs={{1,0},{2,1},{3,2},{5,4},{6,5},{7,6},{9,8},{10,9},{11,10},{13,12},{... | collective-permute-start | bytes 129032 | tf_op jit(solution)/shard_map/ppermute | solution.py:49
  135.2 0.8 copy-start.14
  144.2 0.9 copy-start.4
  (18 other events, 12.1 us)

commit v3 on v2

--- a/solution.py
+++ b/solution.py
@@ -27,6 +27,7 @@
     11,
 )
 STAT_ROWS = 12
+NEAR_VMEM, FAR_VMEM = 32, 60
 OUTER_EDGE, OUTER_ZONE, HALF_SPEED = 0, 3, 6
 FACT_ROWS = 15
 REMOTE_BLOCKS = (
@@ -168,7 +169,45 @@
     to_down,
     x_tiles,
     sent_ref,
+    *fetched,
 ):
+    *fetched, sems = fetched
+    sources = [
+        partner_ref,
+        send_ref,
+        cot_ref,
+        x_ref.at[:, 0, 0, 0:16],
+        area_ref,
+        edge_ref,
+        rough_ref,
+        soil_ref,
+        friction_ref,
+        conduct_ref,
+        wet_ref,
+        zone_ref,
+    ]
+    copies = [
+        pltpu.make_async_copy(source, target, sems.at[n])
+        for n, (source, target) in enumerate(zip(sources, fetched))
+    ]
+    for copy in copies:
+        copy.start()
+    for copy in copies:
+        copy.wait()
+    (
+        partner_ref,
+        send_ref,
+        cot_ref,
+        x_ref,
+        area_ref,
+        edge_ref,
+        rough_ref,
+        soil_ref,
+        friction_ref,
+        conduct_ref,
+        wet_ref,
+        zone_ref,
+    ) = fetched
     rows = cot_ref.shape[0] // SUB
     sections = x_ref.shape[0]
     face_total = 3 * SUB * LANES
@@ -223,7 +262,7 @@
     stat_ref[EDGE * SUB : (EDGE + 3) * SUB, :] = edge_ref[...]
     for k in range(sections):
         rows_to_tiles(
-            lambda b: x_ref[k, 0, 0, 0:16, lanes_of(b)].astype(jnp.float32), x_tiles, 16
+            lambda b: x_ref[k, :, lanes_of(b)].astype(jnp.float32), x_tiles, 16
         )
         squares = [tile(x_tiles, r) * tile(x_tiles, r) for r in range(12)]
         node_sum = [squares[i] + squares[3 + i] + squares[6 + i] + squares[9 + i] for i in range(3)]
@@ -260,10 +299,10 @@
 
 def corner_kernel(left_ref, right_ref, up_in, down_in, *rest):
     up_ref, down_ref = rest[-2:]
-    first = lax.broadcasted_iota(jnp.int32, left_ref.shape, 2) < 4
-    left, right = left_ref[...], right_ref[...]
-    up_ref[...] = jnp.where(first, right, left)
-    down_ref[...] = jnp.where(first, left, right)
+    left, right = left_ref[2], right_ref[2]
+    first = lax.broadcasted_iota(jnp.int32, left.shape, 1) < 4
+    up_ref[2] = jnp.where(first, right, left)
+    down_ref[2] = jnp.where(first, left, right)
 
 
 def outer_states(src, first_comp, comps, first_row, received, index, out_ref):
@@ -535,7 +574,7 @@
 
 
 def zone_kernel(term_ref, stat_ref, fact_ref, conduct_ref, out_ref):
-    zones = out_ref.shape[1]
+    zones = out_ref.shape[2]
     zone_iota = lax.broadcasted_iota(jnp.int32, (zones, LANES), 0).astype(jnp.float32)
     sub_iota = lax.broadcasted_iota(jnp.int32, (SUB, zones), 0)
 
@@ -568,10 +607,11 @@
     friction, conduct = by_zone([tile(term_ref, 0), tile(term_ref, 1)], stat_ref, ZONE_ID)
     for f in range(3):
         conduct = conduct + by_zone([tile(term_ref, 2 + f)], fact_ref, OUTER_ZONE + f)[0]
-    out_ref[0:1, :] = GRAD_WEIGHT * jnp.sum(friction, axis=0, keepdims=True)
-    out_ref[1:2, :] = (
-        GRAD_WEIGHT * jnp.sum(conduct, axis=0, keepdims=True) / conduct_ref[...]
-    )
+    friction = GRAD_WEIGHT * jnp.sum(friction, axis=0, keepdims=True)
+    conduct = GRAD_WEIGHT * jnp.sum(conduct, axis=0, keepdims=True) / conduct_ref[...]
+    for device in range(out_ref.shape[0]):
+        out_ref[device, 0:1, :] = friction
+        out_ref[device, 1:2, :] = conduct
 
 
 def last_kernel(
@@ -589,6 +629,7 @@
     from_down,
     from_up,
     adjoint_ref,
+    last_ref,
     outer_ref,
 ):
     received = (from_left, from_right, from_down, from_up)
@@ -601,6 +642,7 @@
     transposed_section(
         0, lam_ref, y_ref, outer_ref, stat_ref, fact_ref, in_ref, out_ref, volume_ref, emit
     )
+    last_ref[...] = tile(adjoint_ref, rows - 1)
 
 
 def total_kernel(zone_ref, adjoint_ref, grads_ref):
@@ -611,37 +653,36 @@
     to_right, to_left, to_up, to_down = messages
     from_left = shifted(to_right, "gx", 1)
     from_right = shifted(to_left, "gx", -1)
-    corner = pl.BlockSpec((1, to_right.shape[1], LANES), lambda i: (2, 0, 0))
-    whole = pl.BlockSpec(memory_space=pl.ANY)
-    to_up, to_down = pl.pallas_call(
+    to_up, to_down = call(
         corner_kernel,
-        grid=(1,),
-        in_specs=[corner, corner, whole, whole] + [pl.BlockSpec(memory_space=pltpu.HBM)] * len(ahead),
-        out_specs=[corner, corner],
-        out_shape=[jax.ShapeDtypeStruct(to_up.shape, to_up.dtype)] * 2,
-        input_output_aliases={2: 0, 3: 1},
-        name="corners",
-    )(from_left, from_right, to_up, to_down, *ahead)
+        "corners",
+        [jax.ShapeDtypeStruct(to_up.shape, to_up.dtype)] * 2,
+        [],
+        [from_left, from_right, to_up, to_down, *ahead],
+        aliases={2: 0, 3: 1},
+    )
     from_down = shifted(to_up, "gy", 1)
     from_up = shifted(to_down, "gy", -1)
     return from_left, from_right, from_down, from_up
 
 
-def call(kernel, name, outs, scratch, operands, scalars=(), anywhere=()):
+def call(kernel, name, outs, scratch, operands, scalars=(), far=False, aliases={}):
     in_memory = pl.BlockSpec(memory_space=pltpu.VMEM)
     in_scalar = pl.BlockSpec(memory_space=pltpu.SMEM)
-    unread = pl.BlockSpec(memory_space=pltpu.HBM)
-    specs = [
-        in_scalar if n in scalars else unread if n in anywhere else in_memory
-        for n in range(len(operands))
-    ]
+    in_place = pl.BlockSpec(memory_space=pl.ANY)
     return pl.pallas_call(
         kernel,
-        in_specs=specs,
+        in_specs=[
+            in_place if far else in_scalar if n in scalars else in_memory
+            for n in range(len(operands))
+        ],
         out_specs=[in_memory] * len(outs),
         out_shape=outs,
         scratch_shapes=scratch,
-        compiler_params=pltpu.CompilerParams(vmem_limit_bytes=32 * 1024 * 1024),
+        input_output_aliases=aliases,
+        compiler_params=pltpu.CompilerParams(
+            vmem_limit_bytes=(FAR_VMEM if far else NEAR_VMEM) * 1024 * 1024
+        ),
         name=name,
     )(*operands)
 
@@ -668,6 +709,7 @@
     channels = rows // 3 * 2
     zones = zone_friction.shape[0]
     slots = send_face.shape[3]
+    devices = lax.axis_size("gx") * lax.axis_size("gy")
     f32 = jnp.float32
 
     def tiles(count, dtype=f32):
@@ -689,7 +731,22 @@
         "prepare",
         [tiles(rows + 13), tiles(STAT_ROWS), tiles(INDEX_ROWS, jnp.int32)]
         + messages(channels + 5),
-        [tile_scratch(16), sent_scratch(channels + 5)],
+        [tile_scratch(16), sent_scratch(channels + 5)]
+        + [
+            tile_scratch(3, jnp.int32),
+            pltpu.VMEM(send_face.shape, jnp.int32),
+            tile_scratch(rows),
+            pltpu.VMEM((section_states.shape[0], 16, SUB * LANES), section_states.dtype),
+            tile_scratch(1),
+            tile_scratch(3),
+            tile_scratch(1),
+            tile_scratch(1),
+            pltpu.VMEM((zones // LANES, LANES), f32),
+            pltpu.VMEM((zones // LANES, LANES), f32),
+            tile_scratch(1, jnp.int32),
+            tile_scratch(1, jnp.int32),
+            pltpu.SemaphoreType.DMA((12,)),
+        ],
         [
             cot,
             section_states,
@@ -704,6 +761,7 @@
             send_face,
             face_partner.reshape(3 * SUB, LANES),
         ],
+        far=True,
     )
     received = exchange(to_send)
     lam, y, fact, term, *to_send = call(
@@ -745,16 +803,16 @@
     (zone_terms,) = call(
         zone_kernel,
         "zone_sums",
-        [jax.ShapeDtypeStruct((2, zones), f32)],
+        [jax.ShapeDtypeStruct((devices, 2, zones), f32)],
         [],
         [term, stat, fact, zone_conductivity.reshape(1, zones)],
     )
-    all_terms = lax.all_gather(zone_terms, ("gx", "gy"))
+    all_terms = lax.all_to_all(zone_terms, ("gx", "gy"), 0, 0)
     received = exchange(to_send, zone_terms)
-    (adjoint,) = call(
+    adjoint, last = call(
         last_kernel,
         "section_zero",
-        [tiles(rows)],
+        [tiles(rows), tiles(1)],
         [tile_scratch(3 * channels)],
         [
             base,
@@ -775,8 +833,7 @@
         "zone_total",
         [jax.ShapeDtypeStruct((2, zones), f32)],
         [],
-        [all_terms, adjoint],
-        anywhere=(1,),
+        [all_terms, last],
     )
     return adjoint.reshape(cotangent.shape), zone_grads
 

time: 147 us -> 99.3 us (0.68)
  blocking collectives: 38.3 us -> 0 us
  local copies, waits for them, and re-layouts: 17.1 us -> 3.51 us
  starting transfers between devices: 32.9 us -> 38 us
    all_gather x1 -> x0, blocking collectives: 38.3 us -> none  [local(): all_terms = lax.all_gather(zone_terms, ('gx', 'gy'))]
    unnamed x76 -> x24, local copies, waits for them, and re-layouts: 17.1 us -> 3.51 us
    all_to_all x0 -> x1, starting transfers between devices: none -> 4.84 us  [local(): all_terms = lax.all_to_all(zone_terms, ('gx', 'gy'), 0, 0)]
  transfers between devices with their start and end apart: 12 -> 13, of which waited for: 6 -> 7; matrix products, arithmetic and copies ran while one was open for 0% -> 0% of each run, Pallas kernels for 0% -> 10%
where the time goes in v3:
time: 99.3 us; the launch traced here: 98.6 us
  starting transfers between devices  38 us (38%)
  Pallas kernels  37.7 us (38%)
  waiting for transfers between devices  18.5 us (19%)
  local copies, waits for them, and re-layouts  3.51 us (4%)
    pallas_call x9, Pallas kernels, call(): pl.pallas_call(kernel, in_specs=[in_place if far else in_scalar if n in s...  37.7 us
    ppermute x12, starting transfers between devices, shifted(): return lax.ppermute(x, axis, pairs)  33.1 us
    ppermute x12, waiting for transfers between devices, shifted(): return lax.ppermute(x, axis, pairs)  18.5 us
    all_to_all x1, starting transfers between devices, local(): all_terms = lax.all_to_all(zone_terms, ('gx', 'gy'), 0, 0)  4.84 us
    unnamed x24, local copies, waits for them, and re-layouts  3.51 us
  transfers between devices with their start and end apart: 13, of which 7 were waited for; matrix products, arithmetic and copies ran while one was open for 0% of the time, Pallas kernels for 10%

profile of v3, /device:TPU:1, one launch (start us, length us, event | category | flops | bytes accessed | tf_op | source)
XLA Modules:
  0.0 98.6 jit_solution(16260442260665329092)
XLA Ops:
  0.6 4.0 %prepare.1 = (f32[440,128]{1,0:T(8,128)}, f32[96,128]{1,0:T(8,128)}, s32[144,128]{1,0:T(8,128)}, f32[3,33,128]{2,1,0:T(8,128)}, f32[3,33,128]{2,1,0:T(8,128)}, /...) custom-call(f32[336,128]{1,0:T(8,128)} %bitcast.11, bf16[3,1,1,42,1024]{4,3,2,1,0:T(8,128)(2,1)} %x_ref.5, f32[8,128]{1,0:T(8,128)} %bitcast.18, ...), custom_call_target="tpu_custom_call" | custom-call | tf_op jit(solution)/shard_map/prepare/pallas_call | solution.py:673
  4.7 4.1 %collective-permute-start = (f32[3,33,128]{2,1,0:T(8,128)}, f32[3,33,128]{2,1,0:T(8,128)S(1)}, u32[]{:S(2)}, u32[]{:S(2)}) collective-permute-start(f32[3,33,128]{2,1,0:T(8,128)} %get-tuple-element.36), channel_id=1, source_target_pairs={{0,4},{4,8},{8,12},{12,16},{16,20},{20,24},{24,28},{1,5},{5,9},{9,... | collective-permute-start | bytes 152072 | tf_op jit(solution)/shard_map/ppermute | solution.py:50
  8.8 1.3 %collective-permute-start.1 = (f32[3,33,128]{2,1,0:T(8,128)}, f32[3,33,128]{2,1,0:T(8,128)S(1)}, u32[]{:S(2)}, u32[]{:S(2)}) collective-permute-start(f32[3,33,128]{2,1,0:T(8,128)} %get-tuple-element.37), channel_id=1, source_target_pairs={{4,0},{8,4},{12,8},{16,12},{20,16},{24,20},{28,24},{5,1},{9,5},{13... | collective-permute-start | bytes 152072 | tf_op jit(solution)/shard_map/ppermute | solution.py:50
  10.1 0.3 collective-permute-done.left_ref.from_left
  10.3 3.6 %collective-permute-done.1.right_ref.from_right = f32[3,33,128]{2,1,0:T(8,128)S(1)} collective-permute-done((f32[3,33,128]{2,1,0:T(8,128)}, f32[3,33,128]{2,1,0:T(8,128)S(1)}, u32[]{:S(2)}, u32[]{:S(2)}) %collective-permute-start.1) | collective-permute-done | bytes 50720 | tf_op jit(solution)/shard_map/ppermute | solution.py:50
  13.9 0.8 copy-done.7
  14.8 0.8 copy-done.8
  15.6 0.0 copy-start.6
  15.6 5.3 %collective-permute-start.2 = (f32[3,33,128]{2,1,0:T(8,128)S(1)}, f32[3,33,128]{2,1,0:T(8,128)S(1)}, u32[]{:S(2)}, u32[]{:S(2)}) collective-permute-start(f32[3,33,128]{2,1,0:T(8,128)S(1)} %get-tuple-element.40), channel_id=1, source_target_pairs={{0,1},{1,2},{2,3},{4,5},{5,6},{6,7},{8,9},{9,10},{10,11},{12,13},{... | collective-permute-start | bytes 152072 | tf_op jit(solution)/shard_map/ppermute | solution.py:50
  20.9 1.9 %collective-permute-start.3 = (f32[3,33,128]{2,1,0:T(8,128)S(1)}, f32[3,33,128]{2,1,0:T(8,128)S(1)}, u32[]{:S(2)}, u32[]{:S(2)}) collective-permute-start(f32[3,33,128]{2,1,0:T(8,128)S(1)} %get-tuple-element.41), channel_id=1, source_target_pairs={{1,0},{2,1},{3,2},{5,4},{6,5},{7,6},{9,8},{10,9},{11,10},{13,12},{... | collective-permute-start | bytes 152072 | tf_op jit(solution)/shard_map/ppermute | solution.py:50
  22.8 3.6 %collective-permute-done.3.from_up = f32[3,33,128]{2,1,0:T(8,128)S(1)} collective-permute-done((f32[3,33,128]{2,1,0:T(8,128)S(1)}, f32[3,33,128]{2,1,0:T(8,128)S(1)}, u32[]{:S(2)}, u32[]{:S(2)}) %collective-permute-start.3) | collective-permute-done | bytes 50720 | tf_op jit(solution)/shard_map/ppermute | solution.py:50
  26.5 0.9 copy-done.3
  27.4 0.9 copy-done.5
  28.3 10.9 %section_two.1 = (f32[336,128]{1,0:T(8,128)S(1)}, f32[336,128]{1,0:T(8,128)S(1)}, f32[120,128]{1,0:T(8,128)S(1)}, f32[40,128]{1,0:T(8,128)S(1)}, f32[3,48,128]{2...) custom-call(f32[336,128]{1,0:T(8,128)S(1)} %bitcast.12, ...), custom_call_target="tpu_custom_call" | custom-call | tf_op jit(solution)/shard_map/section_two/pallas_call | solution.py:673
  39.2 4.1 %collective-permute-start.4 = (f32[3,48,128]{2,1,0:T(8,128)S(1)}, f32[3,48,128]{2,1,0:T(8,128)S(1)}, u32[]{:S(2)}, u32[]{:S(2)}) collective-permute-start(f32[3,48,128]{2,1,0:T(8,128)S(1)} %get-tuple-element.46), channel_id=1, source_target_pairs={{0,4},{4,8},{8,12},{12,16},{16,20},{20,24},{24,28},{1,5},{5,9},{9,... | collective-permute-start | bytes 221192 | tf_op jit(solution)/shard_map/ppermute | solution.py:50
  43.3 1.3 %collective-permute-start.5 = (f32[3,48,128]{2,1,0:T(8,128)S(1)}, f32[3,48,128]{2,1,0:T(8,128)S(1)}, u32[]{:S(2)}, u32[]{:S(2)}) collective-permute-start(f32[3,48,128]{2,1,0:T(8,128)S(1)} %get-tuple-element.47), channel_id=1, source_target_pairs={{4,0},{8,4},{12,8},{16,12},{20,16},{24,20},{28,24},{5,1},{9,5},{13... | collective-permute-start | bytes 221192 | tf_op jit(solution)/shard_map/ppermute | solution.py:50
  44.6 0.1 collective-permute-done.4.left_ref.from_left
  44.7 3.7 %collective-permute-done.5.right_ref.from_right = f32[3,48,128]{2,1,0:T(8,128)S(1)} collective-permute-done((f32[3,48,128]{2,1,0:T(8,128)S(1)}, f32[3,48,128]{2,1,0:T(8,128)S(1)}, u32[]{:S(2)}, u32[]{:S(2)}) %collective-permute-start.5) | collective-permute-done | bytes 73760 | tf_op jit(solution)/shard_map/ppermute | solution.py:50
  48.4 3.4 %collective-permute-start.6 = (f32[3,48,128]{2,1,0:T(8,128)S(1)}, f32[3,48,128]{2,1,0:T(8,128)S(1)}, u32[]{:S(2)}, u32[]{:S(2)}) collective-permute-start(f32[3,48,128]{2,1,0:T(8,128)S(1)} %get-tuple-element.50), channel_id=1, source_target_pairs={{0,1},{1,2},{2,3},{4,5},{5,6},{6,7},{8,9},{9,10},{10,11},{12,13},{... | collective-permute-start | bytes 221192 | tf_op jit(solution)/shard_map/ppermute | solution.py:50
  51.8 1.9 %collective-permute-start.7 = (f32[3,48,128]{2,1,0:T(8,128)S(1)}, f32[3,48,128]{2,1,0:T(8,128)S(1)}, u32[]{:S(2)}, u32[]{:S(2)}) collective-permute-start(f32[3,48,128]{2,1,0:T(8,128)S(1)} %get-tuple-element.51), channel_id=1, source_target_pairs={{1,0},{2,1},{3,2},{5,4},{6,5},{7,6},{9,8},{10,9},{11,10},{13,12},{... | collective-permute-start | bytes 221192 | tf_op jit(solution)/shard_map/ppermute | solution.py:50
  53.8 3.7 %collective-permute-done.7.from_up = f32[3,48,128]{2,1,0:T(8,128)S(1)} collective-permute-done((f32[3,48,128]{2,1,0:T(8,128)S(1)}, f32[3,48,128]{2,1,0:T(8,128)S(1)}, u32[]{:S(2)}, u32[]{:S(2)}) %collective-permute-start.7) | collective-permute-done | bytes 73760 | tf_op jit(solution)/shard_map/ppermute | solution.py:50
  57.5 12.7 %section_one.1 = (f32[336,128]{1,0:T(8,128)S(1)}, f32[336,128]{1,0:T(8,128)S(1)}, f32[336,128]{1,0:T(8,128)S(1)}, f32[40,128]{1,0:T(8,128)S(1)}, f32[3,28,128]{2...) custom-call(f32[336,128]{1,0:T(8,128)S(1)} %bitcast.13, ...), custom_call_target="tpu_custom_call" | custom-call | tf_op jit(solution)/shard_map/section_one/pallas_call | solution.py:673
  70.2 3.1 %collective-permute-start.8 = (f32[3,28,128]{2,1,0:T(8,128)S(1)}, f32[3,28,128]{2,1,0:T(8,128)S(1)}, u32[]{:S(2)}, u32[]{:S(2)}) collective-permute-start(f32[3,28,128]{2,1,0:T(8,128)S(1)} %get-tuple-element.55), channel_id=1, source_target_pairs={{0,4},{4,8},{8,12},{12,16},{16,20},{20,24},{24,28},{1,5},{5,9},{9,... | collective-permute-start | bytes 129032 | tf_op jit(solution)/shard_map/ppermute | solution.py:50
  73.3 1.3 %collective-permute-start.9 = (f32[3,28,128]{2,1,0:T(8,128)S(1)}, f32[3,28,128]{2,1,0:T(8,128)S(1)}, u32[]{:S(2)}, u32[]{:S(2)}) collective-permute-start(f32[3,28,128]{2,1,0:T(8,128)S(1)} %get-tuple-element.56), channel_id=1, source_target_pairs={{4,0},{8,4},{12,8},{16,12},{20,16},{24,20},{28,24},{5,1},{9,5},{13... | collective-permute-start | bytes 129032 | tf_op jit(solution)/shard_map/ppermute | solution.py:50
  74.6 1.3 %zone_sums.1.rest_0_ = f32[32,2,128]{2,1,0:T(2,128)} custom-call(f32[40,128]{1,0:T(8,128)S(1)} %get-tuple-element.59.term_ref, f32[96,128]{1,0:T(8,128)S(1)} %copy-done.2, f32[120,128]{1,0:T(8,128)S(1)} %get-tuple-element.44.fact_ref, f32[1,128]{1,0:T(1,128)S(1)} %bitcast.15), custom_call_target="tpu_custom_call" | custom-call | tf_op jit(solution)/shard_map/zone_sums/pallas_call | solution.py:673
  76.0 4.8 %all-to-all-start = ((f32[32,2,128]{2,1,0:T(2,128)}), f32[32,2,128]{2,1,0:T(2,128)S(1)}, u32[]{:S(2)}, u32[]{:S(2)}) async-start(f32[32,2,128]{2,1,0:T(2,128)} %zone_sums.1.rest_0_), calls=%async_computation | async-start | bytes 65536 | tf_op jit(solution)/shard_map/all_to_all | solution.py:810
  80.8 0.8 corners.5
  81.6 3.5 %collective-permute-start.10 = (f32[3,28,128]{2,1,0:T(8,128)S(1)}, f32[3,28,128]{2,1,0:T(8,128)S(1)}, u32[]{:S(2)}, u32[]{:S(2)}) collective-permute-start(f32[3,28,128]{2,1,0:T(8,128)S(1)} %get-tuple-element.60), channel_id=1, source_target_pairs={{0,1},{1,2},{2,3},{4,5},{5,6},{6,7},{8,9},{9,10},{10,11},{12,13},{... | collective-permute-start | bytes 129032 | tf_op jit(solution)/shard_map/ppermute | solution.py:50
  85.2 1.9 %collective-permute-start.11 = (f32[3,28,128]{2,1,0:T(8,128)S(1)}, f32[3,28,128]{2,1,0:T(8,128)S(1)}, u32[]{:S(2)}, u32[]{:S(2)}) collective-permute-start(f32[3,28,128]{2,1,0:T(8,128)S(1)} %get-tuple-element.61), channel_id=1, source_target_pairs={{1,0},{2,1},{3,2},{5,4},{6,5},{7,6},{9,8},{10,9},{11,10},{13,12},{... | collective-permute-start | bytes 129032 | tf_op jit(solution)/shard_map/ppermute | solution.py:50
  87.1 3.5 %collective-permute-done.11.from_up = f32[3,28,128]{2,1,0:T(8,128)S(1)} collective-permute-done((f32[3,28,128]{2,1,0:T(8,128)S(1)}, f32[3,28,128]{2,1,0:T(8,128)S(1)}, u32[]{:S(2)}, u32[]{:S(2)}) %collective-permute-start.11) | collective-permute-done | bytes 43040 | tf_op jit(solution)/shard_map/ppermute | solution.py:50
  90.6 7.4 %section_zero.1 = (f32[336,128]{1,0:T(8,128)}, f32[8,128]{1,0:T(8,128)S(1)}) custom-call(f32[336,128]{1,0:T(8,128)S(1)} %get-tuple-element.52.base_ref, f32[336,128]{1,0:T(8,128)S(1)} %get-tuple-element.53.lam_ref, f32[336,128]{1,0:T(8,128)S(1)} %get-tuple-element.54.y_ref, f32[96,128]{1,0:T(8,128)S(1)} %copy-done.2, s32[144,128]{1,0:T(8,128)S(1)} %copy-done.4, ...), custom_call_target="tpu_custom_call" | custom-call | tf_op jit(solution)/shard_map/section_zero/pallas_call | solution.py:673
  98.0 0.6 zone_total.1
  (27 shorter events, 0.1 us)
Async XLA Ops:
  0.6 25.8 %copy-start = (bf16[3,1,1,42,1024]{4,3,2,1,0:T(8,128)(2,1)S(1)}, bf16[3,1,1,42,1024]{4,3,2,1,0:T(8,128)(2,1)}, u32[]{:S(2)}) copy-start(bf16[3,1,1,42,1024]{4,3,2,1,0:T(8,128)(2,1)} %x_ref.5) | copy-start | bytes 774148
  4.7 21.8 %copy-start.1 = (f32[1,1,42,1024]{3,1,2,0:T(1,128)S(1)}, f32[1,1,42,1024]{3,1,2,0:T(1,128)}, u32[]{:S(2)}) copy-start(f32[1,1,42,1024]{3,1,2,0:T(1,128)} %param.16) | copy-start | bytes 516100
  4.7 5.7 %collective-permute-start = (f32[3,33,128]{2,1,0:T(8,128)}, f32[3,33,128]{2,1,0:T(8,128)S(1)}, u32[]{:S(2)}, u32[]{:S(2)}) collective-permute-start(f32[3,33,128]{2,1,0:T(8,128)} %get-tuple-element.36), channel_id=1, source_target_pairs={{0,4},{4,8},{8,12},{12,16},{16,20},{20,24},{24,28},{1,5},{5,9},{9,... | collective-permute-start | bytes 152072 | tf_op jit(solution)/shard_map/ppermute | solution.py:50
  8.8 5.2 %collective-permute-start.1 = (f32[3,33,128]{2,1,0:T(8,128)}, f32[3,33,128]{2,1,0:T(8,128)S(1)}, u32[]{:S(2)}, u32[]{:S(2)}) collective-permute-start(f32[3,33,128]{2,1,0:T(8,128)} %get-tuple-element.37), channel_id=1, source_target_pairs={{4,0},{8,4},{12,8},{16,12},{20,16},{24,20},{28,24},{5,1},{9,5},{13... | collective-permute-start | bytes 152072 | tf_op jit(solution)/shard_map/ppermute | solution.py:50
  13.9 0.8 copy-start.7
  14.8 0.8 copy-start.8
  15.6 10.9 %copy-start.2 = (f32[96,128]{1,0:T(8,128)S(1)}, f32[96,128]{1,0:T(8,128)}, u32[]{:S(2)}) copy-start(f32[96,128]{1,0:T(8,128)} %get-tuple-element.34.stat_ref) | copy-start | bytes 147460
  15.6 10.9 %copy-start.9 = (f32[8,8]{1,0:T(8,128)S(1)}, f32[8,8]{1,0:T(8,128)}, u32[]{:S(2)}) copy-start(f32[8,8]{1,0:T(8,128)} %in_ref.5) | copy-start | bytes 772
  15.6 10.9 %copy-start.10 = (f32[8,8]{1,0:T(8,128)S(1)}, f32[8,8]{1,0:T(8,128)}, u32[]{:S(2)}) copy-start(f32[8,8]{1,0:T(8,128)} %out_ref.5) | copy-start | bytes 772
  15.6 10.9 %copy-start.6 = (f32[12,12]{1,0:T(8,128)S(1)}, f32[12,12]{1,0:T(8,128)}, u32[]{:S(2)}) copy-start(f32[12,12]{1,0:T(8,128)} %volume_ref.5) | copy-start | bytes 1732
  15.6 7.2 %collective-permute-start.2 = (f32[3,33,128]{2,1,0:T(8,128)S(1)}, f32[3,33,128]{2,1,0:T(8,128)S(1)}, u32[]{:S(2)}, u32[]{:S(2)}) collective-permute-start(f32[3,33,128]{2,1,0:T(8,128)S(1)} %get-tuple-element.40), channel_id=1, source_target_pairs={{0,1},{1,2},{2,3},{4,5},{5,6},{6,7},{8,9},{9,10},{10,11},{12,13},{... | collective-permute-start | bytes 152072 | tf_op jit(solution)/shard_map/ppermute | solution.py:50
  20.9 5.5 %collective-permute-start.3 = (f32[3,33,128]{2,1,0:T(8,128)S(1)}, f32[3,33,128]{2,1,0:T(8,128)S(1)}, u32[]{:S(2)}, u32[]{:S(2)}) collective-permute-start(f32[3,33,128]{2,1,0:T(8,128)S(1)} %get-tuple-element.41), channel_id=1, source_target_pairs={{1,0},{2,1},{3,2},{5,4},{6,5},{7,6},{9,8},{10,9},{11,10},{13,12},{... | collective-permute-start | bytes 152072 | tf_op jit(solution)/shard_map/ppermute | solution.py:50
  26.5 0.9 copy-start.3
  27.4 0.9 copy-start.5
  39.2 5.5 %collective-permute-start.4 = (f32[3,48,128]{2,1,0:T(8,128)S(1)}, f32[3,48,128]{2,1,0:T(8,128)S(1)}, u32[]{:S(2)}, u32[]{:S(2)}) collective-permute-start(f32[3,48,128]{2,1,0:T(8,128)S(1)} %get-tuple-element.46), channel_id=1, source_target_pairs={{0,4},{4,8},{8,12},{12,16},{16,20},{20,24},{24,28},{1,5},{5,9},{9,... | collective-permute-start | bytes 221192 | tf_op jit(solution)/shard_map/ppermute | solution.py:50
  43.3 5.1 %collective-permute-start.5 = (f32[3,48,128]{2,1,0:T(8,128)S(1)}, f32[3,48,128]{2,1,0:T(8,128)S(1)}, u32[]{:S(2)}, u32[]{:S(2)}) collective-permute-start(f32[3,48,128]{2,1,0:T(8,128)S(1)} %get-tuple-element.47), channel_id=1, source_target_pairs={{4,0},{8,4},{12,8},{16,12},{20,16},{24,20},{28,24},{5,1},{9,5},{13... | collective-permute-start | bytes 221192 | tf_op jit(solution)/shard_map/ppermute | solution.py:50
  48.4 9.1 %copy-start.4 = (s32[144,128]{1,0:T(8,128)S(1)}, s32[144,128]{1,0:T(8,128)}, u32[]{:S(2)}) copy-start(s32[144,128]{1,0:T(8,128)} %get-tuple-element.35.index_ref) | copy-start | bytes 221188
  48.4 5.4 %collective-permute-start.6 = (f32[3,48,128]{2,1,0:T(8,128)S(1)}, f32[3,48,128]{2,1,0:T(8,128)S(1)}, u32[]{:S(2)}, u32[]{:S(2)}) collective-permute-start(f32[3,48,128]{2,1,0:T(8,128)S(1)} %get-tuple-element.50), channel_id=1, source_target_pairs={{0,1},{1,2},{2,3},{4,5},{5,6},{6,7},{8,9},{9,10},{10,11},{12,13},{... | collective-permute-start | bytes 221192 | tf_op jit(solution)/shard_map/ppermute | solution.py:50
  51.8 5.7 %collective-permute-start.7 = (f32[3,48,128]{2,1,0:T(8,128)S(1)}, f32[3,48,128]{2,1,0:T(8,128)S(1)}, u32[]{:S(2)}, u32[]{:S(2)}) collective-permute-start(f32[3,48,128]{2,1,0:T(8,128)S(1)} %get-tuple-element.51), channel_id=1, source_target_pairs={{1,0},{2,1},{3,2},{5,4},{6,5},{7,6},{9,8},{10,9},{11,10},{13,12},{... | collective-permute-start | bytes 221192 | tf_op jit(solution)/shard_map/ppermute | solution.py:50
  70.2 10.6 %collective-permute-start.8 = (f32[3,28,128]{2,1,0:T(8,128)S(1)}, f32[3,28,128]{2,1,0:T(8,128)S(1)}, u32[]{:S(2)}, u32[]{:S(2)}) collective-permute-start(f32[3,28,128]{2,1,0:T(8,128)S(1)} %get-tuple-element.55), channel_id=1, source_target_pairs={{0,4},{4,8},{8,12},{12,16},{16,20},{20,24},{24,28},{1,5},{5,9},{9,... | collective-permute-start | bytes 129032 | tf_op jit(solution)/shard_map/ppermute | solution.py:50
  73.3 1.3 %copy-start.11 = (f32[128]{0:T(128)S(1)}, f32[128]{0:T(128)}, u32[]{:S(2)}) copy-start(f32[128]{0:T(128)} %param.23) | copy-start | bytes 1540
  73.3 7.5 %collective-permute-start.9 = (f32[3,28,128]{2,1,0:T(8,128)S(1)}, f32[3,28,128]{2,1,0:T(8,128)S(1)}, u32[]{:S(2)}, u32[]{:S(2)}) collective-permute-start(f32[3,28,128]{2,1,0:T(8,128)S(1)} %get-tuple-element.56), channel_id=1, source_target_pairs={{4,0},{8,4},{12,8},{16,12},{20,16},{24,20},{28,24},{5,1},{9,5},{13... | collective-permute-start | bytes 129032 | tf_op jit(solution)/shard_map/ppermute | solution.py:50
  76.0 22.0 %all-to-all-start = ((f32[32,2,128]{2,1,0:T(2,128)}), f32[32,2,128]{2,1,0:T(2,128)S(1)}, u32[]{:S(2)}, u32[]{:S(2)}) async-start(f32[32,2,128]{2,1,0:T(2,128)} %zone_sums.1.rest_0_), calls=%async_computation | async-start | bytes 65536 | tf_op jit(solution)/shard_map/all_to_all | solution.py:810
  81.6 5.5 %collective-permute-start.10 = (f32[3,28,128]{2,1,0:T(8,128)S(1)}, f32[3,28,128]{2,1,0:T(8,128)S(1)}, u32[]{:S(2)}, u32[]{:S(2)}) collective-permute-start(f32[3,28,128]{2,1,0:T(8,128)S(1)} %get-tuple-element.60), channel_id=1, source_target_pairs={{0,1},{1,2},{2,3},{4,5},{5,6},{6,7},{8,9},{9,10},{10,11},{12,13},{... | collective-permute-start | bytes 129032 | tf_op jit(solution)/shard_map/ppermute | solution.py:50
  85.2 5.4 %collective-permute-start.11 = (f32[3,28,128]{2,1,0:T(8,128)S(1)}, f32[3,28,128]{2,1,0:T(8,128)S(1)}, u32[]{:S(2)}, u32[]{:S(2)}) collective-permute-start(f32[3,28,128]{2,1,0:T(8,128)S(1)} %get-tuple-element.61), channel_id=1, source_target_pairs={{1,0},{2,1},{3,2},{5,4},{6,5},{7,6},{9,8},{10,9},{11,10},{13,12},{... | collective-permute-start | bytes 129032 | tf_op jit(solution)/shard_map/ppermute | solution.py:50

commit v4 on v3

--- a/solution.py
+++ b/solution.py
@@ -76,12 +76,10 @@
 
 
 def gather_tile(src, row, lane_index, sublane_index):
-    found = [None] * len(lane_index)
-    for sub in range(SUB):
-        line = spread(src, row * SUB + sub)
-        for d, lane in enumerate(lane_index):
-            got = take(line, lane)
-            found[d] = got if sub == 0 else jnp.where(sublane_index[d] == sub, got, found[d])
+    found = take(spread(src, row * SUB), lane_index)
+    for sub in range(1, SUB):
+        got = take(spread(src, row * SUB + sub), lane_index)
+        found = jnp.where(sublane_index == sub, got, found)
     return found
 
 
@@ -90,51 +88,46 @@
 
 
 def gather_ends(src, row, lane_index, sublane_index, face):
-    nodes = [gather_tile(src, row + i, lane_index, sublane_index) for i in range(3)]
-    ends = []
-    for d, which in enumerate(face):
-        n0, n1, n2 = nodes[0][d], nodes[1][d], nodes[2][d]
-        ends.append((pick(which, n1, n2, n0), pick(which, n2, n0, n1)))
-    return ends
+    n0, n1, n2 = [gather_tile(src, row + i, lane_index, sublane_index) for i in range(3)]
+    return pick(face, n1, n2, n0), pick(face, n2, n0, n1)
 
 
 def gather_by_face(src, row, lane_index, sublane_index, face):
-    faces = [gather_tile(src, row + i, lane_index, sublane_index) for i in range(3)]
-    return [pick(which, faces[0][d], faces[1][d], faces[2][d]) for d, which in enumerate(face)]
-
-
-def fill_remote(received, row, lane_index, remote_index, values):
-    values = list(values)
+    return pick(
+        face, *[gather_tile(src, row + i, lane_index, sublane_index) for i in range(3)]
+    )
+
+
+def fill_remote(received, row, lane_index, remote_index, value):
     for number, (message, block) in enumerate(REMOTE_BLOCKS):
-        line = spread(received[message].at[block], row)
-        for d, lane in enumerate(lane_index):
-            values[d] = jnp.where(remote_index[d] == number, take(line, lane), values[d])
-    return values
-
-
-def partner_index(index_ref):
-    return [[tile(index_ref, part * 3 + f) for f in range(3)] for part in range(4)]
-
-
-def sent_index(index_ref):
-    return [[tile(index_ref, 12 + part * 2 + d) for d in range(2)] for part in range(3)]
+        got = take(spread(received[message].at[block], row), lane_index)
+        value = jnp.where(remote_index == number, got, value)
+    return value
+
+
+def partner_index(index_ref, f):
+    return [tile(index_ref, part * 3 + f) for part in range(4)]
+
+
+def sent_index(index_ref, d):
+    return [tile(index_ref, 12 + part * 2 + d) for part in range(3)]
 
 
 INDEX_ROWS = 18
 
 
-def send_states(src, first_comp, comps, first_row, sent, sent_ref):
-    lane, sublane, face = sent
-
-    def body(step, carry):
-        ends = gather_ends(src, (first_comp + step) * 3, lane, sublane, face)
-        for d in range(2):
+def send_states(src, first_comp, comps, first_row, index_ref, sent_ref):
+    for d in range(2):
+        lane, sublane, face = sent_index(index_ref, d)
+
+        def body(step, carry):
+            ends = gather_ends(src, (first_comp + step) * 3, lane, sublane, face)
             for j in range(2):
                 at = pl.multiple_of((first_row + step * 2 + j) * SUB, SUB)
-                sent_ref[d, pl.ds(at, SUB), :] = ends[d][j]
-        return carry
-
-    lax.fori_loop(0, comps, body, 0)
+                sent_ref[d, pl.ds(at, SUB), :] = ends[j]
+            return carry
+
+        lax.fori_loop(0, comps, body, 0)
 
 
 def write_messages(sent_ref, messages):
@@ -282,18 +275,17 @@
     put(table_ref, rows + 12, zone.astype(jnp.float32))
     for r in range(rows):
         put(table_ref, r, tile(cot_ref, r) * (wet_area if r < 12 else half_kappa_area))
-    sent = sent_index(index_ref)
     comps = rows // 3
-    send_states(table_ref, 0, comps, 0, sent, sent_ref)
-    for group in range(4):
-        values = gather_by_face(table_ref, rows + 3 * group, *sent)
-        for d in range(2):
-            at = (comps * 2 + group) * SUB
-            sent_ref[d, at : at + SUB, :] = values[d]
-    values = gather_tile(table_ref, rows + 12, sent[0], sent[1])
+    send_states(table_ref, 0, comps, 0, index_ref, sent_ref)
     for d in range(2):
-        at = (comps * 2 + 4) * SUB
-        sent_ref[d, at : at + SUB, :] = values[d]
+        lane, sublane, face = sent_index(index_ref, d)
+        at = comps * 2 * SUB
+        for group in range(4):
+            sent_ref[d, at : at + SUB, :] = gather_by_face(
+                table_ref, rows + 3 * group, lane, sublane, face
+            )
+            at += SUB
+        sent_ref[d, at : at + SUB, :] = gather_tile(table_ref, rows + 12, lane, sublane)
     write_messages(sent_ref, (to_right, to_left, to_up, to_down))
 
 
@@ -305,21 +297,20 @@
     down_ref[2] = jnp.where(first, left, right)
 
 
-def outer_states(src, first_comp, comps, first_row, received, index, out_ref):
-    lane, sublane, face, remote = index
-
-    def body(step, carry):
-        ends = gather_ends(src, (first_comp + step) * 3, lane, sublane, face)
-        for j in range(2):
-            values = fill_remote(
-                received, first_row + step * 2 + j, lane, remote, [ends[f][j] for f in range(3)]
-            )
-            for f in range(3):
+def outer_states(src, first_comp, comps, first_row, received, index_ref, out_ref):
+    for f in range(3):
+        lane, sublane, face, remote = partner_index(index_ref, f)
+
+        def body(step, carry):
+            ends = gather_ends(src, (first_comp + step) * 3, lane, sublane, face)
+            for j in range(2):
                 at = pl.multiple_of((f * comps * 2 + step * 2 + j) * SUB, SUB)
-                out_ref[pl.ds(at, SUB), :] = values[f]
-        return carry
-
-    lax.fori_loop(0, comps, body, 0)
+                out_ref[pl.ds(at, SUB), :] = fill_remote(
+                    received, first_row + step * 2 + j, lane, remote, ends[j]
+                )
+            return carry
+
+        lax.fori_loop(0, comps, body, 0)
 
 
 def transposed_section(
@@ -456,27 +447,23 @@
     received = (from_left, from_right, from_down, from_up)
     rows = cot_ref.shape[0] // SUB
     comps = rows // 3
-    index = partner_index(index_ref)
-    lane, sublane, face, remote = index
-    outer_states(table_ref, 0, comps, 0, received, index, outer_ref)
-    for group in range(4):
-        values = gather_by_face(table_ref, rows + 3 * group, lane, sublane, face)
-        values = fill_remote(received, comps * 2 + group, lane, remote, values)
-        for f in range(3):
+    outer_states(table_ref, 0, comps, 0, received, index_ref, outer_ref)
+    for f in range(3):
+        lane, sublane, face, remote = partner_index(index_ref, f)
+        for group in range(4):
+            value = gather_by_face(table_ref, rows + 3 * group, lane, sublane, face)
+            value = fill_remote(received, comps * 2 + group, lane, remote, value)
             if group == 0:
-                put(fact_ref, OUTER_EDGE + f, values[f])
+                put(fact_ref, OUTER_EDGE + f, value)
             else:
-                k = group - 1
-                both = tile(table_ref, rows + 3 * group + f) + values[f]
+                both = tile(table_ref, rows + 3 * group + f) + value
                 put(
                     fact_ref,
-                    HALF_SPEED + 3 * k + f,
+                    HALF_SPEED + 3 * (group - 1) + f,
                     0.5 * jnp.sqrt(1.0 + (0.25 / 8.0) * both),
                 )
-    values = gather_tile(table_ref, rows + 12, lane, sublane)
-    values = fill_remote(received, comps * 2 + 4, lane, remote, values)
-    for f in range(3):
-        put(fact_ref, OUTER_ZONE + f, values[f])
+        value = gather_tile(table_ref, rows + 12, lane, sublane)
+        put(fact_ref, OUTER_ZONE + f, fill_remote(received, comps * 2 + 4, lane, remote, value))
     wet_area = tile(stat_ref, WET_AREA)
     half_kappa_area = tile(stat_ref, HALF_KAPPA_AREA)
 
@@ -489,9 +476,8 @@
         2, cot_ref, table_ref, outer_ref, stat_ref, fact_ref, in_ref, out_ref, volume_ref, emit
     )
     x_to_tiles(x_ref, 0, x_tiles)
-    sent = sent_index(index_ref)
-    send_states(y_ref, 0, comps, 0, sent, sent_ref)
-    send_states(x_tiles, 4, comps - 4, comps * 2, sent, sent_ref)
+    send_states(y_ref, 0, comps, 0, index_ref, sent_ref)
+    send_states(x_tiles, 4, comps - 4, comps * 2, index_ref, sent_ref)
     write_messages(sent_ref, (to_right, to_left, to_up, to_down))
     x_to_tiles(x_ref, 2, x_tiles)
     weight = TIME_STEP * 2.0 / 3.0
@@ -534,8 +520,7 @@
     received = (from_left, from_right, from_down, from_up)
     rows = lam_ref.shape[0] // SUB
     comps = rows // 3
-    index = partner_index(index_ref)
-    outer_states(y_ref, 0, comps, 0, received, index, outer_ref)
+    outer_states(y_ref, 0, comps, 0, received, index_ref, outer_ref)
     wet_area = tile(stat_ref, WET_AREA)
     half_kappa_area = tile(stat_ref, HALF_KAPPA_AREA)
 
@@ -549,7 +534,7 @@
     transposed_section(
         1, lam_ref, y_ref, outer_ref, stat_ref, fact_ref, in_ref, out_ref, volume_ref, emit
     )
-    send_states(next_y_ref, 0, comps, 0, sent_index(index_ref), sent_ref)
+    send_states(next_y_ref, 0, comps, 0, index_ref, sent_ref)
     write_messages(sent_ref, (to_right, to_left, to_up, to_down))
     x_to_tiles(x_ref, 1, x_tiles)
     weight = TIME_STEP * 0.25
@@ -557,7 +542,7 @@
     for f, value in enumerate(outer_gradients(weight, outer_ref, x_tiles, fact_ref)):
         put(new_term_ref, 2 + f, tile(term_ref, 2 + f) + value)
     x_to_tiles(x_ref, 0, x_tiles)
-    outer_states(x_tiles, 4, comps - 4, comps * 2, received, index, x_outer_ref)
+    outer_states(x_tiles, 4, comps - 4, comps * 2, received, index_ref, x_outer_ref)
     friction_0, conduct_0 = own_gradients(0, TIME_STEP, next_ref, next_y_ref, x_tiles, stat_ref)
     friction = friction + friction_0
     conduct = conduct + conduct_0
@@ -634,7 +619,7 @@
 ):
     received = (from_left, from_right, from_down, from_up)
     rows = lam_ref.shape[0] // SUB
-    outer_states(y_ref, 0, rows // 3, 0, received, partner_index(index_ref), outer_ref)
+    outer_states(y_ref, 0, rows // 3, 0, received, index_ref, outer_ref)
 
     def emit(r, value):
         put(adjoint_ref, r, tile(base_ref, r) + TIME_STEP * value)

time: 99.3 us -> 99.5 us (level)
  transfers between devices with their start and end apart: 13 -> 13, of which waited for: 7 -> 7; matrix products, arithmetic and copies ran while one was open for 0% -> 0% of each run, Pallas kernels for 10% -> 9%
where the time goes in v4:
time: 99.5 us; the launch traced here: 98.8 us
  starting transfers between devices  38 us (38%)
  Pallas kernels  37.9 us (38%)
  waiting for transfers between devices  18.5 us (19%)
  local copies, waits for them, and re-layouts  3.51 us (4%)
    pallas_call x9, Pallas kernels, call(): pl.pallas_call(kernel, in_specs=[in_place if far else in_scalar if n in s...  37.9 us
    ppermute x12, starting transfers between devices, shifted(): return lax.ppermute(x, axis, pairs)  33.1 us
    ppermute x12, waiting for transfers between devices, shifted(): return lax.ppermute(x, axis, pairs)  18.5 us
    all_to_all x1, starting transfers between devices, local(): all_terms = lax.all_to_all(zone_terms, ('gx', 'gy'), 0, 0)  4.83 us
    unnamed x24, local copies, waits for them, and re-layouts  3.51 us
  transfers between devices with their start and end apart: 13, of which 7 were waited for; matrix products, arithmetic and copies ran while one was open for 0% of the time, Pallas kernels for 9%

profile of v4, /device:TPU:1, one launch (start us, length us, event | category | flops | bytes accessed | tf_op | source)
XLA Modules:
  0.0 98.8 jit_solution(13069077456812174499)
XLA Ops:
  0.6 4.9 %prepare.1 = (f32[440,128]{1,0:T(8,128)}, f32[96,128]{1,0:T(8,128)}, s32[144,128]{1,0:T(8,128)}, f32[3,33,128]{2,1,0:T(8,128)}, f32[3,33,128]{2,1,0:T(8,128)}, /...) custom-call(f32[336,128]{1,0:T(8,128)} %bitcast.11, bf16[3,1,1,42,1024]{4,3,2,1,0:T(8,128)(2,1)} %x_ref.5, f32[8,128]{1,0:T(8,128)} %bitcast.18, ...), custom_call_target="tpu_custom_call" | custom-call | tf_op jit(solution)/shard_map/prepare/pallas_call | solution.py:658
  5.6 4.1 %collective-permute-start = (f32[3,33,128]{2,1,0:T(8,128)}, f32[3,33,128]{2,1,0:T(8,128)S(1)}, u32[]{:S(2)}, u32[]{:S(2)}) collective-permute-start(f32[3,33,128]{2,1,0:T(8,128)} %get-tuple-element.36), channel_id=1, source_target_pairs={{0,4},{4,8},{8,12},{12,16},{16,20},{20,24},{24,28},{1,5},{5,9},{9,... | collective-permute-start | bytes 152072 | tf_op jit(solution)/shard_map/ppermute | solution.py:50
  9.7 1.3 %collective-permute-start.1 = (f32[3,33,128]{2,1,0:T(8,128)}, f32[3,33,128]{2,1,0:T(8,128)S(1)}, u32[]{:S(2)}, u32[]{:S(2)}) collective-permute-start(f32[3,33,128]{2,1,0:T(8,128)} %get-tuple-element.37), channel_id=1, source_target_pairs={{4,0},{8,4},{12,8},{16,12},{20,16},{24,20},{28,24},{5,1},{9,5},{13... | collective-permute-start | bytes 152072 | tf_op jit(solution)/shard_map/ppermute | solution.py:50
  11.0 0.3 collective-permute-done.left_ref.from_left
  11.3 3.6 %collective-permute-done.1.right_ref.from_right = f32[3,33,128]{2,1,0:T(8,128)S(1)} collective-permute-done((f32[3,33,128]{2,1,0:T(8,128)}, f32[3,33,128]{2,1,0:T(8,128)S(1)}, u32[]{:S(2)}, u32[]{:S(2)}) %collective-permute-start.1) | collective-permute-done | bytes 50720 | tf_op jit(solution)/shard_map/ppermute | solution.py:50
  14.8 0.8 copy-done.7
  15.7 0.8 copy-done.8
  16.5 0.0 copy-start.6
  16.5 5.3 %collective-permute-start.2 = (f32[3,33,128]{2,1,0:T(8,128)S(1)}, f32[3,33,128]{2,1,0:T(8,128)S(1)}, u32[]{:S(2)}, u32[]{:S(2)}) collective-permute-start(f32[3,33,128]{2,1,0:T(8,128)S(1)} %get-tuple-element.40), channel_id=1, source_target_pairs={{0,1},{1,2},{2,3},{4,5},{5,6},{6,7},{8,9},{9,10},{10,11},{12,13},{... | collective-permute-start | bytes 152072 | tf_op jit(solution)/shard_map/ppermute | solution.py:50
  21.8 1.9 %collective-permute-start.3 = (f32[3,33,128]{2,1,0:T(8,128)S(1)}, f32[3,33,128]{2,1,0:T(8,128)S(1)}, u32[]{:S(2)}, u32[]{:S(2)}) collective-permute-start(f32[3,33,128]{2,1,0:T(8,128)S(1)} %get-tuple-element.41), channel_id=1, source_target_pairs={{1,0},{2,1},{3,2},{5,4},{6,5},{7,6},{9,8},{10,9},{11,10},{13,12},{... | collective-permute-start | bytes 152072 | tf_op jit(solution)/shard_map/ppermute | solution.py:50
  23.8 3.6 %collective-permute-done.3.from_up = f32[3,33,128]{2,1,0:T(8,128)S(1)} collective-permute-done((f32[3,33,128]{2,1,0:T(8,128)S(1)}, f32[3,33,128]{2,1,0:T(8,128)S(1)}, u32[]{:S(2)}, u32[]{:S(2)}) %collective-permute-start.3) | collective-permute-done | bytes 50720 | tf_op jit(solution)/shard_map/ppermute | solution.py:50
  27.4 0.9 copy-done.3
  28.3 0.9 copy-done.5
  29.2 11.2 %section_two.1 = (f32[336,128]{1,0:T(8,128)S(1)}, f32[336,128]{1,0:T(8,128)S(1)}, f32[120,128]{1,0:T(8,128)S(1)}, f32[40,128]{1,0:T(8,128)S(1)}, f32[3,48,128]{2...) custom-call(f32[336,128]{1,0:T(8,128)S(1)} %bitcast.12, ...), custom_call_target="tpu_custom_call" | custom-call | tf_op jit(solution)/shard_map/section_two/pallas_call | solution.py:658
  40.4 4.1 %collective-permute-start.4 = (f32[3,48,128]{2,1,0:T(8,128)S(1)}, f32[3,48,128]{2,1,0:T(8,128)S(1)}, u32[]{:S(2)}, u32[]{:S(2)}) collective-permute-start(f32[3,48,128]{2,1,0:T(8,128)S(1)} %get-tuple-element.46), channel_id=1, source_target_pairs={{0,4},{4,8},{8,12},{12,16},{16,20},{20,24},{24,28},{1,5},{5,9},{9,... | collective-permute-start | bytes 221192 | tf_op jit(solution)/shard_map/ppermute | solution.py:50
  44.5 1.3 %collective-permute-start.5 = (f32[3,48,128]{2,1,0:T(8,128)S(1)}, f32[3,48,128]{2,1,0:T(8,128)S(1)}, u32[]{:S(2)}, u32[]{:S(2)}) collective-permute-start(f32[3,48,128]{2,1,0:T(8,128)S(1)} %get-tuple-element.47), channel_id=1, source_target_pairs={{4,0},{8,4},{12,8},{16,12},{20,16},{24,20},{28,24},{5,1},{9,5},{13... | collective-permute-start | bytes 221192 | tf_op jit(solution)/shard_map/ppermute | solution.py:50
  45.8 0.1 collective-permute-done.4.left_ref.from_left
  45.9 3.7 %collective-permute-done.5.right_ref.from_right = f32[3,48,128]{2,1,0:T(8,128)S(1)} collective-permute-done((f32[3,48,128]{2,1,0:T(8,128)S(1)}, f32[3,48,128]{2,1,0:T(8,128)S(1)}, u32[]{:S(2)}, u32[]{:S(2)}) %collective-permute-start.5) | collective-permute-done | bytes 73760 | tf_op jit(solution)/shard_map/ppermute | solution.py:50
  49.6 3.4 %collective-permute-start.6 = (f32[3,48,128]{2,1,0:T(8,128)S(1)}, f32[3,48,128]{2,1,0:T(8,128)S(1)}, u32[]{:S(2)}, u32[]{:S(2)}) collective-permute-start(f32[3,48,128]{2,1,0:T(8,128)S(1)} %get-tuple-element.50), channel_id=1, source_target_pairs={{0,1},{1,2},{2,3},{4,5},{5,6},{6,7},{8,9},{9,10},{10,11},{12,13},{... | collective-permute-start | bytes 221192 | tf_op jit(solution)/shard_map/ppermute | solution.py:50
  53.0 1.9 %collective-permute-start.7 = (f32[3,48,128]{2,1,0:T(8,128)S(1)}, f32[3,48,128]{2,1,0:T(8,128)S(1)}, u32[]{:S(2)}, u32[]{:S(2)}) collective-permute-start(f32[3,48,128]{2,1,0:T(8,128)S(1)} %get-tuple-element.51), channel_id=1, source_target_pairs={{1,0},{2,1},{3,2},{5,4},{6,5},{7,6},{9,8},{10,9},{11,10},{13,12},{... | collective-permute-start | bytes 221192 | tf_op jit(solution)/shard_map/ppermute | solution.py:50
  55.0 3.7 %collective-permute-done.7.from_up = f32[3,48,128]{2,1,0:T(8,128)S(1)} collective-permute-done((f32[3,48,128]{2,1,0:T(8,128)S(1)}, f32[3,48,128]{2,1,0:T(8,128)S(1)}, u32[]{:S(2)}, u32[]{:S(2)}) %collective-permute-start.7) | collective-permute-done | bytes 73760 | tf_op jit(solution)/shard_map/ppermute | solution.py:50
  58.7 12.5 %section_one.1 = (f32[336,128]{1,0:T(8,128)S(1)}, f32[336,128]{1,0:T(8,128)S(1)}, f32[336,128]{1,0:T(8,128)S(1)}, f32[40,128]{1,0:T(8,128)S(1)}, f32[3,28,128]{2...) custom-call(f32[336,128]{1,0:T(8,128)S(1)} %bitcast.13, ...), custom_call_target="tpu_custom_call" | custom-call | tf_op jit(solution)/shard_map/section_one/pallas_call | solution.py:658
  71.2 3.1 %collective-permute-start.8 = (f32[3,28,128]{2,1,0:T(8,128)S(1)}, f32[3,28,128]{2,1,0:T(8,128)S(1)}, u32[]{:S(2)}, u32[]{:S(2)}) collective-permute-start(f32[3,28,128]{2,1,0:T(8,128)S(1)} %get-tuple-element.55), channel_id=1, source_target_pairs={{0,4},{4,8},{8,12},{12,16},{16,20},{20,24},{24,28},{1,5},{5,9},{9,... | collective-permute-start | bytes 129032 | tf_op jit(solution)/shard_map/ppermute | solution.py:50
  74.3 1.3 %collective-permute-start.9 = (f32[3,28,128]{2,1,0:T(8,128)S(1)}, f32[3,28,128]{2,1,0:T(8,128)S(1)}, u32[]{:S(2)}, u32[]{:S(2)}) collective-permute-start(f32[3,28,128]{2,1,0:T(8,128)S(1)} %get-tuple-element.56), channel_id=1, source_target_pairs={{4,0},{8,4},{12,8},{16,12},{20,16},{24,20},{28,24},{5,1},{9,5},{13... | collective-permute-start | bytes 129032 | tf_op jit(solution)/shard_map/ppermute | solution.py:50
  75.6 1.3 %zone_sums.1.rest_0_ = f32[32,2,128]{2,1,0:T(2,128)} custom-call(f32[40,128]{1,0:T(8,128)S(1)} %get-tuple-element.59.term_ref, f32[96,128]{1,0:T(8,128)S(1)} %copy-done.2, f32[120,128]{1,0:T(8,128)S(1)} %get-tuple-element.44.fact_ref, f32[1,128]{1,0:T(1,128)S(1)} %bitcast.15), custom_call_target="tpu_custom_call" | custom-call | tf_op jit(solution)/shard_map/zone_sums/pallas_call | solution.py:658
  77.0 4.8 %all-to-all-start = ((f32[32,2,128]{2,1,0:T(2,128)}), f32[32,2,128]{2,1,0:T(2,128)S(1)}, u32[]{:S(2)}, u32[]{:S(2)}) async-start(f32[32,2,128]{2,1,0:T(2,128)} %zone_sums.1.rest_0_), calls=%async_computation | async-start | bytes 65536 | tf_op jit(solution)/shard_map/all_to_all | solution.py:795
  81.8 0.8 corners.5
  82.6 3.5 %collective-permute-start.10 = (f32[3,28,128]{2,1,0:T(8,128)S(1)}, f32[3,28,128]{2,1,0:T(8,128)S(1)}, u32[]{:S(2)}, u32[]{:S(2)}) collective-permute-start(f32[3,28,128]{2,1,0:T(8,128)S(1)} %get-tuple-element.60), channel_id=1, source_target_pairs={{0,1},{1,2},{2,3},{4,5},{5,6},{6,7},{8,9},{9,10},{10,11},{12,13},{... | collective-permute-start | bytes 129032 | tf_op jit(solution)/shard_map/ppermute | solution.py:50
  86.1 1.9 %collective-permute-start.11 = (f32[3,28,128]{2,1,0:T(8,128)S(1)}, f32[3,28,128]{2,1,0:T(8,128)S(1)}, u32[]{:S(2)}, u32[]{:S(2)}) collective-permute-start(f32[3,28,128]{2,1,0:T(8,128)S(1)} %get-tuple-element.61), channel_id=1, source_target_pairs={{1,0},{2,1},{3,2},{5,4},{6,5},{7,6},{9,8},{10,9},{11,10},{13,12},{... | collective-permute-start | bytes 129032 | tf_op jit(solution)/shard_map/ppermute | solution.py:50
  88.1 3.5 %collective-permute-done.11.from_up = f32[3,28,128]{2,1,0:T(8,128)S(1)} collective-permute-done((f32[3,28,128]{2,1,0:T(8,128)S(1)}, f32[3,28,128]{2,1,0:T(8,128)S(1)}, u32[]{:S(2)}, u32[]{:S(2)}) %collective-permute-start.11) | collective-permute-done | bytes 43040 | tf_op jit(solution)/shard_map/ppermute | solution.py:50
  91.6 6.6 %section_zero.1 = (f32[336,128]{1,0:T(8,128)}, f32[8,128]{1,0:T(8,128)S(1)}) custom-call(f32[336,128]{1,0:T(8,128)S(1)} %get-tuple-element.52.base_ref, f32[336,128]{1,0:T(8,128)S(1)} %get-tuple-element.53.lam_ref, f32[336,128]{1,0:T(8,128)S(1)} %get-tuple-element.54.y_ref, f32[96,128]{1,0:T(8,128)S(1)} %copy-done.2, s32[144,128]{1,0:T(8,128)S(1)} %copy-done.4, ...), custom_call_target="tpu_custom_call" | custom-call | tf_op jit(solution)/shard_map/section_zero/pallas_call | solution.py:658
  98.2 0.6 zone_total.1
  (27 shorter events, 0.1 us)
Async XLA Ops:
  0.6 26.7 %copy-start = (bf16[3,1,1,42,1024]{4,3,2,1,0:T(8,128)(2,1)S(1)}, bf16[3,1,1,42,1024]{4,3,2,1,0:T(8,128)(2,1)}, u32[]{:S(2)}) copy-start(bf16[3,1,1,42,1024]{4,3,2,1,0:T(8,128)(2,1)} %x_ref.5) | copy-start | bytes 774148
  5.6 21.8 %copy-start.1 = (f32[1,1,42,1024]{3,1,2,0:T(1,128)S(1)}, f32[1,1,42,1024]{3,1,2,0:T(1,128)}, u32[]{:S(2)}) copy-start(f32[1,1,42,1024]{3,1,2,0:T(1,128)} %param.16) | copy-start | bytes 516100
  5.6 5.7 %collective-permute-start = (f32[3,33,128]{2,1,0:T(8,128)}, f32[3,33,128]{2,1,0:T(8,128)S(1)}, u32[]{:S(2)}, u32[]{:S(2)}) collective-permute-start(f32[3,33,128]{2,1,0:T(8,128)} %get-tuple-element.36), channel_id=1, source_target_pairs={{0,4},{4,8},{8,12},{12,16},{16,20},{20,24},{24,28},{1,5},{5,9},{9,... | collective-permute-start | bytes 152072 | tf_op jit(solution)/shard_map/ppermute | solution.py:50
  9.7 5.2 %collective-permute-start.1 = (f32[3,33,128]{2,1,0:T(8,128)}, f32[3,33,128]{2,1,0:T(8,128)S(1)}, u32[]{:S(2)}, u32[]{:S(2)}) collective-permute-start(f32[3,33,128]{2,1,0:T(8,128)} %get-tuple-element.37), channel_id=1, source_target_pairs={{4,0},{8,4},{12,8},{16,12},{20,16},{24,20},{28,24},{5,1},{9,5},{13... | collective-permute-start | bytes 152072 | tf_op jit(solution)/shard_map/ppermute | solution.py:50
  14.8 0.8 copy-start.7
  15.7 0.8 copy-start.8
  16.5 10.9 %copy-start.2 = (f32[96,128]{1,0:T(8,128)S(1)}, f32[96,128]{1,0:T(8,128)}, u32[]{:S(2)}) copy-start(f32[96,128]{1,0:T(8,128)} %get-tuple-element.34.stat_ref) | copy-start | bytes 147460
  16.5 10.9 %copy-start.9 = (f32[8,8]{1,0:T(8,128)S(1)}, f32[8,8]{1,0:T(8,128)}, u32[]{:S(2)}) copy-start(f32[8,8]{1,0:T(8,128)} %in_ref.5) | copy-start | bytes 772
  16.5 10.9 %copy-start.10 = (f32[8,8]{1,0:T(8,128)S(1)}, f32[8,8]{1,0:T(8,128)}, u32[]{:S(2)}) copy-start(f32[8,8]{1,0:T(8,128)} %out_ref.5) | copy-start | bytes 772
  16.5 10.9 %copy-start.6 = (f32[12,12]{1,0:T(8,128)S(1)}, f32[12,12]{1,0:T(8,128)}, u32[]{:S(2)}) copy-start(f32[12,12]{1,0:T(8,128)} %volume_ref.5) | copy-start | bytes 1732
  16.5 7.2 %collective-permute-start.2 = (f32[3,33,128]{2,1,0:T(8,128)S(1)}, f32[3,33,128]{2,1,0:T(8,128)S(1)}, u32[]{:S(2)}, u32[]{:S(2)}) collective-permute-start(f32[3,33,128]{2,1,0:T(8,128)S(1)} %get-tuple-element.40), channel_id=1, source_target_pairs={{0,1},{1,2},{2,3},{4,5},{5,6},{6,7},{8,9},{9,10},{10,11},{12,13},{... | collective-permute-start | bytes 152072 | tf_op jit(solution)/shard_map/ppermute | solution.py:50
  21.8 5.5 %collective-permute-start.3 = (f32[3,33,128]{2,1,0:T(8,128)S(1)}, f32[3,33,128]{2,1,0:T(8,128)S(1)}, u32[]{:S(2)}, u32[]{:S(2)}) collective-permute-start(f32[3,33,128]{2,1,0:T(8,128)S(1)} %get-tuple-element.41), channel_id=1, source_target_pairs={{1,0},{2,1},{3,2},{5,4},{6,5},{7,6},{9,8},{10,9},{11,10},{13,12},{... | collective-permute-start | bytes 152072 | tf_op jit(solution)/shard_map/ppermute | solution.py:50
  27.4 0.9 copy-start.3
  28.3 0.9 copy-start.5
  40.4 5.5 %collective-permute-start.4 = (f32[3,48,128]{2,1,0:T(8,128)S(1)}, f32[3,48,128]{2,1,0:T(8,128)S(1)}, u32[]{:S(2)}, u32[]{:S(2)}) collective-permute-start(f32[3,48,128]{2,1,0:T(8,128)S(1)} %get-tuple-element.46), channel_id=1, source_target_pairs={{0,4},{4,8},{8,12},{12,16},{16,20},{20,24},{24,28},{1,5},{5,9},{9,... | collective-permute-start | bytes 221192 | tf_op jit(solution)/shard_map/ppermute | solution.py:50
  44.5 5.1 %collective-permute-start.5 = (f32[3,48,128]{2,1,0:T(8,128)S(1)}, f32[3,48,128]{2,1,0:T(8,128)S(1)}, u32[]{:S(2)}, u32[]{:S(2)}) collective-permute-start(f32[3,48,128]{2,1,0:T(8,128)S(1)} %get-tuple-element.47), channel_id=1, source_target_pairs={{4,0},{8,4},{12,8},{16,12},{20,16},{24,20},{28,24},{5,1},{9,5},{13... | collective-permute-start | bytes 221192 | tf_op jit(solution)/shard_map/ppermute | solution.py:50
  49.6 9.1 %copy-start.4 = (s32[144,128]{1,0:T(8,128)S(1)}, s32[144,128]{1,0:T(8,128)}, u32[]{:S(2)}) copy-start(s32[144,128]{1,0:T(8,128)} %get-tuple-element.35.index_ref) | copy-start | bytes 221188
  49.6 5.4 %collective-permute-start.6 = (f32[3,48,128]{2,1,0:T(8,128)S(1)}, f32[3,48,128]{2,1,0:T(8,128)S(1)}, u32[]{:S(2)}, u32[]{:S(2)}) collective-permute-start(f32[3,48,128]{2,1,0:T(8,128)S(1)} %get-tuple-element.50), channel_id=1, source_target_pairs={{0,1},{1,2},{2,3},{4,5},{5,6},{6,7},{8,9},{9,10},{10,11},{12,13},{... | collective-permute-start | bytes 221192 | tf_op jit(solution)/shard_map/ppermute | solution.py:50
  53.0 5.7 %collective-permute-start.7 = (f32[3,48,128]{2,1,0:T(8,128)S(1)}, f32[3,48,128]{2,1,0:T(8,128)S(1)}, u32[]{:S(2)}, u32[]{:S(2)}) collective-permute-start(f32[3,48,128]{2,1,0:T(8,128)S(1)} %get-tuple-element.51), channel_id=1, source_target_pairs={{1,0},{2,1},{3,2},{5,4},{6,5},{7,6},{9,8},{10,9},{11,10},{13,12},{... | collective-permute-start | bytes 221192 | tf_op jit(solution)/shard_map/ppermute | solution.py:50
  71.2 10.6 %collective-permute-start.8 = (f32[3,28,128]{2,1,0:T(8,128)S(1)}, f32[3,28,128]{2,1,0:T(8,128)S(1)}, u32[]{:S(2)}, u32[]{:S(2)}) collective-permute-start(f32[3,28,128]{2,1,0:T(8,128)S(1)} %get-tuple-element.55), channel_id=1, source_target_pairs={{0,4},{4,8},{8,12},{12,16},{16,20},{20,24},{24,28},{1,5},{5,9},{9,... | collective-permute-start | bytes 129032 | tf_op jit(solution)/shard_map/ppermute | solution.py:50
  74.3 1.3 %copy-start.11 = (f32[128]{0:T(128)S(1)}, f32[128]{0:T(128)}, u32[]{:S(2)}) copy-start(f32[128]{0:T(128)} %param.23) | copy-start | bytes 1540
  74.3 7.5 %collective-permute-start.9 = (f32[3,28,128]{2,1,0:T(8,128)S(1)}, f32[3,28,128]{2,1,0:T(8,128)S(1)}, u32[]{:S(2)}, u32[]{:S(2)}) collective-permute-start(f32[3,28,128]{2,1,0:T(8,128)S(1)} %get-tuple-element.56), channel_id=1, source_target_pairs={{4,0},{8,4},{12,8},{16,12},{20,16},{24,20},{28,24},{5,1},{9,5},{13... | collective-permute-start | bytes 129032 | tf_op jit(solution)/shard_map/ppermute | solution.py:50
  77.0 21.2 %all-to-all-start = ((f32[32,2,128]{2,1,0:T(2,128)}), f32[32,2,128]{2,1,0:T(2,128)S(1)}, u32[]{:S(2)}, u32[]{:S(2)}) async-start(f32[32,2,128]{2,1,0:T(2,128)} %zone_sums.1.rest_0_), calls=%async_computation | async-start | bytes 65536 | tf_op jit(solution)/shard_map/all_to_all | solution.py:795
  82.6 5.5 %collective-permute-start.10 = (f32[3,28,128]{2,1,0:T(8,128)S(1)}, f32[3,28,128]{2,1,0:T(8,128)S(1)}, u32[]{:S(2)}, u32[]{:S(2)}) collective-permute-start(f32[3,28,128]{2,1,0:T(8,128)S(1)} %get-tuple-element.60), channel_id=1, source_target_pairs={{0,1},{1,2},{2,3},{4,5},{5,6},{6,7},{8,9},{9,10},{10,11},{12,13},{... | collective-permute-start | bytes 129032 | tf_op jit(solution)/shard_map/ppermute | solution.py:50
  86.1 5.4 %collective-permute-start.11 = (f32[3,28,128]{2,1,0:T(8,128)S(1)}, f32[3,28,128]{2,1,0:T(8,128)S(1)}, u32[]{:S(2)}, u32[]{:S(2)}) collective-permute-start(f32[3,28,128]{2,1,0:T(8,128)S(1)} %get-tuple-element.61), channel_id=1, source_target_pairs={{1,0},{2,1},{3,2},{5,4},{6,5},{7,6},{9,8},{10,9},{11,10},{13,12},{... | collective-permute-start | bytes 129032 | tf_op jit(solution)/shard_map/ppermute | solution.py:50

commit v5 on v4

--- a/solution.py
+++ b/solution.py
@@ -116,18 +116,33 @@
 INDEX_ROWS = 18
 
 
+def turns(comps):
+    width = 7 if comps % 7 == 0 else 5
+    return width, comps // width
+
+
+def tile_at(ref, row):
+    return ref[pl.ds(pl.multiple_of(row * SUB, SUB), SUB), :]
+
+
+def put_at(ref, row, value):
+    ref[pl.ds(pl.multiple_of(row * SUB, SUB), SUB), :] = value
+
+
 def send_states(src, first_comp, comps, first_row, index_ref, sent_ref):
-    for d in range(2):
-        lane, sublane, face = sent_index(index_ref, d)
-
-        def body(step, carry):
-            ends = gather_ends(src, (first_comp + step) * 3, lane, sublane, face)
+    width, parts = turns(comps)
+
+    def body(step, carry):
+        d, part = step // parts, step % parts
+        lane, sublane, face = [tile_at(index_ref, 12 + n * 2 + d) for n in range(3)]
+        for w in range(width):
+            comp = part * width + w
+            ends = gather_ends(src, (first_comp + comp) * 3, lane, sublane, face)
             for j in range(2):
-                at = pl.multiple_of((first_row + step * 2 + j) * SUB, SUB)
-                sent_ref[d, pl.ds(at, SUB), :] = ends[j]
-            return carry
-
-        lax.fori_loop(0, comps, body, 0)
+                put_at(sent_ref.at[d], first_row + comp * 2 + j, ends[j])
+        return carry
+
+    lax.fori_loop(0, 2 * parts, body, 0)
 
 
 def write_messages(sent_ref, messages):
@@ -298,19 +313,20 @@
 
 
 def outer_states(src, first_comp, comps, first_row, received, index_ref, out_ref):
-    for f in range(3):
-        lane, sublane, face, remote = partner_index(index_ref, f)
-
-        def body(step, carry):
-            ends = gather_ends(src, (first_comp + step) * 3, lane, sublane, face)
+    width, parts = turns(comps)
+
+    def body(step, carry):
+        f, part = step // parts, step % parts
+        lane, sublane, face, remote = [tile_at(index_ref, n * 3 + f) for n in range(4)]
+        for w in range(width):
+            comp = part * width + w
+            ends = gather_ends(src, (first_comp + comp) * 3, lane, sublane, face)
             for j in range(2):
-                at = pl.multiple_of((f * comps * 2 + step * 2 + j) * SUB, SUB)
-                out_ref[pl.ds(at, SUB), :] = fill_remote(
-                    received, first_row + step * 2 + j, lane, remote, ends[j]
-                )
-            return carry
-
-        lax.fori_loop(0, comps, body, 0)
+                value = fill_remote(received, first_row + comp * 2 + j, lane, remote, ends[j])
+                put_at(out_ref, f * comps * 2 + comp * 2 + j, value)
+        return carry
+
+    lax.fori_loop(0, 3 * parts, body, 0)
 
 
 def transposed_section(

time: 99.5 us -> 84 us (0.84)
  Pallas kernels: 37.9 us -> 22.4 us
    pallas_call x9, Pallas kernels: 37.9 us -> 22.4 us  [call(): pl.pallas_call(kernel, in_specs=[in_place if far else in_scalar if n in s...]
  transfers between devices with their start and end apart: 13 -> 13, of which waited for: 7 -> 7; matrix products, arithmetic and copies ran while one was open for 0% -> 0% of each run, Pallas kernels for 9% -> 8%
where the time goes in v5:
time: 84 us; the launch traced here: 83.2 us
  starting transfers between devices  38 us (45%)
  Pallas kernels  22.4 us (27%)
  waiting for transfers between devices  18.5 us (22%)
  local copies, waits for them, and re-layouts  3.51 us (4%)
  between operations  0.89 us (1%)
    ppermute x12, starting transfers between devices, shifted(): return lax.ppermute(x, axis, pairs)  33.1 us
    pallas_call x9, Pallas kernels, call(): pl.pallas_call(kernel, in_specs=[in_place if far else in_scalar if n in s...  22.4 us
    ppermute x12, waiting for transfers between devices, shifted(): return lax.ppermute(x, axis, pairs)  18.5 us
    all_to_all x1, starting transfers between devices, local(): all_terms = lax.all_to_all(zone_terms, ('gx', 'gy'), 0, 0)  4.84 us
    unnamed x24, local copies, waits for them, and re-layouts  3.51 us
  transfers between devices with their start and end apart: 13, of which 7 were waited for; matrix products, arithmetic and copies ran while one was open for 0% of the time, Pallas kernels for 8%

profile of v5, /device:TPU:1, one launch (start us, length us, event | category | flops | bytes accessed | tf_op | source)
XLA Modules:
  0.0 83.2 jit_solution(6731812771913623513)
XLA Ops:
  0.6 3.2 %prepare.1 = (f32[440,128]{1,0:T(8,128)}, f32[96,128]{1,0:T(8,128)}, s32[144,128]{1,0:T(8,128)}, f32[3,33,128]{2,1,0:T(8,128)}, f32[3,33,128]{2,1,0:T(8,128)}, /...) custom-call(f32[336,128]{1,0:T(8,128)} %bitcast.11, bf16[3,1,1,42,1024]{4,3,2,1,0:T(8,128)(2,1)} %x_ref.5, f32[8,128]{1,0:T(8,128)} %bitcast.18, ...), custom_call_target="tpu_custom_call" | custom-call | tf_op jit(solution)/shard_map/prepare/pallas_call | solution.py:674
  3.9 4.1 %collective-permute-start = (f32[3,33,128]{2,1,0:T(8,128)}, f32[3,33,128]{2,1,0:T(8,128)S(1)}, u32[]{:S(2)}, u32[]{:S(2)}) collective-permute-start(f32[3,33,128]{2,1,0:T(8,128)} %get-tuple-element.36), channel_id=1, source_target_pairs={{0,4},{4,8},{8,12},{12,16},{16,20},{20,24},{24,28},{1,5},{5,9},{9,... | collective-permute-start | bytes 152072 | tf_op jit(solution)/shard_map/ppermute | solution.py:50
  8.0 1.3 %collective-permute-start.1 = (f32[3,33,128]{2,1,0:T(8,128)}, f32[3,33,128]{2,1,0:T(8,128)S(1)}, u32[]{:S(2)}, u32[]{:S(2)}) collective-permute-start(f32[3,33,128]{2,1,0:T(8,128)} %get-tuple-element.37), channel_id=1, source_target_pairs={{4,0},{8,4},{12,8},{16,12},{20,16},{24,20},{28,24},{5,1},{9,5},{13... | collective-permute-start | bytes 152072 | tf_op jit(solution)/shard_map/ppermute | solution.py:50
  9.3 0.3 collective-permute-done.left_ref.from_left
  9.6 3.6 %collective-permute-done.1.right_ref.from_right = f32[3,33,128]{2,1,0:T(8,128)S(1)} collective-permute-done((f32[3,33,128]{2,1,0:T(8,128)}, f32[3,33,128]{2,1,0:T(8,128)S(1)}, u32[]{:S(2)}, u32[]{:S(2)}) %collective-permute-start.1) | collective-permute-done | bytes 50720 | tf_op jit(solution)/shard_map/ppermute | solution.py:50
  13.2 0.8 copy-done.7
  14.0 0.8 copy-done.8
  14.8 5.3 %collective-permute-start.2 = (f32[3,33,128]{2,1,0:T(8,128)S(1)}, f32[3,33,128]{2,1,0:T(8,128)S(1)}, u32[]{:S(2)}, u32[]{:S(2)}) collective-permute-start(f32[3,33,128]{2,1,0:T(8,128)S(1)} %get-tuple-element.40), channel_id=1, source_target_pairs={{0,1},{1,2},{2,3},{4,5},{5,6},{6,7},{8,9},{9,10},{10,11},{12,13},{... | collective-permute-start | bytes 152072 | tf_op jit(solution)/shard_map/ppermute | solution.py:50
  20.1 1.9 %collective-permute-start.3 = (f32[3,33,128]{2,1,0:T(8,128)S(1)}, f32[3,33,128]{2,1,0:T(8,128)S(1)}, u32[]{:S(2)}, u32[]{:S(2)}) collective-permute-start(f32[3,33,128]{2,1,0:T(8,128)S(1)} %get-tuple-element.41), channel_id=1, source_target_pairs={{1,0},{2,1},{3,2},{5,4},{6,5},{7,6},{9,8},{10,9},{11,10},{13,12},{... | collective-permute-start | bytes 152072 | tf_op jit(solution)/shard_map/ppermute | solution.py:50
  22.1 3.6 %collective-permute-done.3.from_up = f32[3,33,128]{2,1,0:T(8,128)S(1)} collective-permute-done((f32[3,33,128]{2,1,0:T(8,128)S(1)}, f32[3,33,128]{2,1,0:T(8,128)S(1)}, u32[]{:S(2)}, u32[]{:S(2)}) %collective-permute-start.3) | collective-permute-done | bytes 50720 | tf_op jit(solution)/shard_map/ppermute | solution.py:50
  25.7 0.9 %copy-done.3 = s32[144,128]{1,0:T(8,128)S(1)} copy-done((s32[144,128]{1,0:T(8,128)S(1)}, s32[144,128]{1,0:T(8,128)}, u32[]{:S(2)}) %copy-start.3) | copy-done | bytes 73752
  26.6 0.9 %copy-done.5 = f32[440,128]{1,0:T(8,128)S(1)} copy-done((f32[440,128]{1,0:T(8,128)S(1)}, f32[440,128]{1,0:T(8,128)}, u32[]{:S(2)}) %copy-start.5) | copy-done | bytes 225304
  27.5 5.8 %section_two.1 = (f32[336,128]{1,0:T(8,128)S(1)}, f32[336,128]{1,0:T(8,128)S(1)}, f32[120,128]{1,0:T(8,128)S(1)}, f32[40,128]{1,0:T(8,128)S(1)}, f32[3,48,128]{2...) custom-call(f32[336,128]{1,0:T(8,128)S(1)} %bitcast.12, ...), custom_call_target="tpu_custom_call" | custom-call | tf_op jit(solution)/shard_map/section_two/pallas_call | solution.py:674
  33.3 4.1 %collective-permute-start.4 = (f32[3,48,128]{2,1,0:T(8,128)S(1)}, f32[3,48,128]{2,1,0:T(8,128)S(1)}, u32[]{:S(2)}, u32[]{:S(2)}) collective-permute-start(f32[3,48,128]{2,1,0:T(8,128)S(1)} %get-tuple-element.46), channel_id=1, source_target_pairs={{0,4},{4,8},{8,12},{12,16},{16,20},{20,24},{24,28},{1,5},{5,9},{9,... | collective-permute-start | bytes 221192 | tf_op jit(solution)/shard_map/ppermute | solution.py:50
  37.4 1.3 %collective-permute-start.5 = (f32[3,48,128]{2,1,0:T(8,128)S(1)}, f32[3,48,128]{2,1,0:T(8,128)S(1)}, u32[]{:S(2)}, u32[]{:S(2)}) collective-permute-start(f32[3,48,128]{2,1,0:T(8,128)S(1)} %get-tuple-element.47), channel_id=1, source_target_pairs={{4,0},{8,4},{12,8},{16,12},{20,16},{24,20},{28,24},{5,1},{9,5},{13... | collective-permute-start | bytes 221192 | tf_op jit(solution)/shard_map/ppermute | solution.py:50
  38.7 0.1 collective-permute-done.4.left_ref.from_left
  38.8 3.7 %collective-permute-done.5.right_ref.from_right = f32[3,48,128]{2,1,0:T(8,128)S(1)} collective-permute-done((f32[3,48,128]{2,1,0:T(8,128)S(1)}, f32[3,48,128]{2,1,0:T(8,128)S(1)}, u32[]{:S(2)}, u32[]{:S(2)}) %collective-permute-start.5) | collective-permute-done | bytes 73760 | tf_op jit(solution)/shard_map/ppermute | solution.py:50
  42.5 3.4 %collective-permute-start.6 = (f32[3,48,128]{2,1,0:T(8,128)S(1)}, f32[3,48,128]{2,1,0:T(8,128)S(1)}, u32[]{:S(2)}, u32[]{:S(2)}) collective-permute-start(f32[3,48,128]{2,1,0:T(8,128)S(1)} %get-tuple-element.50), channel_id=1, source_target_pairs={{0,1},{1,2},{2,3},{4,5},{5,6},{6,7},{8,9},{9,10},{10,11},{12,13},{... | collective-permute-start | bytes 221192 | tf_op jit(solution)/shard_map/ppermute | solution.py:50
  45.9 1.9 %collective-permute-start.7 = (f32[3,48,128]{2,1,0:T(8,128)S(1)}, f32[3,48,128]{2,1,0:T(8,128)S(1)}, u32[]{:S(2)}, u32[]{:S(2)}) collective-permute-start(f32[3,48,128]{2,1,0:T(8,128)S(1)} %get-tuple-element.51), channel_id=1, source_target_pairs={{1,0},{2,1},{3,2},{5,4},{6,5},{7,6},{9,8},{10,9},{11,10},{13,12},{... | collective-permute-start | bytes 221192 | tf_op jit(solution)/shard_map/ppermute | solution.py:50
  47.9 3.7 %collective-permute-done.7.from_up = f32[3,48,128]{2,1,0:T(8,128)S(1)} collective-permute-done((f32[3,48,128]{2,1,0:T(8,128)S(1)}, f32[3,48,128]{2,1,0:T(8,128)S(1)}, u32[]{:S(2)}, u32[]{:S(2)}) %collective-permute-start.7) | collective-permute-done | bytes 73760 | tf_op jit(solution)/shard_map/ppermute | solution.py:50
  51.6 6.5 %section_one.1 = (f32[336,128]{1,0:T(8,128)S(1)}, f32[336,128]{1,0:T(8,128)S(1)}, f32[336,128]{1,0:T(8,128)S(1)}, f32[40,128]{1,0:T(8,128)S(1)}, f32[3,28,128]{2...) custom-call(f32[336,128]{1,0:T(8,128)S(1)} %bitcast.13, ...), custom_call_target="tpu_custom_call" | custom-call | tf_op jit(solution)/shard_map/section_one/pallas_call | solution.py:674
  58.1 3.1 %collective-permute-start.8 = (f32[3,28,128]{2,1,0:T(8,128)S(1)}, f32[3,28,128]{2,1,0:T(8,128)S(1)}, u32[]{:S(2)}, u32[]{:S(2)}) collective-permute-start(f32[3,28,128]{2,1,0:T(8,128)S(1)} %get-tuple-element.55), channel_id=1, source_target_pairs={{0,4},{4,8},{8,12},{12,16},{16,20},{20,24},{24,28},{1,5},{5,9},{9,... | collective-permute-start | bytes 129032 | tf_op jit(solution)/shard_map/ppermute | solution.py:50
  61.3 0.0 copy-start.11
  61.3 1.3 %collective-permute-start.9 = (f32[3,28,128]{2,1,0:T(8,128)S(1)}, f32[3,28,128]{2,1,0:T(8,128)S(1)}, u32[]{:S(2)}, u32[]{:S(2)}) collective-permute-start(f32[3,28,128]{2,1,0:T(8,128)S(1)} %get-tuple-element.56), channel_id=1, source_target_pairs={{4,0},{8,4},{12,8},{16,12},{20,16},{24,20},{28,24},{5,1},{9,5},{13... | collective-permute-start | bytes 129032 | tf_op jit(solution)/shard_map/ppermute | solution.py:50
  62.6 1.3 %zone_sums.1.rest_0_ = f32[32,2,128]{2,1,0:T(2,128)} custom-call(f32[40,128]{1,0:T(8,128)S(1)} %get-tuple-element.59.term_ref, f32[96,128]{1,0:T(8,128)S(1)} %copy-done.2, f32[120,128]{1,0:T(8,128)S(1)} %get-tuple-element.44.fact_ref, f32[1,128]{1,0:T(1,128)S(1)} %bitcast.15), custom_call_target="tpu_custom_call" | custom-call | tf_op jit(solution)/shard_map/zone_sums/pallas_call | solution.py:674
  63.9 4.8 %all-to-all-start = ((f32[32,2,128]{2,1,0:T(2,128)}), f32[32,2,128]{2,1,0:T(2,128)S(1)}, u32[]{:S(2)}, u32[]{:S(2)}) async-start(f32[32,2,128]{2,1,0:T(2,128)} %zone_sums.1.rest_0_), calls=%async_computation | async-start | bytes 65536 | tf_op jit(solution)/shard_map/all_to_all | solution.py:811
  68.8 0.8 corners.5
  69.6 3.5 %collective-permute-start.10 = (f32[3,28,128]{2,1,0:T(8,128)S(1)}, f32[3,28,128]{2,1,0:T(8,128)S(1)}, u32[]{:S(2)}, u32[]{:S(2)}) collective-permute-start(f32[3,28,128]{2,1,0:T(8,128)S(1)} %get-tuple-element.60), channel_id=1, source_target_pairs={{0,1},{1,2},{2,3},{4,5},{5,6},{6,7},{8,9},{9,10},{10,11},{12,13},{... | collective-permute-start | bytes 129032 | tf_op jit(solution)/shard_map/ppermute | solution.py:50
  73.1 1.9 %collective-permute-start.11 = (f32[3,28,128]{2,1,0:T(8,128)S(1)}, f32[3,28,128]{2,1,0:T(8,128)S(1)}, u32[]{:S(2)}, u32[]{:S(2)}) collective-permute-start(f32[3,28,128]{2,1,0:T(8,128)S(1)} %get-tuple-element.61), channel_id=1, source_target_pairs={{1,0},{2,1},{3,2},{5,4},{6,5},{7,6},{9,8},{10,9},{11,10},{13,12},{... | collective-permute-start | bytes 129032 | tf_op jit(solution)/shard_map/ppermute | solution.py:50
  75.1 3.5 %collective-permute-done.11.from_up = f32[3,28,128]{2,1,0:T(8,128)S(1)} collective-permute-done((f32[3,28,128]{2,1,0:T(8,128)S(1)}, f32[3,28,128]{2,1,0:T(8,128)S(1)}, u32[]{:S(2)}, u32[]{:S(2)}) %collective-permute-start.11) | collective-permute-done | bytes 43040 | tf_op jit(solution)/shard_map/ppermute | solution.py:50
  78.5 4.1 %section_zero.1 = (f32[336,128]{1,0:T(8,128)}, f32[8,128]{1,0:T(8,128)S(1)}) custom-call(f32[336,128]{1,0:T(8,128)S(1)} %get-tuple-element.52.base_ref, f32[336,128]{1,0:T(8,128)S(1)} %get-tuple-element.53.lam_ref, f32[336,128]{1,0:T(8,128)S(1)} %get-tuple-element.54.y_ref, f32[96,128]{1,0:T(8,128)S(1)} %copy-done.2, s32[144,128]{1,0:T(8,128)S(1)} %copy-done.4, ...), custom_call_target="tpu_custom_call" | custom-call | tf_op jit(solution)/shard_map/section_zero/pallas_call | solution.py:674
  82.6 0.6 zone_total.1
  (27 shorter events, 0.1 us)
Async XLA Ops:
  0.6 25.0 %copy-start = (bf16[3,1,1,42,1024]{4,3,2,1,0:T(8,128)(2,1)S(1)}, bf16[3,1,1,42,1024]{4,3,2,1,0:T(8,128)(2,1)}, u32[]{:S(2)}) copy-start(bf16[3,1,1,42,1024]{4,3,2,1,0:T(8,128)(2,1)} %x_ref.5) | copy-start | bytes 774148
  3.9 21.8 %copy-start.1 = (f32[1,1,42,1024]{3,1,2,0:T(1,128)S(1)}, f32[1,1,42,1024]{3,1,2,0:T(1,128)}, u32[]{:S(2)}) copy-start(f32[1,1,42,1024]{3,1,2,0:T(1,128)} %param.16) | copy-start | bytes 516100
  3.9 5.7 %collective-permute-start = (f32[3,33,128]{2,1,0:T(8,128)}, f32[3,33,128]{2,1,0:T(8,128)S(1)}, u32[]{:S(2)}, u32[]{:S(2)}) collective-permute-start(f32[3,33,128]{2,1,0:T(8,128)} %get-tuple-element.36), channel_id=1, source_target_pairs={{0,4},{4,8},{8,12},{12,16},{16,20},{20,24},{24,28},{1,5},{5,9},{9,... | collective-permute-start | bytes 152072 | tf_op jit(solution)/shard_map/ppermute | solution.py:50
  8.0 5.2 %collective-permute-start.1 = (f32[3,33,128]{2,1,0:T(8,128)}, f32[3,33,128]{2,1,0:T(8,128)S(1)}, u32[]{:S(2)}, u32[]{:S(2)}) collective-permute-start(f32[3,33,128]{2,1,0:T(8,128)} %get-tuple-element.37), channel_id=1, source_target_pairs={{4,0},{8,4},{12,8},{16,12},{20,16},{24,20},{28,24},{5,1},{9,5},{13... | collective-permute-start | bytes 152072 | tf_op jit(solution)/shard_map/ppermute | solution.py:50
  13.2 0.8 copy-start.7
  14.0 0.8 copy-start.8
  14.8 10.9 %copy-start.2 = (f32[96,128]{1,0:T(8,128)S(1)}, f32[96,128]{1,0:T(8,128)}, u32[]{:S(2)}) copy-start(f32[96,128]{1,0:T(8,128)} %get-tuple-element.34.stat_ref) | copy-start | bytes 147460
  14.8 10.9 %copy-start.9 = (f32[8,8]{1,0:T(8,128)S(1)}, f32[8,8]{1,0:T(8,128)}, u32[]{:S(2)}) copy-start(f32[8,8]{1,0:T(8,128)} %in_ref.5) | copy-start | bytes 772
  14.8 10.9 %copy-start.10 = (f32[8,8]{1,0:T(8,128)S(1)}, f32[8,8]{1,0:T(8,128)}, u32[]{:S(2)}) copy-start(f32[8,8]{1,0:T(8,128)} %out_ref.5) | copy-start | bytes 772
  14.8 10.9 %copy-start.6 = (f32[12,12]{1,0:T(8,128)S(1)}, f32[12,12]{1,0:T(8,128)}, u32[]{:S(2)}) copy-start(f32[12,12]{1,0:T(8,128)} %volume_ref.5) | copy-start | bytes 1732
  14.8 7.2 %collective-permute-start.2 = (f32[3,33,128]{2,1,0:T(8,128)S(1)}, f32[3,33,128]{2,1,0:T(8,128)S(1)}, u32[]{:S(2)}, u32[]{:S(2)}) collective-permute-start(f32[3,33,128]{2,1,0:T(8,128)S(1)} %get-tuple-element.40), channel_id=1, source_target_pairs={{0,1},{1,2},{2,3},{4,5},{5,6},{6,7},{8,9},{9,10},{10,11},{12,13},{... | collective-permute-start | bytes 152072 | tf_op jit(solution)/shard_map/ppermute | solution.py:50
  20.1 5.5 %collective-permute-start.3 = (f32[3,33,128]{2,1,0:T(8,128)S(1)}, f32[3,33,128]{2,1,0:T(8,128)S(1)}, u32[]{:S(2)}, u32[]{:S(2)}) collective-permute-start(f32[3,33,128]{2,1,0:T(8,128)S(1)} %get-tuple-element.41), channel_id=1, source_target_pairs={{1,0},{2,1},{3,2},{5,4},{6,5},{7,6},{9,8},{10,9},{11,10},{13,12},{... | collective-permute-start | bytes 152072 | tf_op jit(solution)/shard_map/ppermute | solution.py:50
  25.7 0.9 %copy-start.3 = (s32[144,128]{1,0:T(8,128)S(1)}, s32[144,128]{1,0:T(8,128)}, u32[]{:S(2)}) copy-start(s32[144,128]{1,0:T(8,128)} %get-tuple-element.35.index_ref) | copy-start | bytes 221188
  26.6 0.9 %copy-start.5 = (f32[440,128]{1,0:T(8,128)S(1)}, f32[440,128]{1,0:T(8,128)}, u32[]{:S(2)}) copy-start(f32[440,128]{1,0:T(8,128)} %get-tuple-element.33.table_ref) | copy-start | bytes 675844
  33.3 5.5 %collective-permute-start.4 = (f32[3,48,128]{2,1,0:T(8,128)S(1)}, f32[3,48,128]{2,1,0:T(8,128)S(1)}, u32[]{:S(2)}, u32[]{:S(2)}) collective-permute-start(f32[3,48,128]{2,1,0:T(8,128)S(1)} %get-tuple-element.46), channel_id=1, source_target_pairs={{0,4},{4,8},{8,12},{12,16},{16,20},{20,24},{24,28},{1,5},{5,9},{9,... | collective-permute-start | bytes 221192 | tf_op jit(solution)/shard_map/ppermute | solution.py:50
  37.4 5.1 %collective-permute-start.5 = (f32[3,48,128]{2,1,0:T(8,128)S(1)}, f32[3,48,128]{2,1,0:T(8,128)S(1)}, u32[]{:S(2)}, u32[]{:S(2)}) collective-permute-start(f32[3,48,128]{2,1,0:T(8,128)S(1)} %get-tuple-element.47), channel_id=1, source_target_pairs={{4,0},{8,4},{12,8},{16,12},{20,16},{24,20},{28,24},{5,1},{9,5},{13... | collective-permute-start | bytes 221192 | tf_op jit(solution)/shard_map/ppermute | solution.py:50
  42.5 9.1 %copy-start.4 = (s32[144,128]{1,0:T(8,128)S(1)}, s32[144,128]{1,0:T(8,128)}, u32[]{:S(2)}) copy-start(s32[144,128]{1,0:T(8,128)} %get-tuple-element.35.index_ref) | copy-start | bytes 221188
  42.5 5.4 %collective-permute-start.6 = (f32[3,48,128]{2,1,0:T(8,128)S(1)}, f32[3,48,128]{2,1,0:T(8,128)S(1)}, u32[]{:S(2)}, u32[]{:S(2)}) collective-permute-start(f32[3,48,128]{2,1,0:T(8,128)S(1)} %get-tuple-element.50), channel_id=1, source_target_pairs={{0,1},{1,2},{2,3},{4,5},{5,6},{6,7},{8,9},{9,10},{10,11},{12,13},{... | collective-permute-start | bytes 221192 | tf_op jit(solution)/shard_map/ppermute | solution.py:50
  45.9 5.7 %collective-permute-start.7 = (f32[3,48,128]{2,1,0:T(8,128)S(1)}, f32[3,48,128]{2,1,0:T(8,128)S(1)}, u32[]{:S(2)}, u32[]{:S(2)}) collective-permute-start(f32[3,48,128]{2,1,0:T(8,128)S(1)} %get-tuple-element.51), channel_id=1, source_target_pairs={{1,0},{2,1},{3,2},{5,4},{6,5},{7,6},{9,8},{10,9},{11,10},{13,12},{... | collective-permute-start | bytes 221192 | tf_op jit(solution)/shard_map/ppermute | solution.py:50
  58.1 10.6 %collective-permute-start.8 = (f32[3,28,128]{2,1,0:T(8,128)S(1)}, f32[3,28,128]{2,1,0:T(8,128)S(1)}, u32[]{:S(2)}, u32[]{:S(2)}) collective-permute-start(f32[3,28,128]{2,1,0:T(8,128)S(1)} %get-tuple-element.55), channel_id=1, source_target_pairs={{0,4},{4,8},{8,12},{12,16},{16,20},{20,24},{24,28},{1,5},{5,9},{9,... | collective-permute-start | bytes 129032 | tf_op jit(solution)/shard_map/ppermute | solution.py:50
  61.3 1.3 %copy-start.11 = (f32[128]{0:T(128)S(1)}, f32[128]{0:T(128)}, u32[]{:S(2)}) copy-start(f32[128]{0:T(128)} %param.23) | copy-start | bytes 1540
  61.3 7.5 %collective-permute-start.9 = (f32[3,28,128]{2,1,0:T(8,128)S(1)}, f32[3,28,128]{2,1,0:T(8,128)S(1)}, u32[]{:S(2)}, u32[]{:S(2)}) collective-permute-start(f32[3,28,128]{2,1,0:T(8,128)S(1)} %get-tuple-element.56), channel_id=1, source_target_pairs={{4,0},{8,4},{12,8},{16,12},{20,16},{24,20},{28,24},{5,1},{9,5},{13... | collective-permute-start | bytes 129032 | tf_op jit(solution)/shard_map/ppermute | solution.py:50
  63.9 18.7 %all-to-all-start = ((f32[32,2,128]{2,1,0:T(2,128)}), f32[32,2,128]{2,1,0:T(2,128)S(1)}, u32[]{:S(2)}, u32[]{:S(2)}) async-start(f32[32,2,128]{2,1,0:T(2,128)} %zone_sums.1.rest_0_), calls=%async_computation | async-start | bytes 65536 | tf_op jit(solution)/shard_map/all_to_all | solution.py:811
  69.6 5.5 %collective-permute-start.10 = (f32[3,28,128]{2,1,0:T(8,128)S(1)}, f32[3,28,128]{2,1,0:T(8,128)S(1)}, u32[]{:S(2)}, u32[]{:S(2)}) collective-permute-start(f32[3,28,128]{2,1,0:T(8,128)S(1)} %get-tuple-element.60), channel_id=1, source_target_pairs={{0,1},{1,2},{2,3},{4,5},{5,6},{6,7},{8,9},{9,10},{10,11},{12,13},{... | collective-permute-start | bytes 129032 | tf_op jit(solution)/shard_map/ppermute | solution.py:50
  73.1 5.4 %collective-permute-start.11 = (f32[3,28,128]{2,1,0:T(8,128)S(1)}, f32[3,28,128]{2,1,0:T(8,128)S(1)}, u32[]{:S(2)}, u32[]{:S(2)}) collective-permute-start(f32[3,28,128]{2,1,0:T(8,128)S(1)} %get-tuple-element.61), channel_id=1, source_target_pairs={{1,0},{2,1},{3,2},{5,4},{6,5},{7,6},{9,8},{10,9},{11,10},{13,12},{... | collective-permute-start | bytes 129032 | tf_op jit(solution)/shard_map/ppermute | solution.py:50

commit v6 on v5

--- a/solution.py
+++ b/solution.py
@@ -30,24 +30,46 @@
 NEAR_VMEM, FAR_VMEM = 32, 60
 OUTER_EDGE, OUTER_ZONE, HALF_SPEED = 0, 3, 6
 FACT_ROWS = 15
-REMOTE_BLOCKS = (
-    (0, 0),
-    (0, 1),
-    (1, 0),
-    (1, 1),
-    (2, 0),
-    (2, 1),
-    (3, 0),
-    (3, 1),
-    (2, 2),
-    (3, 2),
-)
-
-
-def shifted(x, axis, by):
-    peers = lax.axis_size(axis)
-    pairs = [(i, i + by) for i in range(peers) if 0 <= i + by < peers]
-    return lax.ppermute(x, axis, pairs)
+CORNER_LANES = 16
+CORNER_BLOCK = 8
+
+
+def blocks_one(size_x, size_y):
+    return [
+        [(2 * i + u) * size_y + 2 * j + v for u in range(2) for v in range(2)]
+        for i in range(size_x // 2)
+        for j in range(size_y // 2)
+    ]
+
+
+def blocks_two(size_x, size_y):
+    pairs = [(2 * j + 1, (2 * j + 2) % size_y) for j in range(size_y // 2)]
+    blocks = [
+        [(2 * i + 1 + u) * size_y + b for u in range(2) for b in pair]
+        for i in range(size_x // 2 - 1)
+        for pair in pairs
+    ]
+    for a in (0, size_x - 1):
+        for j in range(0, len(pairs), 2):
+            blocks.append([a * size_y + b for pair in pairs[j : j + 2] for b in pair])
+    return blocks
+
+
+def places():
+    a, b = lax.axis_index("gx"), lax.axis_index("gy")
+    size_x, size_y = lax.axis_size("gx"), lax.axis_size("gy")
+    odd_a, odd_b = a % 2, b % 2
+    one = odd_a * 2 + odd_b
+    pair = (b + size_y - 1) % size_y // 2
+    at_end = (a == 0) | (a == size_x - 1)
+    two = jnp.where(at_end, pair % 2, 1 - odd_a) * 2 + 1 - odd_b
+    return one, two, odd_a, odd_b
+
+
+def slots_of(place):
+    base = place - place % 2
+    other = 1 - place % 2
+    return (place + 2) % 4, base + other, (base + 2) % 4 + other
 
 
 def tile(ref, row):
@@ -98,11 +120,37 @@
     )
 
 
-def fill_remote(received, row, lane_index, remote_index, value):
-    for number, (message, block) in enumerate(REMOTE_BLOCKS):
-        got = take(spread(received[message].at[block], row), lane_index)
-        value = jnp.where(remote_index == number, got, value)
-    return value
+def corner_rows(channels):
+    return (channels * CORNER_LANES + LANES - 1) // LANES
+
+
+def message_rows(channels):
+    return channels + corner_rows(channels)
+
+
+class Received:
+    def __init__(self, first, second, channels, corner_ref):
+        one, two, _, _ = places()
+        x1, y1, d11 = slots_of(one)
+        x2, y2, d22 = slots_of(two)
+        self.mains = [(first, x1), (first, y1), (second, x2), (second, y2)]
+        self.corner_ref = corner_ref
+        rows = slice(channels, message_rows(channels))
+        lane = lax.broadcasted_iota(jnp.int32, (corner_rows(channels), LANES), 1) % CORNER_LANES
+        far = jnp.where(lane < 12, second[y2, 0, rows, :], second[x2, 0, rows, :])
+        near = jnp.where(lane < 4, first[d11, 0, rows, :], second[d22, 0, rows, :])
+        corner_ref[0 : corner_rows(channels), :] = jnp.where(lane < 8, near, far)
+
+    def fill(self, row, lane_index, remote_index, value):
+        for number, (ref, slot) in enumerate(self.mains):
+            for half in range(2):
+                got = take(spread(ref.at[slot, half], row), lane_index)
+                value = jnp.where(remote_index == 2 * number + half, got, value)
+        channels_a_row = LANES // CORNER_LANES
+        lane = lane_index + row % channels_a_row * CORNER_LANES
+        line = spread(self.corner_ref, row // channels_a_row)
+        got = take(line, jnp.bitwise_and(lane, LANES - 1))
+        return jnp.where(remote_index == CORNER_BLOCK, got, value)
 
 
 def partner_index(index_ref, f):
@@ -145,14 +193,29 @@
     lax.fori_loop(0, 2 * parts, body, 0)
 
 
-def write_messages(sent_ref, messages):
-    to_right, to_left, to_up, to_down = messages
-    count = to_right.shape[1]
-    for ref, direction in ((to_right, 6), (to_left, 1), (to_up, 4), (to_down, 3)):
-        for block in range(2):
-            ref[block] = sent_ref.at[block][pl.ds(direction, count, stride=SUB), :]
-    for ref, direction in ((to_right, 5), (to_left, 2)):
-        ref[2] = sent_ref.at[0][pl.ds(direction, count, stride=SUB), :]
+def write_messages(sent_ref, channels, first_out, second_out):
+    one, two, _, _ = places()
+    lane = lax.broadcasted_iota(jnp.int32, (SUB, LANES), 1)
+    sub = lax.broadcasted_iota(jnp.int32, (SUB, LANES), 0)
+    packed = []
+    for group in range(corner_rows(channels)):
+        values = sent_ref.at[1][pl.ds(group * SUB * SUB, SUB, stride=SUB), :]
+        moved = pltpu.roll(values, 0, 1, stride=CORNER_LANES, stride_axis=0)
+        own = jnp.where(lane // CORNER_LANES == sub, moved, 0.0)
+        packed.append(jnp.sum(own, axis=0, keepdims=True))
+    x1, y1, d11 = slots_of(one)
+    x2, y2, d22 = slots_of(two)
+    for role, (out, slot) in enumerate(
+        ((first_out, x1), (first_out, y1), (second_out, x2), (second_out, y2))
+    ):
+        for half in range(2):
+            out[slot, half, 0:channels, :] = sent_ref.at[0][
+                pl.ds(role * 2 + half, channels, stride=SUB), :
+            ]
+    for out, slot in ((first_out, x1), (first_out, y1), (first_out, d11), (second_out, d22)):
+        for group, row in enumerate(packed):
+            at = channels + group
+            out[slot, 0, at : at + 1, :] = row
 
 
 def prepare_kernel(
@@ -171,10 +234,8 @@
     table_ref,
     stat_ref,
     index_ref,
-    to_right,
-    to_left,
-    to_up,
-    to_down,
+    first_out,
+    second_out,
     x_tiles,
     sent_ref,
     *fetched,
@@ -218,6 +279,15 @@
     ) = fetched
     rows = cot_ref.shape[0] // SUB
     sections = x_ref.shape[0]
+    _, _, odd_a, odd_b = places()
+    straight = (6 - 5 * odd_a, 4 - odd_b, 1 + 5 * odd_a, 3 + odd_b)
+    right, up = 1 - odd_a, 1 - odd_b
+    corners = (
+        5 * right + 2 * up,
+        7 - 5 * right - 2 * up,
+        5 * right + 2 - 2 * up,
+        5 - 5 * right + 2 * up,
+    )
     face_total = 3 * SUB * LANES
     for f in range(3):
         partner = tile(partner_ref, f)
@@ -225,24 +295,46 @@
         direction = jnp.right_shift(beyond, 8)
         half = jnp.bitwise_and(jnp.right_shift(beyond, 7), 1)
         lane = jnp.bitwise_and(partner, LANES - 1)
-        remote = jnp.where(beyond >= 0, 8, -1)
-        remote = jnp.where((direction == 2) | (direction == 7), 9, remote)
-        for number, first in ((1, 0), (6, 2), (3, 4), (4, 6)):
-            remote = jnp.where(direction == number, first + half, remote)
-        lane = jnp.where((direction == 0) | (direction == 7), jnp.bitwise_and(lane + 4, LANES - 1), lane)
+        remote = jnp.where(beyond >= 0, CORNER_BLOCK, -1)
+        for number, toward in enumerate(straight):
+            remote = jnp.where(direction == toward, 2 * number + half, remote)
+        for number, toward in enumerate(corners):
+            lane = jnp.where(direction == toward, lane % 4 + 4 * number, lane)
         put(index_ref, f, lane)
         put(index_ref, 3 + f, jnp.bitwise_and(jnp.right_shift(partner, 7), SUB - 1))
         put(index_ref, 6 + f, jnp.right_shift(partner, 10))
         put(index_ref, 9 + f, remote)
     sub_iota = lax.broadcasted_iota(jnp.int32, (SUB, LANES), 0)
     lane_iota = lax.broadcasted_iota(jnp.int32, (SUB, LANES), 1)
-    for d in range(2):
-        slots = send_ref[0, 0, :, lanes_of(d)]
-        if d == 0:
-            moved = pltpu.roll(slots, 4, 1)
-            second = (lane_iota >= 4) & (lane_iota < 8)
-            slots = jnp.where(second & (sub_iota == 5), pltpu.roll(moved, 6, 0), slots)
-            slots = jnp.where(second & (sub_iota == 2), pltpu.roll(moved, 2, 0), slots)
+
+    def slots_to(choices, choice, half):
+        rows_of = [
+            jnp.broadcast_to(send_ref[0, 0, n : n + 1, lanes_of(half)], (SUB, LANES))
+            for n in choices
+        ]
+        found = rows_of[0]
+        for n, row in zip(choices[1:], rows_of[1:]):
+            found = jnp.where(choice == n, row, found)
+        return found
+
+    straight_slots = None
+    for number, toward in enumerate(straight):
+        for half in range(2):
+            row = slots_to((1, 6) if number % 2 == 0 else (3, 4), toward, half)
+            straight_slots = (
+                row
+                if straight_slots is None
+                else jnp.where(sub_iota == 2 * number + half, row, straight_slots)
+            )
+    corner_slots = None
+    for number, toward in enumerate(corners):
+        row = slots_to((0, 2, 5, 7), toward, 0)
+        if number == 0:
+            corner_slots = row
+        else:
+            moved = pltpu.roll(row, 4 * number, 1)
+            corner_slots = jnp.where(lane_iota // 4 == number, moved, corner_slots)
+    for d, slots in enumerate((straight_slots, corner_slots)):
         put(index_ref, 12 + d, jnp.bitwise_and(slots, LANES - 1))
         put(index_ref, 14 + d, jnp.bitwise_and(jnp.right_shift(slots, 7), SUB - 1))
         put(index_ref, 16 + d, jnp.right_shift(slots, 10))
@@ -301,15 +393,17 @@
             )
             at += SUB
         sent_ref[d, at : at + SUB, :] = gather_tile(table_ref, rows + 12, lane, sublane)
-    write_messages(sent_ref, (to_right, to_left, to_up, to_down))
-
-
-def corner_kernel(left_ref, right_ref, up_in, down_in, *rest):
-    up_ref, down_ref = rest[-2:]
-    left, right = left_ref[2], right_ref[2]
-    first = lax.broadcasted_iota(jnp.int32, left.shape, 1) < 4
-    up_ref[2] = jnp.where(first, right, left)
-    down_ref[2] = jnp.where(first, left, right)
+    write_messages(sent_ref, comps * 2 + 5, first_out, second_out)
+
+
+def corner_kernel(channels, first_in, second_old, *rest):
+    second_out = rest[-1]
+    one, two, _, _ = places()
+    x1, y1, _ = slots_of(one)
+    x2, y2, _ = slots_of(two)
+    rows = slice(channels, message_rows(channels))
+    second_out[x2, 0, rows, :] = first_in[y1, 0, rows, :]
+    second_out[y2, 0, rows, :] = first_in[x1, 0, rows, :]
 
 
 def outer_states(src, first_comp, comps, first_row, received, index_ref, out_ref):
@@ -322,7 +416,7 @@
             comp = part * width + w
             ends = gather_ends(src, (first_comp + comp) * 3, lane, sublane, face)
             for j in range(2):
-                value = fill_remote(received, first_row + comp * 2 + j, lane, remote, ends[j])
+                value = received.fill(first_row + comp * 2 + j, lane, remote, ends[j])
                 put_at(out_ref, f * comps * 2 + comp * 2 + j, value)
         return carry
 
@@ -444,31 +538,28 @@
     in_ref,
     out_ref,
     volume_ref,
-    from_left,
-    from_right,
-    from_down,
-    from_up,
+    first_in,
+    second_in,
     lam_ref,
     y_ref,
     fact_ref,
     term_ref,
-    to_right,
-    to_left,
-    to_up,
-    to_down,
+    first_out,
+    second_out,
     outer_ref,
     x_tiles,
     sent_ref,
+    corner_ref,
 ):
-    received = (from_left, from_right, from_down, from_up)
     rows = cot_ref.shape[0] // SUB
     comps = rows // 3
+    received = Received(first_in, second_in, comps * 2 + 5, corner_ref)
     outer_states(table_ref, 0, comps, 0, received, index_ref, outer_ref)
     for f in range(3):
         lane, sublane, face, remote = partner_index(index_ref, f)
         for group in range(4):
             value = gather_by_face(table_ref, rows + 3 * group, lane, sublane, face)
-            value = fill_remote(received, comps * 2 + group, lane, remote, value)
+            value = received.fill(comps * 2 + group, lane, remote, value)
             if group == 0:
                 put(fact_ref, OUTER_EDGE + f, value)
             else:
@@ -479,7 +570,7 @@
                     0.5 * jnp.sqrt(1.0 + (0.25 / 8.0) * both),
                 )
         value = gather_tile(table_ref, rows + 12, lane, sublane)
-        put(fact_ref, OUTER_ZONE + f, fill_remote(received, comps * 2 + 4, lane, remote, value))
+        put(fact_ref, OUTER_ZONE + f, received.fill(comps * 2 + 4, lane, remote, value))
     wet_area = tile(stat_ref, WET_AREA)
     half_kappa_area = tile(stat_ref, HALF_KAPPA_AREA)
 
@@ -494,7 +585,7 @@
     x_to_tiles(x_ref, 0, x_tiles)
     send_states(y_ref, 0, comps, 0, index_ref, sent_ref)
     send_states(x_tiles, 4, comps - 4, comps * 2, index_ref, sent_ref)
-    write_messages(sent_ref, (to_right, to_left, to_up, to_down))
+    write_messages(sent_ref, comps * 4 - 8, first_out, second_out)
     x_to_tiles(x_ref, 2, x_tiles)
     weight = TIME_STEP * 2.0 / 3.0
     friction, conduct = own_gradients(2, weight, cot_ref, table_ref, x_tiles, stat_ref)
@@ -516,26 +607,23 @@
     in_ref,
     out_ref,
     volume_ref,
-    from_left,
-    from_right,
-    from_down,
-    from_up,
+    first_in,
+    second_in,
     base_ref,
     next_ref,
     next_y_ref,
     new_term_ref,
-    to_right,
-    to_left,
-    to_up,
-    to_down,
+    first_out,
+    second_out,
     outer_ref,
     x_outer_ref,
     x_tiles,
     sent_ref,
+    corner_ref,
 ):
-    received = (from_left, from_right, from_down, from_up)
     rows = lam_ref.shape[0] // SUB
     comps = rows // 3
+    received = Received(first_in, second_in, comps * 4 - 8, corner_ref)
     outer_states(y_ref, 0, comps, 0, received, index_ref, outer_ref)
     wet_area = tile(stat_ref, WET_AREA)
     half_kappa_area = tile(stat_ref, HALF_KAPPA_AREA)
@@ -551,7 +639,7 @@
         1, lam_ref, y_ref, outer_ref, stat_ref, fact_ref, in_ref, out_ref, volume_ref, emit
     )
     send_states(next_y_ref, 0, comps, 0, index_ref, sent_ref)
-    write_messages(sent_ref, (to_right, to_left, to_up, to_down))
+    write_messages(sent_ref, comps * 2, first_out, second_out)
     x_to_tiles(x_ref, 1, x_tiles)
     weight = TIME_STEP * 0.25
     friction, conduct = own_gradients(1, weight, lam_ref, y_ref, x_tiles, stat_ref)
@@ -625,16 +713,15 @@
     in_ref,
     out_ref,
     volume_ref,
-    from_left,
-    from_right,
-    from_down,
-    from_up,
+    first_in,
+    second_in,
     adjoint_ref,
     last_ref,
     outer_ref,
+    corner_ref,
 ):
-    received = (from_left, from_right, from_down, from_up)
     rows = lam_ref.shape[0] // SUB
+    received = Received(first_in, second_in, rows // 3 * 2, corner_ref)
     outer_states(y_ref, 0, rows // 3, 0, received, index_ref, outer_ref)
 
     def emit(r, value):
@@ -650,21 +737,19 @@
     grads_ref[...] = jnp.sum(zone_ref[...], axis=0)
 
 
-def exchange(messages, *ahead):
-    to_right, to_left, to_up, to_down = messages
-    from_left = shifted(to_right, "gx", 1)
-    from_right = shifted(to_left, "gx", -1)
-    to_up, to_down = call(
-        corner_kernel,
+def exchange(channels, first, second, *ahead):
+    sizes = lax.axis_size("gx"), lax.axis_size("gy")
+    first = lax.all_to_all(first, ("gx", "gy"), 0, 0, axis_index_groups=blocks_one(*sizes))
+    (second,) = call(
+        functools.partial(corner_kernel, channels),
         "corners",
-        [jax.ShapeDtypeStruct(to_up.shape, to_up.dtype)] * 2,
+        [jax.ShapeDtypeStruct(second.shape, second.dtype)],
         [],
-        [from_left, from_right, to_up, to_down, *ahead],
-        aliases={2: 0, 3: 1},
-    )
-    from_down = shifted(to_up, "gy", 1)
-    from_up = shifted(to_down, "gy", -1)
-    return from_left, from_right, from_down, from_up
+        [first, second, *ahead],
+        aliases={1: 0},
+    )
+    second = lax.all_to_all(second, ("gx", "gy"), 0, 0, axis_index_groups=blocks_two(*sizes))
+    return first, second
 
 
 def call(kernel, name, outs, scratch, operands, scalars=(), far=False, aliases={}):
@@ -720,10 +805,12 @@
         return pltpu.VMEM((count * SUB, LANES), dtype)
 
     def messages(count):
-        return [jax.ShapeDtypeStruct((slots // LANES + 1, count, LANES), f32)] * 4
+        return [jax.ShapeDtypeStruct((4, slots // LANES, message_rows(count), LANES), f32)] * 2
 
     def sent_scratch(count):
-        return pltpu.VMEM((slots // LANES, count * SUB, LANES), f32)
+        return pltpu.VMEM((slots // LANES, corner_rows(count) * SUB * SUB, LANES), f32)
+
+    corner_scratch = pltpu.VMEM((SUB, LANES), f32)
 
     square = lambda one: one.reshape(SUB, LANES)
     cot = cotangent.reshape(rows * SUB, LANES)
@@ -764,17 +851,22 @@
         ],
         far=True,
     )
-    received = exchange(to_send)
+    received = exchange(channels + 5, *to_send)
     lam, y, fact, term, *to_send = call(
         second_kernel,
         "section_two",
         [tiles(rows), tiles(rows), tiles(FACT_ROWS), tiles(5)]
         + messages(channels + channels - 8),
-        [tile_scratch(3 * channels), tile_scratch(rows), sent_scratch(2 * channels - 8)],
+        [
+            tile_scratch(3 * channels),
+            tile_scratch(rows),
+            sent_scratch(2 * channels - 8),
+            corner_scratch,
+        ],
         [cot, table, stat, index, section_states, flux_in, flux_out, volume_matrix, *received],
         (5, 6, 7),
     )
-    received = exchange(to_send)
+    received = exchange(channels + channels - 8, *to_send)
     base, lam, y, term, *to_send = call(
         first_kernel,
         "section_one",
@@ -784,6 +876,7 @@
             tile_scratch(3 * (channels - 8)),
             tile_scratch(rows),
             sent_scratch(channels),
+            corner_scratch,
         ],
         [
             cot,
@@ -809,12 +902,12 @@
         [term, stat, fact, zone_conductivity.reshape(1, zones)],
     )
     all_terms = lax.all_to_all(zone_terms, ("gx", "gy"), 0, 0)
-    received = exchange(to_send, zone_terms)
+    received = exchange(channels, *to_send, zone_terms)
     adjoint, last = call(
         last_kernel,
         "section_zero",
         [tiles(rows), tiles(1)],
-        [tile_scratch(3 * channels)],
+        [tile_scratch(3 * channels), corner_scratch],
         [
             base,
             lam,

time: 84 us -> 84.3 us (level)
  blocking collectives: 0 us -> 39.3 us
  starting transfers between devices: 38 us -> 11.3 us
  waiting for transfers between devices: 18.5 us -> 4.42 us
  Pallas kernels: 22.4 us -> 23.7 us
    all_to_all x0 -> x5, blocking collectives: none -> 39.3 us  [the longest x3 21.2 us: exchange(): lax.all_to_all(second, ('gx', 'gy'), 0, 0, axis_index_groups=blocks_two(*...]
    ppermute x12 -> x0, starting transfers between devices: 33.1 us -> none  [shifted(): return lax.ppermute(x, axis, pairs)]
    ppermute x12 -> x0, waiting for transfers between devices: 18.5 us -> none  [shifted(): return lax.ppermute(x, axis, pairs)]
    all_to_all x0 -> x1, starting transfers between devices: none -> 5.49 us  [exchange(): lax.all_to_all(first, ('gx', 'gy'), 0, 0, axis_index_groups=blocks_one(*s...]
    all_to_all x1, waiting for transfers between devices: 0.01 us -> 2.81 us  [local(): all_terms = lax.all_to_all(zone_terms, ('gx', 'gy'), 0, 0)]
    all_to_all x0 -> x1, waiting for transfers between devices: none -> 1.61 us  [exchange(): lax.all_to_all(first, ('gx', 'gy'), 0, 0, axis_index_groups=blocks_one(*s...]
    pallas_call x9, Pallas kernels: 22.4 us -> 23.7 us  [call(): pl.pallas_call(kernel, in_specs=[in_place if far else in_scalar if n in s...]
    pallas_call x0 -> x4, local copies, waits for them, and re-layouts: none -> 1.31 us  [call(): pl.pallas_call(kernel, in_specs=[in_place if far else in_scalar if n in s...]
  transfers between devices with their start and end apart: 13 -> 2, of which waited for: 7 -> 2; matrix products, arithmetic and copies ran while one was open for 0% -> 0% of each run, Pallas kernels for 8% -> 7%
where the time goes in v6:
time: 84.3 us; the launch traced here: 83.4 us
  blocking collectives  39.3 us (47%)
  Pallas kernels  23.7 us (28%)
  starting transfers between devices  11.3 us (13%)
  waiting for transfers between devices  4.42 us (5%)
  local copies, waits for them, and re-layouts  3.87 us (5%)
    pallas_call x9, Pallas kernels, call(): pl.pallas_call(kernel, in_specs=[in_place if far else in_scalar if n in s...  23.7 us
    all_to_all x3, blocking collectives, exchange(): lax.all_to_all(second, ('gx', 'gy'), 0, 0, axis_index_groups=blocks_two(*...  21.2 us
    all_to_all x2, blocking collectives, exchange(): lax.all_to_all(first, ('gx', 'gy'), 0, 0, axis_index_groups=blocks_one(*s...  18.1 us
    all_to_all x1, starting transfers between devices, local(): all_terms = lax.all_to_all(zone_terms, ('gx', 'gy'), 0, 0)  5.77 us
    all_to_all x1, starting transfers between devices, exchange(): lax.all_to_all(first, ('gx', 'gy'), 0, 0, axis_index_groups=blocks_one(*s...  5.49 us
    all_to_all x1, waiting for transfers between devices, local(): all_terms = lax.all_to_all(zone_terms, ('gx', 'gy'), 0, 0)  2.81 us
    unnamed x20, local copies, waits for them, and re-layouts  2.5 us
  transfers between devices with their start and end apart: 2, of which 2 were waited for; matrix products, arithmetic and copies ran while one was open for 0% of the time, Pallas kernels for 7%

profile of v6, /device:TPU:1, one launch (start us, length us, event | category | flops | bytes accessed | tf_op | source)
XLA Modules:
  0.0 83.4 jit_solution(16937823874363491285)
XLA Ops:
  0.6 3.3 %prepare.1 = (f32[440,128]{1,0:T(8,128)}, f32[96,128]{1,0:T(8,128)}, s32[144,128]{1,0:T(8,128)}, f32[4,2,38,128]{3,2,1,0:T(8,128)}, f32[4,2,38,128]{3,2,1,0:T(8,128)}) custom-call(f32[336,128]{1,0:T(8,128)} %bitcast.11, bf16[3,1,1,42,1024]{4,3,2,1,0:T(8,128)(2,1)} %x_ref.5, f32[8,128]{1,0:T(8,128)} %bitcast.18, f32[24,128]{1,0:T(8,128)} %bitcast.16, ...), custom_call_target="tpu_custom_call" | custom-call | tf_op jit(solution)/shard_map/prepare/pallas_call | solution.py:759
  4.0 1.0 %copy.22 = f32[4,2,38,128]{3,1,2,0:T(2,128)S(1)} copy(f32[4,2,38,128]{3,2,1,0:T(8,128)} %get-tuple-element.24) | data formatting | bytes 311296 | tf_op jit(solution)/shard_map/prepare/pallas_call | solution.py:759
  5.0 8.4 %all_to_all.35 = f32[4,2,38,128]{3,1,2,0:T(2,128)S(1)} all-to-all(f32[4,2,38,128]{3,1,2,0:T(2,128)S(1)} %copy.22), channel_id=1, replica_groups={{0,1,4,5},{2,3,6,7},{8,9,12,13},{10,11,14,15},{16,17,20,21},{18,19,22,2..., dimensions={0} | all-to-all | bytes 311296 | tf_op jit(solution)/shard_map/all_to_all | solution.py:742
  13.4 0.9 %copy-done.4 = f32[4,2,38,128]{3,2,1,0:T(8,128)S(1)} copy-done((f32[4,2,38,128]{3,2,1,0:T(8,128)S(1)}, f32[4,2,38,128]{3,2,1,0:T(8,128)}, u32[]{:S(2)}) %copy-start.4) | copy-done | bytes 155672
  14.3 0.1 copy.24
  14.4 0.0 copy-start
  14.4 7.3 %all_to_all.36 = f32[4,2,38,128]{3,1,2,0:T(2,128)S(1)} all-to-all(f32[4,2,38,128]{3,1,2,0:T(2,128)S(1)} %copy.24), channel_id=1, replica_groups={{5,6,9,10},{7,4,11,8},{13,14,17,18},{15,12,19,16},{21,22,25,26},{23,20,..., dimensions={0} | all-to-all | bytes 311296 | tf_op jit(solution)/shard_map/all_to_all | solution.py:751
  21.8 0.0 copy-start.8
  21.8 0.0 copy-start.7
  21.8 0.0 copy-done.5
  21.8 0.0 copy-done
  21.8 0.8 %copy-done.1 = f32[1,1,42,1024]{3,1,2,0:T(1,128)S(1)} copy-done((f32[1,1,42,1024]{3,1,2,0:T(1,128)S(1)}, f32[1,1,42,1024]{3,1,2,0:T(1,128)}, u32[]{:S(2)}) %copy-start.1) | copy-done | bytes 172056
  22.7 0.0 copy-done.2
  22.7 0.1 copy-done.3
  22.7 0.0 copy-done.6
  22.7 0.0 copy-done.8
  22.8 6.0 %section_two.1 = (f32[336,128]{1,0:T(8,128)S(1)}, f32[336,128]{1,0:T(8,128)S(1)}, f32[120,128]{1,0:T(8,128)S(1)}, f32[40,128]{1,0:T(8,128)S(1)}, f32[4,2,54,128]...) custom-call(f32[336,128]{1,0:T(8,128)S(1)} %bitcast.12, f32[440,128]{1,0:T(8,128)S(1)} %copy-done.5, ...), custom_call_target="tpu_custom_call" | custom-call | tf_op jit(solution)/shard_map/section_two/pallas_call | solution.py:759
  28.7 0.1 copy.27
  28.9 9.7 %all_to_all.37 = f32[4,2,54,128]{3,1,2,0:T(2,128)S(1)} all-to-all(f32[4,2,54,128]{3,1,2,0:T(2,128)S(1)} %copy.27), channel_id=1, replica_groups={{0,1,4,5},{2,3,6,7},{8,9,12,13},{10,11,14,15},{16,17,20,21},{18,19,22,2..., dimensions={0} | all-to-all | bytes 442368 | tf_op jit(solution)/shard_map/all_to_all | solution.py:742
  38.6 0.1 copy.29
  38.7 7.6 %all_to_all.38 = f32[4,2,54,128]{3,1,2,0:T(2,128)S(1)} all-to-all(f32[4,2,54,128]{3,1,2,0:T(2,128)S(1)} %copy.29), channel_id=1, replica_groups={{5,6,9,10},{7,4,11,8},{13,14,17,18},{15,12,19,16},{21,22,25,26},{23,20,..., dimensions={0} | all-to-all | bytes 442368 | tf_op jit(solution)/shard_map/all_to_all | solution.py:751
  46.3 7.4 %section_one.1 = (f32[336,128]{1,0:T(8,128)S(1)}, f32[336,128]{1,0:T(8,128)S(1)}, f32[336,128]{1,0:T(8,128)S(1)}, f32[40,128]{1,0:T(8,128)S(1)}, f32[4,2,32,128]...) custom-call(f32[336,128]{1,0:T(8,128)S(1)} %bitcast.13, f32[336,128]{1,0:T(8,128)S(1)} %get-tuple-element.26.lam_ref, ...), custom_call_target="tpu_custom_call" | custom-call | tf_op jit(solution)/shard_map/section_one/pallas_call | solution.py:759
  53.7 5.5 %all-to-all-start.4 = ((f32[4,2,32,128]{3,2,1,0:T(8,128)}), f32[4,2,32,128]{3,2,1,0:T(8,128)S(1)}, u32[]{:S(2)}, u32[]{:S(2)}) async-start(f32[4,2,32,128]{3,2,1,0:T(8,128)} %get-tuple-element.35), calls=%async_computation.4 | async-start | bytes 262144 | tf_op jit(solution)/shard_map/all_to_all | solution.py:742
  59.2 0.7 copy-done.9
  59.9 1.3 %zone_sums.1.rest_0_ = f32[32,2,128]{2,1,0:T(2,128)} custom-call(f32[40,128]{1,0:T(8,128)S(1)} %get-tuple-element.37.term_ref, f32[96,128]{1,0:T(8,128)S(1)} %copy-done.2, f32[120,128]{1,0:T(8,128)S(1)} %get-tuple-element.28.fact_ref, f32[1,128]{1,0:T(1,128)S(1)} %bitcast.15), custom_call_target="tpu_custom_call" | custom-call | tf_op jit(solution)/shard_map/zone_sums/pallas_call | solution.py:759
  61.2 1.6 %all-to-all-done.4.first_in = f32[4,2,32,128]{3,2,1,0:T(8,128)S(1)} async-done(((f32[4,2,32,128]{3,2,1,0:T(8,128)}), f32[4,2,32,128]{3,2,1,0:T(8,128)S(1)}, u32[]{:S(2)}, u32[]{:S(2)}) %all-to-all-start.4) | async-done | bytes 131104 | tf_op jit(solution)/shard_map/all_to_all | solution.py:742
  62.8 0.8 corners.5
  63.6 6.3 %all_to_all.39.second_in = f32[4,2,32,128]{3,2,1,0:T(8,128)S(1)} all-to-all(f32[4,2,32,128]{3,2,1,0:T(8,128)S(1)} %corners.5), channel_id=1, replica_groups={{5,6,9,10},{7,4,11,8},{13,14,17,18},{15,12,19,16},{21,22,25,26},{23,20,..., dimensions={0} | all-to-all | bytes 262144 | tf_op jit(solution)/shard_map/all_to_all | solution.py:751
  69.9 5.8 %all-to-all-start.6 = ((f32[32,2,128]{2,1,0:T(2,128)}), f32[32,2,128]{2,1,0:T(2,128)S(1)}, u32[]{:S(2)}, u32[]{:S(2)}) async-start(f32[32,2,128]{2,1,0:T(2,128)} %zone_sums.1.rest_0_), calls=%async_computation.6 | async-start | bytes 65536 | tf_op jit(solution)/shard_map/all_to_all | solution.py:904
  75.7 4.3 %section_zero.1 = (f32[336,128]{1,0:T(8,128)}, f32[8,128]{1,0:T(8,128)S(1)}) custom-call(f32[336,128]{1,0:T(8,128)S(1)} %get-tuple-element.32.base_ref, f32[336,128]{1,0:T(8,128)S(1)} %get-tuple-element.33.lam_ref, f32[336,128]{1,0:T(8,128)S(1)} %get-tuple-element.34.y_ref, f32[96,128]{1,0:T(8,128)S(1)} %copy-done.2, s32[144,128]{1,0:T(8,128)S(1)} %copy-done.3, ...), custom_call_target="tpu_custom_call" | custom-call | tf_op jit(solution)/shard_map/section_zero/pallas_call | solution.py:759
  80.0 2.8 %all-to-all-done.6.zone_ref = f32[32,2,128]{2,1,0:T(2,128)S(1)} async-done(((f32[32,2,128]{2,1,0:T(2,128)}), f32[32,2,128]{2,1,0:T(2,128)S(1)}, u32[]{:S(2)}, u32[]{:S(2)}) %all-to-all-start.6) | async-done | bytes 32800 | tf_op jit(solution)/shard_map/all_to_all | solution.py:904
  82.8 0.6 zone_total.1
  (14 shorter events, 0.1 us)
Async XLA Ops:
  13.4 0.9 %copy-start.4 = (f32[4,2,38,128]{3,2,1,0:T(8,128)S(1)}, f32[4,2,38,128]{3,2,1,0:T(8,128)}, u32[]{:S(2)}) copy-start(f32[4,2,38,128]{3,2,1,0:T(8,128)} %get-tuple-element.25.second_old) | copy-start | bytes 466948
  14.3 7.5 %copy-start.5 = (f32[440,128]{1,0:T(8,128)S(1)}, f32[440,128]{1,0:T(8,128)}, u32[]{:S(2)}) copy-start(f32[440,128]{1,0:T(8,128)} %get-tuple-element.21.table_ref) | copy-start | bytes 675844
  14.4 7.4 %copy-start = (bf16[3,1,1,42,1024]{4,3,2,1,0:T(8,128)(2,1)S(1)}, bf16[3,1,1,42,1024]{4,3,2,1,0:T(8,128)(2,1)}, u32[]{:S(2)}) copy-start(bf16[3,1,1,42,1024]{4,3,2,1,0:T(8,128)(2,1)} %x_ref.5) | copy-start | bytes 774148
  21.8 0.9 %copy-start.1 = (f32[1,1,42,1024]{3,1,2,0:T(1,128)S(1)}, f32[1,1,42,1024]{3,1,2,0:T(1,128)}, u32[]{:S(2)}) copy-start(f32[1,1,42,1024]{3,1,2,0:T(1,128)} %param.16) | copy-start | bytes 516100
  21.8 0.9 %copy-start.2 = (f32[96,128]{1,0:T(8,128)S(1)}, f32[96,128]{1,0:T(8,128)}, u32[]{:S(2)}) copy-start(f32[96,128]{1,0:T(8,128)} %get-tuple-element.22.stat_ref) | copy-start | bytes 147460
  21.8 1.0 %copy-start.3 = (s32[144,128]{1,0:T(8,128)S(1)}, s32[144,128]{1,0:T(8,128)}, u32[]{:S(2)}) copy-start(s32[144,128]{1,0:T(8,128)} %get-tuple-element.23.index_ref) | copy-start | bytes 221188
  21.8 1.0 %copy-start.6 = (f32[12,12]{1,0:T(8,128)S(1)}, f32[12,12]{1,0:T(8,128)}, u32[]{:S(2)}) copy-start(f32[12,12]{1,0:T(8,128)} %volume_ref.5) | copy-start | bytes 1732
  21.8 1.0 %copy-start.8 = (f32[8,8]{1,0:T(8,128)S(1)}, f32[8,8]{1,0:T(8,128)}, u32[]{:S(2)}) copy-start(f32[8,8]{1,0:T(8,128)} %out_ref.5) | copy-start | bytes 772
  21.8 1.0 %copy-start.7 = (f32[8,8]{1,0:T(8,128)S(1)}, f32[8,8]{1,0:T(8,128)}, u32[]{:S(2)}) copy-start(f32[8,8]{1,0:T(8,128)} %in_ref.5) | copy-start | bytes 772
  53.7 9.1 %all-to-all-start.4 = ((f32[4,2,32,128]{3,2,1,0:T(8,128)}), f32[4,2,32,128]{3,2,1,0:T(8,128)S(1)}, u32[]{:S(2)}, u32[]{:S(2)}) async-start(f32[4,2,32,128]{3,2,1,0:T(8,128)} %get-tuple-element.35), calls=%async_computation.4 | async-start | bytes 262144 | tf_op jit(solution)/shard_map/all_to_all | solution.py:742
  59.2 0.7 copy-start.9
  69.9 12.9 %all-to-all-start.6 = ((f32[32,2,128]{2,1,0:T(2,128)}), f32[32,2,128]{2,1,0:T(2,128)S(1)}, u32[]{:S(2)}, u32[]{:S(2)}) async-start(f32[32,2,128]{2,1,0:T(2,128)} %zone_sums.1.rest_0_), calls=%async_computation.6 | async-start | bytes 65536 | tf_op jit(solution)/shard_map/all_to_all | solution.py:904

commit v7 on v6

--- a/solution.py
+++ b/solution.py
@@ -30,46 +30,15 @@
 NEAR_VMEM, FAR_VMEM = 32, 60
 OUTER_EDGE, OUTER_ZONE, HALF_SPEED = 0, 3, 6
 FACT_ROWS = 15
+X_ROWS = 24
 CORNER_LANES = 16
 CORNER_BLOCK = 8
 
 
-def blocks_one(size_x, size_y):
-    return [
-        [(2 * i + u) * size_y + 2 * j + v for u in range(2) for v in range(2)]
-        for i in range(size_x // 2)
-        for j in range(size_y // 2)
-    ]
-
-
-def blocks_two(size_x, size_y):
-    pairs = [(2 * j + 1, (2 * j + 2) % size_y) for j in range(size_y // 2)]
-    blocks = [
-        [(2 * i + 1 + u) * size_y + b for u in range(2) for b in pair]
-        for i in range(size_x // 2 - 1)
-        for pair in pairs
-    ]
-    for a in (0, size_x - 1):
-        for j in range(0, len(pairs), 2):
-            blocks.append([a * size_y + b for pair in pairs[j : j + 2] for b in pair])
-    return blocks
-
-
-def places():
-    a, b = lax.axis_index("gx"), lax.axis_index("gy")
-    size_x, size_y = lax.axis_size("gx"), lax.axis_size("gy")
-    odd_a, odd_b = a % 2, b % 2
-    one = odd_a * 2 + odd_b
-    pair = (b + size_y - 1) % size_y // 2
-    at_end = (a == 0) | (a == size_x - 1)
-    two = jnp.where(at_end, pair % 2, 1 - odd_a) * 2 + 1 - odd_b
-    return one, two, odd_a, odd_b
-
-
-def slots_of(place):
-    base = place - place % 2
-    other = 1 - place % 2
-    return (place + 2) % 4, base + other, (base + 2) % 4 + other
+def swapped(x, axis, first):
+    peers = lax.axis_size(axis)
+    lows = range(first, peers - 1, 2)
+    return lax.ppermute(x, axis, [(i, i + 1) for i in lows] + [(i + 1, i) for i in lows])
 
 
 def tile(ref, row):
@@ -128,23 +97,26 @@
     return channels + corner_rows(channels)
 
 
+def corner_lane(shape):
+    return lax.broadcasted_iota(jnp.int32, shape, 1) % CORNER_LANES
+
+
 class Received:
-    def __init__(self, first, second, channels, corner_ref):
-        one, two, _, _ = places()
-        x1, y1, d11 = slots_of(one)
-        x2, y2, d22 = slots_of(two)
-        self.mains = [(first, x1), (first, y1), (second, x2), (second, y2)]
+    def __init__(self, messages, channels, corner_ref):
+        _, _, y1, y2 = messages
+        self.mains = messages
         self.corner_ref = corner_ref
         rows = slice(channels, message_rows(channels))
-        lane = lax.broadcasted_iota(jnp.int32, (corner_rows(channels), LANES), 1) % CORNER_LANES
-        far = jnp.where(lane < 12, second[y2, 0, rows, :], second[x2, 0, rows, :])
-        near = jnp.where(lane < 4, first[d11, 0, rows, :], second[d22, 0, rows, :])
-        corner_ref[0 : corner_rows(channels), :] = jnp.where(lane < 8, near, far)
+        count = corner_rows(channels)
+        lane = corner_lane((count, LANES))
+        corner_ref[0:count, :] = jnp.where(
+            jnp.bitwise_and(lane, 4) == 0, y1[0, rows, :], y2[0, rows, :]
+        )
 
     def fill(self, row, lane_index, remote_index, value):
-        for number, (ref, slot) in enumerate(self.mains):
+        for number, ref in enumerate(self.mains):
             for half in range(2):
-                got = take(spread(ref.at[slot, half], row), lane_index)
+                got = take(spread(ref.at[half], row), lane_index)
                 value = jnp.where(remote_index == 2 * number + half, got, value)
         channels_a_row = LANES // CORNER_LANES
         lane = lane_index + row % channels_a_row * CORNER_LANES
@@ -164,11 +136,6 @@
 INDEX_ROWS = 18
 
 
-def turns(comps):
-    width = 7 if comps % 7 == 0 else 5
-    return width, comps // width
-
-
 def tile_at(ref, row):
     return ref[pl.ds(pl.multiple_of(row * SUB, SUB), SUB), :]
 
@@ -177,45 +144,34 @@
     ref[pl.ds(pl.multiple_of(row * SUB, SUB), SUB), :] = value
 
 
-def send_states(src, first_comp, comps, first_row, index_ref, sent_ref):
-    width, parts = turns(comps)
-
-    def body(step, carry):
-        d, part = step // parts, step % parts
+def send_states(src, first_comp, comps, index_ref, sent_ref):
+    def body(d, carry):
         lane, sublane, face = [tile_at(index_ref, 12 + n * 2 + d) for n in range(3)]
-        for w in range(width):
-            comp = part * width + w
+        for comp in range(comps):
             ends = gather_ends(src, (first_comp + comp) * 3, lane, sublane, face)
             for j in range(2):
-                put_at(sent_ref.at[d], first_row + comp * 2 + j, ends[j])
+                put(sent_ref.at[d], comp * 2 + j, ends[j])
         return carry
 
-    lax.fori_loop(0, 2 * parts, body, 0)
-
-
-def write_messages(sent_ref, channels, first_out, second_out):
-    one, two, _, _ = places()
+    lax.fori_loop(0, 2, body, 0)
+
+
+def write_messages(sent_ref, first, channels, outs, total):
     lane = lax.broadcasted_iota(jnp.int32, (SUB, LANES), 1)
     sub = lax.broadcasted_iota(jnp.int32, (SUB, LANES), 0)
-    packed = []
+    for role, out in enumerate(outs):
+        for half in range(2):
+            out[half, first : first + channels, :] = sent_ref.at[0][
+                pl.ds(role * 2 + half, channels, stride=SUB), :
+            ]
     for group in range(corner_rows(channels)):
         values = sent_ref.at[1][pl.ds(group * SUB * SUB, SUB, stride=SUB), :]
         moved = pltpu.roll(values, 0, 1, stride=CORNER_LANES, stride_axis=0)
         own = jnp.where(lane // CORNER_LANES == sub, moved, 0.0)
-        packed.append(jnp.sum(own, axis=0, keepdims=True))
-    x1, y1, d11 = slots_of(one)
-    x2, y2, d22 = slots_of(two)
-    for role, (out, slot) in enumerate(
-        ((first_out, x1), (first_out, y1), (second_out, x2), (second_out, y2))
-    ):
-        for half in range(2):
-            out[slot, half, 0:channels, :] = sent_ref.at[0][
-                pl.ds(role * 2 + half, channels, stride=SUB), :
-            ]
-    for out, slot in ((first_out, x1), (first_out, y1), (first_out, d11), (second_out, d22)):
-        for group, row in enumerate(packed):
-            at = channels + group
-            out[slot, 0, at : at + 1, :] = row
+        row = jnp.sum(own, axis=0, keepdims=True)
+        at = total + first // SUB + group
+        for out in outs[:2]:
+            out[0, at : at + 1, :] = row
 
 
 def prepare_kernel(
@@ -234,8 +190,10 @@
     table_ref,
     stat_ref,
     index_ref,
-    first_out,
-    second_out,
+    to_x1,
+    to_x2,
+    to_y1,
+    to_y2,
     x_tiles,
     sent_ref,
     *fetched,
@@ -279,14 +237,14 @@
     ) = fetched
     rows = cot_ref.shape[0] // SUB
     sections = x_ref.shape[0]
-    _, _, odd_a, odd_b = places()
-    straight = (6 - 5 * odd_a, 4 - odd_b, 1 + 5 * odd_a, 3 + odd_b)
+    odd_a, odd_b = lax.axis_index("gx") % 2, lax.axis_index("gy") % 2
+    straight = (6 - 5 * odd_a, 1 + 5 * odd_a, 4 - odd_b, 3 + odd_b)
     right, up = 1 - odd_a, 1 - odd_b
     corners = (
         5 * right + 2 * up,
-        7 - 5 * right - 2 * up,
         5 * right + 2 - 2 * up,
         5 - 5 * right + 2 * up,
+        7 - 5 * right - 2 * up,
     )
     face_total = 3 * SUB * LANES
     for f in range(3):
@@ -320,7 +278,7 @@
     straight_slots = None
     for number, toward in enumerate(straight):
         for half in range(2):
-            row = slots_to((1, 6) if number % 2 == 0 else (3, 4), toward, half)
+            row = slots_to((1, 6) if number < 2 else (3, 4), toward, half)
             straight_slots = (
                 row
                 if straight_slots is None
@@ -383,7 +341,7 @@
     for r in range(rows):
         put(table_ref, r, tile(cot_ref, r) * (wet_area if r < 12 else half_kappa_area))
     comps = rows // 3
-    send_states(table_ref, 0, comps, 0, index_ref, sent_ref)
+    send_states(table_ref, 0, comps, index_ref, sent_ref)
     for d in range(2):
         lane, sublane, face = sent_index(index_ref, d)
         at = comps * 2 * SUB
@@ -393,34 +351,42 @@
             )
             at += SUB
         sent_ref[d, at : at + SUB, :] = gather_tile(table_ref, rows + 12, lane, sublane)
-    write_messages(sent_ref, comps * 2 + 5, first_out, second_out)
-
-
-def corner_kernel(channels, first_in, second_old, *rest):
-    second_out = rest[-1]
-    one, two, _, _ = places()
-    x1, y1, _ = slots_of(one)
-    x2, y2, _ = slots_of(two)
+    channels = comps * 2 + 5
+    write_messages(sent_ref, 0, channels, (to_x1, to_x2, to_y1, to_y2), channels)
+
+
+def corner_kernel(channels, x1, x2, old_y1, old_y2, *rest):
+    y1, y2 = rest[-2:]
     rows = slice(channels, message_rows(channels))
-    second_out[x2, 0, rows, :] = first_in[y1, 0, rows, :]
-    second_out[y2, 0, rows, :] = first_in[x1, 0, rows, :]
-
-
-def outer_states(src, first_comp, comps, first_row, received, index_ref, out_ref):
-    width, parts = turns(comps)
-
-    def body(step, carry):
-        f, part = step // parts, step % parts
-        lane, sublane, face, remote = [tile_at(index_ref, n * 3 + f) for n in range(4)]
-        for w in range(width):
-            comp = part * width + w
+    lane = corner_lane((corner_rows(channels), LANES))
+    merged = jnp.where(lane < 8, x1[0, rows, :], x2[0, rows, :])
+    y1[0, rows, :] = merged
+    y2[0, rows, :] = merged
+
+
+def local_states(src, first_comp, comps, index_ref, out_ref):
+    def body(f, carry):
+        lane, sublane, face = [tile_at(index_ref, n * 3 + f) for n in range(3)]
+        for comp in range(comps):
             ends = gather_ends(src, (first_comp + comp) * 3, lane, sublane, face)
             for j in range(2):
-                value = received.fill(first_row + comp * 2 + j, lane, remote, ends[j])
-                put_at(out_ref, f * comps * 2 + comp * 2 + j, value)
+                put_at(out_ref, f * comps * 2 + comp * 2 + j, ends[j])
         return carry
 
-    lax.fori_loop(0, 3 * parts, body, 0)
+    lax.fori_loop(0, 3, body, 0)
+
+
+def remote_states(received, first_row, channels, index_ref, local_ref, out_ref):
+    def body(f, carry):
+        lane, remote = tile_at(index_ref, f), tile_at(index_ref, 9 + f)
+        for ch in range(channels):
+            value = tile_at(local_ref, f * channels + ch)
+            put_at(
+                out_ref, f * channels + ch, received.fill(first_row + ch, lane, remote, value)
+            )
+        return carry
+
+    lax.fori_loop(0, 3, body, 0)
 
 
 def transposed_section(
@@ -529,39 +495,71 @@
     )
 
 
+def local_two_kernel(
+    cot_ref, table_ref, stat_ref, index_ref, x_ref, outer_ref, near_ref, term_ref, x_tiles
+):
+    rows = cot_ref.shape[0] // SUB
+    local_states(table_ref, 0, rows // 3, index_ref, outer_ref)
+    for f in range(3):
+        lane, sublane, face = [tile(index_ref, n * 3 + f) for n in range(3)]
+        for group in range(4):
+            value = gather_by_face(table_ref, rows + 3 * group, lane, sublane, face)
+            put(near_ref, f * 5 + group, value)
+        put(near_ref, f * 5 + 4, gather_tile(table_ref, rows + 12, lane, sublane))
+    x_to_tiles(x_ref, 2, x_tiles)
+    friction, conduct = own_gradients(
+        2, TIME_STEP * 2.0 / 3.0, cot_ref, table_ref, x_tiles, stat_ref
+    )
+    put(term_ref, 0, friction)
+    put(term_ref, 1, conduct)
+
+
+def local_x_kernel(index_ref, x_ref, x_outer_ref, sent_ref, x_tiles):
+    comps = x_ref.shape[3] // 3
+    x_to_tiles(x_ref, 0, x_tiles)
+    local_states(x_tiles, 4, comps - 4, index_ref, x_outer_ref)
+    send_states(x_tiles, 4, comps - 4, index_ref, sent_ref)
+
+
 def second_kernel(
     cot_ref,
     table_ref,
     stat_ref,
     index_ref,
-    x_ref,
+    near_outer_ref,
+    near_ref,
+    x_sent_ref,
     in_ref,
     out_ref,
     volume_ref,
-    first_in,
-    second_in,
+    from_x1,
+    from_x2,
+    from_y1,
+    from_y2,
     lam_ref,
     y_ref,
     fact_ref,
-    term_ref,
-    first_out,
-    second_out,
     outer_ref,
-    x_tiles,
+    to_x1,
+    to_x2,
+    to_y1,
+    to_y2,
     sent_ref,
     corner_ref,
 ):
     rows = cot_ref.shape[0] // SUB
     comps = rows // 3
-    received = Received(first_in, second_in, comps * 2 + 5, corner_ref)
-    outer_states(table_ref, 0, comps, 0, received, index_ref, outer_ref)
+    channels = comps * 2
+    received = Received((from_x1, from_x2, from_y1, from_y2), channels + 5, corner_ref)
+    remote_states(received, 0, channels, index_ref, near_outer_ref, outer_ref)
     for f in range(3):
-        lane, sublane, face, remote = partner_index(index_ref, f)
-        for group in range(4):
-            value = gather_by_face(table_ref, rows + 3 * group, lane, sublane, face)
-            value = received.fill(comps * 2 + group, lane, remote, value)
+        lane, remote = tile(index_ref, f), tile(index_ref, 9 + f)
+        for group in range(5):
+            value = received.fill(channels + group, lane, remote, tile(near_ref, f * 5 + group))
             if group == 0:
                 put(fact_ref, OUTER_EDGE + f, value)
+            elif group == 4:
+                put(fact_ref, OUTER_ZONE + f, value)
             else:
                 both = tile(table_ref, rows + 3 * group + f) + value
                 put(
@@ -569,8 +567,6 @@
                     HALF_SPEED + 3 * (group - 1) + f,
                     0.5 * jnp.sqrt(1.0 + (0.25 / 8.0) * both),
                 )
-        value = gather_tile(table_ref, rows + 12, lane, sublane)
-        put(fact_ref, OUTER_ZONE + f, received.fill(comps * 2 + 4, lane, remote, value))
     wet_area = tile(stat_ref, WET_AREA)
     half_kappa_area = tile(stat_ref, HALF_KAPPA_AREA)
 
@@ -582,17 +578,34 @@
     transposed_section(
         2, cot_ref, table_ref, outer_ref, stat_ref, fact_ref, in_ref, out_ref, volume_ref, emit
     )
-    x_to_tiles(x_ref, 0, x_tiles)
-    send_states(y_ref, 0, comps, 0, index_ref, sent_ref)
-    send_states(x_tiles, 4, comps - 4, comps * 2, index_ref, sent_ref)
-    write_messages(sent_ref, comps * 4 - 8, first_out, second_out)
+    send_states(y_ref, 0, comps, index_ref, sent_ref)
+    outs = (to_x1, to_x2, to_y1, to_y2)
+    write_messages(x_sent_ref, 0, channels - 8, outs, X_ROWS + channels)
+    write_messages(sent_ref, X_ROWS, channels, outs, X_ROWS + channels)
+
+
+def local_one_kernel(
+    lam_ref,
+    y_ref,
+    stat_ref,
+    index_ref,
+    fact_ref,
+    old_outer_ref,
+    old_term_ref,
+    x_ref,
+    outer_ref,
+    term_ref,
+    x_tiles,
+):
+    local_states(y_ref, 0, lam_ref.shape[0] // SUB // 3, index_ref, outer_ref)
     x_to_tiles(x_ref, 2, x_tiles)
     weight = TIME_STEP * 2.0 / 3.0
-    friction, conduct = own_gradients(2, weight, cot_ref, table_ref, x_tiles, stat_ref)
-    put(term_ref, 0, friction)
-    put(term_ref, 1, conduct)
-    for f, value in enumerate(outer_gradients(weight, outer_ref, x_tiles, fact_ref)):
+    for f, value in enumerate(outer_gradients(weight, old_outer_ref, x_tiles, fact_ref)):
         put(term_ref, 2 + f, value)
+    x_to_tiles(x_ref, 1, x_tiles)
+    terms = own_gradients(1, TIME_STEP * 0.25, lam_ref, y_ref, x_tiles, stat_ref)
+    for n in range(2):
+        put(term_ref, n, tile(old_term_ref, n) + terms[n])
 
 
 def first_kernel(
@@ -602,29 +615,29 @@
     stat_ref,
     index_ref,
     fact_ref,
-    term_ref,
-    x_ref,
+    near_outer_ref,
     in_ref,
     out_ref,
     volume_ref,
-    first_in,
-    second_in,
+    from_x1,
+    from_x2,
+    from_y1,
+    from_y2,
     base_ref,
     next_ref,
     next_y_ref,
-    new_term_ref,
-    first_out,
-    second_out,
     outer_ref,
-    x_outer_ref,
-    x_tiles,
+    to_x1,
+    to_x2,
+    to_y1,
+    to_y2,
     sent_ref,
     corner_ref,
 ):
-    rows = lam_ref.shape[0] // SUB
-    comps = rows // 3
-    received = Received(first_in, second_in, comps * 4 - 8, corner_ref)
-    outer_states(y_ref, 0, comps, 0, received, index_ref, outer_ref)
+    comps = lam_ref.shape[0] // SUB // 3
+    channels = comps * 2
+    received = Received((from_x1, from_x2, from_y1, from_y2), X_ROWS + channels, corner_ref)
+    remote_states(received, X_ROWS, channels, index_ref, near_outer_ref, outer_ref)
     wet_area = tile(stat_ref, WET_AREA)
     half_kappa_area = tile(stat_ref, HALF_KAPPA_AREA)
 
@@ -638,31 +651,52 @@
     transposed_section(
         1, lam_ref, y_ref, outer_ref, stat_ref, fact_ref, in_ref, out_ref, volume_ref, emit
     )
-    send_states(next_y_ref, 0, comps, 0, index_ref, sent_ref)
-    write_messages(sent_ref, comps * 2, first_out, second_out)
+    send_states(next_y_ref, 0, comps, index_ref, sent_ref)
+    write_messages(sent_ref, 0, channels, (to_x1, to_x2, to_y1, to_y2), channels)
+
+
+def zone_kernel(
+    lam_ref,
+    y_ref,
+    stat_ref,
+    index_ref,
+    fact_ref,
+    old_outer_ref,
+    term_ref,
+    x_ref,
+    x_near_ref,
+    conduct_ref,
+    from_x1,
+    from_x2,
+    from_y1,
+    from_y2,
+    out_ref,
+    x_outer_ref,
+    x_tiles,
+    corner_ref,
+):
+    rows = lam_ref.shape[0] // SUB
+    channels = rows // 3 * 2
+    x_channels = channels - 8
+    received = Received((from_x1, from_x2, from_y1, from_y2), X_ROWS + channels, corner_ref)
+    remote_states(received, 0, x_channels, index_ref, x_near_ref, x_outer_ref)
     x_to_tiles(x_ref, 1, x_tiles)
-    weight = TIME_STEP * 0.25
-    friction, conduct = own_gradients(1, weight, lam_ref, y_ref, x_tiles, stat_ref)
-    for f, value in enumerate(outer_gradients(weight, outer_ref, x_tiles, fact_ref)):
-        put(new_term_ref, 2 + f, tile(term_ref, 2 + f) + value)
+    outer_terms = outer_gradients(TIME_STEP * 0.25, old_outer_ref, x_tiles, fact_ref)
+    outer_terms = [tile(term_ref, 2 + f) + outer_terms[f] for f in range(3)]
     x_to_tiles(x_ref, 0, x_tiles)
-    outer_states(x_tiles, 4, comps - 4, comps * 2, received, index_ref, x_outer_ref)
-    friction_0, conduct_0 = own_gradients(0, TIME_STEP, next_ref, next_y_ref, x_tiles, stat_ref)
-    friction = friction + friction_0
-    conduct = conduct + conduct_0
-    channels = (comps - 4) * 2
+    friction_term, conduct_term = own_gradients(
+        0, TIME_STEP, lam_ref, y_ref, x_tiles, stat_ref
+    )
+    friction_term = friction_term + tile(term_ref, 0)
+    conduct_term = conduct_term + tile(term_ref, 1)
     for f in range(3):
         total = None
-        for ch in range(channels):
+        for ch in range(x_channels):
             row = 12 + ch // 2 * 3 + FACE_NODES[f][ch % 2]
-            term = tile(x_outer_ref, f * channels + ch) * tile(next_y_ref, row)
+            term = tile(x_outer_ref, f * x_channels + ch) * tile(y_ref, row)
             total = term if total is None else total + term
-        conduct = conduct + TIME_STEP * tile(stat_ref, EDGE + f) * total
-    put(new_term_ref, 0, tile(term_ref, 0) + friction)
-    put(new_term_ref, 1, tile(term_ref, 1) + conduct)
-
-
-def zone_kernel(term_ref, stat_ref, fact_ref, conduct_ref, out_ref):
+        conduct_term = conduct_term + TIME_STEP * tile(stat_ref, EDGE + f) * total
+
     zones = out_ref.shape[2]
     zone_iota = lax.broadcasted_iota(jnp.int32, (zones, LANES), 0).astype(jnp.float32)
     sub_iota = lax.broadcasted_iota(jnp.int32, (SUB, zones), 0)
@@ -693,14 +727,18 @@
                 totals[n] = totals[n] + jnp.where(sub_iota == sub, three, 0.0)
         return totals
 
-    friction, conduct = by_zone([tile(term_ref, 0), tile(term_ref, 1)], stat_ref, ZONE_ID)
+    friction, conduct = by_zone([friction_term, conduct_term], stat_ref, ZONE_ID)
     for f in range(3):
-        conduct = conduct + by_zone([tile(term_ref, 2 + f)], fact_ref, OUTER_ZONE + f)[0]
+        conduct = conduct + by_zone([outer_terms[f]], fact_ref, OUTER_ZONE + f)[0]
     friction = GRAD_WEIGHT * jnp.sum(friction, axis=0, keepdims=True)
     conduct = GRAD_WEIGHT * jnp.sum(conduct, axis=0, keepdims=True) / conduct_ref[...]
     for device in range(out_ref.shape[0]):
         out_ref[device, 0:1, :] = friction
         out_ref[device, 1:2, :] = conduct
+
+
+def local_zero_kernel(y_ref, index_ref, outer_ref):
+    local_states(y_ref, 0, y_ref.shape[0] // SUB // 3, index_ref, outer_ref)
 
 
 def last_kernel(
@@ -710,19 +748,23 @@
     stat_ref,
     index_ref,
     fact_ref,
+    near_outer_ref,
     in_ref,
     out_ref,
     volume_ref,
-    first_in,
-    second_in,
+    from_x1,
+    from_x2,
+    from_y1,
+    from_y2,
     adjoint_ref,
     last_ref,
     outer_ref,
     corner_ref,
 ):
     rows = lam_ref.shape[0] // SUB
-    received = Received(first_in, second_in, rows // 3 * 2, corner_ref)
-    outer_states(y_ref, 0, rows // 3, 0, received, index_ref, outer_ref)
+    channels = rows // 3 * 2
+    received = Received((from_x1, from_x2, from_y1, from_y2), channels, corner_ref)
+    remote_states(received, 0, channels, index_ref, near_outer_ref, outer_ref)
 
     def emit(r, value):
         put(adjoint_ref, r, tile(base_ref, r) + TIME_STEP * value)
@@ -737,19 +779,18 @@
     grads_ref[...] = jnp.sum(zone_ref[...], axis=0)
 
 
-def exchange(channels, first, second, *ahead):
-    sizes = lax.axis_size("gx"), lax.axis_size("gy")
-    first = lax.all_to_all(first, ("gx", "gy"), 0, 0, axis_index_groups=blocks_one(*sizes))
-    (second,) = call(
+def exchange(channels, messages, ahead=()):
+    x1, x2, y1, y2 = messages
+    x1, x2 = swapped(x1, "gx", 0), swapped(x2, "gx", 1)
+    y1, y2 = call(
         functools.partial(corner_kernel, channels),
         "corners",
-        [jax.ShapeDtypeStruct(second.shape, second.dtype)],
+        [jax.ShapeDtypeStruct(y1.shape, y1.dtype)] * 2,
         [],
-        [first, second, *ahead],
-        aliases={1: 0},
-    )
-    second = lax.all_to_all(second, ("gx", "gy"), 0, 0, axis_index_groups=blocks_two(*sizes))
-    return first, second
+        [x1, x2, y1, y2, *ahead],
+        aliases={2: 0, 3: 1},
+    )
+    return x1, x2, swapped(y1, "gy", 0), swapped(y2, "gy", 1)
 
 
 def call(kernel, name, outs, scratch, operands, scalars=(), far=False, aliases={}):
@@ -805,10 +846,13 @@
         return pltpu.VMEM((count * SUB, LANES), dtype)
 
     def messages(count):
-        return [jax.ShapeDtypeStruct((4, slots // LANES, message_rows(count), LANES), f32)] * 2
+        return [jax.ShapeDtypeStruct((slots // LANES, message_rows(count), LANES), f32)] * 4
 
     def sent_scratch(count):
-        return pltpu.VMEM((slots // LANES, corner_rows(count) * SUB * SUB, LANES), f32)
+        return pltpu.VMEM(sent_shape(count), f32)
+
+    def sent_shape(count):
+        return (slots // LANES, corner_rows(count) * SUB * SUB, LANES)
 
     corner_scratch = pltpu.VMEM((SUB, LANES), f32)
 
@@ -851,76 +895,81 @@
         ],
         far=True,
     )
-    received = exchange(channels + 5, *to_send)
-    lam, y, fact, term, *to_send = call(
+    matrices = [flux_in, flux_out, volume_matrix]
+    near_outer, near, term = call(
+        local_two_kernel,
+        "local_two",
+        [tiles(3 * channels), tiles(15), tiles(2)],
+        [tile_scratch(rows)],
+        [cot, table, stat, index, section_states],
+    )
+    x_near, x_sent = call(
+        local_x_kernel,
+        "local_x",
+        [
+            tiles(3 * (channels - 8)),
+            jax.ShapeDtypeStruct(sent_shape(channels - 8), f32),
+        ],
+        [tile_scratch(rows)],
+        [index, section_states],
+    )
+    received = exchange(channels + 5, to_send, [term])
+    lam, y, fact, outer, *to_send = call(
         second_kernel,
         "section_two",
-        [tiles(rows), tiles(rows), tiles(FACT_ROWS), tiles(5)]
-        + messages(channels + channels - 8),
-        [
-            tile_scratch(3 * channels),
-            tile_scratch(rows),
-            sent_scratch(2 * channels - 8),
-            corner_scratch,
-        ],
-        [cot, table, stat, index, section_states, flux_in, flux_out, volume_matrix, *received],
-        (5, 6, 7),
-    )
-    received = exchange(channels + channels - 8, *to_send)
-    base, lam, y, term, *to_send = call(
+        [tiles(rows), tiles(rows), tiles(FACT_ROWS), tiles(3 * channels)]
+        + messages(X_ROWS + channels),
+        [sent_scratch(channels), corner_scratch],
+        [cot, table, stat, index, near_outer, near, x_sent, *matrices, *received],
+        (7, 8, 9),
+    )
+    near_outer, term = call(
+        local_one_kernel,
+        "local_one",
+        [tiles(3 * channels), tiles(5)],
+        [tile_scratch(rows)],
+        [lam, y, stat, index, fact, outer, term, section_states],
+    )
+    received = exchange(X_ROWS + channels, to_send, [term])
+    base, lam, y, outer, *to_send = call(
         first_kernel,
         "section_one",
-        [tiles(rows), tiles(rows), tiles(rows), tiles(5)] + messages(channels),
+        [tiles(rows), tiles(rows), tiles(rows), tiles(3 * channels)] + messages(channels),
+        [sent_scratch(channels), corner_scratch],
+        [cot, lam, y, stat, index, fact, near_outer, *matrices, *received],
+        (7, 8, 9),
+    )
+    (zone_terms,) = call(
+        zone_kernel,
+        "zone_sums",
+        [jax.ShapeDtypeStruct((devices, 2, zones), f32)],
+        [tile_scratch(3 * (channels - 8)), tile_scratch(rows), corner_scratch],
         [
-            tile_scratch(3 * channels),
-            tile_scratch(3 * (channels - 8)),
-            tile_scratch(rows),
-            sent_scratch(channels),
-            corner_scratch,
-        ],
-        [
-            cot,
             lam,
             y,
             stat,
             index,
             fact,
+            outer,
             term,
             section_states,
-            flux_in,
-            flux_out,
-            volume_matrix,
+            x_near,
+            zone_conductivity.reshape(1, zones),
             *received,
         ],
-        (8, 9, 10),
-    )
-    (zone_terms,) = call(
-        zone_kernel,
-        "zone_sums",
-        [jax.ShapeDtypeStruct((devices, 2, zones), f32)],
-        [],
-        [term, stat, fact, zone_conductivity.reshape(1, zones)],
-    )
+    )
+    received = exchange(channels, to_send, [zone_terms])
     all_terms = lax.all_to_all(zone_terms, ("gx", "gy"), 0, 0)
-    received = exchange(channels, *to_send, zone_terms)
+    (near_outer,) = call(
+        local_zero_kernel, "local_zero", [tiles(3 * channels)], [], [y, index]
+    )
     adjoint, last = call(
         last_kernel,
         "section_zero",
         [tiles(rows), tiles(1)],
         [tile_scratch(3 * channels), corner_scratch],
-        [
-            base,
-            lam,
-            y,
-            stat,
-            index,
-            fact,
-            flux_in,
-            flux_out,
-            volume_matrix,
-            *received,
-        ],
-        (6, 7, 8),
+        [base, lam, y, stat, index, fact, near_outer, *matrices, *received],
+        (7, 8, 9),
     )
     (zone_grads,) = call(
         total_kernel,

time: 84.3 us -> 63.5 us (0.75)
  blocking collectives: 39.3 us -> 0 us
  starting transfers between devices: 11.3 us -> 32.7 us
  Pallas kernels: 23.7 us -> 22.5 us
  waiting for transfers between devices: 4.42 us -> 3.33 us
    all_to_all x5 -> x0, blocking collectives: 39.3 us -> none  [the longest x3 21.2 us: exchange(): lax.all_to_all(second, ('gx', 'gy'), 0, 0, axis_index_groups=blocks_two(*...]
    ppermute x0 -> x12, starting transfers between devices: none -> 24.1 us  [swapped(): lax.ppermute(x, axis, [(i, i + 1) for i in lows] + [(i + 1, i) for i in l...]
    all_to_all x1 -> x0, starting transfers between devices: 5.49 us -> none  [exchange(): lax.all_to_all(first, ('gx', 'gy'), 0, 0, axis_index_groups=blocks_one(*s...]
    ppermute x0 -> x12, waiting for transfers between devices: none -> 3.33 us  [swapped(): lax.ppermute(x, axis, [(i, i + 1) for i in lows] + [(i + 1, i) for i in l...]
    all_to_all x1, starting transfers between devices: 5.77 us -> 8.58 us  [local(): all_terms = lax.all_to_all(zone_terms, ('gx', 'gy'), 0, 0)]
    all_to_all x1, waiting for transfers between devices: 2.81 us -> 0.01 us  [local(): all_terms = lax.all_to_all(zone_terms, ('gx', 'gy'), 0, 0)]
    all_to_all x1 -> x0, waiting for transfers between devices: 1.61 us -> none  [exchange(): lax.all_to_all(first, ('gx', 'gy'), 0, 0, axis_index_groups=blocks_one(*s...]
    pallas_call x4 -> x0, local copies, waits for them, and re-layouts: 1.31 us -> none  [call(): pl.pallas_call(kernel, in_specs=[in_place if far else in_scalar if n in s...]
  transfers between devices with their start and end apart: 2 -> 13, of which waited for: 2 -> 3; matrix products, arithmetic and copies ran while one was open for 0% -> 0% of each run, Pallas kernels for 7% -> 19%
where the time goes in v7:
time: 63.5 us; the launch traced here: 62.9 us
  starting transfers between devices  32.7 us (51%)
  Pallas kernels  22.5 us (35%)
  local copies, waits for them, and re-layouts  3.42 us (5%)
  waiting for transfers between devices  3.33 us (5%)
  between operations  0.95 us (1%)
    ppermute x12, starting transfers between devices, swapped(): lax.ppermute(x, axis, [(i, i + 1) for i in lows] + [(i + 1, i) for i in l...  24.1 us
    pallas_call x13, Pallas kernels, call(): pl.pallas_call(kernel, in_specs=[in_place if far else in_scalar if n in s...  22.5 us
    all_to_all x1, starting transfers between devices, local(): all_terms = lax.all_to_all(zone_terms, ('gx', 'gy'), 0, 0)  8.58 us
    unnamed x28, local copies, waits for them, and re-layouts  3.42 us
    ppermute x12, waiting for transfers between devices, swapped(): lax.ppermute(x, axis, [(i, i + 1) for i in lows] + [(i + 1, i) for i in l...  3.33 us
  transfers between devices with their start and end apart: 13, of which 3 were waited for; matrix products, arithmetic and copies ran while one was open for 0% of the time, Pallas kernels for 19%

profile of v7, /device:TPU:1, one launch (start us, length us, event | category | flops | bytes accessed | tf_op | source)
XLA Modules:
  0.0 62.9 jit_solution(18278886986936775506)
XLA Ops:
  0.7 3.1 %prepare.1 = (f32[440,128]{1,0:T(8,128)}, f32[96,128]{1,0:T(8,128)}, s32[144,128]{1,0:T(8,128)}, f32[2,38,128]{2,1,0:T(8,128)}, f32[2,38,128]{2,1,0:T(8,128)}, /...) custom-call(f32[336,128]{1,0:T(8,128)} %bitcast.11, bf16[3,1,1,42,1024]{4,3,2,1,0:T(8,128)(2,1)} %x_ref.9, f32[8,128]{1,0:T(8,128)} %bitcast.19, ...), custom_call_target="tpu_custom_call" | custom-call | tf_op jit(solution)/shard_map/prepare/pallas_call | solution.py:800
  3.8 2.1 %collective-permute-start = (f32[2,38,128]{2,1,0:T(8,128)}, f32[2,38,128]{2,1,0:T(8,128)S(1)}, u32[]{:S(2)}, u32[]{:S(2)}) collective-permute-start(f32[2,38,128]{2,1,0:T(8,128)} %get-tuple-element.46), channel_id=1, source_target_pairs={{0,4},{8,12},{16,20},{24,28},{4,0},{12,8},{20,16},{28,24},{1,5},{9... | collective-permute-start | bytes 116744 | tf_op jit(solution)/shard_map/ppermute | solution.py:41
  5.9 0.7 %collective-permute-start.1 = (f32[2,38,128]{2,1,0:T(8,128)}, f32[2,38,128]{2,1,0:T(8,128)S(1)}, u32[]{:S(2)}, u32[]{:S(2)}) collective-permute-start(f32[2,38,128]{2,1,0:T(8,128)} %get-tuple-element.47), channel_id=1, source_target_pairs={{4,8},{12,16},{20,24},{8,4},{16,12},{24,20},{5,9},{13,17},{21,25},... | collective-permute-start | bytes 116744 | tf_op jit(solution)/shard_map/ppermute | solution.py:41
  6.6 0.9 %copy-done.1 = s32[144,128]{1,0:T(8,128)S(1)} copy-done((s32[144,128]{1,0:T(8,128)S(1)}, s32[144,128]{1,0:T(8,128)}, u32[]{:S(2)}) %copy-start.1) | copy-done | bytes 73752
  7.5 0.8 %copy-done.4 = f32[96,128]{1,0:T(8,128)S(1)} copy-done((f32[96,128]{1,0:T(8,128)S(1)}, f32[96,128]{1,0:T(8,128)}, u32[]{:S(2)}) %copy-start.4) | copy-done | bytes 49176
  8.3 0.9 %copy-done.6 = f32[440,128]{1,0:T(8,128)S(1)} copy-done((f32[440,128]{1,0:T(8,128)S(1)}, f32[440,128]{1,0:T(8,128)}, u32[]{:S(2)}) %copy-start.6) | copy-done | bytes 225304
  9.2 1.7 %local_two.1 = (f32[672,128]{1,0:T(8,128)S(1)}, f32[120,128]{1,0:T(8,128)S(1)}, f32[16,128]{1,0:T(8,128)S(1)}) custom-call(f32[336,128]{1,0:T(8,128)S(1)} %bitcast.12, f32[440,128]{1,0:T(8,128)S(1)} %copy-done.6, f32[96,128]{1,0:T(8,128)S(1)} %copy-done.4, s32[144,128]{1,0:T(8,128)S(1)} %copy-done.1, bf16[3,1,1,42,1024]{4,3,2,1,0:T(8,128)(2,1)S(1)} %copy-done), custom_call_target="tpu_custom_call" | custom-call | tf_op jit(solution)/shard_map/local_two/pallas_call | solution.py:800
  10.9 1.0 %collective-permute-start.2 = (f32[2,38,128]{2,1,0:T(8,128)S(1)}, f32[2,38,128]{2,1,0:T(8,128)S(1)}, u32[]{:S(2)}, u32[]{:S(2)}) collective-permute-start(f32[2,38,128]{2,1,0:T(8,128)S(1)} %get-tuple-element.51), channel_id=1, source_target_pairs={{0,1},{2,3},{1,0},{3,2},{4,5},{6,7},{5,4},{7,6},{8,9},{10,11},{9,8... | collective-permute-start | bytes 116744 | tf_op jit(solution)/shard_map/ppermute | solution.py:41
  12.0 3.2 %collective-permute-start.3 = (f32[2,38,128]{2,1,0:T(8,128)S(1)}, f32[2,38,128]{2,1,0:T(8,128)S(1)}, u32[]{:S(2)}, u32[]{:S(2)}) collective-permute-start(f32[2,38,128]{2,1,0:T(8,128)S(1)} %get-tuple-element.52), channel_id=1, source_target_pairs={{1,2},{2,1},{5,6},{6,5},{9,10},{10,9},{13,14},{14,13},{17,18},{18,... | collective-permute-start | bytes 116744 | tf_op jit(solution)/shard_map/ppermute | solution.py:41
  15.2 1.6 %local_x.1 = (f32[480,128]{1,0:T(8,128)S(1)}, f32[2,192,128]{2,1,0:T(8,128)S(1)}) custom-call(s32[144,128]{1,0:T(8,128)S(1)} %copy-done.2, bf16[3,1,1,42,1024]{4,3,2,1,0:T(8,128)(2,1)S(1)} %copy-done), custom_call_target="tpu_custom_call" | custom-call | tf_op jit(solution)/shard_map/local_x/pallas_call | solution.py:800
  16.9 0.5 collective-permute-done.3.from_y2
  17.4 0.1 copy-done.11
  17.5 3.4 %section_two.1 = (f32[336,128]{1,0:T(8,128)S(1)}, f32[336,128]{1,0:T(8,128)S(1)}, f32[120,128]{1,0:T(8,128)S(1)}, f32[672,128]{1,0:T(8,128)S(1)}, f32[2,59,128]{...) custom-call(f32[336,128]{1,0:T(8,128)S(1)} %bitcast.13, ...), custom_call_target="tpu_custom_call" | custom-call | tf_op jit(solution)/shard_map/section_two/pallas_call | solution.py:800
  20.9 4.1 %collective-permute-start.4 = (f32[2,59,128]{2,1,0:T(8,128)S(1)}, f32[2,59,128]{2,1,0:T(8,128)S(1)}, u32[]{:S(2)}, u32[]{:S(2)}) collective-permute-start(f32[2,59,128]{2,1,0:T(8,128)S(1)} %get-tuple-element.58), channel_id=1, source_target_pairs={{0,4},{8,12},{16,20},{24,28},{4,0},{12,8},{20,16},{28,24},{1,5},{9... | collective-permute-start | bytes 181256 | tf_op jit(solution)/shard_map/ppermute | solution.py:41
  25.0 0.7 %collective-permute-start.5 = (f32[2,59,128]{2,1,0:T(8,128)S(1)}, f32[2,59,128]{2,1,0:T(8,128)S(1)}, u32[]{:S(2)}, u32[]{:S(2)}) collective-permute-start(f32[2,59,128]{2,1,0:T(8,128)S(1)} %get-tuple-element.59), channel_id=1, source_target_pairs={{4,8},{12,16},{20,24},{8,4},{16,12},{24,20},{5,9},{13,17},{21,25},... | collective-permute-start | bytes 181256 | tf_op jit(solution)/shard_map/ppermute | solution.py:41
  25.6 1.4 %local_one.1 = (f32[672,128]{1,0:T(8,128)S(1)}, f32[40,128]{1,0:T(8,128)S(1)}) custom-call(f32[336,128]{1,0:T(8,128)S(1)} %get-tuple-element.53.lam_ref, f32[336,128]{1,0:T(8,128)S(1)} %get-tuple-element.54.y_ref, f32[96,128]{1,0:T(8,128)S(1)} %copy-done.5, s32[144,128]{1,0:T(8,128)S(1)} %copy-done.2, f32[120,128]{1,0:T(8,128)S(1)} %get-tuple-element.55.fact_ref, ...), custom_call_target="tpu_custom_call" | custom-call | tf_op jit(solution)/shard_map/local_one/pallas_call | solution.py:800
  27.1 0.1 collective-permute-start.6
  27.2 3.6 %collective-permute-start.7 = (f32[2,59,128]{2,1,0:T(8,128)S(1)}, f32[2,59,128]{2,1,0:T(8,128)S(1)}, u32[]{:S(2)}, u32[]{:S(2)}) collective-permute-start(f32[2,59,128]{2,1,0:T(8,128)S(1)} %get-tuple-element.64), channel_id=1, source_target_pairs={{1,2},{2,1},{5,6},{6,5},{9,10},{10,9},{13,14},{14,13},{17,18},{18,... | collective-permute-start | bytes 181256 | tf_op jit(solution)/shard_map/ppermute | solution.py:41
  30.8 1.9 %collective-permute-done.7.from_y2 = f32[2,59,128]{2,1,0:T(8,128)S(1)} collective-permute-done((f32[2,59,128]{2,1,0:T(8,128)S(1)}, f32[2,59,128]{2,1,0:T(8,128)S(1)}, u32[]{:S(2)}, u32[]{:S(2)}) %collective-permute-start.7) | collective-permute-done | bytes 60448 | tf_op jit(solution)/shard_map/ppermute | solution.py:41
  32.7 3.3 %section_one.1 = (f32[336,128]{1,0:T(8,128)S(1)}, f32[336,128]{1,0:T(8,128)S(1)}, f32[336,128]{1,0:T(8,128)S(1)}, f32[672,128]{1,0:T(8,128)S(1)}, f32[2,32,128]{...) custom-call(f32[336,128]{1,0:T(8,128)S(1)} %bitcast.14, ...), custom_call_target="tpu_custom_call" | custom-call | tf_op jit(solution)/shard_map/section_one/pallas_call | solution.py:800
  36.0 4.4 %collective-permute-start.8 = (f32[2,32,128]{2,1,0:T(8,128)S(1)}, f32[2,32,128]{2,1,0:T(8,128)S(1)}, u32[]{:S(2)}, u32[]{:S(2)}) collective-permute-start(f32[2,32,128]{2,1,0:T(8,128)S(1)} %get-tuple-element.68), channel_id=1, source_target_pairs={{0,4},{8,12},{16,20},{24,28},{4,0},{12,8},{20,16},{28,24},{1,5},{9... | collective-permute-start | bytes 98312 | tf_op jit(solution)/shard_map/ppermute | solution.py:41
  40.5 0.7 %collective-permute-start.9 = (f32[2,32,128]{2,1,0:T(8,128)S(1)}, f32[2,32,128]{2,1,0:T(8,128)S(1)}, u32[]{:S(2)}, u32[]{:S(2)}) collective-permute-start(f32[2,32,128]{2,1,0:T(8,128)S(1)} %get-tuple-element.69), channel_id=1, source_target_pairs={{4,8},{12,16},{20,24},{8,4},{16,12},{24,20},{5,9},{13,17},{21,25},... | collective-permute-start | bytes 98312 | tf_op jit(solution)/shard_map/ppermute | solution.py:41
  41.1 0.6 %copy-done.13 = f32[128]{0:T(128)S(1)} copy-done((f32[128]{0:T(128)S(1)}, f32[128]{0:T(128)}, u32[]{:S(2)}) %copy-start.13) | copy-done | bytes 536
  41.8 2.3 %zone_sums.1.rest_0_ = f32[32,2,128]{2,1,0:T(2,128)} custom-call(f32[336,128]{1,0:T(8,128)S(1)} %get-tuple-element.66.lam_ref, f32[336,128]{1,0:T(8,128)S(1)} %get-tuple-element.67.y_ref, f32[96,128]{1,0:T(8,128)S(1)} %copy-done.5, s32[144,128]{1,0:T(8,128)S(1)} %copy-done.2, f32[120,128]{1,0:T(8,128)S(1)} %get-tuple-element.55.fact_ref, ...), custom_call_target="tpu_custom_call" | custom-call | tf_op jit(solution)/shard_map/zone_sums/pallas_call | solution.py:800
  44.1 8.6 %all-to-all-start = ((f32[32,2,128]{2,1,0:T(2,128)}), f32[32,2,128]{2,1,0:T(2,128)S(1)}, u32[]{:S(2)}, u32[]{:S(2)}) async-start(f32[32,2,128]{2,1,0:T(2,128)} %zone_sums.1.rest_0_), calls=%async_computation | async-start | bytes 65536 | tf_op jit(solution)/shard_map/all_to_all | solution.py:962
  52.7 0.8 %corners.5 = (f32[2,32,128]{2,1,0:T(8,128)S(1)}, f32[2,32,128]{2,1,0:T(8,128)S(1)}) custom-call(f32[2,32,128]{2,1,0:T(8,128)S(1)} %collective-permute-done.8.x1.from_x1, f32[2,32,128]{2,1,0:T(8,128)S(1)} %collective-permute-done.9.x2.from_x2, f32[2,32,128]{2,1,0:T(8,128)S(1)} %get-tuple-element.70.old_y1, ...), custom_call_target="tpu_custom_call", output_to_operand_aliasing={{0}: (2, {}), {1}: (3, {})} | custom-call | tf_op jit(solution)/shard_map/corners/pallas_call | solution.py:800
  53.5 0.3 collective-permute-start.10
  53.8 3.4 %collective-permute-start.11 = (f32[2,32,128]{2,1,0:T(8,128)S(1)}, f32[2,32,128]{2,1,0:T(8,128)S(1)}, u32[]{:S(2)}, u32[]{:S(2)}) collective-permute-start(f32[2,32,128]{2,1,0:T(8,128)S(1)} %get-tuple-element.75), channel_id=1, source_target_pairs={{1,2},{2,1},{5,6},{6,5},{9,10},{10,9},{13,14},{14,13},{17,18},{18,... | collective-permute-start | bytes 98312 | tf_op jit(solution)/shard_map/ppermute | solution.py:41
  57.2 1.3 %local_zero.1.near_outer_ref = f32[672,128]{1,0:T(8,128)S(1)} custom-call(f32[336,128]{1,0:T(8,128)S(1)} %get-tuple-element.67.y_ref, s32[144,128]{1,0:T(8,128)S(1)} %copy-done.2), custom_call_target="tpu_custom_call" | custom-call | tf_op jit(solution)/shard_map/local_zero/pallas_call | solution.py:800
  58.5 0.8 %collective-permute-done.11.from_y2 = f32[2,32,128]{2,1,0:T(8,128)S(1)} collective-permute-done((f32[2,32,128]{2,1,0:T(8,128)S(1)}, f32[2,32,128]{2,1,0:T(8,128)S(1)}, u32[]{:S(2)}, u32[]{:S(2)}) %collective-permute-start.11) | collective-permute-done | bytes 32800 | tf_op jit(solution)/shard_map/ppermute | solution.py:41
  59.3 3.0 %section_zero.1 = (f32[336,128]{1,0:T(8,128)}, f32[8,128]{1,0:T(8,128)S(1)}) custom-call(f32[336,128]{1,0:T(8,128)S(1)} %get-tuple-element.65.base_ref, f32[336,128]{1,0:T(8,128)S(1)} %get-tuple-element.66.lam_ref, f32[336,128]{1,0:T(8,128)S(1)} %get-tuple-element.67.y_ref, f32[96,128]{1,0:T(8,128)S(1)} %copy-done.5, s32[144,128]{1,0:T(8,128)S(1)} %copy-done.2, ...), custom_call_target="tpu_custom_call" | custom-call | tf_op jit(solution)/shard_map/section_zero/pallas_call | solution.py:800
  62.3 0.6 zone_total.1
  (35 shorter events, 0.1 us)
Async XLA Ops:
  0.6 5.9 %copy-start = (bf16[3,1,1,42,1024]{4,3,2,1,0:T(8,128)(2,1)S(1)}, bf16[3,1,1,42,1024]{4,3,2,1,0:T(8,128)(2,1)}, u32[]{:S(2)}) copy-start(bf16[3,1,1,42,1024]{4,3,2,1,0:T(8,128)(2,1)} %x_ref.9) | copy-start | bytes 774148
  0.6 5.9 %copy-start.3 = (f32[1,1,42,1024]{3,1,2,0:T(1,128)S(1)}, f32[1,1,42,1024]{3,1,2,0:T(1,128)}, u32[]{:S(2)}) copy-start(f32[1,1,42,1024]{3,1,2,0:T(1,128)} %param.16) | copy-start | bytes 516100
  3.8 7.1 %collective-permute-start = (f32[2,38,128]{2,1,0:T(8,128)}, f32[2,38,128]{2,1,0:T(8,128)S(1)}, u32[]{:S(2)}, u32[]{:S(2)}) collective-permute-start(f32[2,38,128]{2,1,0:T(8,128)} %get-tuple-element.46), channel_id=1, source_target_pairs={{0,4},{8,12},{16,20},{24,28},{4,0},{12,8},{20,16},{28,24},{1,5},{9... | collective-permute-start | bytes 116744 | tf_op jit(solution)/shard_map/ppermute | solution.py:41
  5.9 5.0 %collective-permute-start.1 = (f32[2,38,128]{2,1,0:T(8,128)}, f32[2,38,128]{2,1,0:T(8,128)S(1)}, u32[]{:S(2)}, u32[]{:S(2)}) collective-permute-start(f32[2,38,128]{2,1,0:T(8,128)} %get-tuple-element.47), channel_id=1, source_target_pairs={{4,8},{12,16},{20,24},{8,4},{16,12},{24,20},{5,9},{13,17},{21,25},... | collective-permute-start | bytes 116744 | tf_op jit(solution)/shard_map/ppermute | solution.py:41
  6.6 0.9 %copy-start.1 = (s32[144,128]{1,0:T(8,128)S(1)}, s32[144,128]{1,0:T(8,128)}, u32[]{:S(2)}) copy-start(s32[144,128]{1,0:T(8,128)} %get-tuple-element.42.index_ref) | copy-start | bytes 221188
  7.5 0.8 %copy-start.4 = (f32[96,128]{1,0:T(8,128)S(1)}, f32[96,128]{1,0:T(8,128)}, u32[]{:S(2)}) copy-start(f32[96,128]{1,0:T(8,128)} %get-tuple-element.41.stat_ref) | copy-start | bytes 147460
  8.3 0.9 %copy-start.6 = (f32[440,128]{1,0:T(8,128)S(1)}, f32[440,128]{1,0:T(8,128)}, u32[]{:S(2)}) copy-start(f32[440,128]{1,0:T(8,128)} %get-tuple-element.40.table_ref) | copy-start | bytes 675844
  9.2 1.7 %copy-start.9 = (f32[2,38,128]{2,1,0:T(8,128)S(1)}, f32[2,38,128]{2,1,0:T(8,128)}, u32[]{:S(2)}) copy-start(f32[2,38,128]{2,1,0:T(8,128)} %get-tuple-element.48.old_y1) | copy-start | bytes 116740
  9.2 1.7 %copy-start.10 = (f32[2,38,128]{2,1,0:T(8,128)S(1)}, f32[2,38,128]{2,1,0:T(8,128)}, u32[]{:S(2)}) copy-start(f32[2,38,128]{2,1,0:T(8,128)} %get-tuple-element.49.old_y2) | copy-start | bytes 116740
  10.9 4.3 %copy-start.2 = (s32[144,128]{1,0:T(8,128)S(1)}, s32[144,128]{1,0:T(8,128)}, u32[]{:S(2)}) copy-start(s32[144,128]{1,0:T(8,128)} %get-tuple-element.42.index_ref) | copy-start | bytes 221188
  10.9 6.5 %copy-start.7 = (f32[440,128]{1,0:T(8,128)S(1)}, f32[440,128]{1,0:T(8,128)}, u32[]{:S(2)}) copy-start(f32[440,128]{1,0:T(8,128)} %get-tuple-element.40.table_ref) | copy-start | bytes 675844
  10.9 5.9 %collective-permute-start.2 = (f32[2,38,128]{2,1,0:T(8,128)S(1)}, f32[2,38,128]{2,1,0:T(8,128)S(1)}, u32[]{:S(2)}, u32[]{:S(2)}) collective-permute-start(f32[2,38,128]{2,1,0:T(8,128)S(1)} %get-tuple-element.51), channel_id=1, source_target_pairs={{0,1},{2,3},{1,0},{3,2},{4,5},{6,7},{5,4},{7,6},{8,9},{10,11},{9,8... | collective-permute-start | bytes 116744 | tf_op jit(solution)/shard_map/ppermute | solution.py:41
  12.0 5.4 %copy-start.5 = (f32[96,128]{1,0:T(8,128)S(1)}, f32[96,128]{1,0:T(8,128)}, u32[]{:S(2)}) copy-start(f32[96,128]{1,0:T(8,128)} %get-tuple-element.41.stat_ref) | copy-start | bytes 147460
  12.0 5.4 %collective-permute-start.3 = (f32[2,38,128]{2,1,0:T(8,128)S(1)}, f32[2,38,128]{2,1,0:T(8,128)S(1)}, u32[]{:S(2)}, u32[]{:S(2)}) collective-permute-start(f32[2,38,128]{2,1,0:T(8,128)S(1)} %get-tuple-element.52), channel_id=1, source_target_pairs={{1,2},{2,1},{5,6},{6,5},{9,10},{10,9},{13,14},{14,13},{17,18},{18,... | collective-permute-start | bytes 116744 | tf_op jit(solution)/shard_map/ppermute | solution.py:41
  15.2 2.2 %copy-start.8 = (f32[12,12]{1,0:T(8,128)S(1)}, f32[12,12]{1,0:T(8,128)}, u32[]{:S(2)}) copy-start(f32[12,12]{1,0:T(8,128)} %volume_ref.5) | copy-start | bytes 1732
  15.2 2.2 %copy-start.12 = (f32[8,8]{1,0:T(8,128)S(1)}, f32[8,8]{1,0:T(8,128)}, u32[]{:S(2)}) copy-start(f32[8,8]{1,0:T(8,128)} %out_ref.5) | copy-start | bytes 772
  16.8 0.7 %copy-start.11 = (f32[8,8]{1,0:T(8,128)S(1)}, f32[8,8]{1,0:T(8,128)}, u32[]{:S(2)}) copy-start(f32[8,8]{1,0:T(8,128)} %in_ref.5) | copy-start | bytes 772
  20.9 6.1 %collective-permute-start.4 = (f32[2,59,128]{2,1,0:T(8,128)S(1)}, f32[2,59,128]{2,1,0:T(8,128)S(1)}, u32[]{:S(2)}, u32[]{:S(2)}) collective-permute-start(f32[2,59,128]{2,1,0:T(8,128)S(1)} %get-tuple-element.58), channel_id=1, source_target_pairs={{0,4},{8,12},{16,20},{24,28},{4,0},{12,8},{20,16},{28,24},{1,5},{9... | collective-permute-start | bytes 181256 | tf_op jit(solution)/shard_map/ppermute | solution.py:41
  25.0 2.1 %collective-permute-start.5 = (f32[2,59,128]{2,1,0:T(8,128)S(1)}, f32[2,59,128]{2,1,0:T(8,128)S(1)}, u32[]{:S(2)}, u32[]{:S(2)}) collective-permute-start(f32[2,59,128]{2,1,0:T(8,128)S(1)} %get-tuple-element.59), channel_id=1, source_target_pairs={{4,8},{12,16},{20,24},{8,4},{16,12},{24,20},{5,9},{13,17},{21,25},... | collective-permute-start | bytes 181256 | tf_op jit(solution)/shard_map/ppermute | solution.py:41
  27.1 3.7 %collective-permute-start.6 = (f32[2,59,128]{2,1,0:T(8,128)S(1)}, f32[2,59,128]{2,1,0:T(8,128)S(1)}, u32[]{:S(2)}, u32[]{:S(2)}) collective-permute-start(f32[2,59,128]{2,1,0:T(8,128)S(1)} %get-tuple-element.63), channel_id=1, source_target_pairs={{0,1},{2,3},{1,0},{3,2},{4,5},{6,7},{5,4},{7,6},{8,9},{10,11},{9,8... | collective-permute-start | bytes 181256 | tf_op jit(solution)/shard_map/ppermute | solution.py:41
  27.2 5.6 %collective-permute-start.7 = (f32[2,59,128]{2,1,0:T(8,128)S(1)}, f32[2,59,128]{2,1,0:T(8,128)S(1)}, u32[]{:S(2)}, u32[]{:S(2)}) collective-permute-start(f32[2,59,128]{2,1,0:T(8,128)S(1)} %get-tuple-element.64), channel_id=1, source_target_pairs={{1,2},{2,1},{5,6},{6,5},{9,10},{10,9},{13,14},{14,13},{17,18},{18,... | collective-permute-start | bytes 181256 | tf_op jit(solution)/shard_map/ppermute | solution.py:41
  36.0 16.7 %collective-permute-start.8 = (f32[2,32,128]{2,1,0:T(8,128)S(1)}, f32[2,32,128]{2,1,0:T(8,128)S(1)}, u32[]{:S(2)}, u32[]{:S(2)}) collective-permute-start(f32[2,32,128]{2,1,0:T(8,128)S(1)} %get-tuple-element.68), channel_id=1, source_target_pairs={{0,4},{8,12},{16,20},{24,28},{4,0},{12,8},{20,16},{28,24},{1,5},{9... | collective-permute-start | bytes 98312 | tf_op jit(solution)/shard_map/ppermute | solution.py:41
  40.5 12.3 %collective-permute-start.9 = (f32[2,32,128]{2,1,0:T(8,128)S(1)}, f32[2,32,128]{2,1,0:T(8,128)S(1)}, u32[]{:S(2)}, u32[]{:S(2)}) collective-permute-start(f32[2,32,128]{2,1,0:T(8,128)S(1)} %get-tuple-element.69), channel_id=1, source_target_pairs={{4,8},{12,16},{20,24},{8,4},{16,12},{24,20},{5,9},{13,17},{21,25},... | collective-permute-start | bytes 98312 | tf_op jit(solution)/shard_map/ppermute | solution.py:41
  41.1 0.7 %copy-start.13 = (f32[128]{0:T(128)S(1)}, f32[128]{0:T(128)}, u32[]{:S(2)}) copy-start(f32[128]{0:T(128)} %param.23) | copy-start | bytes 1540
  44.1 18.2 %all-to-all-start = ((f32[32,2,128]{2,1,0:T(2,128)}), f32[32,2,128]{2,1,0:T(2,128)S(1)}, u32[]{:S(2)}, u32[]{:S(2)}) async-start(f32[32,2,128]{2,1,0:T(2,128)} %zone_sums.1.rest_0_), calls=%async_computation | async-start | bytes 65536 | tf_op jit(solution)/shard_map/all_to_all | solution.py:962
  53.5 5.0 %collective-permute-start.10 = (f32[2,32,128]{2,1,0:T(8,128)S(1)}, f32[2,32,128]{2,1,0:T(8,128)S(1)}, u32[]{:S(2)}, u32[]{:S(2)}) collective-permute-start(f32[2,32,128]{2,1,0:T(8,128)S(1)} %get-tuple-element.74), channel_id=1, source_target_pairs={{0,1},{2,3},{1,0},{3,2},{4,5},{6,7},{5,4},{7,6},{8,9},{10,11},{9,8... | collective-permute-start | bytes 98312 | tf_op jit(solution)/shard_map/ppermute | solution.py:41
  53.8 5.5 %collective-permute-start.11 = (f32[2,32,128]{2,1,0:T(8,128)S(1)}, f32[2,32,128]{2,1,0:T(8,128)S(1)}, u32[]{:S(2)}, u32[]{:S(2)}) collective-permute-start(f32[2,32,128]{2,1,0:T(8,128)S(1)} %get-tuple-element.75), channel_id=1, source_target_pairs={{1,2},{2,1},{5,6},{6,5},{9,10},{10,9},{13,14},{14,13},{17,18},{18,... | collective-permute-start | bytes 98312 | tf_op jit(solution)/shard_map/ppermute | solution.py:41

commit v8 on v7

--- a/solution.py
+++ b/solution.py
@@ -26,7 +26,8 @@
     10,
     11,
 )
-STAT_ROWS = 12
+CONDUCTIVITY = 12
+STAT_ROWS = 13
 NEAR_VMEM, FAR_VMEM = 32, 60
 OUTER_EDGE, OUTER_ZONE, HALF_SPEED = 0, 3, 6
 FACT_ROWS = 15
@@ -125,53 +126,99 @@
         return jnp.where(remote_index == CORNER_BLOCK, got, value)
 
 
-def partner_index(index_ref, f):
-    return [tile(index_ref, part * 3 + f) for part in range(4)]
-
-
-def sent_index(index_ref, d):
-    return [tile(index_ref, 12 + part * 2 + d) for part in range(3)]
-
-
 INDEX_ROWS = 18
+MATRIX_ROWS = 4
+
+
+def plan_rows(rows):
+    return STAT_ROWS + INDEX_ROWS + MATRIX_ROWS + rows + 13
+
+
+def plan_parts(plan_ref):
+    parts, at = [], 0
+    for count in (STAT_ROWS, INDEX_ROWS, MATRIX_ROWS):
+        parts.append(plan_ref.at[at * SUB : (at + count) * SUB])
+        at += count
+    return (*parts, plan_ref.at[at * SUB :])
 
 
 def tile_at(ref, row):
     return ref[pl.ds(pl.multiple_of(row * SUB, SUB), SUB), :]
 
 
+def index_at(ref, row):
+    return tile_at(ref, row).astype(jnp.int32)
+
+
+def index_of(ref, row):
+    return tile(ref, row).astype(jnp.int32)
+
+
+def put_index(ref, row, value):
+    put(ref, row, value.astype(jnp.float32))
+
+
+def load_matrices(plan_ref, matrix_ref, sem):
+    copy = pltpu.make_async_copy(plan_parts(plan_ref)[2], matrix_ref, sem.at[0])
+    copy.start()
+    return copy
+
+
 def put_at(ref, row, value):
     ref[pl.ds(pl.multiple_of(row * SUB, SUB), SUB), :] = value
 
 
-def send_states(src, first_comp, comps, index_ref, sent_ref):
-    def body(d, carry):
-        lane, sublane, face = [tile_at(index_ref, 12 + n * 2 + d) for n in range(3)]
+class Sender:
+    def __init__(self, index_ref, sent_ref, packed_ref):
+        self.straight = [index_of(index_ref, 12 + 2 * n) for n in range(3)]
+        self.lane, sublane, self.face = [index_of(index_ref, 13 + 2 * n) for n in range(3)]
+        sub = lax.broadcasted_iota(jnp.int32, (SUB, LANES), 0)
+        slot = lax.broadcasted_iota(jnp.int32, (SUB, LANES), 1)
+        self.own = (sub == sublane) & (slot < CORNER_LANES)
+        self.sent_ref, self.packed_ref = sent_ref, packed_ref
+        self.group = None
+
+    def corner(self, src, row):
+        return jnp.where(self.own, take(tile(src, row), self.lane), 0.0)
+
+    def put(self, channel, value, corner):
+        put(self.sent_ref, channel, value)
+        place = channel % SUB
+        moved = corner if place == 0 else pltpu.roll(corner, CORNER_LANES * place, 1)
+        self.group = moved if place == 0 else self.group + moved
+        if place == SUB - 1:
+            self.flush(channel)
+
+    def flush(self, channel):
+        at = channel // SUB
+        self.packed_ref[at : at + 1, :] = jnp.sum(self.group, axis=0, keepdims=True)
+
+    def states(self, src, first_comp, comps):
         for comp in range(comps):
-            ends = gather_ends(src, (first_comp + comp) * 3, lane, sublane, face)
+            row = (first_comp + comp) * 3
+            ends = gather_ends(src, row, *self.straight)
+            n0, n1, n2 = [self.corner(src, row + i) for i in range(3)]
+            corners = pick(self.face, n1, n2, n0), pick(self.face, n2, n0, n1)
             for j in range(2):
-                put(sent_ref.at[d], comp * 2 + j, ends[j])
-        return carry
-
-    lax.fori_loop(0, 2, body, 0)
-
-
-def write_messages(sent_ref, first, channels, outs, total):
-    lane = lax.broadcasted_iota(jnp.int32, (SUB, LANES), 1)
-    sub = lax.broadcasted_iota(jnp.int32, (SUB, LANES), 0)
+                self.put(comp * 2 + j, ends[j], corners[j])
+
+    def by_face(self, src, row, channel):
+        corner = pick(self.face, *[self.corner(src, row + i) for i in range(3)])
+        self.put(channel, gather_by_face(src, row, *self.straight), corner)
+
+    def by_element(self, src, row, channel):
+        self.put(channel, gather_tile(src, row, *self.straight[:2]), self.corner(src, row))
+
+
+def write_messages(sent_ref, packed_ref, first, channels, outs, total):
     for role, out in enumerate(outs):
         for half in range(2):
-            out[half, first : first + channels, :] = sent_ref.at[0][
+            out[half, first : first + channels, :] = sent_ref[
                 pl.ds(role * 2 + half, channels, stride=SUB), :
             ]
-    for group in range(corner_rows(channels)):
-        values = sent_ref.at[1][pl.ds(group * SUB * SUB, SUB, stride=SUB), :]
-        moved = pltpu.roll(values, 0, 1, stride=CORNER_LANES, stride_axis=0)
-        own = jnp.where(lane // CORNER_LANES == sub, moved, 0.0)
-        row = jnp.sum(own, axis=0, keepdims=True)
-        at = total + first // SUB + group
-        for out in outs[:2]:
-            out[0, at : at + 1, :] = row
+    count, at = corner_rows(channels), total + first // SUB
+    for out in outs[:2]:
+        out[0, at : at + count, :] = packed_ref[0:count, :]
 
 
 def prepare_kernel(
@@ -187,18 +234,21 @@
     zone_ref,
     send_ref,
     partner_ref,
-    table_ref,
-    stat_ref,
-    index_ref,
+    in_ref,
+    out_ref,
+    volume_ref,
+    plan_ref,
     to_x1,
     to_x2,
     to_y1,
     to_y2,
     x_tiles,
     sent_ref,
+    packed_ref,
     *fetched,
 ):
     *fetched, sems = fetched
+    stat_ref, index_ref, matrix_ref, table_ref = plan_parts(plan_ref)
     sources = [
         partner_ref,
         send_ref,
@@ -212,6 +262,9 @@
         conduct_ref,
         wet_ref,
         zone_ref,
+        in_ref,
+        out_ref,
+        volume_ref,
     ]
     copies = [
         pltpu.make_async_copy(source, target, sems.at[n])
@@ -234,7 +287,13 @@
         conduct_ref,
         wet_ref,
         zone_ref,
+        in_ref,
+        out_ref,
+        volume_ref,
     ) = fetched
+    matrix_ref[0:8, 0:8] = in_ref[...]
+    matrix_ref[8:16, 0:8] = out_ref[...]
+    matrix_ref[16:28, 0:12] = volume_ref[...]
     rows = cot_ref.shape[0] // SUB
     sections = x_ref.shape[0]
     odd_a, odd_b = lax.axis_index("gx") % 2, lax.axis_index("gy") % 2
@@ -258,10 +317,10 @@
             remote = jnp.where(direction == toward, 2 * number + half, remote)
         for number, toward in enumerate(corners):
             lane = jnp.where(direction == toward, lane % 4 + 4 * number, lane)
-        put(index_ref, f, lane)
-        put(index_ref, 3 + f, jnp.bitwise_and(jnp.right_shift(partner, 7), SUB - 1))
-        put(index_ref, 6 + f, jnp.right_shift(partner, 10))
-        put(index_ref, 9 + f, remote)
+        put_index(index_ref, f, lane)
+        put_index(index_ref, 3 + f, jnp.bitwise_and(jnp.right_shift(partner, 7), SUB - 1))
+        put_index(index_ref, 6 + f, jnp.right_shift(partner, 10))
+        put_index(index_ref, 9 + f, remote)
     sub_iota = lax.broadcasted_iota(jnp.int32, (SUB, LANES), 0)
     lane_iota = lax.broadcasted_iota(jnp.int32, (SUB, LANES), 1)
 
@@ -293,9 +352,9 @@
             moved = pltpu.roll(row, 4 * number, 1)
             corner_slots = jnp.where(lane_iota // 4 == number, moved, corner_slots)
     for d, slots in enumerate((straight_slots, corner_slots)):
-        put(index_ref, 12 + d, jnp.bitwise_and(slots, LANES - 1))
-        put(index_ref, 14 + d, jnp.bitwise_and(jnp.right_shift(slots, 7), SUB - 1))
-        put(index_ref, 16 + d, jnp.right_shift(slots, 10))
+        put_index(index_ref, 12 + d, jnp.bitwise_and(slots, LANES - 1))
+        put_index(index_ref, 14 + d, jnp.bitwise_and(jnp.right_shift(slots, 7), SUB - 1))
+        put_index(index_ref, 16 + d, jnp.right_shift(slots, 10))
     zone = zone_ref[...]
     zone_lane = jnp.bitwise_and(zone, LANES - 1)
     zone_block = jnp.right_shift(zone, 7)
@@ -317,6 +376,7 @@
     put(stat_ref, WET, wet)
     put(stat_ref, ZONE_FRICTION, factors[0])
     put(stat_ref, ZONE_ID, zone.astype(jnp.float32))
+    stat_ref[CONDUCTIVITY * SUB : CONDUCTIVITY * SUB + conduct_ref.shape[0], :] = conduct_ref[...]
     stat_ref[EDGE * SUB : (EDGE + 3) * SUB, :] = edge_ref[...]
     for k in range(sections):
         rows_to_tiles(
@@ -341,22 +401,18 @@
     for r in range(rows):
         put(table_ref, r, tile(cot_ref, r) * (wet_area if r < 12 else half_kappa_area))
     comps = rows // 3
-    send_states(table_ref, 0, comps, index_ref, sent_ref)
-    for d in range(2):
-        lane, sublane, face = sent_index(index_ref, d)
-        at = comps * 2 * SUB
-        for group in range(4):
-            sent_ref[d, at : at + SUB, :] = gather_by_face(
-                table_ref, rows + 3 * group, lane, sublane, face
-            )
-            at += SUB
-        sent_ref[d, at : at + SUB, :] = gather_tile(table_ref, rows + 12, lane, sublane)
     channels = comps * 2 + 5
-    write_messages(sent_ref, 0, channels, (to_x1, to_x2, to_y1, to_y2), channels)
+    sender = Sender(index_ref, sent_ref, packed_ref)
+    sender.states(table_ref, 0, comps)
+    for group in range(4):
+        sender.by_face(table_ref, rows + 3 * group, comps * 2 + group)
+    sender.by_element(table_ref, rows + 12, channels - 1)
+    sender.flush(channels - 1)
+    write_messages(sent_ref, packed_ref, 0, channels, (to_x1, to_x2, to_y1, to_y2), channels)
 
 
 def corner_kernel(channels, x1, x2, old_y1, old_y2, *rest):
-    y1, y2 = rest[-2:]
+    y1, y2 = rest[1:3]
     rows = slice(channels, message_rows(channels))
     lane = corner_lane((corner_rows(channels), LANES))
     merged = jnp.where(lane < 8, x1[0, rows, :], x2[0, rows, :])
@@ -366,7 +422,7 @@
 
 def local_states(src, first_comp, comps, index_ref, out_ref):
     def body(f, carry):
-        lane, sublane, face = [tile_at(index_ref, n * 3 + f) for n in range(3)]
+        lane, sublane, face = [index_at(index_ref, n * 3 + f) for n in range(3)]
         for comp in range(comps):
             ends = gather_ends(src, (first_comp + comp) * 3, lane, sublane, face)
             for j in range(2):
@@ -378,7 +434,7 @@
 
 def remote_states(received, first_row, channels, index_ref, local_ref, out_ref):
     def body(f, carry):
-        lane, remote = tile_at(index_ref, f), tile_at(index_ref, 9 + f)
+        lane, remote = index_at(index_ref, f), index_at(index_ref, 9 + f)
         for ch in range(channels):
             value = tile_at(local_ref, f * channels + ch)
             put_at(
@@ -390,7 +446,7 @@
 
 
 def transposed_section(
-    section, lam_ref, y_ref, outer_ref, stat_ref, fact_ref, in_ref, out_ref, volume_ref, emit
+    section, lam_ref, y_ref, outer_ref, stat_ref, fact_ref, matrix_ref, emit
 ):
     rows = lam_ref.shape[0] // SUB
     channels = rows // 3 * 2
@@ -403,9 +459,9 @@
     own = [tile(y_ref, r) for r in range(12)]
     result = []
     for r in range(12):
-        total = volume_ref[0, r] * own[0]
+        total = matrix_ref[16, r] * own[0]
         for q in range(1, 12):
-            total = total + volume_ref[q, r] * own[q]
+            total = total + matrix_ref[16 + q, r] * own[q]
         result.append(total)
     for f in range(3):
         ends = FACE_NODES[f]
@@ -414,7 +470,7 @@
         for b in range(8):
             total = half_speed[f] * (inner[b] - outer[b])
             for a in range(8):
-                total = total + in_ref[a, b] * inner[a] - out_ref[a, b] * outer[a]
+                total = total + matrix_ref[a, b] * inner[a] - matrix_ref[8 + a, b] * outer[a]
             at = (b // 2) * 3 + ends[b % 2]
             result[at] = result[at] + total
     friction = tile(stat_ref, ZONE_FRICTION) * tile(stat_ref, FRICTION_BASE + section) * wet
@@ -496,12 +552,13 @@
 
 
 def local_two_kernel(
-    cot_ref, table_ref, stat_ref, index_ref, x_ref, outer_ref, near_ref, term_ref, x_tiles
+    cot_ref, plan_ref, x_ref, outer_ref, near_ref, term_ref, x_tiles
 ):
+    stat_ref, index_ref, _, table_ref = plan_parts(plan_ref)
     rows = cot_ref.shape[0] // SUB
     local_states(table_ref, 0, rows // 3, index_ref, outer_ref)
     for f in range(3):
-        lane, sublane, face = [tile(index_ref, n * 3 + f) for n in range(3)]
+        lane, sublane, face = [index_of(index_ref, n * 3 + f) for n in range(3)]
         for group in range(4):
             value = gather_by_face(table_ref, rows + 3 * group, lane, sublane, face)
             put(near_ref, f * 5 + group, value)
@@ -514,24 +571,23 @@
     put(term_ref, 1, conduct)
 
 
-def local_x_kernel(index_ref, x_ref, x_outer_ref, sent_ref, x_tiles):
+def local_x_kernel(plan_ref, x_ref, x_outer_ref, sent_ref, packed_ref, x_tiles):
+    index_ref = plan_parts(plan_ref)[1]
     comps = x_ref.shape[3] // 3
     x_to_tiles(x_ref, 0, x_tiles)
     local_states(x_tiles, 4, comps - 4, index_ref, x_outer_ref)
-    send_states(x_tiles, 4, comps - 4, index_ref, sent_ref)
+    sender = Sender(index_ref, sent_ref, packed_ref)
+    sender.states(x_tiles, 4, comps - 4)
+    sender.flush(comps * 2 - 9)
 
 
 def second_kernel(
     cot_ref,
-    table_ref,
-    stat_ref,
-    index_ref,
+    plan_ref,
     near_outer_ref,
     near_ref,
     x_sent_ref,
-    in_ref,
-    out_ref,
-    volume_ref,
+    x_packed_ref,
     from_x1,
     from_x2,
     from_y1,
@@ -545,15 +601,20 @@
     to_y1,
     to_y2,
     sent_ref,
+    packed_ref,
     corner_ref,
+    matrix_ref,
+    sem,
 ):
+    matrices = load_matrices(plan_ref, matrix_ref, sem)
+    stat_ref, index_ref, _, table_ref = plan_parts(plan_ref)
     rows = cot_ref.shape[0] // SUB
     comps = rows // 3
     channels = comps * 2
     received = Received((from_x1, from_x2, from_y1, from_y2), channels + 5, corner_ref)
     remote_states(received, 0, channels, index_ref, near_outer_ref, outer_ref)
     for f in range(3):
-        lane, remote = tile(index_ref, f), tile(index_ref, 9 + f)
+        lane, remote = index_of(index_ref, f), index_of(index_ref, 9 + f)
         for group in range(5):
             value = received.fill(channels + group, lane, remote, tile(near_ref, f * 5 + group))
             if group == 0:
@@ -575,20 +636,22 @@
         put(lam_ref, r, lam)
         put(y_ref, r, lam * (wet_area if r < 12 else half_kappa_area))
 
+    matrices.wait()
     transposed_section(
-        2, cot_ref, table_ref, outer_ref, stat_ref, fact_ref, in_ref, out_ref, volume_ref, emit
-    )
-    send_states(y_ref, 0, comps, index_ref, sent_ref)
+        2, cot_ref, table_ref, outer_ref, stat_ref, fact_ref, matrix_ref, emit
+    )
+    sender = Sender(index_ref, sent_ref, packed_ref)
+    sender.states(y_ref, 0, comps)
+    sender.flush(channels - 1)
     outs = (to_x1, to_x2, to_y1, to_y2)
-    write_messages(x_sent_ref, 0, channels - 8, outs, X_ROWS + channels)
-    write_messages(sent_ref, X_ROWS, channels, outs, X_ROWS + channels)
+    write_messages(x_sent_ref, x_packed_ref, 0, channels - 8, outs, X_ROWS + channels)
+    write_messages(sent_ref, packed_ref, X_ROWS, channels, outs, X_ROWS + channels)
 
 
 def local_one_kernel(
     lam_ref,
     y_ref,
-    stat_ref,
-    index_ref,
+    plan_ref,
     fact_ref,
     old_outer_ref,
     old_term_ref,
@@ -597,6 +660,7 @@
     term_ref,
     x_tiles,
 ):
+    stat_ref, index_ref, _, _ = plan_parts(plan_ref)
     local_states(y_ref, 0, lam_ref.shape[0] // SUB // 3, index_ref, outer_ref)
     x_to_tiles(x_ref, 2, x_tiles)
     weight = TIME_STEP * 2.0 / 3.0
@@ -612,13 +676,9 @@
     cot_ref,
     lam_ref,
     y_ref,
-    stat_ref,
-    index_ref,
+    plan_ref,
     fact_ref,
     near_outer_ref,
-    in_ref,
-    out_ref,
-    volume_ref,
     from_x1,
     from_x2,
     from_y1,
@@ -632,8 +692,13 @@
     to_y1,
     to_y2,
     sent_ref,
+    packed_ref,
     corner_ref,
+    matrix_ref,
+    sem,
 ):
+    matrices = load_matrices(plan_ref, matrix_ref, sem)
+    stat_ref, index_ref, _, _ = plan_parts(plan_ref)
     comps = lam_ref.shape[0] // SUB // 3
     channels = comps * 2
     received = Received((from_x1, from_x2, from_y1, from_y2), X_ROWS + channels, corner_ref)
@@ -648,24 +713,25 @@
         put(next_y_ref, r, lam * (wet_area if r < 12 else half_kappa_area))
         put(base_ref, r, (1.0 / 3.0) * tile(cot_ref, r) + 0.75 * old + lam)
 
+    matrices.wait()
     transposed_section(
-        1, lam_ref, y_ref, outer_ref, stat_ref, fact_ref, in_ref, out_ref, volume_ref, emit
-    )
-    send_states(next_y_ref, 0, comps, index_ref, sent_ref)
-    write_messages(sent_ref, 0, channels, (to_x1, to_x2, to_y1, to_y2), channels)
+        1, lam_ref, y_ref, outer_ref, stat_ref, fact_ref, matrix_ref, emit
+    )
+    sender = Sender(index_ref, sent_ref, packed_ref)
+    sender.states(next_y_ref, 0, comps)
+    sender.flush(channels - 1)
+    write_messages(sent_ref, packed_ref, 0, channels, (to_x1, to_x2, to_y1, to_y2), channels)
 
 
 def zone_kernel(
     lam_ref,
     y_ref,
-    stat_ref,
-    index_ref,
+    plan_ref,
     fact_ref,
     old_outer_ref,
     term_ref,
     x_ref,
     x_near_ref,
-    conduct_ref,
     from_x1,
     from_x2,
     from_y1,
@@ -675,6 +741,7 @@
     x_tiles,
     corner_ref,
 ):
+    stat_ref, index_ref, _, _ = plan_parts(plan_ref)
     rows = lam_ref.shape[0] // SUB
     channels = rows // 3 * 2
     x_channels = channels - 8
@@ -731,13 +798,19 @@
     for f in range(3):
         conduct = conduct + by_zone([outer_terms[f]], fact_ref, OUTER_ZONE + f)[0]
     friction = GRAD_WEIGHT * jnp.sum(friction, axis=0, keepdims=True)
-    conduct = GRAD_WEIGHT * jnp.sum(conduct, axis=0, keepdims=True) / conduct_ref[...]
+    conduct = GRAD_WEIGHT * jnp.sum(conduct, axis=0, keepdims=True)
+    factors = [
+        stat_ref[CONDUCTIVITY * SUB + n : CONDUCTIVITY * SUB + n + 1, :]
+        for n in range(zones // LANES)
+    ]
+    conduct = conduct / jnp.concatenate(factors, axis=1)
     for device in range(out_ref.shape[0]):
         out_ref[device, 0:1, :] = friction
         out_ref[device, 1:2, :] = conduct
 
 
-def local_zero_kernel(y_ref, index_ref, outer_ref):
+def local_zero_kernel(y_ref, plan_ref, outer_ref):
+    index_ref = plan_parts(plan_ref)[1]
     local_states(y_ref, 0, y_ref.shape[0] // SUB // 3, index_ref, outer_ref)
 
 
@@ -745,13 +818,9 @@
     base_ref,
     lam_ref,
     y_ref,
-    stat_ref,
-    index_ref,
+    plan_ref,
     fact_ref,
     near_outer_ref,
-    in_ref,
-    out_ref,
-    volume_ref,
     from_x1,
     from_x2,
     from_y1,
@@ -760,7 +829,11 @@
     last_ref,
     outer_ref,
     corner_ref,
+    matrix_ref,
+    sem,
 ):
+    matrices = load_matrices(plan_ref, matrix_ref, sem)
+    stat_ref, index_ref, _, _ = plan_parts(plan_ref)
     rows = lam_ref.shape[0] // SUB
     channels = rows // 3 * 2
     received = Received((from_x1, from_x2, from_y1, from_y2), channels, corner_ref)
@@ -769,8 +842,9 @@
     def emit(r, value):
         put(adjoint_ref, r, tile(base_ref, r) + TIME_STEP * value)
 
+    matrices.wait()
     transposed_section(
-        0, lam_ref, y_ref, outer_ref, stat_ref, fact_ref, in_ref, out_ref, volume_ref, emit
+        0, lam_ref, y_ref, outer_ref, stat_ref, fact_ref, matrix_ref, emit
     )
     last_ref[...] = tile(adjoint_ref, rows - 1)
 
@@ -779,31 +853,30 @@
     grads_ref[...] = jnp.sum(zone_ref[...], axis=0)
 
 
-def exchange(channels, messages, ahead=()):
+def exchange(channels, messages, ahead):
     x1, x2, y1, y2 = messages
     x1, x2 = swapped(x1, "gx", 0), swapped(x2, "gx", 1)
-    y1, y2 = call(
+    y1, y2, ahead = call(
         functools.partial(corner_kernel, channels),
         "corners",
-        [jax.ShapeDtypeStruct(y1.shape, y1.dtype)] * 2,
+        [jax.ShapeDtypeStruct(one.shape, one.dtype) for one in (y1, y2, ahead)],
         [],
-        [x1, x2, y1, y2, *ahead],
-        aliases={2: 0, 3: 1},
-    )
-    return x1, x2, swapped(y1, "gy", 0), swapped(y2, "gy", 1)
-
-
-def call(kernel, name, outs, scratch, operands, scalars=(), far=False, aliases={}):
-    in_memory = pl.BlockSpec(memory_space=pltpu.VMEM)
-    in_scalar = pl.BlockSpec(memory_space=pltpu.SMEM)
+        [x1, x2, y1, y2, ahead],
+        apart=(4,),
+        aliases={2: 0, 3: 1, 4: 2},
+    )
+    return (x1, x2, swapped(y1, "gy", 0), swapped(y2, "gy", 1)), ahead
+
+
+def call(kernel, name, outs, scratch, operands, far=False, apart=(), aliases={}):
+    near = pl.BlockSpec(memory_space=pltpu.VMEM)
     in_place = pl.BlockSpec(memory_space=pl.ANY)
+    specs = [in_place if far or n in apart else near for n in range(len(operands))]
+    handed_on = [aliases[n] for n in apart]
     return pl.pallas_call(
         kernel,
-        in_specs=[
-            in_place if far else in_scalar if n in scalars else in_memory
-            for n in range(len(operands))
-        ],
-        out_specs=[in_memory] * len(outs),
+        in_specs=specs,
+        out_specs=[in_place if n in handed_on else near for n in range(len(outs))],
         out_shape=outs,
         scratch_shapes=scratch,
         input_output_aliases=aliases,
@@ -848,23 +921,25 @@
     def messages(count):
         return [jax.ShapeDtypeStruct((slots // LANES, message_rows(count), LANES), f32)] * 4
 
-    def sent_scratch(count):
-        return pltpu.VMEM(sent_shape(count), f32)
-
-    def sent_shape(count):
-        return (slots // LANES, corner_rows(count) * SUB * SUB, LANES)
-
-    corner_scratch = pltpu.VMEM((SUB, LANES), f32)
+    def sent_tiles(count):
+        return corner_rows(count) * SUB
+
+    section_scratch = [
+        pltpu.VMEM((SUB, LANES), f32),
+        pltpu.SMEM((MATRIX_ROWS * SUB, LANES), f32),
+        pltpu.SemaphoreType.DMA((1,)),
+    ]
 
     square = lambda one: one.reshape(SUB, LANES)
     cot = cotangent.reshape(rows * SUB, LANES)
-    table, stat, index, *to_send = call(
+    plan, *to_send = call(
         prepare_kernel,
         "prepare",
-        [tiles(rows + 13), tiles(STAT_ROWS), tiles(INDEX_ROWS, jnp.int32)]
-        + messages(channels + 5),
-        [tile_scratch(16), sent_scratch(channels + 5)]
-        + [
+        [tiles(plan_rows(rows))] + messages(channels + 5),
+        [
+            tile_scratch(16),
+            tile_scratch(sent_tiles(channels + 5)),
+            tile_scratch(1),
             tile_scratch(3, jnp.int32),
             pltpu.VMEM(send_face.shape, jnp.int32),
             tile_scratch(rows),
@@ -877,7 +952,10 @@
             pltpu.VMEM((zones // LANES, LANES), f32),
             tile_scratch(1, jnp.int32),
             tile_scratch(1, jnp.int32),
-            pltpu.SemaphoreType.DMA((12,)),
+            pltpu.VMEM(flux_in.shape, f32),
+            pltpu.VMEM(flux_out.shape, f32),
+            pltpu.VMEM(volume_matrix.shape, f32),
+            pltpu.SemaphoreType.DMA((15,)),
         ],
         [
             cot,
@@ -892,84 +970,66 @@
             square(element_zone),
             send_face,
             face_partner.reshape(3 * SUB, LANES),
+            flux_in,
+            flux_out,
+            volume_matrix,
         ],
         far=True,
     )
-    matrices = [flux_in, flux_out, volume_matrix]
     near_outer, near, term = call(
         local_two_kernel,
         "local_two",
         [tiles(3 * channels), tiles(15), tiles(2)],
         [tile_scratch(rows)],
-        [cot, table, stat, index, section_states],
-    )
-    x_near, x_sent = call(
+        [cot, plan, section_states],
+    )
+    x_near, x_sent, x_packed = call(
         local_x_kernel,
         "local_x",
-        [
-            tiles(3 * (channels - 8)),
-            jax.ShapeDtypeStruct(sent_shape(channels - 8), f32),
-        ],
+        [tiles(3 * (channels - 8)), tiles(sent_tiles(channels - 8)), tiles(1)],
         [tile_scratch(rows)],
-        [index, section_states],
-    )
-    received = exchange(channels + 5, to_send, [term])
+        [plan, section_states],
+    )
+    received, term = exchange(channels + 5, to_send, term)
     lam, y, fact, outer, *to_send = call(
         second_kernel,
         "section_two",
         [tiles(rows), tiles(rows), tiles(FACT_ROWS), tiles(3 * channels)]
         + messages(X_ROWS + channels),
-        [sent_scratch(channels), corner_scratch],
-        [cot, table, stat, index, near_outer, near, x_sent, *matrices, *received],
-        (7, 8, 9),
+        [tile_scratch(sent_tiles(channels)), tile_scratch(1)] + section_scratch,
+        [cot, plan, near_outer, near, x_sent, x_packed, *received],
     )
     near_outer, term = call(
         local_one_kernel,
         "local_one",
         [tiles(3 * channels), tiles(5)],
         [tile_scratch(rows)],
-        [lam, y, stat, index, fact, outer, term, section_states],
-    )
-    received = exchange(X_ROWS + channels, to_send, [term])
+        [lam, y, plan, fact, outer, term, section_states],
+    )
+    received, term = exchange(X_ROWS + channels, to_send, term)
     base, lam, y, outer, *to_send = call(
         first_kernel,
         "section_one",
         [tiles(rows), tiles(rows), tiles(rows), tiles(3 * channels)] + messages(channels),
-        [sent_scratch(channels), corner_scratch],
-        [cot, lam, y, stat, index, fact, near_outer, *matrices, *received],
-        (7, 8, 9),
+        [tile_scratch(sent_tiles(channels)), tile_scratch(1)] + section_scratch,
+        [cot, lam, y, plan, fact, near_outer, *received],
     )
     (zone_terms,) = call(
         zone_kernel,
         "zone_sums",
         [jax.ShapeDtypeStruct((devices, 2, zones), f32)],
-        [tile_scratch(3 * (channels - 8)), tile_scratch(rows), corner_scratch],
-        [
-            lam,
-            y,
-            stat,
-            index,
-            fact,
-            outer,
-            term,
-            section_states,
-            x_near,
-            zone_conductivity.reshape(1, zones),
-            *received,
-        ],
-    )
-    received = exchange(channels, to_send, [zone_terms])
+        [tile_scratch(3 * (channels - 8)), tile_scratch(rows), tile_scratch(1)],
+        [lam, y, plan, fact, outer, term, section_states, x_near, *received],
+    )
+    received, zone_terms = exchange(channels, to_send, zone_terms)
     all_terms = lax.all_to_all(zone_terms, ("gx", "gy"), 0, 0)
-    (near_outer,) = call(
-        local_zero_kernel, "local_zero", [tiles(3 * channels)], [], [y, index]
-    )
+    (near_outer,) = call(local_zero_kernel, "local_zero", [tiles(3 * channels)], [], [y, plan])
     adjoint, last = call(
         last_kernel,
         "section_zero",
         [tiles(rows), tiles(1)],
-        [tile_scratch(3 * channels), corner_scratch],
-        [base, lam, y, stat, index, fact, near_outer, *matrices, *received],
-        (7, 8, 9),
+        [tile_scratch(3 * channels)] + section_scratch,
+        [base, lam, y, plan, fact, near_outer, *received],
     )
     (zone_grads,) = call(
         total_kernel,

time: 63.5 us -> 60 us (0.945)
  local copies, waits for them, and re-layouts: 3.42 us -> 1 us
  Pallas kernels: 22.5 us -> 21.1 us
  starting transfers between devices: 32.7 us -> 33.6 us
    unnamed x28 -> x12, local copies, waits for them, and re-layouts: 3.42 us -> 1 us
    pallas_call x13, Pallas kernels: 22.5 us -> 21.1 us  [call(): pl.pallas_call(kernel, in_specs=specs, out_specs=[in_place if n in handed...]
    all_to_all x1, starting transfers between devices: 8.58 us -> 9.55 us  [local(): all_terms = lax.all_to_all(zone_terms, ('gx', 'gy'), 0, 0)]
  transfers between devices with their start and end apart: 13 -> 13, of which waited for: 3 -> 3; matrix products, arithmetic and copies ran while one was open for 0% -> 0% of each run, Pallas kernels for 19% -> 18%
where the time goes in v8:
time: 60 us; the launch traced here: 59.7 us
  starting transfers between devices  33.6 us (56%)
  Pallas kernels  21.1 us (35%)
  waiting for transfers between devices  3.12 us (5%)
  local copies, waits for them, and re-layouts  1 us (2%)
  between operations  0.9 us (2%)
    ppermute x12, starting transfers between devices, swapped(): lax.ppermute(x, axis, [(i, i + 1) for i in lows] + [(i + 1, i) for i in l...  24 us
    pallas_call x13, Pallas kernels, call(): pl.pallas_call(kernel, in_specs=specs, out_specs=[in_place if n in handed...  21.1 us
    all_to_all x1, starting transfers between devices, local(): all_terms = lax.all_to_all(zone_terms, ('gx', 'gy'), 0, 0)  9.55 us
    ppermute x12, waiting for transfers between devices, swapped(): lax.ppermute(x, axis, [(i, i + 1) for i in lows] + [(i + 1, i) for i in l...  3.12 us
  transfers between devices with their start and end apart: 13, of which 3 were waited for; matrix products, arithmetic and copies ran while one was open for 0% of the time, Pallas kernels for 18%

profile of v8, /device:TPU:1, one launch (start us, length us, event | category | flops | bytes accessed | tf_op | source)
XLA Modules:
  0.0 59.7 jit_solution(13142065755875643590)
XLA Ops:
  0.7 3.5 %prepare.1 = (f32[720,128]{1,0:T(8,128)}, f32[2,38,128]{2,1,0:T(8,128)}, f32[2,38,128]{2,1,0:T(8,128)}, f32[2,38,128]{2,1,0:T(8,128)}, f32[2,38,128]{2,1,0:T(8,128)}) custom-call(f32[336,128]{1,0:T(8,128)} %bitcast.11, bf16[3,1,1,42,1024]{4,3,2,1,0:T(8,128)(2,1)} %x_ref.9, f32[8,128]{1,0:T(8,128)} %bitcast.17, f32[24,128]{1,0:T(8,128)} %bitcast.15, ...), custom_call_target="tpu_custom_call" | custom-call | tf_op jit(solution)/shard_map/prepare/pallas_call | solution.py:876
  4.2 2.1 %collective-permute-start = (f32[2,38,128]{2,1,0:T(8,128)}, f32[2,38,128]{2,1,0:T(8,128)S(1)}, u32[]{:S(2)}, u32[]{:S(2)}) collective-permute-start(f32[2,38,128]{2,1,0:T(8,128)} %get-tuple-element.47), channel_id=1, source_target_pairs={{0,4},{8,12},{16,20},{24,28},{4,0},{12,8},{20,16},{28,24},{1,5},{9... | collective-permute-start | bytes 116744 | tf_op jit(solution)/shard_map/ppermute | solution.py:42
  6.3 0.7 %collective-permute-start.1 = (f32[2,38,128]{2,1,0:T(8,128)}, f32[2,38,128]{2,1,0:T(8,128)S(1)}, u32[]{:S(2)}, u32[]{:S(2)}) collective-permute-start(f32[2,38,128]{2,1,0:T(8,128)} %get-tuple-element.48), channel_id=1, source_target_pairs={{4,8},{12,16},{20,24},{8,4},{16,12},{24,20},{5,9},{13,17},{21,25},... | collective-permute-start | bytes 116744 | tf_op jit(solution)/shard_map/ppermute | solution.py:42
  7.0 1.0 %copy-done = f32[720,128]{1,0:T(8,128)S(1)} copy-done((f32[720,128]{1,0:T(8,128)S(1)}, f32[720,128]{1,0:T(8,128)}, u32[]{:S(2)}) %copy-start) | copy-done | bytes 368664
  8.0 1.7 %local_two.1 = (f32[672,128]{1,0:T(8,128)S(1)}, f32[120,128]{1,0:T(8,128)S(1)}, f32[16,128]{1,0:T(8,128)S(1)}) custom-call(f32[336,128]{1,0:T(8,128)S(1)} %bitcast.12, f32[720,128]{1,0:T(8,128)S(1)} %copy-done, bf16[3,1,1,42,1024]{4,3,2,1,0:T(8,128)(2,1)S(1)} %copy-done.2), custom_call_target="tpu_custom_call" | custom-call | tf_op jit(solution)/shard_map/local_two/pallas_call | solution.py:876
  9.7 0.0 collective-permute-done.1.x2.from_x2
  9.7 1.0 %collective-permute-start.2 = (f32[2,38,128]{2,1,0:T(8,128)S(1)}, f32[2,38,128]{2,1,0:T(8,128)S(1)}, u32[]{:S(2)}, u32[]{:S(2)}) collective-permute-start(f32[2,38,128]{2,1,0:T(8,128)S(1)} %get-tuple-element.52), channel_id=1, source_target_pairs={{0,1},{2,3},{1,0},{3,2},{4,5},{6,7},{5,4},{7,6},{8,9},{10,11},{9,8... | collective-permute-start | bytes 116744 | tf_op jit(solution)/shard_map/ppermute | solution.py:42
  10.7 3.0 %collective-permute-start.3 = (f32[2,38,128]{2,1,0:T(8,128)S(1)}, f32[2,38,128]{2,1,0:T(8,128)S(1)}, u32[]{:S(2)}, u32[]{:S(2)}) collective-permute-start(f32[2,38,128]{2,1,0:T(8,128)S(1)} %get-tuple-element.53), channel_id=1, source_target_pairs={{1,2},{2,1},{5,6},{6,5},{9,10},{10,9},{13,14},{14,13},{17,18},{18,... | collective-permute-start | bytes 116744 | tf_op jit(solution)/shard_map/ppermute | solution.py:42
  13.8 2.0 %local_x.1 = (f32[480,128]{1,0:T(8,128)S(1)}, f32[192,128]{1,0:T(8,128)S(1)}, f32[8,128]{1,0:T(8,128)S(1)}) custom-call(f32[720,128]{1,0:T(8,128)S(1)} %copy-done.1, bf16[3,1,1,42,1024]{4,3,2,1,0:T(8,128)(2,1)S(1)} %copy-done.2), custom_call_target="tpu_custom_call" | custom-call | tf_op jit(solution)/shard_map/local_x/pallas_call | solution.py:876
  15.8 0.2 collective-permute-done.3.from_y2
  16.1 3.1 %section_two.1 = (f32[336,128]{1,0:T(8,128)S(1)}, f32[336,128]{1,0:T(8,128)S(1)}, f32[120,128]{1,0:T(8,128)S(1)}, f32[672,128]{1,0:T(8,128)S(1)}, f32[2,59,128]{...) custom-call(f32[336,128]{1,0:T(8,128)S(1)} %bitcast.13, ...), custom_call_target="tpu_custom_call" | custom-call | tf_op jit(solution)/shard_map/section_two/pallas_call | solution.py:876
  19.2 4.1 %collective-permute-start.4 = (f32[2,59,128]{2,1,0:T(8,128)S(1)}, f32[2,59,128]{2,1,0:T(8,128)S(1)}, u32[]{:S(2)}, u32[]{:S(2)}) collective-permute-start(f32[2,59,128]{2,1,0:T(8,128)S(1)} %get-tuple-element.60), channel_id=1, source_target_pairs={{0,4},{8,12},{16,20},{24,28},{4,0},{12,8},{20,16},{28,24},{1,5},{9... | collective-permute-start | bytes 181256 | tf_op jit(solution)/shard_map/ppermute | solution.py:42
  23.2 0.7 %collective-permute-start.5 = (f32[2,59,128]{2,1,0:T(8,128)S(1)}, f32[2,59,128]{2,1,0:T(8,128)S(1)}, u32[]{:S(2)}, u32[]{:S(2)}) collective-permute-start(f32[2,59,128]{2,1,0:T(8,128)S(1)} %get-tuple-element.61), channel_id=1, source_target_pairs={{4,8},{12,16},{20,24},{8,4},{16,12},{24,20},{5,9},{13,17},{21,25},... | collective-permute-start | bytes 181256 | tf_op jit(solution)/shard_map/ppermute | solution.py:42
  23.9 1.4 %local_one.1 = (f32[672,128]{1,0:T(8,128)S(1)}, f32[40,128]{1,0:T(8,128)S(1)}) custom-call(f32[336,128]{1,0:T(8,128)S(1)} %get-tuple-element.54.lam_ref, f32[336,128]{1,0:T(8,128)S(1)} %get-tuple-element.55.y_ref, f32[720,128]{1,0:T(8,128)S(1)} %copy-done.1, f32[120,128]{1,0:T(8,128)S(1)} %get-tuple-element.56.fact_ref, ...), custom_call_target="tpu_custom_call" | custom-call | tf_op jit(solution)/shard_map/local_one/pallas_call | solution.py:876
  25.3 0.0 collective-permute-done.4.x1.from_x1
  25.3 0.0 collective-permute-done.5.x2.from_x2
  25.3 0.1 collective-permute-start.6
  25.4 3.5 %collective-permute-start.7 = (f32[2,59,128]{2,1,0:T(8,128)S(1)}, f32[2,59,128]{2,1,0:T(8,128)S(1)}, u32[]{:S(2)}, u32[]{:S(2)}) collective-permute-start(f32[2,59,128]{2,1,0:T(8,128)S(1)} %get-tuple-element.66), channel_id=1, source_target_pairs={{1,2},{2,1},{5,6},{6,5},{9,10},{10,9},{13,14},{14,13},{17,18},{18,... | collective-permute-start | bytes 181256 | tf_op jit(solution)/shard_map/ppermute | solution.py:42
  28.9 0.0 collective-permute-done.6.from_y1
  29.0 2.0 %collective-permute-done.7.from_y2 = f32[2,59,128]{2,1,0:T(8,128)S(1)} collective-permute-done((f32[2,59,128]{2,1,0:T(8,128)S(1)}, f32[2,59,128]{2,1,0:T(8,128)S(1)}, u32[]{:S(2)}, u32[]{:S(2)}) %collective-permute-start.7) | collective-permute-done | bytes 60448 | tf_op jit(solution)/shard_map/ppermute | solution.py:42
  31.0 2.9 %section_one.1 = (f32[336,128]{1,0:T(8,128)S(1)}, f32[336,128]{1,0:T(8,128)S(1)}, f32[336,128]{1,0:T(8,128)S(1)}, f32[672,128]{1,0:T(8,128)S(1)}, f32[2,32,128]{...) custom-call(f32[336,128]{1,0:T(8,128)S(1)} %bitcast.14, ...), custom_call_target="tpu_custom_call" | custom-call | tf_op jit(solution)/shard_map/section_one/pallas_call | solution.py:876
  33.9 4.5 %collective-permute-start.8 = (f32[2,32,128]{2,1,0:T(8,128)S(1)}, f32[2,32,128]{2,1,0:T(8,128)S(1)}, u32[]{:S(2)}, u32[]{:S(2)}) collective-permute-start(f32[2,32,128]{2,1,0:T(8,128)S(1)} %get-tuple-element.70), channel_id=1, source_target_pairs={{0,4},{8,12},{16,20},{24,28},{4,0},{12,8},{20,16},{28,24},{1,5},{9... | collective-permute-start | bytes 98312 | tf_op jit(solution)/shard_map/ppermute | solution.py:42
  38.4 0.7 %collective-permute-start.9 = (f32[2,32,128]{2,1,0:T(8,128)S(1)}, f32[2,32,128]{2,1,0:T(8,128)S(1)}, u32[]{:S(2)}, u32[]{:S(2)}) collective-permute-start(f32[2,32,128]{2,1,0:T(8,128)S(1)} %get-tuple-element.71), channel_id=1, source_target_pairs={{4,8},{12,16},{20,24},{8,4},{16,12},{24,20},{5,9},{13,17},{21,25},... | collective-permute-start | bytes 98312 | tf_op jit(solution)/shard_map/ppermute | solution.py:42
  39.0 2.3 %zone_sums.1.rest_0_ = f32[32,2,128]{2,1,0:T(2,128)} custom-call(f32[336,128]{1,0:T(8,128)S(1)} %get-tuple-element.68.lam_ref, f32[336,128]{1,0:T(8,128)S(1)} %get-tuple-element.69.y_ref, f32[720,128]{1,0:T(8,128)S(1)} %copy-done.1, f32[120,128]{1,0:T(8,128)S(1)} %get-tuple-element.56.fact_ref, f32[672,128]{1,0:T(8,128)S(1)} %get-tuple-element.74.old_outer_ref, ...), custom_call_target="tpu_custom_call" | custom-call | tf_op jit(solution)/shard_map/zone_sums/pallas_call | solution.py:876
  41.4 0.0 collective-permute-done.8.x1.from_x1
  41.4 9.6 %all-to-all-start = ((f32[32,2,128]{2,1,0:T(2,128)}), f32[32,2,128]{2,1,0:T(2,128)S(1)}, u32[]{:S(2)}, u32[]{:S(2)}) async-start(f32[32,2,128]{2,1,0:T(2,128)} %get-tuple-element.80), calls=%async_computation | async-start | bytes 65536 | tf_op jit(solution)/shard_map/all_to_all | solution.py:1025
  51.0 0.3 collective-permute-start.10
  51.3 3.4 %collective-permute-start.11 = (f32[2,32,128]{2,1,0:T(8,128)S(1)}, f32[2,32,128]{2,1,0:T(8,128)S(1)}, u32[]{:S(2)}, u32[]{:S(2)}) collective-permute-start(f32[2,32,128]{2,1,0:T(8,128)S(1)} %get-tuple-element.78), channel_id=1, source_target_pairs={{1,2},{2,1},{5,6},{6,5},{9,10},{10,9},{13,14},{14,13},{17,18},{18,... | collective-permute-start | bytes 98312 | tf_op jit(solution)/shard_map/ppermute | solution.py:42
  54.7 1.3 %local_zero.1.near_outer_ref = f32[672,128]{1,0:T(8,128)S(1)} custom-call(f32[336,128]{1,0:T(8,128)S(1)} %get-tuple-element.69.y_ref, f32[720,128]{1,0:T(8,128)S(1)} %copy-done.1), custom_call_target="tpu_custom_call" | custom-call | tf_op jit(solution)/shard_map/local_zero/pallas_call | solution.py:876
  56.0 0.8 %collective-permute-done.11.from_y2 = f32[2,32,128]{2,1,0:T(8,128)S(1)} collective-permute-done((f32[2,32,128]{2,1,0:T(8,128)S(1)}, f32[2,32,128]{2,1,0:T(8,128)S(1)}, u32[]{:S(2)}, u32[]{:S(2)}) %collective-permute-start.11) | collective-permute-done | bytes 32800 | tf_op jit(solution)/shard_map/ppermute | solution.py:42
  56.9 2.2 %section_zero.1 = (f32[336,128]{1,0:T(8,128)}, f32[8,128]{1,0:T(8,128)S(1)}) custom-call(f32[336,128]{1,0:T(8,128)S(1)} %get-tuple-element.67.base_ref, f32[336,128]{1,0:T(8,128)S(1)} %get-tuple-element.68.lam_ref, f32[336,128]{1,0:T(8,128)S(1)} %get-tuple-element.69.y_ref, f32[720,128]{1,0:T(8,128)S(1)} %copy-done.1, ...), custom_call_target="tpu_custom_call" | custom-call | tf_op jit(solution)/shard_map/section_zero/pallas_call | solution.py:876
  59.1 0.6 %zone_total.1 = f32[2,128]{1,0:T(2,128)} custom-call(f32[32,2,128]{2,1,0:T(2,128)S(1)} %all-to-all-done.zone_ref, f32[8,128]{1,0:T(8,128)S(1)} %get-tuple-element.81.adjoint_ref), custom_call_target="tpu_custom_call" | custom-call | tf_op jit(solution)/shard_map/zone_total/pallas_call | solution.py:876
  (19 shorter events, 0.1 us)
Async XLA Ops:
  0.6 6.3 %copy-start.2 = (bf16[3,1,1,42,1024]{4,3,2,1,0:T(8,128)(2,1)S(1)}, bf16[3,1,1,42,1024]{4,3,2,1,0:T(8,128)(2,1)}, u32[]{:S(2)}) copy-start(bf16[3,1,1,42,1024]{4,3,2,1,0:T(8,128)(2,1)} %x_ref.9) | copy-start | bytes 774148
  0.6 6.3 %copy-start.3 = (f32[1,1,42,1024]{3,1,2,0:T(1,128)S(1)}, f32[1,1,42,1024]{3,1,2,0:T(1,128)}, u32[]{:S(2)}) copy-start(f32[1,1,42,1024]{3,1,2,0:T(1,128)} %param.16) | copy-start | bytes 516100
  4.2 5.5 %collective-permute-start = (f32[2,38,128]{2,1,0:T(8,128)}, f32[2,38,128]{2,1,0:T(8,128)S(1)}, u32[]{:S(2)}, u32[]{:S(2)}) collective-permute-start(f32[2,38,128]{2,1,0:T(8,128)} %get-tuple-element.47), channel_id=1, source_target_pairs={{0,4},{8,12},{16,20},{24,28},{4,0},{12,8},{20,16},{28,24},{1,5},{9... | collective-permute-start | bytes 116744 | tf_op jit(solution)/shard_map/ppermute | solution.py:42
  6.3 3.4 %collective-permute-start.1 = (f32[2,38,128]{2,1,0:T(8,128)}, f32[2,38,128]{2,1,0:T(8,128)S(1)}, u32[]{:S(2)}, u32[]{:S(2)}) collective-permute-start(f32[2,38,128]{2,1,0:T(8,128)} %get-tuple-element.48), channel_id=1, source_target_pairs={{4,8},{12,16},{20,24},{8,4},{16,12},{24,20},{5,9},{13,17},{21,25},... | collective-permute-start | bytes 116744 | tf_op jit(solution)/shard_map/ppermute | solution.py:42
  7.0 1.0 %copy-start = (f32[720,128]{1,0:T(8,128)S(1)}, f32[720,128]{1,0:T(8,128)}, u32[]{:S(2)}) copy-start(f32[720,128]{1,0:T(8,128)} %get-tuple-element.42.plan_ref) | copy-start | bytes 1105924
  8.0 1.7 %copy-start.4 = (f32[2,38,128]{2,1,0:T(8,128)S(1)}, f32[2,38,128]{2,1,0:T(8,128)}, u32[]{:S(2)}) copy-start(f32[2,38,128]{2,1,0:T(8,128)} %get-tuple-element.49.old_y1) | copy-start | bytes 116740
  8.0 1.7 %copy-start.5 = (f32[2,38,128]{2,1,0:T(8,128)S(1)}, f32[2,38,128]{2,1,0:T(8,128)}, u32[]{:S(2)}) copy-start(f32[2,38,128]{2,1,0:T(8,128)} %get-tuple-element.50.old_y2) | copy-start | bytes 116740
  8.0 5.8 %copy-start.1 = (f32[720,128]{1,0:T(8,128)S(1)}, f32[720,128]{1,0:T(8,128)}, u32[]{:S(2)}) copy-start(f32[720,128]{1,0:T(8,128)} %get-tuple-element.42.plan_ref) | copy-start | bytes 1105924
  9.7 6.1 %collective-permute-start.2 = (f32[2,38,128]{2,1,0:T(8,128)S(1)}, f32[2,38,128]{2,1,0:T(8,128)S(1)}, u32[]{:S(2)}, u32[]{:S(2)}) collective-permute-start(f32[2,38,128]{2,1,0:T(8,128)S(1)} %get-tuple-element.52), channel_id=1, source_target_pairs={{0,1},{2,3},{1,0},{3,2},{4,5},{6,7},{5,4},{7,6},{8,9},{10,11},{9,8... | collective-permute-start | bytes 116744 | tf_op jit(solution)/shard_map/ppermute | solution.py:42
  10.7 5.3 %collective-permute-start.3 = (f32[2,38,128]{2,1,0:T(8,128)S(1)}, f32[2,38,128]{2,1,0:T(8,128)S(1)}, u32[]{:S(2)}, u32[]{:S(2)}) collective-permute-start(f32[2,38,128]{2,1,0:T(8,128)S(1)} %get-tuple-element.53), channel_id=1, source_target_pairs={{1,2},{2,1},{5,6},{6,5},{9,10},{10,9},{13,14},{14,13},{17,18},{18,... | collective-permute-start | bytes 116744 | tf_op jit(solution)/shard_map/ppermute | solution.py:42
  19.2 6.1 %collective-permute-start.4 = (f32[2,59,128]{2,1,0:T(8,128)S(1)}, f32[2,59,128]{2,1,0:T(8,128)S(1)}, u32[]{:S(2)}, u32[]{:S(2)}) collective-permute-start(f32[2,59,128]{2,1,0:T(8,128)S(1)} %get-tuple-element.60), channel_id=1, source_target_pairs={{0,4},{8,12},{16,20},{24,28},{4,0},{12,8},{20,16},{28,24},{1,5},{9... | collective-permute-start | bytes 181256 | tf_op jit(solution)/shard_map/ppermute | solution.py:42
  23.2 2.1 %collective-permute-start.5 = (f32[2,59,128]{2,1,0:T(8,128)S(1)}, f32[2,59,128]{2,1,0:T(8,128)S(1)}, u32[]{:S(2)}, u32[]{:S(2)}) collective-permute-start(f32[2,59,128]{2,1,0:T(8,128)S(1)} %get-tuple-element.61), channel_id=1, source_target_pairs={{4,8},{12,16},{20,24},{8,4},{16,12},{24,20},{5,9},{13,17},{21,25},... | collective-permute-start | bytes 181256 | tf_op jit(solution)/shard_map/ppermute | solution.py:42
  25.3 3.6 %collective-permute-start.6 = (f32[2,59,128]{2,1,0:T(8,128)S(1)}, f32[2,59,128]{2,1,0:T(8,128)S(1)}, u32[]{:S(2)}, u32[]{:S(2)}) collective-permute-start(f32[2,59,128]{2,1,0:T(8,128)S(1)} %get-tuple-element.65), channel_id=1, source_target_pairs={{0,1},{2,3},{1,0},{3,2},{4,5},{6,7},{5,4},{7,6},{8,9},{10,11},{9,8... | collective-permute-start | bytes 181256 | tf_op jit(solution)/shard_map/ppermute | solution.py:42
  25.4 5.6 %collective-permute-start.7 = (f32[2,59,128]{2,1,0:T(8,128)S(1)}, f32[2,59,128]{2,1,0:T(8,128)S(1)}, u32[]{:S(2)}, u32[]{:S(2)}) collective-permute-start(f32[2,59,128]{2,1,0:T(8,128)S(1)} %get-tuple-element.66), channel_id=1, source_target_pairs={{1,2},{2,1},{5,6},{6,5},{9,10},{10,9},{13,14},{14,13},{17,18},{18,... | collective-permute-start | bytes 181256 | tf_op jit(solution)/shard_map/ppermute | solution.py:42
  33.9 7.5 %collective-permute-start.8 = (f32[2,32,128]{2,1,0:T(8,128)S(1)}, f32[2,32,128]{2,1,0:T(8,128)S(1)}, u32[]{:S(2)}, u32[]{:S(2)}) collective-permute-start(f32[2,32,128]{2,1,0:T(8,128)S(1)} %get-tuple-element.70), channel_id=1, source_target_pairs={{0,4},{8,12},{16,20},{24,28},{4,0},{12,8},{20,16},{28,24},{1,5},{9... | collective-permute-start | bytes 98312 | tf_op jit(solution)/shard_map/ppermute | solution.py:42
  38.4 3.0 %collective-permute-start.9 = (f32[2,32,128]{2,1,0:T(8,128)S(1)}, f32[2,32,128]{2,1,0:T(8,128)S(1)}, u32[]{:S(2)}, u32[]{:S(2)}) collective-permute-start(f32[2,32,128]{2,1,0:T(8,128)S(1)} %get-tuple-element.71), channel_id=1, source_target_pairs={{4,8},{12,16},{20,24},{8,4},{16,12},{24,20},{5,9},{13,17},{21,25},... | collective-permute-start | bytes 98312 | tf_op jit(solution)/shard_map/ppermute | solution.py:42
  41.4 17.7 %all-to-all-start = ((f32[32,2,128]{2,1,0:T(2,128)}), f32[32,2,128]{2,1,0:T(2,128)S(1)}, u32[]{:S(2)}, u32[]{:S(2)}) async-start(f32[32,2,128]{2,1,0:T(2,128)} %get-tuple-element.80), calls=%async_computation | async-start | bytes 65536 | tf_op jit(solution)/shard_map/all_to_all | solution.py:1025
  51.0 5.0 %collective-permute-start.10 = (f32[2,32,128]{2,1,0:T(8,128)S(1)}, f32[2,32,128]{2,1,0:T(8,128)S(1)}, u32[]{:S(2)}, u32[]{:S(2)}) collective-permute-start(f32[2,32,128]{2,1,0:T(8,128)S(1)} %get-tuple-element.77), channel_id=1, source_target_pairs={{0,1},{2,3},{1,0},{3,2},{4,5},{6,7},{5,4},{7,6},{8,9},{10,11},{9,8... | collective-permute-start | bytes 98312 | tf_op jit(solution)/shard_map/ppermute | solution.py:42
  51.3 5.6 %collective-permute-start.11 = (f32[2,32,128]{2,1,0:T(8,128)S(1)}, f32[2,32,128]{2,1,0:T(8,128)S(1)}, u32[]{:S(2)}, u32[]{:S(2)}) collective-permute-start(f32[2,32,128]{2,1,0:T(8,128)S(1)} %get-tuple-element.78), channel_id=1, source_target_pairs={{1,2},{2,1},{5,6},{6,5},{9,10},{10,9},{13,14},{14,13},{17,18},{18,... | collective-permute-start | bytes 98312 | tf_op jit(solution)/shard_map/ppermute | solution.py:42

commit v9 on v8

--- a/solution.py
+++ b/solution.py
@@ -296,7 +296,7 @@
     matrix_ref[16:28, 0:12] = volume_ref[...]
     rows = cot_ref.shape[0] // SUB
     sections = x_ref.shape[0]
-    odd_a, odd_b = lax.axis_index("gx") % 2, lax.axis_index("gy") % 2
+    odd_a, odd_b = 1 - lax.axis_index("gx") % 2, 1 - lax.axis_index("gy") % 2
     straight = (6 - 5 * odd_a, 1 + 5 * odd_a, 4 - odd_b, 3 + odd_b)
     right, up = 1 - odd_a, 1 - odd_b
     corners = (
@@ -445,15 +445,10 @@
     lax.fori_loop(0, 3, body, 0)
 
 
-def transposed_section(
-    section, lam_ref, y_ref, outer_ref, stat_ref, fact_ref, matrix_ref, emit
-):
+def transposed_own(section, lam_ref, y_ref, stat_ref, matrix_ref, own_ref):
     rows = lam_ref.shape[0] // SUB
-    channels = rows // 3 * 2
     layers = (rows - 12) // 3
     edge = [tile(stat_ref, EDGE + f) for f in range(3)]
-    outer_edge = [tile(fact_ref, OUTER_EDGE + f) for f in range(3)]
-    half_speed = [tile(fact_ref, HALF_SPEED + 3 * section + f) for f in range(3)]
     kappa = tile(stat_ref, KAPPA)
     wet = tile(stat_ref, WET)
     own = [tile(y_ref, r) for r in range(12)]
@@ -466,11 +461,10 @@
     for f in range(3):
         ends = FACE_NODES[f]
         inner = [edge[f] * own[(ch // 2) * 3 + ends[ch % 2]] for ch in range(8)]
-        outer = [outer_edge[f] * tile(outer_ref, f * channels + ch) for ch in range(8)]
         for b in range(8):
-            total = half_speed[f] * (inner[b] - outer[b])
-            for a in range(8):
-                total = total + matrix_ref[a, b] * inner[a] - matrix_ref[8 + a, b] * outer[a]
+            total = matrix_ref[0, b] * inner[0]
+            for a in range(1, 8):
+                total = total + matrix_ref[a, b] * inner[a]
             at = (b // 2) * 3 + ends[b % 2]
             result[at] = result[at] + total
     friction = tile(stat_ref, ZONE_FRICTION) * tile(stat_ref, FRICTION_BASE + section) * wet
@@ -482,23 +476,51 @@
         exchange.append(kappa * top)
         result[9 + i] = result[9 + i] + exchange[i]
     for r in range(12):
-        emit(r, result[r])
+        put(own_ref, r, result[r])
     for i in range(3):
-        (f0, j0), (f1, j1) = NODE_FACES[i]
+        (f0, _), (f1, _) = NODE_FACES[i]
         both = edge[f0] + edge[f1]
         from_above = exchange[i]
         for layer in range(layers):
             r = 12 + layer * 3 + i
-            value = (
-                outer_edge[f0] * tile(outer_ref, f0 * channels + 8 + layer * 2 + j0)
-                + outer_edge[f1] * tile(outer_ref, f1 * channels + 8 + layer * 2 + j1)
-                - both * tile(y_ref, r)
-                - from_above
-            )
+            value = -(both * tile(y_ref, r)) - from_above
             if layer + 1 < layers:
                 from_above = kappa * (tile(lam_ref, r + 3) - tile(lam_ref, r))
                 value = value + from_above
-            emit(r, value)
+            put(own_ref, r, value)
+
+
+def transposed_section(
+    section, own_ref, y_ref, outer_ref, stat_ref, fact_ref, matrix_ref, emit
+):
+    rows = own_ref.shape[0] // SUB
+    channels = rows // 3 * 2
+    layers = (rows - 12) // 3
+    outer_edge = [tile(fact_ref, OUTER_EDGE + f) for f in range(3)]
+    result = [tile(own_ref, r) for r in range(12)]
+    for f in range(3):
+        edge = tile(stat_ref, EDGE + f)
+        half_speed = tile(fact_ref, HALF_SPEED + 3 * section + f)
+        ends = FACE_NODES[f]
+        outer = [outer_edge[f] * tile(outer_ref, f * channels + ch) for ch in range(8)]
+        for b in range(8):
+            at = (b // 2) * 3 + ends[b % 2]
+            total = half_speed * (edge * tile(y_ref, at) - outer[b])
+            for a in range(8):
+                total = total - matrix_ref[8 + a, b] * outer[a]
+            result[at] = result[at] + total
+    for r in range(12):
+        emit(r, result[r])
+    for i in range(3):
+        (f0, j0), (f1, j1) = NODE_FACES[i]
+        for layer in range(layers):
+            r = 12 + layer * 3 + i
+            emit(
+                r,
+                tile(own_ref, r)
+                + outer_edge[f0] * tile(outer_ref, f0 * channels + 8 + layer * 2 + j0)
+                + outer_edge[f1] * tile(outer_ref, f1 * channels + 8 + layer * 2 + j1),
+            )
 
 
 def own_gradients(section, weight, lam_ref, y_ref, x_tiles, stat_ref):
@@ -552,8 +574,18 @@
 
 
 def local_two_kernel(
-    cot_ref, plan_ref, x_ref, outer_ref, near_ref, term_ref, x_tiles
+    cot_ref,
+    plan_ref,
+    x_ref,
+    outer_ref,
+    near_ref,
+    term_ref,
+    own_ref,
+    x_tiles,
+    matrix_ref,
+    sem,
 ):
+    matrices = load_matrices(plan_ref, matrix_ref, sem)
     stat_ref, index_ref, _, table_ref = plan_parts(plan_ref)
     rows = cot_ref.shape[0] // SUB
     local_states(table_ref, 0, rows // 3, index_ref, outer_ref)
@@ -569,6 +601,8 @@
     )
     put(term_ref, 0, friction)
     put(term_ref, 1, conduct)
+    matrices.wait()
+    transposed_own(2, cot_ref, table_ref, stat_ref, matrix_ref, own_ref)
 
 
 def local_x_kernel(plan_ref, x_ref, x_outer_ref, sent_ref, packed_ref, x_tiles):
@@ -584,6 +618,7 @@
 def second_kernel(
     cot_ref,
     plan_ref,
+    own_ref,
     near_outer_ref,
     near_ref,
     x_sent_ref,
@@ -638,7 +673,7 @@
 
     matrices.wait()
     transposed_section(
-        2, cot_ref, table_ref, outer_ref, stat_ref, fact_ref, matrix_ref, emit
+        2, own_ref, table_ref, outer_ref, stat_ref, fact_ref, matrix_ref, emit
     )
     sender = Sender(index_ref, sent_ref, packed_ref)
     sender.states(y_ref, 0, comps)
@@ -658,8 +693,12 @@
     x_ref,
     outer_ref,
     term_ref,
+    own_ref,
     x_tiles,
+    matrix_ref,
+    sem,
 ):
+    matrices = load_matrices(plan_ref, matrix_ref, sem)
     stat_ref, index_ref, _, _ = plan_parts(plan_ref)
     local_states(y_ref, 0, lam_ref.shape[0] // SUB // 3, index_ref, outer_ref)
     x_to_tiles(x_ref, 2, x_tiles)
@@ -670,6 +709,8 @@
     terms = own_gradients(1, TIME_STEP * 0.25, lam_ref, y_ref, x_tiles, stat_ref)
     for n in range(2):
         put(term_ref, n, tile(old_term_ref, n) + terms[n])
+    matrices.wait()
+    transposed_own(1, lam_ref, y_ref, stat_ref, matrix_ref, own_ref)
 
 
 def first_kernel(
@@ -678,6 +719,7 @@
     y_ref,
     plan_ref,
     fact_ref,
+    own_ref,
     near_outer_ref,
     from_x1,
     from_x2,
@@ -715,7 +757,7 @@
 
     matrices.wait()
     transposed_section(
-        1, lam_ref, y_ref, outer_ref, stat_ref, fact_ref, matrix_ref, emit
+        1, own_ref, y_ref, outer_ref, stat_ref, fact_ref, matrix_ref, emit
     )
     sender = Sender(index_ref, sent_ref, packed_ref)
     sender.states(next_y_ref, 0, comps)
@@ -809,17 +851,22 @@
         out_ref[device, 1:2, :] = conduct
 
 
-def local_zero_kernel(y_ref, plan_ref, outer_ref):
-    index_ref = plan_parts(plan_ref)[1]
+def local_zero_kernel(
+    lam_ref, y_ref, plan_ref, zone_in, outer_ref, own_ref, zone_ref, matrix_ref, sem
+):
+    matrices = load_matrices(plan_ref, matrix_ref, sem)
+    stat_ref, index_ref, _, _ = plan_parts(plan_ref)
     local_states(y_ref, 0, y_ref.shape[0] // SUB // 3, index_ref, outer_ref)
+    matrices.wait()
+    transposed_own(0, lam_ref, y_ref, stat_ref, matrix_ref, own_ref)
 
 
 def last_kernel(
     base_ref,
-    lam_ref,
     y_ref,
     plan_ref,
     fact_ref,
+    own_ref,
     near_outer_ref,
     from_x1,
     from_x2,
@@ -834,7 +881,7 @@
 ):
     matrices = load_matrices(plan_ref, matrix_ref, sem)
     stat_ref, index_ref, _, _ = plan_parts(plan_ref)
-    rows = lam_ref.shape[0] // SUB
+    rows = y_ref.shape[0] // SUB
     channels = rows // 3 * 2
     received = Received((from_x1, from_x2, from_y1, from_y2), channels, corner_ref)
     remote_states(received, 0, channels, index_ref, near_outer_ref, outer_ref)
@@ -844,7 +891,7 @@
 
     matrices.wait()
     transposed_section(
-        0, lam_ref, y_ref, outer_ref, stat_ref, fact_ref, matrix_ref, emit
+        0, own_ref, y_ref, outer_ref, stat_ref, fact_ref, matrix_ref, emit
     )
     last_ref[...] = tile(adjoint_ref, rows - 1)
 
@@ -855,7 +902,7 @@
 
 def exchange(channels, messages, ahead):
     x1, x2, y1, y2 = messages
-    x1, x2 = swapped(x1, "gx", 0), swapped(x2, "gx", 1)
+    x1, x2 = swapped(x1, "gx", 1), swapped(x2, "gx", 0)
     y1, y2, ahead = call(
         functools.partial(corner_kernel, channels),
         "corners",
@@ -865,7 +912,7 @@
         apart=(4,),
         aliases={2: 0, 3: 1, 4: 2},
     )
-    return (x1, x2, swapped(y1, "gy", 0), swapped(y2, "gy", 1)), ahead
+    return (x1, x2, swapped(y1, "gy", 1), swapped(y2, "gy", 0)), ahead
 
 
 def call(kernel, name, outs, scratch, operands, far=False, apart=(), aliases={}):
@@ -924,11 +971,11 @@
     def sent_tiles(count):
         return corner_rows(count) * SUB
 
-    section_scratch = [
-        pltpu.VMEM((SUB, LANES), f32),
+    matrix_scratch = [
         pltpu.SMEM((MATRIX_ROWS * SUB, LANES), f32),
         pltpu.SemaphoreType.DMA((1,)),
     ]
+    section_scratch = [pltpu.VMEM((SUB, LANES), f32)] + matrix_scratch
 
     square = lambda one: one.reshape(SUB, LANES)
     cot = cotangent.reshape(rows * SUB, LANES)
@@ -976,11 +1023,11 @@
         ],
         far=True,
     )
-    near_outer, near, term = call(
+    near_outer, near, term, own = call(
         local_two_kernel,
         "local_two",
-        [tiles(3 * channels), tiles(15), tiles(2)],
-        [tile_scratch(rows)],
+        [tiles(3 * channels), tiles(15), tiles(2), tiles(rows)],
+        [tile_scratch(rows)] + matrix_scratch,
         [cot, plan, section_states],
     )
     x_near, x_sent, x_packed = call(
@@ -997,13 +1044,13 @@
         [tiles(rows), tiles(rows), tiles(FACT_ROWS), tiles(3 * channels)]
         + messages(X_ROWS + channels),
         [tile_scratch(sent_tiles(channels)), tile_scratch(1)] + section_scratch,
-        [cot, plan, near_outer, near, x_sent, x_packed, *received],
-    )
-    near_outer, term = call(
+        [cot, plan, own, near_outer, near, x_sent, x_packed, *received],
+    )
+    near_outer, term, own = call(
         local_one_kernel,
         "local_one",
-        [tiles(3 * channels), tiles(5)],
-        [tile_scratch(rows)],
+        [tiles(3 * channels), tiles(5), tiles(rows)],
+        [tile_scratch(rows)] + matrix_scratch,
         [lam, y, plan, fact, outer, term, section_states],
     )
     received, term = exchange(X_ROWS + channels, to_send, term)
@@ -1012,7 +1059,7 @@
         "section_one",
         [tiles(rows), tiles(rows), tiles(rows), tiles(3 * channels)] + messages(channels),
         [tile_scratch(sent_tiles(channels)), tile_scratch(1)] + section_scratch,
-        [cot, lam, y, plan, fact, near_outer, *received],
+        [cot, lam, y, plan, fact, own, near_outer, *received],
     )
     (zone_terms,) = call(
         zone_kernel,
@@ -1022,14 +1069,26 @@
         [lam, y, plan, fact, outer, term, section_states, x_near, *received],
     )
     received, zone_terms = exchange(channels, to_send, zone_terms)
+    near_outer, own, zone_terms = call(
+        local_zero_kernel,
+        "local_zero",
+        [
+            tiles(3 * channels),
+            tiles(rows),
+            jax.ShapeDtypeStruct(zone_terms.shape, f32),
+        ],
+        matrix_scratch,
+        [lam, y, plan, zone_terms],
+        apart=(3,),
+        aliases={3: 2},
+    )
     all_terms = lax.all_to_all(zone_terms, ("gx", "gy"), 0, 0)
-    (near_outer,) = call(local_zero_kernel, "local_zero", [tiles(3 * channels)], [], [y, plan])
     adjoint, last = call(
         last_kernel,
         "section_zero",
         [tiles(rows), tiles(1)],
         [tile_scratch(3 * channels)] + section_scratch,
-        [base, lam, y, plan, fact, near_outer, *received],
+        [base, y, plan, fact, own, near_outer, *received],
     )
     (zone_grads,) = call(
         total_kernel,

time: 60 us -> 60.1 us (level)
  starting transfers between devices: 33.6 us -> 32.2 us
  waiting for transfers between devices: 3.12 us -> 4.27 us
    all_to_all x1, starting transfers between devices: 9.55 us -> 4.85 us  [local(): all_terms = lax.all_to_all(zone_terms, ('gx', 'gy'), 0, 0)]
    ppermute x12, starting transfers between devices: 24 us -> 27.4 us  [swapped(): lax.ppermute(x, axis, [(i, i + 1) for i in lows] + [(i + 1, i) for i in l...]
    ppermute x12, waiting for transfers between devices: 3.12 us -> 4.27 us  [swapped(): lax.ppermute(x, axis, [(i, i + 1) for i in lows] + [(i + 1, i) for i in l...]
  transfers between devices with their start and end apart: 13 -> 13, of which waited for: 3 -> 3; matrix products, arithmetic and copies ran while one was open for 0% -> 0% of each run, Pallas kernels for 18% -> 17%
where the time goes in v9:
time: 60.1 us; the launch traced here: 59.7 us
  starting transfers between devices  32.2 us (54%)
  Pallas kernels  21.4 us (36%)
  waiting for transfers between devices  4.27 us (7%)
  local copies, waits for them, and re-layouts  1.01 us (2%)
  between operations  0.88 us (1%)
    ppermute x12, starting transfers between devices, swapped(): lax.ppermute(x, axis, [(i, i + 1) for i in lows] + [(i + 1, i) for i in l...  27.4 us
    pallas_call x13, Pallas kernels, call(): pl.pallas_call(kernel, in_specs=specs, out_specs=[in_place if n in handed...  21.4 us
    all_to_all x1, starting transfers between devices, local(): all_terms = lax.all_to_all(zone_terms, ('gx', 'gy'), 0, 0)  4.85 us
    ppermute x12, waiting for transfers between devices, swapped(): lax.ppermute(x, axis, [(i, i + 1) for i in lows] + [(i + 1, i) for i in l...  4.27 us
  transfers between devices with their start and end apart: 13, of which 3 were waited for; matrix products, arithmetic and copies ran while one was open for 0% of the time, Pallas kernels for 17%

profile of v9, /device:TPU:1, one launch (start us, length us, event | category | flops | bytes accessed | tf_op | source)
XLA Modules:
  0.0 59.7 jit_solution(12448937984950881121)
XLA Ops:
  0.7 3.6 %prepare.1 = (f32[720,128]{1,0:T(8,128)}, f32[2,38,128]{2,1,0:T(8,128)}, f32[2,38,128]{2,1,0:T(8,128)}, f32[2,38,128]{2,1,0:T(8,128)}, f32[2,38,128]{2,1,0:T(8,128)}) custom-call(f32[336,128]{1,0:T(8,128)} %bitcast.11, bf16[3,1,1,42,1024]{4,3,2,1,0:T(8,128)(2,1)} %x_ref.9, f32[8,128]{1,0:T(8,128)} %bitcast.17, f32[24,128]{1,0:T(8,128)} %bitcast.15, ...), custom_call_target="tpu_custom_call" | custom-call | tf_op jit(solution)/shard_map/prepare/pallas_call | solution.py:923
  4.2 0.7 %collective-permute-start = (f32[2,38,128]{2,1,0:T(8,128)}, f32[2,38,128]{2,1,0:T(8,128)S(1)}, u32[]{:S(2)}, u32[]{:S(2)}) collective-permute-start(f32[2,38,128]{2,1,0:T(8,128)} %get-tuple-element.53), channel_id=1, source_target_pairs={{4,8},{12,16},{20,24},{8,4},{16,12},{24,20},{5,9},{13,17},{21,25},... | collective-permute-start | bytes 116744 | tf_op jit(solution)/shard_map/ppermute | solution.py:42
  4.9 4.6 %collective-permute-start.1 = (f32[2,38,128]{2,1,0:T(8,128)}, f32[2,38,128]{2,1,0:T(8,128)S(1)}, u32[]{:S(2)}, u32[]{:S(2)}) collective-permute-start(f32[2,38,128]{2,1,0:T(8,128)} %get-tuple-element.54), channel_id=1, source_target_pairs={{0,4},{8,12},{16,20},{24,28},{4,0},{12,8},{20,16},{28,24},{1,5},{9... | collective-permute-start | bytes 116744 | tf_op jit(solution)/shard_map/ppermute | solution.py:42
  9.5 1.0 %copy-done = f32[720,128]{1,0:T(8,128)S(1)} copy-done((f32[720,128]{1,0:T(8,128)S(1)}, f32[720,128]{1,0:T(8,128)}, u32[]{:S(2)}) %copy-start) | copy-done | bytes 368664
  10.5 1.8 %local_two.1 = (f32[672,128]{1,0:T(8,128)S(1)}, f32[120,128]{1,0:T(8,128)S(1)}, f32[16,128]{1,0:T(8,128)S(1)}, f32[336,128]{1,0:T(8,128)S(1)}) custom-call(f32[336,128]{1,0:T(8,128)S(1)} %bitcast.12, f32[720,128]{1,0:T(8,128)S(1)} %copy-done, bf16[3,1,1,42,1024]{4,3,2,1,0:T(8,128)(2,1)S(1)} %copy-done.2), custom_call_target="tpu_custom_call" | custom-call | tf_op jit(solution)/shard_map/local_two/pallas_call | solution.py:923
  12.4 0.0 collective-permute-done.x1.from_x1
  12.4 0.0 collective-permute-done.1.x2.from_x2
  12.4 4.3 %collective-permute-start.2 = (f32[2,38,128]{2,1,0:T(8,128)S(1)}, f32[2,38,128]{2,1,0:T(8,128)S(1)}, u32[]{:S(2)}, u32[]{:S(2)}) collective-permute-start(f32[2,38,128]{2,1,0:T(8,128)S(1)} %get-tuple-element.58), channel_id=1, source_target_pairs={{1,2},{2,1},{5,6},{6,5},{9,10},{10,9},{13,14},{14,13},{17,18},{18,... | collective-permute-start | bytes 116744 | tf_op jit(solution)/shard_map/ppermute | solution.py:42
  16.7 0.1 collective-permute-start.3
  16.8 2.0 %local_x.1 = (f32[480,128]{1,0:T(8,128)S(1)}, f32[192,128]{1,0:T(8,128)S(1)}, f32[8,128]{1,0:T(8,128)S(1)}) custom-call(f32[720,128]{1,0:T(8,128)S(1)} %copy-done.1, bf16[3,1,1,42,1024]{4,3,2,1,0:T(8,128)(2,1)S(1)} %copy-done.2), custom_call_target="tpu_custom_call" | custom-call | tf_op jit(solution)/shard_map/local_x/pallas_call | solution.py:923
  18.8 0.0 collective-permute-done.2.from_y1
  18.8 0.0 collective-permute-done.3.from_y2
  18.8 3.1 %section_two.1 = (f32[336,128]{1,0:T(8,128)S(1)}, f32[336,128]{1,0:T(8,128)S(1)}, f32[120,128]{1,0:T(8,128)S(1)}, f32[672,128]{1,0:T(8,128)S(1)}, f32[2,59,128]{...) custom-call(f32[336,128]{1,0:T(8,128)S(1)} %bitcast.13, ...), custom_call_target="tpu_custom_call" | custom-call | tf_op jit(solution)/shard_map/section_two/pallas_call | solution.py:923
  21.9 0.7 %collective-permute-start.4 = (f32[2,59,128]{2,1,0:T(8,128)S(1)}, f32[2,59,128]{2,1,0:T(8,128)S(1)}, u32[]{:S(2)}, u32[]{:S(2)}) collective-permute-start(f32[2,59,128]{2,1,0:T(8,128)S(1)} %get-tuple-element.67), channel_id=1, source_target_pairs={{4,8},{12,16},{20,24},{8,4},{16,12},{24,20},{5,9},{13,17},{21,25},... | collective-permute-start | bytes 181256 | tf_op jit(solution)/shard_map/ppermute | solution.py:42
  22.6 3.8 %collective-permute-start.5 = (f32[2,59,128]{2,1,0:T(8,128)S(1)}, f32[2,59,128]{2,1,0:T(8,128)S(1)}, u32[]{:S(2)}, u32[]{:S(2)}) collective-permute-start(f32[2,59,128]{2,1,0:T(8,128)S(1)} %get-tuple-element.68), channel_id=1, source_target_pairs={{0,4},{8,12},{16,20},{24,28},{4,0},{12,8},{20,16},{28,24},{1,5},{9... | collective-permute-start | bytes 181256 | tf_op jit(solution)/shard_map/ppermute | solution.py:42
  26.3 1.6 %local_one.1 = (f32[672,128]{1,0:T(8,128)S(1)}, f32[40,128]{1,0:T(8,128)S(1)}, f32[336,128]{1,0:T(8,128)S(1)}) custom-call(f32[336,128]{1,0:T(8,128)S(1)} %get-tuple-element.60.lam_ref, f32[336,128]{1,0:T(8,128)S(1)} %get-tuple-element.61.y_ref, f32[720,128]{1,0:T(8,128)S(1)} %copy-done.1, f32[120,128]{1,0:T(8,128)S(1)} %get-tuple-element.62.fact_ref, ...), custom_call_target="tpu_custom_call" | custom-call | tf_op jit(solution)/shard_map/local_one/pallas_call | solution.py:923
  27.9 0.0 collective-permute-done.4.x1.from_x1
  27.9 0.5 collective-permute-done.5.x2.from_x2
  28.4 3.9 %collective-permute-start.6 = (f32[2,59,128]{2,1,0:T(8,128)S(1)}, f32[2,59,128]{2,1,0:T(8,128)S(1)}, u32[]{:S(2)}, u32[]{:S(2)}) collective-permute-start(f32[2,59,128]{2,1,0:T(8,128)S(1)} %get-tuple-element.72), channel_id=1, source_target_pairs={{1,2},{2,1},{5,6},{6,5},{9,10},{10,9},{13,14},{14,13},{17,18},{18,... | collective-permute-start | bytes 181256 | tf_op jit(solution)/shard_map/ppermute | solution.py:42
  32.3 0.1 collective-permute-start.7
  32.4 1.9 %collective-permute-done.6.from_y1 = f32[2,59,128]{2,1,0:T(8,128)S(1)} collective-permute-done((f32[2,59,128]{2,1,0:T(8,128)S(1)}, f32[2,59,128]{2,1,0:T(8,128)S(1)}, u32[]{:S(2)}, u32[]{:S(2)}) %collective-permute-start.6) | collective-permute-done | bytes 60448 | tf_op jit(solution)/shard_map/ppermute | solution.py:42
  34.3 2.8 %section_one.1 = (f32[336,128]{1,0:T(8,128)S(1)}, f32[336,128]{1,0:T(8,128)S(1)}, f32[336,128]{1,0:T(8,128)S(1)}, f32[672,128]{1,0:T(8,128)S(1)}, f32[2,32,128]{...) custom-call(f32[336,128]{1,0:T(8,128)S(1)} %bitcast.14, ...), custom_call_target="tpu_custom_call" | custom-call | tf_op jit(solution)/shard_map/section_one/pallas_call | solution.py:923
  37.1 0.7 %collective-permute-start.8 = (f32[2,32,128]{2,1,0:T(8,128)S(1)}, f32[2,32,128]{2,1,0:T(8,128)S(1)}, u32[]{:S(2)}, u32[]{:S(2)}) collective-permute-start(f32[2,32,128]{2,1,0:T(8,128)S(1)} %get-tuple-element.77), channel_id=1, source_target_pairs={{4,8},{12,16},{20,24},{8,4},{16,12},{24,20},{5,9},{13,17},{21,25},... | collective-permute-start | bytes 98312 | tf_op jit(solution)/shard_map/ppermute | solution.py:42
  37.8 5.0 %collective-permute-start.9 = (f32[2,32,128]{2,1,0:T(8,128)S(1)}, f32[2,32,128]{2,1,0:T(8,128)S(1)}, u32[]{:S(2)}, u32[]{:S(2)}) collective-permute-start(f32[2,32,128]{2,1,0:T(8,128)S(1)} %get-tuple-element.78), channel_id=1, source_target_pairs={{0,4},{8,12},{16,20},{24,28},{4,0},{12,8},{20,16},{28,24},{1,5},{9... | collective-permute-start | bytes 98312 | tf_op jit(solution)/shard_map/ppermute | solution.py:42
  42.8 2.3 %zone_sums.1.rest_0_ = f32[32,2,128]{2,1,0:T(2,128)} custom-call(f32[336,128]{1,0:T(8,128)S(1)} %get-tuple-element.76.lam_ref, f32[336,128]{1,0:T(8,128)S(1)} %get-tuple-element.75.y_ref, f32[720,128]{1,0:T(8,128)S(1)} %copy-done.1, f32[120,128]{1,0:T(8,128)S(1)} %get-tuple-element.62.fact_ref, f32[672,128]{1,0:T(8,128)S(1)} %get-tuple-element.81.old_outer_ref, ...), custom_call_target="tpu_custom_call" | custom-call | tf_op jit(solution)/shard_map/zone_sums/pallas_call | solution.py:923
  45.1 1.5 %local_zero.1 = (f32[672,128]{1,0:T(8,128)S(1)}, f32[336,128]{1,0:T(8,128)S(1)}, f32[32,2,128]{2,1,0:T(2,128)}) custom-call(f32[336,128]{1,0:T(8,128)S(1)} %get-tuple-element.76.lam_ref, f32[336,128]{1,0:T(8,128)S(1)} %get-tuple-element.75.y_ref, f32[720,128]{1,0:T(8,128)S(1)} %copy-done.1, ...), custom_call_target="tpu_custom_call", output_to_operand_aliasing={{2}: (3, {})} | custom-call | tf_op jit(solution)/shard_map/local_zero/pallas_call | solution.py:923
  46.6 4.8 %all-to-all-start = ((f32[32,2,128]{2,1,0:T(2,128)}), f32[32,2,128]{2,1,0:T(2,128)S(1)}, u32[]{:S(2)}, u32[]{:S(2)}) async-start(f32[32,2,128]{2,1,0:T(2,128)} %get-tuple-element.90), calls=%async_computation | async-start | bytes 65536 | tf_op jit(solution)/shard_map/all_to_all | solution.py:1085
  51.5 3.5 %collective-permute-start.10 = (f32[2,32,128]{2,1,0:T(8,128)S(1)}, f32[2,32,128]{2,1,0:T(8,128)S(1)}, u32[]{:S(2)}, u32[]{:S(2)}) collective-permute-start(f32[2,32,128]{2,1,0:T(8,128)S(1)} %get-tuple-element.87), channel_id=1, source_target_pairs={{1,2},{2,1},{5,6},{6,5},{9,10},{10,9},{13,14},{14,13},{17,18},{18,... | collective-permute-start | bytes 98312 | tf_op jit(solution)/shard_map/ppermute | solution.py:42
  55.0 0.1 collective-permute-start.11
  55.1 1.9 %collective-permute-done.10.from_y1 = f32[2,32,128]{2,1,0:T(8,128)S(1)} collective-permute-done((f32[2,32,128]{2,1,0:T(8,128)S(1)}, f32[2,32,128]{2,1,0:T(8,128)S(1)}, u32[]{:S(2)}, u32[]{:S(2)}) %collective-permute-start.10) | collective-permute-done | bytes 32800 | tf_op jit(solution)/shard_map/ppermute | solution.py:42
  57.0 2.1 %section_zero.1 = (f32[336,128]{1,0:T(8,128)}, f32[8,128]{1,0:T(8,128)S(1)}) custom-call(f32[336,128]{1,0:T(8,128)S(1)} %get-tuple-element.74.base_ref, f32[336,128]{1,0:T(8,128)S(1)} %get-tuple-element.75.y_ref, f32[720,128]{1,0:T(8,128)S(1)} %copy-done.1, f32[120,128]{1,0:T(8,128)S(1)} %get-tuple-element.62.fact_ref, ...), custom_call_target="tpu_custom_call" | custom-call | tf_op jit(solution)/shard_map/section_zero/pallas_call | solution.py:923
  59.1 0.6 %zone_total.1 = f32[2,128]{1,0:T(2,128)} custom-call(f32[32,2,128]{2,1,0:T(2,128)S(1)} %all-to-all-done.zone_ref, f32[8,128]{1,0:T(8,128)S(1)} %get-tuple-element.91.adjoint_ref), custom_call_target="tpu_custom_call" | custom-call | tf_op jit(solution)/shard_map/zone_total/pallas_call | solution.py:923
  (19 shorter events, 0.1 us)
Async XLA Ops:
  0.6 8.9 %copy-start.2 = (bf16[3,1,1,42,1024]{4,3,2,1,0:T(8,128)(2,1)S(1)}, bf16[3,1,1,42,1024]{4,3,2,1,0:T(8,128)(2,1)}, u32[]{:S(2)}) copy-start(bf16[3,1,1,42,1024]{4,3,2,1,0:T(8,128)(2,1)} %x_ref.9) | copy-start | bytes 774148
  0.6 8.9 %copy-start.3 = (f32[1,1,42,1024]{3,1,2,0:T(1,128)S(1)}, f32[1,1,42,1024]{3,1,2,0:T(1,128)}, u32[]{:S(2)}) copy-start(f32[1,1,42,1024]{3,1,2,0:T(1,128)} %param.16) | copy-start | bytes 516100
  4.2 8.2 %collective-permute-start = (f32[2,38,128]{2,1,0:T(8,128)}, f32[2,38,128]{2,1,0:T(8,128)S(1)}, u32[]{:S(2)}, u32[]{:S(2)}) collective-permute-start(f32[2,38,128]{2,1,0:T(8,128)} %get-tuple-element.53), channel_id=1, source_target_pairs={{4,8},{12,16},{20,24},{8,4},{16,12},{24,20},{5,9},{13,17},{21,25},... | collective-permute-start | bytes 116744 | tf_op jit(solution)/shard_map/ppermute | solution.py:42
  4.9 7.5 %collective-permute-start.1 = (f32[2,38,128]{2,1,0:T(8,128)}, f32[2,38,128]{2,1,0:T(8,128)S(1)}, u32[]{:S(2)}, u32[]{:S(2)}) collective-permute-start(f32[2,38,128]{2,1,0:T(8,128)} %get-tuple-element.54), channel_id=1, source_target_pairs={{0,4},{8,12},{16,20},{24,28},{4,0},{12,8},{20,16},{28,24},{1,5},{9... | collective-permute-start | bytes 116744 | tf_op jit(solution)/shard_map/ppermute | solution.py:42
  9.5 1.0 %copy-start = (f32[720,128]{1,0:T(8,128)S(1)}, f32[720,128]{1,0:T(8,128)}, u32[]{:S(2)}) copy-start(f32[720,128]{1,0:T(8,128)} %get-tuple-element.47.plan_ref) | copy-start | bytes 1105924
  10.5 1.9 %copy-start.4 = (f32[2,38,128]{2,1,0:T(8,128)S(1)}, f32[2,38,128]{2,1,0:T(8,128)}, u32[]{:S(2)}) copy-start(f32[2,38,128]{2,1,0:T(8,128)} %get-tuple-element.55.old_y1) | copy-start | bytes 116740
  10.5 1.9 %copy-start.5 = (f32[2,38,128]{2,1,0:T(8,128)S(1)}, f32[2,38,128]{2,1,0:T(8,128)}, u32[]{:S(2)}) copy-start(f32[2,38,128]{2,1,0:T(8,128)} %get-tuple-element.56.old_y2) | copy-start | bytes 116740
  10.5 6.3 %copy-start.1 = (f32[720,128]{1,0:T(8,128)S(1)}, f32[720,128]{1,0:T(8,128)}, u32[]{:S(2)}) copy-start(f32[720,128]{1,0:T(8,128)} %get-tuple-element.47.plan_ref) | copy-start | bytes 1105924
  12.4 6.4 %collective-permute-start.2 = (f32[2,38,128]{2,1,0:T(8,128)S(1)}, f32[2,38,128]{2,1,0:T(8,128)S(1)}, u32[]{:S(2)}, u32[]{:S(2)}) collective-permute-start(f32[2,38,128]{2,1,0:T(8,128)S(1)} %get-tuple-element.58), channel_id=1, source_target_pairs={{1,2},{2,1},{5,6},{6,5},{9,10},{10,9},{13,14},{14,13},{17,18},{18,... | collective-permute-start | bytes 116744 | tf_op jit(solution)/shard_map/ppermute | solution.py:42
  16.7 2.1 %collective-permute-start.3 = (f32[2,38,128]{2,1,0:T(8,128)S(1)}, f32[2,38,128]{2,1,0:T(8,128)S(1)}, u32[]{:S(2)}, u32[]{:S(2)}) collective-permute-start(f32[2,38,128]{2,1,0:T(8,128)S(1)} %get-tuple-element.59), channel_id=1, source_target_pairs={{0,1},{2,3},{1,0},{3,2},{4,5},{6,7},{5,4},{7,6},{8,9},{10,11},{9,8... | collective-permute-start | bytes 116744 | tf_op jit(solution)/shard_map/ppermute | solution.py:42
  21.9 6.0 %collective-permute-start.4 = (f32[2,59,128]{2,1,0:T(8,128)S(1)}, f32[2,59,128]{2,1,0:T(8,128)S(1)}, u32[]{:S(2)}, u32[]{:S(2)}) collective-permute-start(f32[2,59,128]{2,1,0:T(8,128)S(1)} %get-tuple-element.67), channel_id=1, source_target_pairs={{4,8},{12,16},{20,24},{8,4},{16,12},{24,20},{5,9},{13,17},{21,25},... | collective-permute-start | bytes 181256 | tf_op jit(solution)/shard_map/ppermute | solution.py:42
  22.6 5.8 %collective-permute-start.5 = (f32[2,59,128]{2,1,0:T(8,128)S(1)}, f32[2,59,128]{2,1,0:T(8,128)S(1)}, u32[]{:S(2)}, u32[]{:S(2)}) collective-permute-start(f32[2,59,128]{2,1,0:T(8,128)S(1)} %get-tuple-element.68), channel_id=1, source_target_pairs={{0,4},{8,12},{16,20},{24,28},{4,0},{12,8},{20,16},{28,24},{1,5},{9... | collective-permute-start | bytes 181256 | tf_op jit(solution)/shard_map/ppermute | solution.py:42
  28.4 5.9 %collective-permute-start.6 = (f32[2,59,128]{2,1,0:T(8,128)S(1)}, f32[2,59,128]{2,1,0:T(8,128)S(1)}, u32[]{:S(2)}, u32[]{:S(2)}) collective-permute-start(f32[2,59,128]{2,1,0:T(8,128)S(1)} %get-tuple-element.72), channel_id=1, source_target_pairs={{1,2},{2,1},{5,6},{6,5},{9,10},{10,9},{13,14},{14,13},{17,18},{18,... | collective-permute-start | bytes 181256 | tf_op jit(solution)/shard_map/ppermute | solution.py:42
  32.3 1.9 %collective-permute-start.7 = (f32[2,59,128]{2,1,0:T(8,128)S(1)}, f32[2,59,128]{2,1,0:T(8,128)S(1)}, u32[]{:S(2)}, u32[]{:S(2)}) collective-permute-start(f32[2,59,128]{2,1,0:T(8,128)S(1)} %get-tuple-element.73), channel_id=1, source_target_pairs={{0,1},{2,3},{1,0},{3,2},{4,5},{6,7},{5,4},{7,6},{8,9},{10,11},{9,8... | collective-permute-start | bytes 181256 | tf_op jit(solution)/shard_map/ppermute | solution.py:42
  37.1 8.0 %collective-permute-start.8 = (f32[2,32,128]{2,1,0:T(8,128)S(1)}, f32[2,32,128]{2,1,0:T(8,128)S(1)}, u32[]{:S(2)}, u32[]{:S(2)}) collective-permute-start(f32[2,32,128]{2,1,0:T(8,128)S(1)} %get-tuple-element.77), channel_id=1, source_target_pairs={{4,8},{12,16},{20,24},{8,4},{16,12},{24,20},{5,9},{13,17},{21,25},... | collective-permute-start | bytes 98312 | tf_op jit(solution)/shard_map/ppermute | solution.py:42
  37.8 7.3 %collective-permute-start.9 = (f32[2,32,128]{2,1,0:T(8,128)S(1)}, f32[2,32,128]{2,1,0:T(8,128)S(1)}, u32[]{:S(2)}, u32[]{:S(2)}) collective-permute-start(f32[2,32,128]{2,1,0:T(8,128)S(1)} %get-tuple-element.78), channel_id=1, source_target_pairs={{0,4},{8,12},{16,20},{24,28},{4,0},{12,8},{20,16},{28,24},{1,5},{9... | collective-permute-start | bytes 98312 | tf_op jit(solution)/shard_map/ppermute | solution.py:42
  46.6 12.5 %all-to-all-start = ((f32[32,2,128]{2,1,0:T(2,128)}), f32[32,2,128]{2,1,0:T(2,128)S(1)}, u32[]{:S(2)}, u32[]{:S(2)}) async-start(f32[32,2,128]{2,1,0:T(2,128)} %get-tuple-element.90), calls=%async_computation | async-start | bytes 65536 | tf_op jit(solution)/shard_map/all_to_all | solution.py:1085
  51.5 5.6 %collective-permute-start.10 = (f32[2,32,128]{2,1,0:T(8,128)S(1)}, f32[2,32,128]{2,1,0:T(8,128)S(1)}, u32[]{:S(2)}, u32[]{:S(2)}) collective-permute-start(f32[2,32,128]{2,1,0:T(8,128)S(1)} %get-tuple-element.87), channel_id=1, source_target_pairs={{1,2},{2,1},{5,6},{6,5},{9,10},{10,9},{13,14},{14,13},{17,18},{18,... | collective-permute-start | bytes 98312 | tf_op jit(solution)/shard_map/ppermute | solution.py:42
  55.0 2.0 %collective-permute-start.11 = (f32[2,32,128]{2,1,0:T(8,128)S(1)}, f32[2,32,128]{2,1,0:T(8,128)S(1)}, u32[]{:S(2)}, u32[]{:S(2)}) collective-permute-start(f32[2,32,128]{2,1,0:T(8,128)S(1)} %get-tuple-element.88), channel_id=1, source_target_pairs={{0,1},{2,3},{1,0},{3,2},{4,5},{6,7},{5,4},{7,6},{8,9},{10,11},{9,8... | collective-permute-start | bytes 98312 | tf_op jit(solution)/shard_map/ppermute | solution.py:42

commit v10 on v9

--- a/solution.py
+++ b/solution.py
@@ -272,7 +272,7 @@
     ]
     for copy in copies:
         copy.start()
-    for copy in copies:
+    for copy in copies[:2]:
         copy.wait()
     (
         partner_ref,
@@ -291,9 +291,6 @@
         out_ref,
         volume_ref,
     ) = fetched
-    matrix_ref[0:8, 0:8] = in_ref[...]
-    matrix_ref[8:16, 0:8] = out_ref[...]
-    matrix_ref[16:28, 0:12] = volume_ref[...]
     rows = cot_ref.shape[0] // SUB
     sections = x_ref.shape[0]
     odd_a, odd_b = 1 - lax.axis_index("gx") % 2, 1 - lax.axis_index("gy") % 2
@@ -355,6 +352,11 @@
         put_index(index_ref, 12 + d, jnp.bitwise_and(slots, LANES - 1))
         put_index(index_ref, 14 + d, jnp.bitwise_and(jnp.right_shift(slots, 7), SUB - 1))
         put_index(index_ref, 16 + d, jnp.right_shift(slots, 10))
+    for copy in copies[2:]:
+        copy.wait()
+    matrix_ref[0:8, 0:8] = in_ref[...]
+    matrix_ref[8:16, 0:8] = out_ref[...]
+    matrix_ref[16:28, 0:12] = volume_ref[...]
     zone = zone_ref[...]
     zone_lane = jnp.bitwise_and(zone, LANES - 1)
     zone_block = jnp.right_shift(zone, 7)
@@ -851,9 +853,11 @@
         out_ref[device, 1:2, :] = conduct
 
 
-def local_zero_kernel(
-    lam_ref, y_ref, plan_ref, zone_in, outer_ref, own_ref, zone_ref, matrix_ref, sem
-):
+def after_kernel(zone_in, message_ref, zone_ref):
+    pass
+
+
+def local_zero_kernel(lam_ref, y_ref, plan_ref, outer_ref, own_ref, matrix_ref, sem):
     matrices = load_matrices(plan_ref, matrix_ref, sem)
     stat_ref, index_ref, _, _ = plan_parts(plan_ref)
     local_states(y_ref, 0, y_ref.shape[0] // SUB // 3, index_ref, outer_ref)
@@ -919,7 +923,7 @@
     near = pl.BlockSpec(memory_space=pltpu.VMEM)
     in_place = pl.BlockSpec(memory_space=pl.ANY)
     specs = [in_place if far or n in apart else near for n in range(len(operands))]
-    handed_on = [aliases[n] for n in apart]
+    handed_on = [aliases[n] for n in apart if n in aliases]
     return pl.pallas_call(
         kernel,
         in_specs=specs,
@@ -1069,20 +1073,23 @@
         [lam, y, plan, fact, outer, term, section_states, x_near, *received],
     )
     received, zone_terms = exchange(channels, to_send, zone_terms)
-    near_outer, own, zone_terms = call(
+    (zone_terms,) = call(
+        after_kernel,
+        "after",
+        [jax.ShapeDtypeStruct(zone_terms.shape, f32)],
+        [],
+        [zone_terms, received[3]],
+        apart=(0, 1),
+        aliases={0: 0},
+    )
+    all_terms = lax.all_to_all(zone_terms, ("gx", "gy"), 0, 0)
+    near_outer, own = call(
         local_zero_kernel,
         "local_zero",
-        [
-            tiles(3 * channels),
-            tiles(rows),
-            jax.ShapeDtypeStruct(zone_terms.shape, f32),
-        ],
+        [tiles(3 * channels), tiles(rows)],
         matrix_scratch,
-        [lam, y, plan, zone_terms],
-        apart=(3,),
-        aliases={3: 2},
-    )
-    all_terms = lax.all_to_all(zone_terms, ("gx", "gy"), 0, 0)
+        [lam, y, plan],
+    )
     adjoint, last = call(
         last_kernel,
         "section_zero",

time: 60.1 us -> 60 us (level)
    pallas_call x13 -> x14, Pallas kernels: 21.4 us -> 21.6 us  [call(): pl.pallas_call(kernel, in_specs=specs, out_specs=[in_place if n in handed...]
  transfers between devices with their start and end apart: 13 -> 13, of which waited for: 3 -> 4; matrix products, arithmetic and copies ran while one was open for 0% -> 0% of each run, Pallas kernels for 17% -> 19%
where the time goes in v10:
time: 60 us; the launch traced here: 59.7 us
  starting transfers between devices  32.1 us (54%)
  Pallas kernels  21.6 us (36%)
  waiting for transfers between devices  4.08 us (7%)
  local copies, waits for them, and re-layouts  1.01 us (2%)
  between operations  0.88 us (1%)
    ppermute x12, starting transfers between devices, swapped(): lax.ppermute(x, axis, [(i, i + 1) for i in lows] + [(i + 1, i) for i in l...  27.4 us
    pallas_call x14, Pallas kernels, call(): pl.pallas_call(kernel, in_specs=specs, out_specs=[in_place if n in handed...  21.6 us
    all_to_all x1, starting transfers between devices, local(): all_terms = lax.all_to_all(zone_terms, ('gx', 'gy'), 0, 0)  4.77 us
    ppermute x12, waiting for transfers between devices, swapped(): lax.ppermute(x, axis, [(i, i + 1) for i in lows] + [(i + 1, i) for i in l...  4.07 us
  transfers between devices with their start and end apart: 13, of which 4 were waited for; matrix products, arithmetic and copies ran while one was open for 0% of the time, Pallas kernels for 19%

profile of v10, /device:TPU:1, one launch (start us, length us, event | category | flops | bytes accessed | tf_op | source)
XLA Modules:
  0.0 59.7 jit_solution(1099202440292496061)
XLA Ops:
  0.7 3.8 %prepare.1 = (f32[720,128]{1,0:T(8,128)}, f32[2,38,128]{2,1,0:T(8,128)}, f32[2,38,128]{2,1,0:T(8,128)}, f32[2,38,128]{2,1,0:T(8,128)}, f32[2,38,128]{2,1,0:T(8,128)}) custom-call(f32[336,128]{1,0:T(8,128)} %bitcast.11, bf16[3,1,1,42,1024]{4,3,2,1,0:T(8,128)(2,1)} %x_ref.9, f32[8,128]{1,0:T(8,128)} %bitcast.17, f32[24,128]{1,0:T(8,128)} %bitcast.15, ...), custom_call_target="tpu_custom_call" | custom-call | tf_op jit(solution)/shard_map/prepare/pallas_call | solution.py:927
  4.5 0.7 %collective-permute-start = (f32[2,38,128]{2,1,0:T(8,128)}, f32[2,38,128]{2,1,0:T(8,128)S(1)}, u32[]{:S(2)}, u32[]{:S(2)}) collective-permute-start(f32[2,38,128]{2,1,0:T(8,128)} %get-tuple-element.52), channel_id=1, source_target_pairs={{4,8},{12,16},{20,24},{8,4},{16,12},{24,20},{5,9},{13,17},{21,25},... | collective-permute-start | bytes 116744 | tf_op jit(solution)/shard_map/ppermute | solution.py:42
  5.2 4.6 %collective-permute-start.1 = (f32[2,38,128]{2,1,0:T(8,128)}, f32[2,38,128]{2,1,0:T(8,128)S(1)}, u32[]{:S(2)}, u32[]{:S(2)}) collective-permute-start(f32[2,38,128]{2,1,0:T(8,128)} %get-tuple-element.53), channel_id=1, source_target_pairs={{0,4},{8,12},{16,20},{24,28},{4,0},{12,8},{20,16},{28,24},{1,5},{9... | collective-permute-start | bytes 116744 | tf_op jit(solution)/shard_map/ppermute | solution.py:42
  9.8 1.0 %copy-done = f32[720,128]{1,0:T(8,128)S(1)} copy-done((f32[720,128]{1,0:T(8,128)S(1)}, f32[720,128]{1,0:T(8,128)}, u32[]{:S(2)}) %copy-start) | copy-done | bytes 368664
  10.8 1.8 %local_two.1 = (f32[672,128]{1,0:T(8,128)S(1)}, f32[120,128]{1,0:T(8,128)S(1)}, f32[16,128]{1,0:T(8,128)S(1)}, f32[336,128]{1,0:T(8,128)S(1)}) custom-call(f32[336,128]{1,0:T(8,128)S(1)} %bitcast.12, f32[720,128]{1,0:T(8,128)S(1)} %copy-done, bf16[3,1,1,42,1024]{4,3,2,1,0:T(8,128)(2,1)S(1)} %copy-done.2), custom_call_target="tpu_custom_call" | custom-call | tf_op jit(solution)/shard_map/local_two/pallas_call | solution.py:927
  12.6 0.0 collective-permute-done.x1.from_x1
  12.6 0.0 collective-permute-done.1.x2.from_x2
  12.7 4.3 %collective-permute-start.2 = (f32[2,38,128]{2,1,0:T(8,128)S(1)}, f32[2,38,128]{2,1,0:T(8,128)S(1)}, u32[]{:S(2)}, u32[]{:S(2)}) collective-permute-start(f32[2,38,128]{2,1,0:T(8,128)S(1)} %get-tuple-element.57), channel_id=1, source_target_pairs={{1,2},{2,1},{5,6},{6,5},{9,10},{10,9},{13,14},{14,13},{17,18},{18,... | collective-permute-start | bytes 116744 | tf_op jit(solution)/shard_map/ppermute | solution.py:42
  17.0 0.1 collective-permute-start.3
  17.0 2.0 %local_x.1 = (f32[480,128]{1,0:T(8,128)S(1)}, f32[192,128]{1,0:T(8,128)S(1)}, f32[8,128]{1,0:T(8,128)S(1)}) custom-call(f32[720,128]{1,0:T(8,128)S(1)} %copy-done.1, bf16[3,1,1,42,1024]{4,3,2,1,0:T(8,128)(2,1)S(1)} %copy-done.2), custom_call_target="tpu_custom_call" | custom-call | tf_op jit(solution)/shard_map/local_x/pallas_call | solution.py:927
  19.1 0.0 collective-permute-done.2.from_y1
  19.1 0.0 collective-permute-done.3.from_y2
  19.1 3.1 %section_two.1 = (f32[336,128]{1,0:T(8,128)S(1)}, f32[336,128]{1,0:T(8,128)S(1)}, f32[120,128]{1,0:T(8,128)S(1)}, f32[672,128]{1,0:T(8,128)S(1)}, f32[2,59,128]{...) custom-call(f32[336,128]{1,0:T(8,128)S(1)} %bitcast.13, ...), custom_call_target="tpu_custom_call" | custom-call | tf_op jit(solution)/shard_map/section_two/pallas_call | solution.py:927
  22.1 0.7 %collective-permute-start.4 = (f32[2,59,128]{2,1,0:T(8,128)S(1)}, f32[2,59,128]{2,1,0:T(8,128)S(1)}, u32[]{:S(2)}, u32[]{:S(2)}) collective-permute-start(f32[2,59,128]{2,1,0:T(8,128)S(1)} %get-tuple-element.66), channel_id=1, source_target_pairs={{4,8},{12,16},{20,24},{8,4},{16,12},{24,20},{5,9},{13,17},{21,25},... | collective-permute-start | bytes 181256 | tf_op jit(solution)/shard_map/ppermute | solution.py:42
  22.8 3.8 %collective-permute-start.5 = (f32[2,59,128]{2,1,0:T(8,128)S(1)}, f32[2,59,128]{2,1,0:T(8,128)S(1)}, u32[]{:S(2)}, u32[]{:S(2)}) collective-permute-start(f32[2,59,128]{2,1,0:T(8,128)S(1)} %get-tuple-element.67), channel_id=1, source_target_pairs={{0,4},{8,12},{16,20},{24,28},{4,0},{12,8},{20,16},{28,24},{1,5},{9... | collective-permute-start | bytes 181256 | tf_op jit(solution)/shard_map/ppermute | solution.py:42
  26.6 1.6 %local_one.1 = (f32[672,128]{1,0:T(8,128)S(1)}, f32[40,128]{1,0:T(8,128)S(1)}, f32[336,128]{1,0:T(8,128)S(1)}) custom-call(f32[336,128]{1,0:T(8,128)S(1)} %get-tuple-element.59.lam_ref, f32[336,128]{1,0:T(8,128)S(1)} %get-tuple-element.60.y_ref, f32[720,128]{1,0:T(8,128)S(1)} %copy-done.1, f32[120,128]{1,0:T(8,128)S(1)} %get-tuple-element.61.fact_ref, ...), custom_call_target="tpu_custom_call" | custom-call | tf_op jit(solution)/shard_map/local_one/pallas_call | solution.py:927
  28.2 0.5 collective-permute-done.5.x2.from_x2
  28.7 3.9 %collective-permute-start.6 = (f32[2,59,128]{2,1,0:T(8,128)S(1)}, f32[2,59,128]{2,1,0:T(8,128)S(1)}, u32[]{:S(2)}, u32[]{:S(2)}) collective-permute-start(f32[2,59,128]{2,1,0:T(8,128)S(1)} %get-tuple-element.71), channel_id=1, source_target_pairs={{1,2},{2,1},{5,6},{6,5},{9,10},{10,9},{13,14},{14,13},{17,18},{18,... | collective-permute-start | bytes 181256 | tf_op jit(solution)/shard_map/ppermute | solution.py:42
  32.6 0.1 collective-permute-start.7
  32.7 1.9 %collective-permute-done.6.from_y1 = f32[2,59,128]{2,1,0:T(8,128)S(1)} collective-permute-done((f32[2,59,128]{2,1,0:T(8,128)S(1)}, f32[2,59,128]{2,1,0:T(8,128)S(1)}, u32[]{:S(2)}, u32[]{:S(2)}) %collective-permute-start.6) | collective-permute-done | bytes 60448 | tf_op jit(solution)/shard_map/ppermute | solution.py:42
  34.5 2.8 %section_one.1 = (f32[336,128]{1,0:T(8,128)S(1)}, f32[336,128]{1,0:T(8,128)S(1)}, f32[336,128]{1,0:T(8,128)S(1)}, f32[672,128]{1,0:T(8,128)S(1)}, f32[2,32,128]{...) custom-call(f32[336,128]{1,0:T(8,128)S(1)} %bitcast.14, ...), custom_call_target="tpu_custom_call" | custom-call | tf_op jit(solution)/shard_map/section_one/pallas_call | solution.py:927
  37.4 0.7 %collective-permute-start.8 = (f32[2,32,128]{2,1,0:T(8,128)S(1)}, f32[2,32,128]{2,1,0:T(8,128)S(1)}, u32[]{:S(2)}, u32[]{:S(2)}) collective-permute-start(f32[2,32,128]{2,1,0:T(8,128)S(1)} %get-tuple-element.78), channel_id=1, source_target_pairs={{4,8},{12,16},{20,24},{8,4},{16,12},{24,20},{5,9},{13,17},{21,25},... | collective-permute-start | bytes 98312 | tf_op jit(solution)/shard_map/ppermute | solution.py:42
  38.0 5.0 %collective-permute-start.9 = (f32[2,32,128]{2,1,0:T(8,128)S(1)}, f32[2,32,128]{2,1,0:T(8,128)S(1)}, u32[]{:S(2)}, u32[]{:S(2)}) collective-permute-start(f32[2,32,128]{2,1,0:T(8,128)S(1)} %get-tuple-element.79), channel_id=1, source_target_pairs={{0,4},{8,12},{16,20},{24,28},{4,0},{12,8},{20,16},{28,24},{1,5},{9... | collective-permute-start | bytes 98312 | tf_op jit(solution)/shard_map/ppermute | solution.py:42
  43.0 2.4 %zone_sums.1.rest_0_ = f32[32,2,128]{2,1,0:T(2,128)} custom-call(f32[336,128]{1,0:T(8,128)S(1)} %get-tuple-element.75.lam_ref, f32[336,128]{1,0:T(8,128)S(1)} %get-tuple-element.74.y_ref, f32[720,128]{1,0:T(8,128)S(1)} %copy-done.1, f32[120,128]{1,0:T(8,128)S(1)} %get-tuple-element.61.fact_ref, f32[672,128]{1,0:T(8,128)S(1)} %get-tuple-element.82.old_outer_ref, ...), custom_call_target="tpu_custom_call" | custom-call | tf_op jit(solution)/shard_map/zone_sums/pallas_call | solution.py:927
  45.4 0.1 collective-permute-start.11
  45.5 1.2 %collective-permute-done.11.from_y2.message_ref = f32[2,32,128]{2,1,0:T(8,128)S(1)} collective-permute-done((f32[2,32,128]{2,1,0:T(8,128)S(1)}, f32[2,32,128]{2,1,0:T(8,128)S(1)}, u32[]{:S(2)}, u32[]{:S(2)}) %collective-permute-start.11) | collective-permute-done | bytes 32800 | tf_op jit(solution)/shard_map/ppermute | solution.py:42
  46.7 4.8 %all-to-all-start = ((f32[32,2,128]{2,1,0:T(2,128)}), f32[32,2,128]{2,1,0:T(2,128)S(1)}, u32[]{:S(2)}, u32[]{:S(2)}) async-start(f32[32,2,128]{2,1,0:T(2,128)} %after.1), calls=%async_computation | async-start | bytes 65536 | tf_op jit(solution)/shard_map/all_to_all | solution.py:1085
  51.5 3.5 %collective-permute-start.10 = (f32[2,32,128]{2,1,0:T(8,128)S(1)}, f32[2,32,128]{2,1,0:T(8,128)S(1)}, u32[]{:S(2)}, u32[]{:S(2)}) collective-permute-start(f32[2,32,128]{2,1,0:T(8,128)S(1)} %get-tuple-element.85), channel_id=1, source_target_pairs={{1,2},{2,1},{5,6},{6,5},{9,10},{10,9},{13,14},{14,13},{17,18},{18,... | collective-permute-start | bytes 98312 | tf_op jit(solution)/shard_map/ppermute | solution.py:42
  55.0 1.5 %local_zero.1 = (f32[672,128]{1,0:T(8,128)S(1)}, f32[336,128]{1,0:T(8,128)S(1)}) custom-call(f32[336,128]{1,0:T(8,128)S(1)} %get-tuple-element.75.lam_ref, f32[336,128]{1,0:T(8,128)S(1)} %get-tuple-element.74.y_ref, f32[720,128]{1,0:T(8,128)S(1)} %copy-done.1), custom_call_target="tpu_custom_call" | custom-call | tf_op jit(solution)/shard_map/local_zero/pallas_call | solution.py:927
  56.5 0.5 collective-permute-done.10.from_y1
  57.0 2.1 %section_zero.1 = (f32[336,128]{1,0:T(8,128)}, f32[8,128]{1,0:T(8,128)S(1)}) custom-call(f32[336,128]{1,0:T(8,128)S(1)} %get-tuple-element.73.base_ref, f32[336,128]{1,0:T(8,128)S(1)} %get-tuple-element.74.y_ref, f32[720,128]{1,0:T(8,128)S(1)} %copy-done.1, f32[120,128]{1,0:T(8,128)S(1)} %get-tuple-element.61.fact_ref, ...), custom_call_target="tpu_custom_call" | custom-call | tf_op jit(solution)/shard_map/section_zero/pallas_call | solution.py:927
  59.1 0.6 %zone_total.1 = f32[2,128]{1,0:T(2,128)} custom-call(f32[32,2,128]{2,1,0:T(2,128)S(1)} %all-to-all-done.zone_ref, f32[8,128]{1,0:T(8,128)S(1)} %get-tuple-element.89.adjoint_ref), custom_call_target="tpu_custom_call" | custom-call | tf_op jit(solution)/shard_map/zone_total/pallas_call | solution.py:927
  (20 shorter events, 0.1 us)
Async XLA Ops:
  0.6 9.1 %copy-start.2 = (bf16[3,1,1,42,1024]{4,3,2,1,0:T(8,128)(2,1)S(1)}, bf16[3,1,1,42,1024]{4,3,2,1,0:T(8,128)(2,1)}, u32[]{:S(2)}) copy-start(bf16[3,1,1,42,1024]{4,3,2,1,0:T(8,128)(2,1)} %x_ref.9) | copy-start | bytes 774148
  0.6 9.1 %copy-start.3 = (f32[1,1,42,1024]{3,1,2,0:T(1,128)S(1)}, f32[1,1,42,1024]{3,1,2,0:T(1,128)}, u32[]{:S(2)}) copy-start(f32[1,1,42,1024]{3,1,2,0:T(1,128)} %param.16) | copy-start | bytes 516100
  4.5 8.2 %collective-permute-start = (f32[2,38,128]{2,1,0:T(8,128)}, f32[2,38,128]{2,1,0:T(8,128)S(1)}, u32[]{:S(2)}, u32[]{:S(2)}) collective-permute-start(f32[2,38,128]{2,1,0:T(8,128)} %get-tuple-element.52), channel_id=1, source_target_pairs={{4,8},{12,16},{20,24},{8,4},{16,12},{24,20},{5,9},{13,17},{21,25},... | collective-permute-start | bytes 116744 | tf_op jit(solution)/shard_map/ppermute | solution.py:42
  5.2 7.5 %collective-permute-start.1 = (f32[2,38,128]{2,1,0:T(8,128)}, f32[2,38,128]{2,1,0:T(8,128)S(1)}, u32[]{:S(2)}, u32[]{:S(2)}) collective-permute-start(f32[2,38,128]{2,1,0:T(8,128)} %get-tuple-element.53), channel_id=1, source_target_pairs={{0,4},{8,12},{16,20},{24,28},{4,0},{12,8},{20,16},{28,24},{1,5},{9... | collective-permute-start | bytes 116744 | tf_op jit(solution)/shard_map/ppermute | solution.py:42
  9.8 1.0 %copy-start = (f32[720,128]{1,0:T(8,128)S(1)}, f32[720,128]{1,0:T(8,128)}, u32[]{:S(2)}) copy-start(f32[720,128]{1,0:T(8,128)} %get-tuple-element.46.plan_ref) | copy-start | bytes 1105924
  10.8 1.9 %copy-start.4 = (f32[2,38,128]{2,1,0:T(8,128)S(1)}, f32[2,38,128]{2,1,0:T(8,128)}, u32[]{:S(2)}) copy-start(f32[2,38,128]{2,1,0:T(8,128)} %get-tuple-element.54.old_y1) | copy-start | bytes 116740
  10.8 1.9 %copy-start.5 = (f32[2,38,128]{2,1,0:T(8,128)S(1)}, f32[2,38,128]{2,1,0:T(8,128)}, u32[]{:S(2)}) copy-start(f32[2,38,128]{2,1,0:T(8,128)} %get-tuple-element.55.old_y2) | copy-start | bytes 116740
  10.8 6.3 %copy-start.1 = (f32[720,128]{1,0:T(8,128)S(1)}, f32[720,128]{1,0:T(8,128)}, u32[]{:S(2)}) copy-start(f32[720,128]{1,0:T(8,128)} %get-tuple-element.46.plan_ref) | copy-start | bytes 1105924
  12.7 6.4 %collective-permute-start.2 = (f32[2,38,128]{2,1,0:T(8,128)S(1)}, f32[2,38,128]{2,1,0:T(8,128)S(1)}, u32[]{:S(2)}, u32[]{:S(2)}) collective-permute-start(f32[2,38,128]{2,1,0:T(8,128)S(1)} %get-tuple-element.57), channel_id=1, source_target_pairs={{1,2},{2,1},{5,6},{6,5},{9,10},{10,9},{13,14},{14,13},{17,18},{18,... | collective-permute-start | bytes 116744 | tf_op jit(solution)/shard_map/ppermute | solution.py:42
  17.0 2.1 %collective-permute-start.3 = (f32[2,38,128]{2,1,0:T(8,128)S(1)}, f32[2,38,128]{2,1,0:T(8,128)S(1)}, u32[]{:S(2)}, u32[]{:S(2)}) collective-permute-start(f32[2,38,128]{2,1,0:T(8,128)S(1)} %get-tuple-element.58), channel_id=1, source_target_pairs={{0,1},{2,3},{1,0},{3,2},{4,5},{6,7},{5,4},{7,6},{8,9},{10,11},{9,8... | collective-permute-start | bytes 116744 | tf_op jit(solution)/shard_map/ppermute | solution.py:42
  22.1 6.0 %collective-permute-start.4 = (f32[2,59,128]{2,1,0:T(8,128)S(1)}, f32[2,59,128]{2,1,0:T(8,128)S(1)}, u32[]{:S(2)}, u32[]{:S(2)}) collective-permute-start(f32[2,59,128]{2,1,0:T(8,128)S(1)} %get-tuple-element.66), channel_id=1, source_target_pairs={{4,8},{12,16},{20,24},{8,4},{16,12},{24,20},{5,9},{13,17},{21,25},... | collective-permute-start | bytes 181256 | tf_op jit(solution)/shard_map/ppermute | solution.py:42
  22.8 5.8 %collective-permute-start.5 = (f32[2,59,128]{2,1,0:T(8,128)S(1)}, f32[2,59,128]{2,1,0:T(8,128)S(1)}, u32[]{:S(2)}, u32[]{:S(2)}) collective-permute-start(f32[2,59,128]{2,1,0:T(8,128)S(1)} %get-tuple-element.67), channel_id=1, source_target_pairs={{0,4},{8,12},{16,20},{24,28},{4,0},{12,8},{20,16},{28,24},{1,5},{9... | collective-permute-start | bytes 181256 | tf_op jit(solution)/shard_map/ppermute | solution.py:42
  28.7 5.9 %collective-permute-start.6 = (f32[2,59,128]{2,1,0:T(8,128)S(1)}, f32[2,59,128]{2,1,0:T(8,128)S(1)}, u32[]{:S(2)}, u32[]{:S(2)}) collective-permute-start(f32[2,59,128]{2,1,0:T(8,128)S(1)} %get-tuple-element.71), channel_id=1, source_target_pairs={{1,2},{2,1},{5,6},{6,5},{9,10},{10,9},{13,14},{14,13},{17,18},{18,... | collective-permute-start | bytes 181256 | tf_op jit(solution)/shard_map/ppermute | solution.py:42
  32.6 1.9 %collective-permute-start.7 = (f32[2,59,128]{2,1,0:T(8,128)S(1)}, f32[2,59,128]{2,1,0:T(8,128)S(1)}, u32[]{:S(2)}, u32[]{:S(2)}) collective-permute-start(f32[2,59,128]{2,1,0:T(8,128)S(1)} %get-tuple-element.72), channel_id=1, source_target_pairs={{0,1},{2,3},{1,0},{3,2},{4,5},{6,7},{5,4},{7,6},{8,9},{10,11},{9,8... | collective-permute-start | bytes 181256 | tf_op jit(solution)/shard_map/ppermute | solution.py:42
  37.4 8.0 %collective-permute-start.8 = (f32[2,32,128]{2,1,0:T(8,128)S(1)}, f32[2,32,128]{2,1,0:T(8,128)S(1)}, u32[]{:S(2)}, u32[]{:S(2)}) collective-permute-start(f32[2,32,128]{2,1,0:T(8,128)S(1)} %get-tuple-element.78), channel_id=1, source_target_pairs={{4,8},{12,16},{20,24},{8,4},{16,12},{24,20},{5,9},{13,17},{21,25},... | collective-permute-start | bytes 98312 | tf_op jit(solution)/shard_map/ppermute | solution.py:42
  38.0 7.4 %collective-permute-start.9 = (f32[2,32,128]{2,1,0:T(8,128)S(1)}, f32[2,32,128]{2,1,0:T(8,128)S(1)}, u32[]{:S(2)}, u32[]{:S(2)}) collective-permute-start(f32[2,32,128]{2,1,0:T(8,128)S(1)} %get-tuple-element.79), channel_id=1, source_target_pairs={{0,4},{8,12},{16,20},{24,28},{4,0},{12,8},{20,16},{28,24},{1,5},{9... | collective-permute-start | bytes 98312 | tf_op jit(solution)/shard_map/ppermute | solution.py:42
  45.4 1.3 %collective-permute-start.11 = (f32[2,32,128]{2,1,0:T(8,128)S(1)}, f32[2,32,128]{2,1,0:T(8,128)S(1)}, u32[]{:S(2)}, u32[]{:S(2)}) collective-permute-start(f32[2,32,128]{2,1,0:T(8,128)S(1)} %get-tuple-element.86), channel_id=1, source_target_pairs={{0,1},{2,3},{1,0},{3,2},{4,5},{6,7},{5,4},{7,6},{8,9},{10,11},{9,8... | collective-permute-start | bytes 98312 | tf_op jit(solution)/shard_map/ppermute | solution.py:42
  46.7 12.4 %all-to-all-start = ((f32[32,2,128]{2,1,0:T(2,128)}), f32[32,2,128]{2,1,0:T(2,128)S(1)}, u32[]{:S(2)}, u32[]{:S(2)}) async-start(f32[32,2,128]{2,1,0:T(2,128)} %after.1), calls=%async_computation | async-start | bytes 65536 | tf_op jit(solution)/shard_map/all_to_all | solution.py:1085
  51.5 5.6 %collective-permute-start.10 = (f32[2,32,128]{2,1,0:T(8,128)S(1)}, f32[2,32,128]{2,1,0:T(8,128)S(1)}, u32[]{:S(2)}, u32[]{:S(2)}) collective-permute-start(f32[2,32,128]{2,1,0:T(8,128)S(1)} %get-tuple-element.85), channel_id=1, source_target_pairs={{1,2},{2,1},{5,6},{6,5},{9,10},{10,9},{13,14},{14,13},{17,18},{18,... | collective-permute-start | bytes 98312 | tf_op jit(solution)/shard_map/ppermute | solution.py:42

commit v11 on v10

--- a/solution.py
+++ b/solution.py
@@ -1078,7 +1078,7 @@
         "after",
         [jax.ShapeDtypeStruct(zone_terms.shape, f32)],
         [],
-        [zone_terms, received[3]],
+        [zone_terms, received[2]],
         apart=(0, 1),
         aliases={0: 0},
     )

time: 60 us -> 63.8 us (1.063)
  waiting for transfers between devices: 4.08 us -> 7.3 us
    all_to_all x1, waiting for transfers between devices: 0.01 us -> 3.22 us  [local(): all_terms = lax.all_to_all(zone_terms, ('gx', 'gy'), 0, 0)]
  transfers between devices with their start and end apart: 13 -> 13, of which waited for: 4 -> 4; matrix products, arithmetic and copies ran while one was open for 0% -> 0% of each run, Pallas kernels for 19% -> 18%
where the time goes in v11:
time: 63.8 us; the launch traced here: 63.2 us
  starting transfers between devices  32.4 us (51%)
  Pallas kernels  21.6 us (34%)
  waiting for transfers between devices  7.3 us (11%)
  local copies, waits for them, and re-layouts  1.01 us (2%)
  between operations  0.87 us (1%)
    ppermute x12, starting transfers between devices, swapped(): lax.ppermute(x, axis, [(i, i + 1) for i in lows] + [(i + 1, i) for i in l...  27.5 us
    pallas_call x14, Pallas kernels, call(): pl.pallas_call(kernel, in_specs=specs, out_specs=[in_place if n in handed...  21.6 us
    all_to_all x1, starting transfers between devices, local(): all_terms = lax.all_to_all(zone_terms, ('gx', 'gy'), 0, 0)  4.82 us
    ppermute x12, waiting for transfers between devices, swapped(): lax.ppermute(x, axis, [(i, i + 1) for i in lows] + [(i + 1, i) for i in l...  4.08 us
    all_to_all x1, waiting for transfers between devices, local(): all_terms = lax.all_to_all(zone_terms, ('gx', 'gy'), 0, 0)  3.22 us
  transfers between devices with their start and end apart: 13, of which 4 were waited for; matrix products, arithmetic and copies ran while one was open for 0% of the time, Pallas kernels for 18%

profile of v11, /device:TPU:1, one launch (start us, length us, event | category | flops | bytes accessed | tf_op | source)
XLA Modules:
  0.0 63.2 jit_solution(18017680266681555930)
XLA Ops:
  0.7 3.8 %prepare.1 = (f32[720,128]{1,0:T(8,128)}, f32[2,38,128]{2,1,0:T(8,128)}, f32[2,38,128]{2,1,0:T(8,128)}, f32[2,38,128]{2,1,0:T(8,128)}, f32[2,38,128]{2,1,0:T(8,128)}) custom-call(f32[336,128]{1,0:T(8,128)} %bitcast.11, bf16[3,1,1,42,1024]{4,3,2,1,0:T(8,128)(2,1)} %x_ref.9, f32[8,128]{1,0:T(8,128)} %bitcast.17, f32[24,128]{1,0:T(8,128)} %bitcast.15, ...), custom_call_target="tpu_custom_call" | custom-call | tf_op jit(solution)/shard_map/prepare/pallas_call | solution.py:927
  4.5 0.7 %collective-permute-start = (f32[2,38,128]{2,1,0:T(8,128)}, f32[2,38,128]{2,1,0:T(8,128)S(1)}, u32[]{:S(2)}, u32[]{:S(2)}) collective-permute-start(f32[2,38,128]{2,1,0:T(8,128)} %get-tuple-element.52), channel_id=1, source_target_pairs={{4,8},{12,16},{20,24},{8,4},{16,12},{24,20},{5,9},{13,17},{21,25},... | collective-permute-start | bytes 116744 | tf_op jit(solution)/shard_map/ppermute | solution.py:42
  5.2 4.6 %collective-permute-start.1 = (f32[2,38,128]{2,1,0:T(8,128)}, f32[2,38,128]{2,1,0:T(8,128)S(1)}, u32[]{:S(2)}, u32[]{:S(2)}) collective-permute-start(f32[2,38,128]{2,1,0:T(8,128)} %get-tuple-element.53), channel_id=1, source_target_pairs={{0,4},{8,12},{16,20},{24,28},{4,0},{12,8},{20,16},{28,24},{1,5},{9... | collective-permute-start | bytes 116744 | tf_op jit(solution)/shard_map/ppermute | solution.py:42
  9.8 1.0 %copy-done = f32[720,128]{1,0:T(8,128)S(1)} copy-done((f32[720,128]{1,0:T(8,128)S(1)}, f32[720,128]{1,0:T(8,128)}, u32[]{:S(2)}) %copy-start) | copy-done | bytes 368664
  10.8 1.8 %local_two.1 = (f32[672,128]{1,0:T(8,128)S(1)}, f32[120,128]{1,0:T(8,128)S(1)}, f32[16,128]{1,0:T(8,128)S(1)}, f32[336,128]{1,0:T(8,128)S(1)}) custom-call(f32[336,128]{1,0:T(8,128)S(1)} %bitcast.12, f32[720,128]{1,0:T(8,128)S(1)} %copy-done, bf16[3,1,1,42,1024]{4,3,2,1,0:T(8,128)(2,1)S(1)} %copy-done.2), custom_call_target="tpu_custom_call" | custom-call | tf_op jit(solution)/shard_map/local_two/pallas_call | solution.py:927
  12.6 0.0 collective-permute-done.1.x2.from_x2
  12.7 4.3 %collective-permute-start.2 = (f32[2,38,128]{2,1,0:T(8,128)S(1)}, f32[2,38,128]{2,1,0:T(8,128)S(1)}, u32[]{:S(2)}, u32[]{:S(2)}) collective-permute-start(f32[2,38,128]{2,1,0:T(8,128)S(1)} %get-tuple-element.57), channel_id=1, source_target_pairs={{1,2},{2,1},{5,6},{6,5},{9,10},{10,9},{13,14},{14,13},{17,18},{18,... | collective-permute-start | bytes 116744 | tf_op jit(solution)/shard_map/ppermute | solution.py:42
  17.0 0.1 collective-permute-start.3
  17.0 2.0 %local_x.1 = (f32[480,128]{1,0:T(8,128)S(1)}, f32[192,128]{1,0:T(8,128)S(1)}, f32[8,128]{1,0:T(8,128)S(1)}) custom-call(f32[720,128]{1,0:T(8,128)S(1)} %copy-done.1, bf16[3,1,1,42,1024]{4,3,2,1,0:T(8,128)(2,1)S(1)} %copy-done.2), custom_call_target="tpu_custom_call" | custom-call | tf_op jit(solution)/shard_map/local_x/pallas_call | solution.py:927
  19.1 0.0 collective-permute-done.3.from_y2
  19.1 3.1 %section_two.1 = (f32[336,128]{1,0:T(8,128)S(1)}, f32[336,128]{1,0:T(8,128)S(1)}, f32[120,128]{1,0:T(8,128)S(1)}, f32[672,128]{1,0:T(8,128)S(1)}, f32[2,59,128]{...) custom-call(f32[336,128]{1,0:T(8,128)S(1)} %bitcast.13, ...), custom_call_target="tpu_custom_call" | custom-call | tf_op jit(solution)/shard_map/section_two/pallas_call | solution.py:927
  22.1 0.7 %collective-permute-start.4 = (f32[2,59,128]{2,1,0:T(8,128)S(1)}, f32[2,59,128]{2,1,0:T(8,128)S(1)}, u32[]{:S(2)}, u32[]{:S(2)}) collective-permute-start(f32[2,59,128]{2,1,0:T(8,128)S(1)} %get-tuple-element.66), channel_id=1, source_target_pairs={{4,8},{12,16},{20,24},{8,4},{16,12},{24,20},{5,9},{13,17},{21,25},... | collective-permute-start | bytes 181256 | tf_op jit(solution)/shard_map/ppermute | solution.py:42
  22.8 3.8 %collective-permute-start.5 = (f32[2,59,128]{2,1,0:T(8,128)S(1)}, f32[2,59,128]{2,1,0:T(8,128)S(1)}, u32[]{:S(2)}, u32[]{:S(2)}) collective-permute-start(f32[2,59,128]{2,1,0:T(8,128)S(1)} %get-tuple-element.67), channel_id=1, source_target_pairs={{0,4},{8,12},{16,20},{24,28},{4,0},{12,8},{20,16},{28,24},{1,5},{9... | collective-permute-start | bytes 181256 | tf_op jit(solution)/shard_map/ppermute | solution.py:42
  26.6 1.6 %local_one.1 = (f32[672,128]{1,0:T(8,128)S(1)}, f32[40,128]{1,0:T(8,128)S(1)}, f32[336,128]{1,0:T(8,128)S(1)}) custom-call(f32[336,128]{1,0:T(8,128)S(1)} %get-tuple-element.59.lam_ref, f32[336,128]{1,0:T(8,128)S(1)} %get-tuple-element.60.y_ref, f32[720,128]{1,0:T(8,128)S(1)} %copy-done.1, f32[120,128]{1,0:T(8,128)S(1)} %get-tuple-element.61.fact_ref, ...), custom_call_target="tpu_custom_call" | custom-call | tf_op jit(solution)/shard_map/local_one/pallas_call | solution.py:927
  28.2 0.5 collective-permute-done.5.x2.from_x2
  28.7 3.9 %collective-permute-start.6 = (f32[2,59,128]{2,1,0:T(8,128)S(1)}, f32[2,59,128]{2,1,0:T(8,128)S(1)}, u32[]{:S(2)}, u32[]{:S(2)}) collective-permute-start(f32[2,59,128]{2,1,0:T(8,128)S(1)} %get-tuple-element.71), channel_id=1, source_target_pairs={{1,2},{2,1},{5,6},{6,5},{9,10},{10,9},{13,14},{14,13},{17,18},{18,... | collective-permute-start | bytes 181256 | tf_op jit(solution)/shard_map/ppermute | solution.py:42
  32.6 0.1 collective-permute-start.7
  32.7 1.9 %collective-permute-done.6.from_y1 = f32[2,59,128]{2,1,0:T(8,128)S(1)} collective-permute-done((f32[2,59,128]{2,1,0:T(8,128)S(1)}, f32[2,59,128]{2,1,0:T(8,128)S(1)}, u32[]{:S(2)}, u32[]{:S(2)}) %collective-permute-start.6) | collective-permute-done | bytes 60448 | tf_op jit(solution)/shard_map/ppermute | solution.py:42
  34.5 0.0 collective-permute-done.7.from_y2
  34.5 2.8 %section_one.1 = (f32[336,128]{1,0:T(8,128)S(1)}, f32[336,128]{1,0:T(8,128)S(1)}, f32[336,128]{1,0:T(8,128)S(1)}, f32[672,128]{1,0:T(8,128)S(1)}, f32[2,32,128]{...) custom-call(f32[336,128]{1,0:T(8,128)S(1)} %bitcast.14, ...), custom_call_target="tpu_custom_call" | custom-call | tf_op jit(solution)/shard_map/section_one/pallas_call | solution.py:927
  37.4 0.7 %collective-permute-start.8 = (f32[2,32,128]{2,1,0:T(8,128)S(1)}, f32[2,32,128]{2,1,0:T(8,128)S(1)}, u32[]{:S(2)}, u32[]{:S(2)}) collective-permute-start(f32[2,32,128]{2,1,0:T(8,128)S(1)} %get-tuple-element.78), channel_id=1, source_target_pairs={{4,8},{12,16},{20,24},{8,4},{16,12},{24,20},{5,9},{13,17},{21,25},... | collective-permute-start | bytes 98312 | tf_op jit(solution)/shard_map/ppermute | solution.py:42
  38.0 5.0 %collective-permute-start.9 = (f32[2,32,128]{2,1,0:T(8,128)S(1)}, f32[2,32,128]{2,1,0:T(8,128)S(1)}, u32[]{:S(2)}, u32[]{:S(2)}) collective-permute-start(f32[2,32,128]{2,1,0:T(8,128)S(1)} %get-tuple-element.79), channel_id=1, source_target_pairs={{0,4},{8,12},{16,20},{24,28},{4,0},{12,8},{20,16},{28,24},{1,5},{9... | collective-permute-start | bytes 98312 | tf_op jit(solution)/shard_map/ppermute | solution.py:42
  43.0 2.4 %zone_sums.1.rest_0_ = f32[32,2,128]{2,1,0:T(2,128)} custom-call(f32[336,128]{1,0:T(8,128)S(1)} %get-tuple-element.75.lam_ref, f32[336,128]{1,0:T(8,128)S(1)} %get-tuple-element.74.y_ref, f32[720,128]{1,0:T(8,128)S(1)} %copy-done.1, f32[120,128]{1,0:T(8,128)S(1)} %get-tuple-element.61.fact_ref, f32[672,128]{1,0:T(8,128)S(1)} %get-tuple-element.82.old_outer_ref, ...), custom_call_target="tpu_custom_call" | custom-call | tf_op jit(solution)/shard_map/zone_sums/pallas_call | solution.py:927
  45.4 0.0 collective-permute-done.8.x1.from_x1
  45.4 3.5 %collective-permute-start.10 = (f32[2,32,128]{2,1,0:T(8,128)S(1)}, f32[2,32,128]{2,1,0:T(8,128)S(1)}, u32[]{:S(2)}, u32[]{:S(2)}) collective-permute-start(f32[2,32,128]{2,1,0:T(8,128)S(1)} %get-tuple-element.85), channel_id=1, source_target_pairs={{1,2},{2,1},{5,6},{6,5},{9,10},{10,9},{13,14},{14,13},{17,18},{18,... | collective-permute-start | bytes 98312 | tf_op jit(solution)/shard_map/ppermute | solution.py:42
  48.9 1.7 %collective-permute-done.10.from_y1.message_ref = f32[2,32,128]{2,1,0:T(8,128)S(1)} collective-permute-done((f32[2,32,128]{2,1,0:T(8,128)S(1)}, f32[2,32,128]{2,1,0:T(8,128)S(1)}, u32[]{:S(2)}, u32[]{:S(2)}) %collective-permute-start.10) | collective-permute-done | bytes 32800 | tf_op jit(solution)/shard_map/ppermute | solution.py:42
  50.6 4.8 %all-to-all-start = ((f32[32,2,128]{2,1,0:T(2,128)}), f32[32,2,128]{2,1,0:T(2,128)S(1)}, u32[]{:S(2)}, u32[]{:S(2)}) async-start(f32[32,2,128]{2,1,0:T(2,128)} %after.1), calls=%async_computation | async-start | bytes 65536 | tf_op jit(solution)/shard_map/all_to_all | solution.py:1085
  55.5 0.3 collective-permute-start.11
  55.8 1.5 %local_zero.1 = (f32[672,128]{1,0:T(8,128)S(1)}, f32[336,128]{1,0:T(8,128)S(1)}) custom-call(f32[336,128]{1,0:T(8,128)S(1)} %get-tuple-element.75.lam_ref, f32[336,128]{1,0:T(8,128)S(1)} %get-tuple-element.74.y_ref, f32[720,128]{1,0:T(8,128)S(1)} %copy-done.1), custom_call_target="tpu_custom_call" | custom-call | tf_op jit(solution)/shard_map/local_zero/pallas_call | solution.py:927
  57.3 2.1 %section_zero.1 = (f32[336,128]{1,0:T(8,128)}, f32[8,128]{1,0:T(8,128)S(1)}) custom-call(f32[336,128]{1,0:T(8,128)S(1)} %get-tuple-element.73.base_ref, f32[336,128]{1,0:T(8,128)S(1)} %get-tuple-element.74.y_ref, f32[720,128]{1,0:T(8,128)S(1)} %copy-done.1, f32[120,128]{1,0:T(8,128)S(1)} %get-tuple-element.61.fact_ref, ...), custom_call_target="tpu_custom_call" | custom-call | tf_op jit(solution)/shard_map/section_zero/pallas_call | solution.py:927
  59.4 3.2 %all-to-all-done.zone_ref = f32[32,2,128]{2,1,0:T(2,128)S(1)} async-done(((f32[32,2,128]{2,1,0:T(2,128)}), f32[32,2,128]{2,1,0:T(2,128)S(1)}, u32[]{:S(2)}, u32[]{:S(2)}) %all-to-all-start) | async-done | bytes 32800 | tf_op jit(solution)/shard_map/all_to_all | solution.py:1085
  62.6 0.6 zone_total.1
  (20 shorter events, 0.1 us)
Async XLA Ops:
  0.6 9.1 %copy-start.2 = (bf16[3,1,1,42,1024]{4,3,2,1,0:T(8,128)(2,1)S(1)}, bf16[3,1,1,42,1024]{4,3,2,1,0:T(8,128)(2,1)}, u32[]{:S(2)}) copy-start(bf16[3,1,1,42,1024]{4,3,2,1,0:T(8,128)(2,1)} %x_ref.9) | copy-start | bytes 774148
  0.6 9.1 %copy-start.3 = (f32[1,1,42,1024]{3,1,2,0:T(1,128)S(1)}, f32[1,1,42,1024]{3,1,2,0:T(1,128)}, u32[]{:S(2)}) copy-start(f32[1,1,42,1024]{3,1,2,0:T(1,128)} %param.16) | copy-start | bytes 516100
  4.5 8.2 %collective-permute-start = (f32[2,38,128]{2,1,0:T(8,128)}, f32[2,38,128]{2,1,0:T(8,128)S(1)}, u32[]{:S(2)}, u32[]{:S(2)}) collective-permute-start(f32[2,38,128]{2,1,0:T(8,128)} %get-tuple-element.52), channel_id=1, source_target_pairs={{4,8},{12,16},{20,24},{8,4},{16,12},{24,20},{5,9},{13,17},{21,25},... | collective-permute-start | bytes 116744 | tf_op jit(solution)/shard_map/ppermute | solution.py:42
  5.2 7.5 %collective-permute-start.1 = (f32[2,38,128]{2,1,0:T(8,128)}, f32[2,38,128]{2,1,0:T(8,128)S(1)}, u32[]{:S(2)}, u32[]{:S(2)}) collective-permute-start(f32[2,38,128]{2,1,0:T(8,128)} %get-tuple-element.53), channel_id=1, source_target_pairs={{0,4},{8,12},{16,20},{24,28},{4,0},{12,8},{20,16},{28,24},{1,5},{9... | collective-permute-start | bytes 116744 | tf_op jit(solution)/shard_map/ppermute | solution.py:42
  9.8 1.0 %copy-start = (f32[720,128]{1,0:T(8,128)S(1)}, f32[720,128]{1,0:T(8,128)}, u32[]{:S(2)}) copy-start(f32[720,128]{1,0:T(8,128)} %get-tuple-element.46.plan_ref) | copy-start | bytes 1105924
  10.8 1.9 %copy-start.4 = (f32[2,38,128]{2,1,0:T(8,128)S(1)}, f32[2,38,128]{2,1,0:T(8,128)}, u32[]{:S(2)}) copy-start(f32[2,38,128]{2,1,0:T(8,128)} %get-tuple-element.54.old_y1) | copy-start | bytes 116740
  10.8 1.9 %copy-start.5 = (f32[2,38,128]{2,1,0:T(8,128)S(1)}, f32[2,38,128]{2,1,0:T(8,128)}, u32[]{:S(2)}) copy-start(f32[2,38,128]{2,1,0:T(8,128)} %get-tuple-element.55.old_y2) | copy-start | bytes 116740
  10.8 6.3 %copy-start.1 = (f32[720,128]{1,0:T(8,128)S(1)}, f32[720,128]{1,0:T(8,128)}, u32[]{:S(2)}) copy-start(f32[720,128]{1,0:T(8,128)} %get-tuple-element.46.plan_ref) | copy-start | bytes 1105924
  12.7 6.4 %collective-permute-start.2 = (f32[2,38,128]{2,1,0:T(8,128)S(1)}, f32[2,38,128]{2,1,0:T(8,128)S(1)}, u32[]{:S(2)}, u32[]{:S(2)}) collective-permute-start(f32[2,38,128]{2,1,0:T(8,128)S(1)} %get-tuple-element.57), channel_id=1, source_target_pairs={{1,2},{2,1},{5,6},{6,5},{9,10},{10,9},{13,14},{14,13},{17,18},{18,... | collective-permute-start | bytes 116744 | tf_op jit(solution)/shard_map/ppermute | solution.py:42
  17.0 2.1 %collective-permute-start.3 = (f32[2,38,128]{2,1,0:T(8,128)S(1)}, f32[2,38,128]{2,1,0:T(8,128)S(1)}, u32[]{:S(2)}, u32[]{:S(2)}) collective-permute-start(f32[2,38,128]{2,1,0:T(8,128)S(1)} %get-tuple-element.58), channel_id=1, source_target_pairs={{0,1},{2,3},{1,0},{3,2},{4,5},{6,7},{5,4},{7,6},{8,9},{10,11},{9,8... | collective-permute-start | bytes 116744 | tf_op jit(solution)/shard_map/ppermute | solution.py:42
  22.1 6.0 %collective-permute-start.4 = (f32[2,59,128]{2,1,0:T(8,128)S(1)}, f32[2,59,128]{2,1,0:T(8,128)S(1)}, u32[]{:S(2)}, u32[]{:S(2)}) collective-permute-start(f32[2,59,128]{2,1,0:T(8,128)S(1)} %get-tuple-element.66), channel_id=1, source_target_pairs={{4,8},{12,16},{20,24},{8,4},{16,12},{24,20},{5,9},{13,17},{21,25},... | collective-permute-start | bytes 181256 | tf_op jit(solution)/shard_map/ppermute | solution.py:42
  22.8 5.8 %collective-permute-start.5 = (f32[2,59,128]{2,1,0:T(8,128)S(1)}, f32[2,59,128]{2,1,0:T(8,128)S(1)}, u32[]{:S(2)}, u32[]{:S(2)}) collective-permute-start(f32[2,59,128]{2,1,0:T(8,128)S(1)} %get-tuple-element.67), channel_id=1, source_target_pairs={{0,4},{8,12},{16,20},{24,28},{4,0},{12,8},{20,16},{28,24},{1,5},{9... | collective-permute-start | bytes 181256 | tf_op jit(solution)/shard_map/ppermute | solution.py:42
  28.7 5.9 %collective-permute-start.6 = (f32[2,59,128]{2,1,0:T(8,128)S(1)}, f32[2,59,128]{2,1,0:T(8,128)S(1)}, u32[]{:S(2)}, u32[]{:S(2)}) collective-permute-start(f32[2,59,128]{2,1,0:T(8,128)S(1)} %get-tuple-element.71), channel_id=1, source_target_pairs={{1,2},{2,1},{5,6},{6,5},{9,10},{10,9},{13,14},{14,13},{17,18},{18,... | collective-permute-start | bytes 181256 | tf_op jit(solution)/shard_map/ppermute | solution.py:42
  32.6 1.9 %collective-permute-start.7 = (f32[2,59,128]{2,1,0:T(8,128)S(1)}, f32[2,59,128]{2,1,0:T(8,128)S(1)}, u32[]{:S(2)}, u32[]{:S(2)}) collective-permute-start(f32[2,59,128]{2,1,0:T(8,128)S(1)} %get-tuple-element.72), channel_id=1, source_target_pairs={{0,1},{2,3},{1,0},{3,2},{4,5},{6,7},{5,4},{7,6},{8,9},{10,11},{9,8... | collective-permute-start | bytes 181256 | tf_op jit(solution)/shard_map/ppermute | solution.py:42
  37.4 8.0 %collective-permute-start.8 = (f32[2,32,128]{2,1,0:T(8,128)S(1)}, f32[2,32,128]{2,1,0:T(8,128)S(1)}, u32[]{:S(2)}, u32[]{:S(2)}) collective-permute-start(f32[2,32,128]{2,1,0:T(8,128)S(1)} %get-tuple-element.78), channel_id=1, source_target_pairs={{4,8},{12,16},{20,24},{8,4},{16,12},{24,20},{5,9},{13,17},{21,25},... | collective-permute-start | bytes 98312 | tf_op jit(solution)/shard_map/ppermute | solution.py:42
  38.0 7.4 %collective-permute-start.9 = (f32[2,32,128]{2,1,0:T(8,128)S(1)}, f32[2,32,128]{2,1,0:T(8,128)S(1)}, u32[]{:S(2)}, u32[]{:S(2)}) collective-permute-start(f32[2,32,128]{2,1,0:T(8,128)S(1)} %get-tuple-element.79), channel_id=1, source_target_pairs={{0,4},{8,12},{16,20},{24,28},{4,0},{12,8},{20,16},{28,24},{1,5},{9... | collective-permute-start | bytes 98312 | tf_op jit(solution)/shard_map/ppermute | solution.py:42
  45.4 5.2 %collective-permute-start.10 = (f32[2,32,128]{2,1,0:T(8,128)S(1)}, f32[2,32,128]{2,1,0:T(8,128)S(1)}, u32[]{:S(2)}, u32[]{:S(2)}) collective-permute-start(f32[2,32,128]{2,1,0:T(8,128)S(1)} %get-tuple-element.85), channel_id=1, source_target_pairs={{1,2},{2,1},{5,6},{6,5},{9,10},{10,9},{13,14},{14,13},{17,18},{18,... | collective-permute-start | bytes 98312 | tf_op jit(solution)/shard_map/ppermute | solution.py:42
  50.6 11.9 %all-to-all-start = ((f32[32,2,128]{2,1,0:T(2,128)}), f32[32,2,128]{2,1,0:T(2,128)S(1)}, u32[]{:S(2)}, u32[]{:S(2)}) async-start(f32[32,2,128]{2,1,0:T(2,128)} %after.1), calls=%async_computation | async-start | bytes 65536 | tf_op jit(solution)/shard_map/all_to_all | solution.py:1085
  55.5 1.8 %collective-permute-start.11 = (f32[2,32,128]{2,1,0:T(8,128)S(1)}, f32[2,32,128]{2,1,0:T(8,128)S(1)}, u32[]{:S(2)}, u32[]{:S(2)}) collective-permute-start(f32[2,32,128]{2,1,0:T(8,128)S(1)} %get-tuple-element.86), channel_id=1, source_target_pairs={{0,1},{2,3},{1,0},{3,2},{4,5},{6,7},{5,4},{7,6},{8,9},{10,11},{9,8... | collective-permute-start | bytes 98312 | tf_op jit(solution)/shard_map/ppermute | solution.py:42

commit v12 on v11

--- a/solution.py
+++ b/solution.py
@@ -853,10 +853,6 @@
         out_ref[device, 1:2, :] = conduct
 
 
-def after_kernel(zone_in, message_ref, zone_ref):
-    pass
-
-
 def local_zero_kernel(lam_ref, y_ref, plan_ref, outer_ref, own_ref, matrix_ref, sem):
     matrices = load_matrices(plan_ref, matrix_ref, sem)
     stat_ref, index_ref, _, _ = plan_parts(plan_ref)
@@ -1073,15 +1069,6 @@
         [lam, y, plan, fact, outer, term, section_states, x_near, *received],
     )
     received, zone_terms = exchange(channels, to_send, zone_terms)
-    (zone_terms,) = call(
-        after_kernel,
-        "after",
-        [jax.ShapeDtypeStruct(zone_terms.shape, f32)],
-        [],
-        [zone_terms, received[2]],
-        apart=(0, 1),
-        aliases={0: 0},
-    )
     all_terms = lax.all_to_all(zone_terms, ("gx", "gy"), 0, 0)
     near_outer, own = call(
         local_zero_kernel,

time: 63.8 us -> 58.8 us (0.922)
  waiting for transfers between devices: 7.3 us -> 2.81 us
    all_to_all x1, waiting for transfers between devices: 3.22 us -> 0.01 us  [local(): all_terms = lax.all_to_all(zone_terms, ('gx', 'gy'), 0, 0)]
    ppermute x12, waiting for transfers between devices: 4.08 us -> 2.8 us  [swapped(): lax.ppermute(x, axis, [(i, i + 1) for i in lows] + [(i + 1, i) for i in l...]
    pallas_call x14 -> x13, Pallas kernels: 21.6 us -> 21.6 us  [call(): pl.pallas_call(kernel, in_specs=specs, out_specs=[in_place if n in handed...]
  transfers between devices with their start and end apart: 13 -> 13, of which waited for: 4 -> 3; matrix products, arithmetic and copies ran while one was open for 0% -> 0% of each run, Pallas kernels for 18% -> 19%
where the time goes in v12:
time: 58.8 us; the launch traced here: 58.5 us
  starting transfers between devices  32.2 us (55%)
  Pallas kernels  21.6 us (37%)
  waiting for transfers between devices  2.81 us (5%)
  local copies, waits for them, and re-layouts  1.01 us (2%)
  between operations  0.88 us (1%)
    ppermute x12, starting transfers between devices, swapped(): lax.ppermute(x, axis, [(i, i + 1) for i in lows] + [(i + 1, i) for i in l...  27.4 us
    pallas_call x13, Pallas kernels, call(): pl.pallas_call(kernel, in_specs=specs, out_specs=[in_place if n in handed...  21.6 us
    all_to_all x1, starting transfers between devices, local(): all_terms = lax.all_to_all(zone_terms, ('gx', 'gy'), 0, 0)  4.83 us
    ppermute x12, waiting for transfers between devices, swapped(): lax.ppermute(x, axis, [(i, i + 1) for i in lows] + [(i + 1, i) for i in l...  2.8 us
  transfers between devices with their start and end apart: 13, of which 3 were waited for; matrix products, arithmetic and copies ran while one was open for 0% of the time, Pallas kernels for 19%

profile of v12, /device:TPU:1, one launch (start us, length us, event | category | flops | bytes accessed | tf_op | source)
XLA Modules:
  0.0 58.5 jit_solution(10540195469350188349)
XLA Ops:
  0.7 3.8 %prepare.1 = (f32[720,128]{1,0:T(8,128)}, f32[2,38,128]{2,1,0:T(8,128)}, f32[2,38,128]{2,1,0:T(8,128)}, f32[2,38,128]{2,1,0:T(8,128)}, f32[2,38,128]{2,1,0:T(8,128)}) custom-call(f32[336,128]{1,0:T(8,128)} %bitcast.11, bf16[3,1,1,42,1024]{4,3,2,1,0:T(8,128)(2,1)} %x_ref.9, f32[8,128]{1,0:T(8,128)} %bitcast.17, f32[24,128]{1,0:T(8,128)} %bitcast.15, ...), custom_call_target="tpu_custom_call" | custom-call | tf_op jit(solution)/shard_map/prepare/pallas_call | solution.py:923
  4.5 0.7 %collective-permute-start = (f32[2,38,128]{2,1,0:T(8,128)}, f32[2,38,128]{2,1,0:T(8,128)S(1)}, u32[]{:S(2)}, u32[]{:S(2)}) collective-permute-start(f32[2,38,128]{2,1,0:T(8,128)} %get-tuple-element.52), channel_id=1, source_target_pairs={{4,8},{12,16},{20,24},{8,4},{16,12},{24,20},{5,9},{13,17},{21,25},... | collective-permute-start | bytes 116744 | tf_op jit(solution)/shard_map/ppermute | solution.py:42
  5.2 4.6 %collective-permute-start.1 = (f32[2,38,128]{2,1,0:T(8,128)}, f32[2,38,128]{2,1,0:T(8,128)S(1)}, u32[]{:S(2)}, u32[]{:S(2)}) collective-permute-start(f32[2,38,128]{2,1,0:T(8,128)} %get-tuple-element.53), channel_id=1, source_target_pairs={{0,4},{8,12},{16,20},{24,28},{4,0},{12,8},{20,16},{28,24},{1,5},{9... | collective-permute-start | bytes 116744 | tf_op jit(solution)/shard_map/ppermute | solution.py:42
  9.8 1.0 %copy-done = f32[720,128]{1,0:T(8,128)S(1)} copy-done((f32[720,128]{1,0:T(8,128)S(1)}, f32[720,128]{1,0:T(8,128)}, u32[]{:S(2)}) %copy-start) | copy-done | bytes 368664
  10.8 1.8 %local_two.1 = (f32[672,128]{1,0:T(8,128)S(1)}, f32[120,128]{1,0:T(8,128)S(1)}, f32[16,128]{1,0:T(8,128)S(1)}, f32[336,128]{1,0:T(8,128)S(1)}) custom-call(f32[336,128]{1,0:T(8,128)S(1)} %bitcast.12, f32[720,128]{1,0:T(8,128)S(1)} %copy-done, bf16[3,1,1,42,1024]{4,3,2,1,0:T(8,128)(2,1)S(1)} %copy-done.2), custom_call_target="tpu_custom_call" | custom-call | tf_op jit(solution)/shard_map/local_two/pallas_call | solution.py:923
  12.6 0.0 collective-permute-done.x1.from_x1
  12.6 0.0 collective-permute-done.1.x2.from_x2
  12.7 4.3 %collective-permute-start.2 = (f32[2,38,128]{2,1,0:T(8,128)S(1)}, f32[2,38,128]{2,1,0:T(8,128)S(1)}, u32[]{:S(2)}, u32[]{:S(2)}) collective-permute-start(f32[2,38,128]{2,1,0:T(8,128)S(1)} %get-tuple-element.57), channel_id=1, source_target_pairs={{1,2},{2,1},{5,6},{6,5},{9,10},{10,9},{13,14},{14,13},{17,18},{18,... | collective-permute-start | bytes 116744 | tf_op jit(solution)/shard_map/ppermute | solution.py:42
  17.0 0.1 collective-permute-start.3
  17.0 2.0 %local_x.1 = (f32[480,128]{1,0:T(8,128)S(1)}, f32[192,128]{1,0:T(8,128)S(1)}, f32[8,128]{1,0:T(8,128)S(1)}) custom-call(f32[720,128]{1,0:T(8,128)S(1)} %copy-done.1, bf16[3,1,1,42,1024]{4,3,2,1,0:T(8,128)(2,1)S(1)} %copy-done.2), custom_call_target="tpu_custom_call" | custom-call | tf_op jit(solution)/shard_map/local_x/pallas_call | solution.py:923
  19.1 0.0 collective-permute-done.2.from_y1
  19.1 0.0 collective-permute-done.3.from_y2
  19.1 3.1 %section_two.1 = (f32[336,128]{1,0:T(8,128)S(1)}, f32[336,128]{1,0:T(8,128)S(1)}, f32[120,128]{1,0:T(8,128)S(1)}, f32[672,128]{1,0:T(8,128)S(1)}, f32[2,59,128]{...) custom-call(f32[336,128]{1,0:T(8,128)S(1)} %bitcast.13, ...), custom_call_target="tpu_custom_call" | custom-call | tf_op jit(solution)/shard_map/section_two/pallas_call | solution.py:923
  22.1 0.7 %collective-permute-start.4 = (f32[2,59,128]{2,1,0:T(8,128)S(1)}, f32[2,59,128]{2,1,0:T(8,128)S(1)}, u32[]{:S(2)}, u32[]{:S(2)}) collective-permute-start(f32[2,59,128]{2,1,0:T(8,128)S(1)} %get-tuple-element.66), channel_id=1, source_target_pairs={{4,8},{12,16},{20,24},{8,4},{16,12},{24,20},{5,9},{13,17},{21,25},... | collective-permute-start | bytes 181256 | tf_op jit(solution)/shard_map/ppermute | solution.py:42
  22.8 3.8 %collective-permute-start.5 = (f32[2,59,128]{2,1,0:T(8,128)S(1)}, f32[2,59,128]{2,1,0:T(8,128)S(1)}, u32[]{:S(2)}, u32[]{:S(2)}) collective-permute-start(f32[2,59,128]{2,1,0:T(8,128)S(1)} %get-tuple-element.67), channel_id=1, source_target_pairs={{0,4},{8,12},{16,20},{24,28},{4,0},{12,8},{20,16},{28,24},{1,5},{9... | collective-permute-start | bytes 181256 | tf_op jit(solution)/shard_map/ppermute | solution.py:42
  26.6 1.6 %local_one.1 = (f32[672,128]{1,0:T(8,128)S(1)}, f32[40,128]{1,0:T(8,128)S(1)}, f32[336,128]{1,0:T(8,128)S(1)}) custom-call(f32[336,128]{1,0:T(8,128)S(1)} %get-tuple-element.59.lam_ref, f32[336,128]{1,0:T(8,128)S(1)} %get-tuple-element.60.y_ref, f32[720,128]{1,0:T(8,128)S(1)} %copy-done.1, f32[120,128]{1,0:T(8,128)S(1)} %get-tuple-element.61.fact_ref, ...), custom_call_target="tpu_custom_call" | custom-call | tf_op jit(solution)/shard_map/local_one/pallas_call | solution.py:923
  28.2 0.0 collective-permute-done.4.x1.from_x1
  28.2 0.5 collective-permute-done.5.x2.from_x2
  28.7 3.9 %collective-permute-start.6 = (f32[2,59,128]{2,1,0:T(8,128)S(1)}, f32[2,59,128]{2,1,0:T(8,128)S(1)}, u32[]{:S(2)}, u32[]{:S(2)}) collective-permute-start(f32[2,59,128]{2,1,0:T(8,128)S(1)} %get-tuple-element.71), channel_id=1, source_target_pairs={{1,2},{2,1},{5,6},{6,5},{9,10},{10,9},{13,14},{14,13},{17,18},{18,... | collective-permute-start | bytes 181256 | tf_op jit(solution)/shard_map/ppermute | solution.py:42
  32.6 0.1 collective-permute-start.7
  32.7 1.9 %collective-permute-done.6.from_y1 = f32[2,59,128]{2,1,0:T(8,128)S(1)} collective-permute-done((f32[2,59,128]{2,1,0:T(8,128)S(1)}, f32[2,59,128]{2,1,0:T(8,128)S(1)}, u32[]{:S(2)}, u32[]{:S(2)}) %collective-permute-start.6) | collective-permute-done | bytes 60448 | tf_op jit(solution)/shard_map/ppermute | solution.py:42
  34.5 2.8 %section_one.1 = (f32[336,128]{1,0:T(8,128)S(1)}, f32[336,128]{1,0:T(8,128)S(1)}, f32[336,128]{1,0:T(8,128)S(1)}, f32[672,128]{1,0:T(8,128)S(1)}, f32[2,32,128]{...) custom-call(f32[336,128]{1,0:T(8,128)S(1)} %bitcast.14, ...), custom_call_target="tpu_custom_call" | custom-call | tf_op jit(solution)/shard_map/section_one/pallas_call | solution.py:923
  37.4 0.7 %collective-permute-start.8 = (f32[2,32,128]{2,1,0:T(8,128)S(1)}, f32[2,32,128]{2,1,0:T(8,128)S(1)}, u32[]{:S(2)}, u32[]{:S(2)}) collective-permute-start(f32[2,32,128]{2,1,0:T(8,128)S(1)} %get-tuple-element.78), channel_id=1, source_target_pairs={{4,8},{12,16},{20,24},{8,4},{16,12},{24,20},{5,9},{13,17},{21,25},... | collective-permute-start | bytes 98312 | tf_op jit(solution)/shard_map/ppermute | solution.py:42
  38.0 5.0 %collective-permute-start.9 = (f32[2,32,128]{2,1,0:T(8,128)S(1)}, f32[2,32,128]{2,1,0:T(8,128)S(1)}, u32[]{:S(2)}, u32[]{:S(2)}) collective-permute-start(f32[2,32,128]{2,1,0:T(8,128)S(1)} %get-tuple-element.79), channel_id=1, source_target_pairs={{0,4},{8,12},{16,20},{24,28},{4,0},{12,8},{20,16},{28,24},{1,5},{9... | collective-permute-start | bytes 98312 | tf_op jit(solution)/shard_map/ppermute | solution.py:42
  43.0 2.4 %zone_sums.1.rest_0_ = f32[32,2,128]{2,1,0:T(2,128)} custom-call(f32[336,128]{1,0:T(8,128)S(1)} %get-tuple-element.75.lam_ref, f32[336,128]{1,0:T(8,128)S(1)} %get-tuple-element.74.y_ref, f32[720,128]{1,0:T(8,128)S(1)} %copy-done.1, f32[120,128]{1,0:T(8,128)S(1)} %get-tuple-element.61.fact_ref, f32[672,128]{1,0:T(8,128)S(1)} %get-tuple-element.82.old_outer_ref, ...), custom_call_target="tpu_custom_call" | custom-call | tf_op jit(solution)/shard_map/zone_sums/pallas_call | solution.py:923
  45.4 4.8 %all-to-all-start = ((f32[32,2,128]{2,1,0:T(2,128)}), f32[32,2,128]{2,1,0:T(2,128)S(1)}, u32[]{:S(2)}, u32[]{:S(2)}) async-start(f32[32,2,128]{2,1,0:T(2,128)} %get-tuple-element.88), calls=%async_computation | async-start | bytes 65536 | tf_op jit(solution)/shard_map/all_to_all | solution.py:1072
  50.2 3.5 %collective-permute-start.10 = (f32[2,32,128]{2,1,0:T(8,128)S(1)}, f32[2,32,128]{2,1,0:T(8,128)S(1)}, u32[]{:S(2)}, u32[]{:S(2)}) collective-permute-start(f32[2,32,128]{2,1,0:T(8,128)S(1)} %get-tuple-element.85), channel_id=1, source_target_pairs={{1,2},{2,1},{5,6},{6,5},{9,10},{10,9},{13,14},{14,13},{17,18},{18,... | collective-permute-start | bytes 98312 | tf_op jit(solution)/shard_map/ppermute | solution.py:42
  53.8 0.1 collective-permute-start.11
  53.9 1.5 %local_zero.1 = (f32[672,128]{1,0:T(8,128)S(1)}, f32[336,128]{1,0:T(8,128)S(1)}) custom-call(f32[336,128]{1,0:T(8,128)S(1)} %get-tuple-element.75.lam_ref, f32[336,128]{1,0:T(8,128)S(1)} %get-tuple-element.74.y_ref, f32[720,128]{1,0:T(8,128)S(1)} %copy-done.1), custom_call_target="tpu_custom_call" | custom-call | tf_op jit(solution)/shard_map/local_zero/pallas_call | solution.py:923
  55.3 0.5 collective-permute-done.10.from_y1
  55.8 2.1 %section_zero.1 = (f32[336,128]{1,0:T(8,128)}, f32[8,128]{1,0:T(8,128)S(1)}) custom-call(f32[336,128]{1,0:T(8,128)S(1)} %get-tuple-element.73.base_ref, f32[336,128]{1,0:T(8,128)S(1)} %get-tuple-element.74.y_ref, f32[720,128]{1,0:T(8,128)S(1)} %copy-done.1, f32[120,128]{1,0:T(8,128)S(1)} %get-tuple-element.61.fact_ref, ...), custom_call_target="tpu_custom_call" | custom-call | tf_op jit(solution)/shard_map/section_zero/pallas_call | solution.py:923
  57.9 0.6 %zone_total.1 = f32[2,128]{1,0:T(2,128)} custom-call(f32[32,2,128]{2,1,0:T(2,128)S(1)} %all-to-all-done.zone_ref, f32[8,128]{1,0:T(8,128)S(1)} %get-tuple-element.89.adjoint_ref), custom_call_target="tpu_custom_call" | custom-call | tf_op jit(solution)/shard_map/zone_total/pallas_call | solution.py:923
  (19 shorter events, 0.1 us)
Async XLA Ops:
  0.6 9.1 %copy-start.2 = (bf16[3,1,1,42,1024]{4,3,2,1,0:T(8,128)(2,1)S(1)}, bf16[3,1,1,42,1024]{4,3,2,1,0:T(8,128)(2,1)}, u32[]{:S(2)}) copy-start(bf16[3,1,1,42,1024]{4,3,2,1,0:T(8,128)(2,1)} %x_ref.9) | copy-start | bytes 774148
  0.6 9.1 %copy-start.3 = (f32[1,1,42,1024]{3,1,2,0:T(1,128)S(1)}, f32[1,1,42,1024]{3,1,2,0:T(1,128)}, u32[]{:S(2)}) copy-start(f32[1,1,42,1024]{3,1,2,0:T(1,128)} %param.16) | copy-start | bytes 516100
  4.5 8.2 %collective-permute-start = (f32[2,38,128]{2,1,0:T(8,128)}, f32[2,38,128]{2,1,0:T(8,128)S(1)}, u32[]{:S(2)}, u32[]{:S(2)}) collective-permute-start(f32[2,38,128]{2,1,0:T(8,128)} %get-tuple-element.52), channel_id=1, source_target_pairs={{4,8},{12,16},{20,24},{8,4},{16,12},{24,20},{5,9},{13,17},{21,25},... | collective-permute-start | bytes 116744 | tf_op jit(solution)/shard_map/ppermute | solution.py:42
  5.2 7.5 %collective-permute-start.1 = (f32[2,38,128]{2,1,0:T(8,128)}, f32[2,38,128]{2,1,0:T(8,128)S(1)}, u32[]{:S(2)}, u32[]{:S(2)}) collective-permute-start(f32[2,38,128]{2,1,0:T(8,128)} %get-tuple-element.53), channel_id=1, source_target_pairs={{0,4},{8,12},{16,20},{24,28},{4,0},{12,8},{20,16},{28,24},{1,5},{9... | collective-permute-start | bytes 116744 | tf_op jit(solution)/shard_map/ppermute | solution.py:42
  9.8 1.0 %copy-start = (f32[720,128]{1,0:T(8,128)S(1)}, f32[720,128]{1,0:T(8,128)}, u32[]{:S(2)}) copy-start(f32[720,128]{1,0:T(8,128)} %get-tuple-element.46.plan_ref) | copy-start | bytes 1105924
  10.8 1.9 %copy-start.4 = (f32[2,38,128]{2,1,0:T(8,128)S(1)}, f32[2,38,128]{2,1,0:T(8,128)}, u32[]{:S(2)}) copy-start(f32[2,38,128]{2,1,0:T(8,128)} %get-tuple-element.54.old_y1) | copy-start | bytes 116740
  10.8 1.9 %copy-start.5 = (f32[2,38,128]{2,1,0:T(8,128)S(1)}, f32[2,38,128]{2,1,0:T(8,128)}, u32[]{:S(2)}) copy-start(f32[2,38,128]{2,1,0:T(8,128)} %get-tuple-element.55.old_y2) | copy-start | bytes 116740
  10.8 6.3 %copy-start.1 = (f32[720,128]{1,0:T(8,128)S(1)}, f32[720,128]{1,0:T(8,128)}, u32[]{:S(2)}) copy-start(f32[720,128]{1,0:T(8,128)} %get-tuple-element.46.plan_ref) | copy-start | bytes 1105924
  12.7 6.4 %collective-permute-start.2 = (f32[2,38,128]{2,1,0:T(8,128)S(1)}, f32[2,38,128]{2,1,0:T(8,128)S(1)}, u32[]{:S(2)}, u32[]{:S(2)}) collective-permute-start(f32[2,38,128]{2,1,0:T(8,128)S(1)} %get-tuple-element.57), channel_id=1, source_target_pairs={{1,2},{2,1},{5,6},{6,5},{9,10},{10,9},{13,14},{14,13},{17,18},{18,... | collective-permute-start | bytes 116744 | tf_op jit(solution)/shard_map/ppermute | solution.py:42
  17.0 2.1 %collective-permute-start.3 = (f32[2,38,128]{2,1,0:T(8,128)S(1)}, f32[2,38,128]{2,1,0:T(8,128)S(1)}, u32[]{:S(2)}, u32[]{:S(2)}) collective-permute-start(f32[2,38,128]{2,1,0:T(8,128)S(1)} %get-tuple-element.58), channel_id=1, source_target_pairs={{0,1},{2,3},{1,0},{3,2},{4,5},{6,7},{5,4},{7,6},{8,9},{10,11},{9,8... | collective-permute-start | bytes 116744 | tf_op jit(solution)/shard_map/ppermute | solution.py:42
  22.1 6.0 %collective-permute-start.4 = (f32[2,59,128]{2,1,0:T(8,128)S(1)}, f32[2,59,128]{2,1,0:T(8,128)S(1)}, u32[]{:S(2)}, u32[]{:S(2)}) collective-permute-start(f32[2,59,128]{2,1,0:T(8,128)S(1)} %get-tuple-element.66), channel_id=1, source_target_pairs={{4,8},{12,16},{20,24},{8,4},{16,12},{24,20},{5,9},{13,17},{21,25},... | collective-permute-start | bytes 181256 | tf_op jit(solution)/shard_map/ppermute | solution.py:42
  22.8 5.8 %collective-permute-start.5 = (f32[2,59,128]{2,1,0:T(8,128)S(1)}, f32[2,59,128]{2,1,0:T(8,128)S(1)}, u32[]{:S(2)}, u32[]{:S(2)}) collective-permute-start(f32[2,59,128]{2,1,0:T(8,128)S(1)} %get-tuple-element.67), channel_id=1, source_target_pairs={{0,4},{8,12},{16,20},{24,28},{4,0},{12,8},{20,16},{28,24},{1,5},{9... | collective-permute-start | bytes 181256 | tf_op jit(solution)/shard_map/ppermute | solution.py:42
  28.7 5.9 %collective-permute-start.6 = (f32[2,59,128]{2,1,0:T(8,128)S(1)}, f32[2,59,128]{2,1,0:T(8,128)S(1)}, u32[]{:S(2)}, u32[]{:S(2)}) collective-permute-start(f32[2,59,128]{2,1,0:T(8,128)S(1)} %get-tuple-element.71), channel_id=1, source_target_pairs={{1,2},{2,1},{5,6},{6,5},{9,10},{10,9},{13,14},{14,13},{17,18},{18,... | collective-permute-start | bytes 181256 | tf_op jit(solution)/shard_map/ppermute | solution.py:42
  32.6 1.9 %collective-permute-start.7 = (f32[2,59,128]{2,1,0:T(8,128)S(1)}, f32[2,59,128]{2,1,0:T(8,128)S(1)}, u32[]{:S(2)}, u32[]{:S(2)}) collective-permute-start(f32[2,59,128]{2,1,0:T(8,128)S(1)} %get-tuple-element.72), channel_id=1, source_target_pairs={{0,1},{2,3},{1,0},{3,2},{4,5},{6,7},{5,4},{7,6},{8,9},{10,11},{9,8... | collective-permute-start | bytes 181256 | tf_op jit(solution)/shard_map/ppermute | solution.py:42
  37.4 8.0 %collective-permute-start.8 = (f32[2,32,128]{2,1,0:T(8,128)S(1)}, f32[2,32,128]{2,1,0:T(8,128)S(1)}, u32[]{:S(2)}, u32[]{:S(2)}) collective-permute-start(f32[2,32,128]{2,1,0:T(8,128)S(1)} %get-tuple-element.78), channel_id=1, source_target_pairs={{4,8},{12,16},{20,24},{8,4},{16,12},{24,20},{5,9},{13,17},{21,25},... | collective-permute-start | bytes 98312 | tf_op jit(solution)/shard_map/ppermute | solution.py:42
  38.0 7.4 %collective-permute-start.9 = (f32[2,32,128]{2,1,0:T(8,128)S(1)}, f32[2,32,128]{2,1,0:T(8,128)S(1)}, u32[]{:S(2)}, u32[]{:S(2)}) collective-permute-start(f32[2,32,128]{2,1,0:T(8,128)S(1)} %get-tuple-element.79), channel_id=1, source_target_pairs={{0,4},{8,12},{16,20},{24,28},{4,0},{12,8},{20,16},{28,24},{1,5},{9... | collective-permute-start | bytes 98312 | tf_op jit(solution)/shard_map/ppermute | solution.py:42
  45.4 12.5 %all-to-all-start = ((f32[32,2,128]{2,1,0:T(2,128)}), f32[32,2,128]{2,1,0:T(2,128)S(1)}, u32[]{:S(2)}, u32[]{:S(2)}) async-start(f32[32,2,128]{2,1,0:T(2,128)} %get-tuple-element.88), calls=%async_computation | async-start | bytes 65536 | tf_op jit(solution)/shard_map/all_to_all | solution.py:1072
  50.2 5.6 %collective-permute-start.10 = (f32[2,32,128]{2,1,0:T(8,128)S(1)}, f32[2,32,128]{2,1,0:T(8,128)S(1)}, u32[]{:S(2)}, u32[]{:S(2)}) collective-permute-start(f32[2,32,128]{2,1,0:T(8,128)S(1)} %get-tuple-element.85), channel_id=1, source_target_pairs={{1,2},{2,1},{5,6},{6,5},{9,10},{10,9},{13,14},{14,13},{17,18},{18,... | collective-permute-start | bytes 98312 | tf_op jit(solution)/shard_map/ppermute | solution.py:42
  53.8 2.0 %collective-permute-start.11 = (f32[2,32,128]{2,1,0:T(8,128)S(1)}, f32[2,32,128]{2,1,0:T(8,128)S(1)}, u32[]{:S(2)}, u32[]{:S(2)}) collective-permute-start(f32[2,32,128]{2,1,0:T(8,128)S(1)} %get-tuple-element.86), channel_id=1, source_target_pairs={{0,1},{2,3},{1,0},{3,2},{4,5},{6,7},{5,4},{7,6},{8,9},{10,11},{9,8... | collective-permute-start | bytes 98312 | tf_op jit(solution)/shard_map/ppermute | solution.py:42
